TPU v7x, 32 devices: a whole 2x2x4 slice. The times are simulated.
32 devices in a mesh: tm: 8 (over z, x), tile: 4 (over y, core).
Axes of the slice: x: 2, y: 2, z: 4, core: 2. Of those that a mesh axis runs over, the one named last changes fastest.
Arguments:
- operator: float32 [8, 768, 768], P('tm', 'tile'), may hold values from -4 to 20, as said below
- initial: float32 [8, 768, 768], P('tm', 'tile'), may hold values from -1 to 2, as said below
- block_sizes: int32 [8], P('tm'), may hold values from 512 to 768, as said below
- link_index: int32 [8, 512], P('tm'), may hold values from 0 to 511, as said below
- link_pair: bfloat16 [8, 768, 512], P('tm', 'tile'), may hold values from -0.4375 to 0.4375
- link_global: bfloat16 [8, 768, 512], P('tm', 'tile'), may hold values from -0.15625 to 0.15625
- schur_base: float32 [512, 512], P('tile'), may hold values from -4 to 20, as said below
- schur_start: float32 [512, 512], P('tile'), may hold values from -1 to 2, as said below
Outputs:
- link_diag: float32 [8, 256, 256], P('tm', 'tile')
- link_off: float32 [8, 256, 256], P('tm', 'tile')
- link_cross: float32 [8, 256, 512], P('tm', 'tile')
- global_schur: float32 [512, 512], P('tile')
- back_cols: float32 [8, 768, 512], P('tm', 'tile')
Inputs may be any that keep to these rules, and one draw needn't show every extreme that they name: `operator`: symmetric. `initial`: symmetric. `schur_base`: symmetric. `schur_start`: symmetric. `block_sizes`: some block has 768 live variables and some has 512. `link_index`: each row is a permutation of 0 to 511 that keeps every index j within its group of 128, j // 128.
All inputs are finite; a program needn't handle non-finite values.
Results may differ from a plain program's by a relative error of at most 0.0003.
Values may be sent and summed in bfloat16 or wider, within the bound.
No kernel may reach another device: no remote copies, remote signals or barrier semaphores. Data moves between devices by JAX's collectives and lax.ppermute only.
A program may use at most 64 MiB of HBM per device.

v0:
```python
import jax
import jax.numpy as jnp
from jax import lax
from jax.sharding import PartitionSpec as P

STEPS = 2


HIGH = lax.Precision.HIGHEST


def shifted_2(value, axis, by):
    size = lax.axis_size(axis)
    pairs = [(i, i + by) for i in range(size) if 0 <= i + by < size]
    return lax.ppermute(value, axis, pairs)


def batched(left_side, right_side):
    return jnp.einsum("bij,bjk->bik", left_side, right_side, precision=HIGH)


def fold_rows(left_side, piece):
    return batched(left_side, piece.astype(jnp.float32))


def fold_plain(left_side, piece):
    return jnp.dot(left_side, piece, precision=HIGH, preferred_element_type=jnp.float32)


def fold_blocks(left_side, piece):
    return jnp.einsum("bij,jk->bik", left_side, piece, precision=HIGH)


def place_terms(own_terms, next_terms, link_width):
    return jnp.concatenate(
        [
            own_terms[:, :, :link_width] + next_terms[:, :, :link_width],
            own_terms[:, :, link_width : 2 * link_width],
            own_terms[:, :, 2 * link_width :] + next_terms[:, :, link_width:],
        ],
        axis=2,
    )


def shards(
    operator, initial, block_sizes, link_index, link_pair, link_global, schur_base, schur_start
):
    tile_part = lax.axis_index("tile")
    block_count, row_count, block_order = operator.shape
    link_width = link_pair.shape[2] // 2
    row_ids = tile_part * row_count + lax.iota(jnp.int32, row_count)
    col_ids = lax.iota(jnp.int32, block_order)
    row_live = (row_ids[None, :] < block_sizes[:, None]).astype(jnp.float32)
    col_live = (col_ids[None, :] < block_sizes[:, None]).astype(jnp.float32)
    unit_rows = (row_ids[:, None] == col_ids[None, :]).astype(jnp.float32)

    def effective(matrix):
        return (
            matrix * row_live[:, :, None] * col_live[:, None, :]
            + unit_rows[None] * (1.0 - row_live)[:, :, None]
        )

    k_rows = effective(operator)
    x_rows = effective(initial)
    k_whole = lax.all_gather(k_rows, "tile", axis=1, tiled=True)
    for step in range(STEPS):
        left_side = batched(x_rows, k_whole)
        product = fold_rows(left_side, lax.all_gather(x_rows, "tile", axis=1, tiled=True))
        x_rows = 2.0 * x_rows - product
    live_half = row_live[:, :, None].astype(jnp.bfloat16)
    pair_live = link_pair * live_half
    glob_live = jnp.take_along_axis(link_global, link_index[:, None, :], axis=2) * live_half
    links_rows = jnp.concatenate([pair_live, glob_live], axis=2)
    solved = fold_rows(x_rows, lax.all_gather(links_rows, "tile", axis=1, tiled=True))
    own_links = links_rows.astype(jnp.float32)
    e_rows = own_links[:, :, :link_width]
    f_rows = own_links[:, :, link_width : 2 * link_width]
    g_rows = own_links[:, :, 2 * link_width :]
    y_e = solved[:, :, :link_width]
    y_f = solved[:, :, link_width : 2 * link_width]
    y_g = solved[:, :, 2 * link_width :]

    def inner(left_side, right_side):
        return jnp.einsum("bri,brj->bij", left_side, right_side, precision=HIGH)

    own_terms = jnp.concatenate(
        [inner(f_rows, y_f), inner(e_rows, y_f), inner(f_rows, y_g)], axis=2
    )
    next_terms = jnp.concatenate([inner(e_rows, y_e), inner(e_rows, y_g)], axis=2)
    global_terms = jnp.einsum("bri,brj->ij", g_rows, y_g, precision=HIGH)
    came = shifted_2(next_terms, "tm", -1)
    shifted = jnp.concatenate([next_terms[1:], came], axis=0)
    summed = lax.psum_scatter(
        place_terms(own_terms, shifted, link_width), "tile", scatter_dimension=1, tiled=True
    )
    share = lax.psum_scatter(global_terms, "tile", scatter_dimension=0, tiled=True)
    panel = lax.psum(share, "tm")
    global_schur = schur_base + panel
    first = fold_plain(schur_start, lax.all_gather(global_schur, "tile", axis=0, tiled=True))
    second = fold_plain(first, lax.all_gather(schur_start, "tile", axis=0, tiled=True))
    inverse_rows = 2.0 * schur_start - second
    back_cols = fold_blocks(y_g, lax.all_gather(inverse_rows, "tile", axis=0, tiled=True))
    link_diag = summed[:, :, :link_width]
    link_off = summed[:, :, link_width : 2 * link_width]
    link_cross = summed[:, :, 2 * link_width :]
    return (link_diag, link_off, link_cross, global_schur, back_cols)


def solution(mesh):
    return jax.shard_map(
        shards,
        mesh=mesh,
        in_specs=(
            P("tm", "tile", None),
            P("tm", "tile", None),
            P("tm"),
            P("tm", None),
            P("tm", "tile", None),
            P("tm", "tile", None),
            P("tile", None),
            P("tile", None),
        ),
        out_specs=(
            P("tm", "tile", None),
            P("tm", "tile", None),
            P("tm", "tile", None),
            P("tile", None),
            P("tm", "tile", None),
        ),
        check_vma=False,
    )
```

profile of v0, /device:TPU:0, one launch (start us, length us, event | category | flops | bytes accessed | tf_op | source)
XLA Modules:
  0.0 320.4 jit_solution(17817479443745114297)
XLA Ops:
  7.9 2.5 select_add_fusion.1
  10.5 0.7 all-gather.10.cloned.1.call-update
  11.3 26.1 %all-gather.8.cloned.1.call-done = f32[1,768,768]{2,1,0:T(8,128)} async-done(((f32[1,192,768]{2,1,0:T(8,128)}), f32[1,768,768]{2,1,0:T(8,128)}) %all-gather.8.cloned.1.call-update) | async-done | bytes 2359312 | tf_op jit(solution)/shard_map/all_gather | solution.py:65
  37.4 3.6 %fusion.6 = f32[192,768]{1,0:T(8,128)S(1)} fusion(f32[1,768,768]{2,1,0:T(8,128)} %all-gather.8.cloned.1.call-done, f32[1,192,768]{2,1,0:T(8,128)} %get-tuple-element.22), kind=kOutput, calls=%fused_computation.7 | convolution fusion | flops 1358954496 | bytes 3538944 | tf_op jit(solution)/shard_map/bij,bjk->bik/dot_general | solution.py:19
  41.0 22.0 %all-gather.10.cloned.1.call-done = f32[1,768,768]{2,1,0:T(8,128)} async-done(((f32[1,192,768]{2,1,0:T(8,128)}), f32[1,768,768]{2,1,0:T(8,128)}) %all-gather.10.cloned.1.call-update) | async-done | bytes 2359312 | tf_op jit(solution)/shard_map/all_gather | solution.py:68
  63.1 4.2 %fusion.25 = f32[1,192,768]{2,1,0:T(8,128)} fusion(f32[192,768]{1,0:T(8,128)S(1)} %fusion.6, f32[1,768,768]{2,1,0:T(8,128)} %all-gather.10.cloned.1.call-done, f32[1,192,768]{2,1,0:T(8,128)S(1)} %copy-done), kind=kOutput, calls=%fused_computation.18 | convolution fusion | flops 1359249408 | bytes 4128768 | tf_op jit(solution)/shard_map/bij,bjk->bik/dot_general | solution.py:19
  67.3 0.0 all-gather.14.cloned.1.call-start
  67.4 0.1 copy.28
  67.5 0.8 copy.27
  68.4 2.6 gather_fusion
  71.0 1.2 broadcast_multiply_fusion
  72.1 0.9 pad_maximum_fusion.2
  73.1 2.0 copy.29
  75.1 0.0 reduce-scatter.2.cloned.1.call-start
  75.2 2.5 fusion.4
  77.7 13.8 %all-gather.12.cloned.1.call-done = f32[1,768,768]{2,1,0:T(8,128)} async-done(((f32[1,192,768]{2,1,0:T(8,128)}), f32[1,768,768]{2,1,0:T(8,128)}) %all-gather.12.cloned.1.call-update) | async-done | bytes 2359312 | tf_op jit(solution)/shard_map/all_gather | solution.py:68
  91.5 3.6 %fusion.22 = f32[192,768]{1,0:T(8,128)S(1)} fusion(f32[192,768]{1,0:T(8,128)} %fusion.4, f32[1,768,768]{2,1,0:T(8,128)} %all-gather.12.cloned.1.call-done, f32[1,192,768]{2,1,0:T(8,128)S(1)} %copy-done.2), kind=kOutput, calls=%fused_computation.17 | convolution fusion | flops 1359249408 | bytes 4128768 | tf_op jit(solution)/shard_map/bij,bjk->bik/dot_general | solution.py:19
  95.2 18.1 %all-gather.14.cloned.1.call-done = bf16[1,768,1024]{2,1,0:T(8,128)(2,1)} async-done(((bf16[1,192,1024]{2,1,0:T(8,128)(2,1)}), bf16[1,768,1024]{2,1,0:T(8,128)(2,1)}) %all-gather.14.cloned.1.call-update) | async-done | bytes 1572880 | tf_op jit(solution)/shard_map/all_gather | solution.py:74
  113.2 2.5 fusion.10
  115.7 1.6 fusion.30
  117.4 0.0 all-reduce.4.cloned.1.call-start
  117.4 25.0 %reduce-scatter.2.cloned.1.call-done = f32[128,512]{1,0:T(8,128)} async-done(((f32[512,512]{1,0:T(8,128)}), f32[128,512]{1,0:T(8,128)}) %reduce-scatter.2.cloned.1.call-update) | async-done | bytes 262160 | tf_op jit(solution)/shard_map/reduce_scatter | solution.py:96
  142.5 74.1 %all-reduce.4.cloned.1.call-done = f32[128,512]{1,0:T(8,128)} async-done(((f32[128,512]{1,0:T(8,128)}), f32[128,512]{1,0:T(8,128)}) %all-reduce.4.cloned.1.call-update) | async-done | bytes 262160 | tf_op jit(solution)/shard_map/psum | solution.py:97
  216.6 1.7 add.81
  218.3 0.7 all-gather.18.cloned.1.call-update
  219.1 0.7 convolution_bitcast_fusion.1
  219.8 0.4 convolution_bitcast_fusion.4
  220.2 0.1 pad_maximum_fusion.1
  220.2 1.5 collective-permute-start
  221.7 0.4 convolution_bitcast_fusion.3
  222.2 17.5 %collective-permute-done = f32[1,256,768]{1,2,0:T(8,128)S(1)} collective-permute-done((f32[1,256,768]{1,2,0:T(8,128)S(1)}, f32[1,256,768]{1,2,0:T(8,128)S(1)}, u32[]{:S(2)}, u32[]{:S(2)}) %collective-permute-start) | collective-permute-done | bytes 786464 | tf_op jit(solution)/shard_map/ppermute | solution.py:15
  239.6 0.4 slice_add_fusion.1
  240.1 0.7 slice_add_fusion
  240.7 0.1 pad_maximum_fusion
  240.8 1.9 copy.32
  242.8 0.0 all-gather.20.cloned.1.call-start
  242.9 3.0 fusion.41
  245.9 7.2 %all-gather.18.cloned.1.call-done = f32[512,512]{1,0:T(8,128)} async-done(((f32[128,512]{1,0:T(8,128)}), f32[512,512]{1,0:T(8,128)}) %all-gather.18.cloned.1.call-update) | async-done | bytes 1048592 | tf_op jit(solution)/shard_map/all_gather | solution.py:100
  253.1 2.7 convolution_subtract_fusion
  255.8 0.6 dynamic-slice
  257.0 34.5 %all-reduce.6.cloned.1.call-done = f32[1,256,1024]{2,0,1:T(1,128)} async-done(((f32[1,256,1024]{2,0,1:T(1,128)}), f32[1,256,1024]{2,0,1:T(1,128)}) %all-reduce.6.cloned.1.call-update) | async-done | bytes 1048592
  291.6 1.2 constant_dynamic-slice_fusion.2
  292.8 0.7 copy.35
  293.5 1.1 constant_dynamic-slice_fusion
  294.6 0.6 copy.33
  295.2 0.6 copy.34
  295.8 14.9 %all-gather.20.cloned.1.call-done = f32[512,512]{1,0:T(8,128)} async-done(((f32[128,512]{1,0:T(8,128)}), f32[512,512]{1,0:T(8,128)}) %all-gather.20.cloned.1.call-update) | async-done | bytes 1048592 | tf_op jit(solution)/shard_map/all_gather | solution.py:102
  310.8 2.8 convolution_bitcast_fusion.2
  (43 shorter events, 0.5 us)
Async XLA Ops:
  7.2 30.2 %all-gather.8.cloned.1.call-start = ((), (), s32[]{:S(2)}) async-start(), calls=%async_computation.1 | async-start | bytes 2949120 | tf_op jit(solution)/shard_map/all_gather | solution.py:65
  10.4 52.6 %copy-start = (f32[1,192,768]{2,1,0:T(8,128)S(1)}, f32[1,192,768]{2,1,0:T(8,128)}, u32[]{:S(2)}) copy-start(f32[1,192,768]{2,1,0:T(8,128)} %get-tuple-element.22) | copy-start | bytes 1769476
  10.5 52.6 %all-gather.10.cloned.1.call-start = ((), (), s32[]{:S(2)}) async-start(), calls=%async_computation.2 | async-start | bytes 2949120 | tf_op jit(solution)/shard_map/all_gather | solution.py:68
  11.2 80.3 %all-gather.12.cloned.1.call-start = ((), (), s32[]{:S(2)}) async-start(), calls=%async_computation.3 | async-start | bytes 2949120 | tf_op jit(solution)/shard_map/all_gather | solution.py:68
  41.0 26.4 %copy-start.6 = (bf16[1,192,512]{2,1,0:T(8,128)(2,1)S(1)}, bf16[1,192,512]{2,1,0:T(8,128)(2,1)}, u32[]{:S(2)}) copy-start(bf16[1,192,512]{2,1,0:T(8,128)(2,1)} %param.13) | copy-start | bytes 589828
  41.0 26.5 %copy-start.7 = (bf16[1,192,512]{2,1,0:T(8,128)(2,1)S(1)}, bf16[1,192,512]{2,1,0:T(8,128)(2,1)}, u32[]{:S(2)}) copy-start(bf16[1,192,512]{2,1,0:T(8,128)(2,1)} %param.12) | copy-start | bytes 589828
  41.0 27.4 %copy-start.8 = (s32[1,512]{1,0:T(1,128)S(1)}, s32[1,512]{1,0:T(1,128)}, u32[]{:S(2)}) copy-start(s32[1,512]{1,0:T(1,128)} %param.11) | copy-start | bytes 6148
  67.3 45.9 %all-gather.14.cloned.1.call-start = ((), (), s32[]{:S(2)}) async-start(), calls=%async_computation.4 | async-start | bytes 1966080 | tf_op jit(solution)/shard_map/all_gather | solution.py:74
  68.4 6.8 %copy-start.1 = (f32[1,768,768]{2,1,0:T(8,128)S(1)}, f32[1,768,768]{2,1,0:T(8,128)}, u32[]{:S(2)}) copy-start(f32[1,768,768]{2,1,0:T(8,128)} %all-gather.8.cloned.1.call-done) | copy-start | bytes 7077892
  68.4 6.8 %copy-start.2 = (f32[1,192,768]{2,1,0:T(8,128)S(1)}, f32[1,192,768]{2,1,0:T(8,128)}, u32[]{:S(2)}) copy-start(f32[1,192,768]{2,1,0:T(8,128)} %fusion.25) | copy-start | bytes 1769476
  75.1 67.3 %reduce-scatter.2.cloned.1.call-start = ((), (), s32[]{:S(2)}) async-start(), calls=%async_computation.5 | async-start | bytes 1310720 | tf_op jit(solution)/shard_map/reduce_scatter | solution.py:96
  95.1 20.6 %copy-start.4 = (bf16[512,192]{1,0:T(8,128)(2,1)S(1)}, bf16[512,192]{1,0:T(8,128)(2,1)}, u32[]{:S(2)}) copy-start(bf16[512,192]{1,0:T(8,128)(2,1)} %gather_fusion) | copy-start | bytes 589828
  95.2 121.4 %copy-start.5 = (f32[128,512]{1,0:T(8,128)S(1)}, f32[128,512]{1,0:T(8,128)}, u32[]{:S(2)}) copy-start(f32[128,512]{1,0:T(8,128)} %param.14) | copy-start | bytes 786436
  117.4 99.2 %all-reduce.4.cloned.1.call-start = ((), (), s32[]{:S(2)}) async-start(), calls=%async_computation.6 | async-start | bytes 524288 | tf_op jit(solution)/shard_map/psum | solution.py:97
  142.4 100.4 %all-gather.16.cloned.1.call-start = ((), (), s32[]{:S(2)}) async-start(), calls=%async_computation.7 | async-start | bytes 1310720 | tf_op jit(solution)/shard_map/all_gather | solution.py:99
  218.3 34.8 %all-gather.18.cloned.1.call-start = ((), (), s32[]{:S(2)}) async-start(), calls=%async_computation.8 | async-start | bytes 1310720 | tf_op jit(solution)/shard_map/all_gather | solution.py:100
  219.0 72.5 %all-reduce.6.cloned.1.call-start = ((), (), s32[]{:S(2)}) async-start(), calls=%async_computation.10 | async-start | bytes 2097152
  220.2 19.4 %collective-permute-start = (f32[1,256,768]{1,2,0:T(8,128)S(1)}, f32[1,256,768]{1,2,0:T(8,128)S(1)}, u32[]{:S(2)}, u32[]{:S(2)}) collective-permute-start(f32[1,256,768]{1,2,0:T(8,128)S(1)} %pad_maximum_fusion.1), channel_id=1, source_target_pairs={{4,0},{8,4},{12,8},{16,12},{20,16},{24,20},{28,24},{5,1},{9,5},{13... | collective-permute-start | bytes 2359304 | tf_op jit(solution)/shard_map/ppermute | solution.py:15
  240.7 2.1 copy-start.3
  242.8 13.0 %copy-start.9 = (u32[32]{0:T(128)S(1)}, u32[32]{0:T(128)}, u32[]{:S(2)}) copy-start(u32[32]{0:T(128)} %constant.37) | copy-start | bytes 388
  242.8 68.0 %all-gather.20.cloned.1.call-start = ((), (), s32[]{:S(2)}) async-start(), calls=%async_computation.9 | async-start | bytes 1310720 | tf_op jit(solution)/shard_map/all_gather | solution.py:102
Sparse Core Ops, SparseCore 0:
  10.6 26.7 all-gather.7
  38.9 24.0 all-gather.9
  67.4 24.0 all-gather.11
  93.5 19.6 all-gather.13
  117.5 24.8 reduce-scatter.1
  146.0 70.5 all-reduce.3
  218.7 16.0 all-gather.15
  236.3 16.7 all-gather.17
  255.4 36.0 all-reduce.5
  293.6 17.0 all-gather.19
where the time goes:
time: 321 us; the launch traced here: 320 us
  waiting for transfers between devices  255 us (79%)
  matrix products  29.2 us (9%)
  between operations  15.7 us (5%)
  local copies, waits for them, and re-layouts  12.4 us (4%)
  other arithmetic  6.45 us (2%)
    psum x1, waiting for transfers between devices, shards(): panel = lax.psum(share, 'tm')  74.1 us
    unnamed x11, waiting for transfers between devices  36 us
    all_gather x2, waiting for transfers between devices, shards(): lax.all_gather(x_rows, 'tile', axis=1, tiled=True)  35.9 us
    all_gather x1, waiting for transfers between devices, shards(): k_whole = lax.all_gather(k_rows, 'tile', axis=1, tiled=True)  26.1 us
    reduce_scatter x1, waiting for transfers between devices, shards(): lax.psum_scatter(global_terms, 'tile', scatter_dimension=0, tiled=True)  25 us
    all_gather x1, waiting for transfers between devices, shards(): lax.all_gather(links_rows, 'tile', axis=1, tiled=True)  18.1 us
    ppermute x1, waiting for transfers between devices, shifted_2(): return lax.ppermute(value, axis, pairs)  17.5 us
    dot_general x5, matrix products, batched(): return jnp.einsum('bij,bjk->bik', left_side, right_side, precision=HIGH)  16.5 us
  transfers between devices with their start and end apart: 11, of which 10 were waited for; matrix products, arithmetic and copies ran while one was open for 10% of the time, Pallas kernels for 0%

commit v1 on v0

v1 whole, which is shorter than its diff:
```python
import functools

import jax
import jax.numpy as jnp
from jax import lax
from jax.experimental import pallas as pl
from jax.experimental.pallas import tpu as pltpu
from jax.sharding import PartitionSpec as P

BF16 = jnp.bfloat16
F32 = jnp.float32
TERMS = 3
VMEM_BYTES = 32 * 2**20


def halves(value):
    high = value.astype(BF16)
    return high, (value - high.astype(F32)).astype(BF16)


def dot(left_side, right_side):
    return jnp.dot(left_side, right_side, preferred_element_type=F32)


def both(value):
    return jnp.concatenate(halves(value), axis=1)


def stacked(value):
    return jnp.concatenate(halves(value), axis=0)


def quadrants(product):
    rows, cols = product.shape[0] // 2, product.shape[1] // 2
    return (product[:rows, :cols] + product[:rows, cols:]) + (
        product[rows:, :cols] + product[rows:, cols:]
    )


def at_rows(start, size, unit=16):
    return pl.ds(pl.multiple_of(start, unit), size)


def live_rows(info, half):
    near, size = info[0] // 2, info[1]
    ids = lax.broadcasted_iota(jnp.int32, (half, 1), 0)
    return jnp.concatenate(
        [(ids + near * half) < size, (ids + (1 - near) * half) < size], axis=0
    )


def put_rows(info, pieces, target, offset=0):
    rows = pieces[0].shape[0]
    core = info[0] % 2
    target[at_rows(offset + core * rows, rows), :] = pieces[0]
    target[at_rows(offset + (1 - core) * rows, rows), :] = pieces[1]


def spread(info, own, other, top, bottom, block):
    rows, order = own.shape
    half = order // 2
    near, core = info[0] // 2, info[0] % 2
    for ref, place in ((own, core), (other, 1 - core)):
        for side in range(2):
            cols = pl.ds(pl.multiple_of((near if side == 0 else 1 - near) * half, 128), half)
            value = ref[:, cols]
            high, low = halves(value)
            top[at_rows(place * rows, rows), side * half : (side + 1) * half] = high
            top[at_rows(half + place * rows, rows), side * half : (side + 1) * half] = low
            if side == 1:
                block[at_rows(place * rows, rows), :] = value
    high, low = halves(block[...].T)
    bottom[0:half, 0:half] = high
    bottom[half : 2 * half, 0:half] = low


def corner(info, own, other, target, first):
    rows, half = own.shape
    core = info[0] % 2
    for ref, place in ((own, core), (other, 1 - core)):
        high, low = halves(ref[...])
        target[at_rows(place * rows, rows), first : first + half] = high
        target[at_rows(half + place * rows, rows), first : first + half] = low


def times_x(top, bottom, columns):
    return jnp.concatenate(
        [quadrants(dot(top[...], columns)), quadrants(dot(bottom[...], columns))], axis=0
    )


def times_k(top, bottom, last, columns):
    half = last.shape[1]
    low = dot(bottom[...], columns[:half]) + dot(last[...], columns[half:])
    return jnp.concatenate([quadrants(dot(top[...], columns)), quadrants(low)], axis=0)


def prepare_kernel(
    info, x_own, x_core, x_far, x_cross, k_own, k_core, g_own, g_core, g_far, g_cross, index,
    x_top, x_bottom, k_top, k_bottom, links, first, block, gathered,
):
    half = x_own.shape[1] // 2
    width = g_own.shape[1]
    spread(info, x_own, x_core, x_top, x_bottom, block)
    corner(info, x_far, x_cross, x_bottom, half)
    put_rows(info, (g_own[...], g_core[...]), gathered)
    put_rows(info, (g_far[...], g_cross[...]), gathered, half)
    live = live_rows(info, half)
    hot = lax.broadcasted_iota(jnp.int32, (width, width), 0) == index[...]
    chosen = dot(gathered[...], hot.astype(F32).astype(BF16))
    links[...] = jnp.where(live, chosen, 0.0).astype(BF16)
    group = width // 4
    columns = links[:, pl.ds(pl.multiple_of(info[0] * group, 128), group)]
    for ref, place in ((x_top, 0), (x_bottom, half)):
        product = dot(ref[...], columns)
        product = product[:half] + product[half:]
        first[place : place + half, :] = both(
            jnp.where(live[place : place + half], product, 0.0)
        )
    spread(info, k_own, k_core, k_top, k_bottom, block)


def solve(columns, first, live, x_top, x_bottom, k_top, k_bottom, k_last):
    state = columns
    for step in range(TERMS):
        product = times_k(k_top, k_bottom, k_last, first)
        state = columns + state - jnp.where(live, product, 0.0)
        result = jnp.where(live, times_x(x_top, x_bottom, both(state)), 0.0)
        first = both(result)
    return result


def global_kernel(
    info, k_far, k_cross, x_top, x_bottom, k_top, k_bottom, links, first, base,
    keep, send, y_own, y_core, y_far, y_cross, k_last, pack, solved,
):
    half = k_far.shape[1]
    rows = k_far.shape[0]
    width = links.shape[1]
    group = width // 4
    part, core = info[0], info[0] % 2
    corner(info, k_far, k_cross, k_last, 0)
    live = live_rows(info, half)
    columns = links[:, pl.ds(pl.multiple_of(part * group, 128), group)].astype(F32)
    result = solve(columns, first[...], live, x_top, x_bottom, k_top, k_bottom, k_last)
    solved[...] = result
    y_own[...] = solved[at_rows(core * rows, rows), :]
    y_core[...] = solved[at_rows((1 - core) * rows, rows), :]
    y_far[...] = solved[at_rows(half + core * rows, rows), :]
    y_cross[...] = solved[at_rows(half + (1 - core) * rows, rows), :]
    left_side = stacked(result.T)

    def block(shift):
        place = pl.ds(pl.multiple_of(((part + shift) % 4) * group, 128), group)
        both_parts = dot(left_side, links[:, place])
        added = jnp.where(info[2] == 0, base[:, place], 0.0)
        return both_parts[:group] + both_parts[group:] + added

    pack[0:group, :] = block(0)
    pack[group : 2 * group, :] = block(1)
    across = block(2)
    pack[2 * group :, :] = jnp.where(
        part < 2, across[: group // 2, :], across.T[group // 2 :, :]
    )
    size = keep.shape[0]
    side = info[2] % 2
    keep[...] = pack[at_rows(side * size, size, 8), :]
    send[...] = pack[at_rows((1 - side) * size, size, 8), :]


def pair_kernel(
    info, p_own, p_core, p_far, p_cross, x_top, x_bottom, k_top, k_bottom, k_last, links,
    own_terms, off_terms, next_terms, gathered,
):
    half = k_last.shape[1]
    width = p_own.shape[1]
    link = width // 2
    share = link // 4
    part = info[0]
    put_rows(info, (p_own[...], p_core[...]), gathered)
    put_rows(info, (p_far[...], p_cross[...]), gathered, half)
    live = live_rows(info, half)
    masked = jnp.where(live, gathered[...], jnp.zeros((), BF16))
    source = lax.broadcasted_iota(jnp.int32, (width, 2 * share), 0)
    place = lax.broadcasted_iota(jnp.int32, (width, 2 * share), 1)
    wanted = part * share + place + jnp.where(place < share, 0, link - share)
    columns = dot(masked, (source == wanted).astype(F32).astype(BF16))
    product = times_x(x_top, x_bottom, both(columns))
    first = both(jnp.where(live, product, 0.0))
    result = solve(columns, first, live, x_top, x_bottom, k_top, k_bottom, k_last)
    left_side = stacked(result.T)
    terms = dot(left_side, masked)
    terms = terms[: 2 * share] + terms[2 * share :]
    cross = dot(left_side, links[...])
    cross = cross[: 2 * share] + cross[2 * share :]
    next_terms[:, :link] = terms[:share, :link]
    next_terms[:, link:] = cross[:share]
    off_terms[...] = terms[:share, link:]
    own_terms[:, :link] = terms[share:, link:]
    own_terms[:, link:] = cross[share:]


def start_kernel(
    info, s_own, s_core, s_far, s_cross, y_own, y_core, y_far, y_cross, start, scaled
):
    part = info[0]
    group = s_own.shape[0]
    width = s_own.shape[1]
    total = None
    for ref, mask, rows in (
        (s_own, 0, y_own), (s_core, 1, y_core), (s_far, 2, y_far), (s_cross, 3, y_cross)
    ):
        value = both(ref[...])
        start[at_rows((part ^ mask) * group, group), :] = value
        product = quadrants(dot(stacked(rows[...]), value))
        total = product if total is None else total + product
    scaled[...] = total


def back_kernel(
    info, *refs
):
    sums, (start, scaled, own_terms, came), outs = refs[:8], refs[8:12], refs[12:]
    link_diag, link_cross, schur, back, whole, full = outs
    part, side = info[0], info[2] % 2
    size = sums[0].shape[0]
    group = schur.shape[0]
    width = schur.shape[1]
    for mask in range(4):
        for half in range(2):
            place = at_rows((part ^ mask) * (2 * size) + (side ^ half) * size, size, 8)
            whole[place, :] = sums[2 * mask + half][...]
    for row in range(4):
        first = row * 2 * size
        diagonal = whole[first : first + group, :]
        after = whole[first + group : first + 2 * group, :]
        nxt = (row + 1) % 4
        full[row * group : (row + 1) * group, row * group : (row + 1) * group] = diagonal
        full[row * group : (row + 1) * group, nxt * group : (nxt + 1) * group] = after
        full[nxt * group : (nxt + 1) * group, row * group : (row + 1) * group] = after.T
        if row < 2:
            other = (row + 2) * 2 * size
            across = jnp.concatenate(
                [whole[first + 2 * group : first + 2 * size, :],
                 whole[other + 2 * group : other + 2 * size, :]], axis=0
            )
            far = row + 2
            full[row * group : (row + 1) * group, far * group : (far + 1) * group] = across
            full[far * group : (far + 1) * group, row * group : (row + 1) * group] = across.T
    schur[...] = full[at_rows(part * group, group, 8), :]
    value = scaled[...]
    product = quadrants(dot(stacked(value), both(full[...])))
    product = quadrants(dot(stacked(product), start[...]))
    back[...] = 2.0 * value - product
    link = link_diag.shape[1]
    link_diag[...] = own_terms[:, :link] + came[:, :link]
    link_cross[...] = own_terms[:, link:] + came[:, link:]


def call(kernel, outs, scratch, flops, *args):
    smem = pl.BlockSpec(memory_space=pltpu.SMEM)
    vmem = pl.BlockSpec(memory_space=pltpu.VMEM)
    moved = sum(a.size * a.dtype.itemsize for a in args)
    return pl.pallas_call(
        kernel,
        out_shape=[jax.ShapeDtypeStruct(shape, dtype) for shape, dtype in outs],
        in_specs=[smem] + [vmem] * (len(args) - 1),
        out_specs=[vmem] * len(outs),
        scratch_shapes=[pltpu.VMEM(shape, dtype) for shape, dtype in scratch],
        compiler_params=pltpu.CompilerParams(vmem_limit_bytes=VMEM_BYTES),
        cost_estimate=pl.CostEstimate(flops=flops, bytes_accessed=moved, transcendentals=0),
        name=kernel.__name__,
    )(*args)


def shards(
    blocks, operator, initial, block_sizes, link_index, link_pair, link_global, schur_base,
    schur_start,
):
    part, block = lax.axis_index("tile"), lax.axis_index("tm")
    info = jnp.stack([part, block_sizes[0], block]).astype(jnp.int32)
    operator, initial = operator[0], initial[0]
    pair, glob = link_pair[0], link_global[0]
    rows, order = operator.shape
    half = order // 2
    link, width = pair.shape[1] // 2, glob.shape[1]
    group, share = width // 4, link // 4
    size = group + group // 4

    def tile_swap(value, mask):
        return lax.ppermute(value, "tile", [(i, i ^ mask) for i in range(4)])

    def block_swap(value, mask):
        return lax.ppermute(value, "tm", [(i, i ^ mask) for i in range(blocks)])

    def gathered(own, sent):
        far = tile_swap(sent, 2)
        return own, tile_swap(own, 1), far, tile_swap(far, 1)

    near_cols = (part // 2) * half
    g_all = gathered(glob, glob)
    x_all = gathered(initial, lax.dynamic_slice_in_dim(initial, near_cols, half, 1))
    k_all = gathered(operator, lax.dynamic_slice_in_dim(operator, near_cols, half, 1))
    p_all = gathered(pair, pair)
    s_all = gathered(schur_start, schur_start)

    apply_flops = 2 * 2 * order * order * 2 * group
    x_top, x_bottom, k_top, k_bottom, links, first = call(
        prepare_kernel,
        [((2 * half, order), BF16), ((2 * half, order), BF16), ((2 * half, order), BF16),
         ((2 * half, half), BF16), ((order, width), BF16), ((order, 2 * group), BF16)],
        [((half, half), F32), ((order, width), BF16)],
        2 * apply_flops,
        info, *x_all, *k_all[:2], *g_all, link_index,
    )
    keep, send, y_own, y_core, y_far, y_cross, k_last = call(
        global_kernel,
        [((size, group), F32)] * 2 + [((rows, group), F32)] * 4 + [((2 * half, half), BF16)],
        [((2 * size, group), F32), ((order, group), F32)],
        7 * apply_flops,
        info, *k_all[2:], x_top, x_bottom, k_top, k_bottom, links, first, schur_base,
    )

    total = keep + block_swap(send, 1)
    step = 2
    while step < blocks:
        if 2 * step < blocks:
            near = total + block_swap(total, step)
            far = block_swap(total, 2 * step) + block_swap(total, 3 * step)
            total = near + far
            step *= 4
        else:
            total = total + block_swap(total, step)
            step *= 2

    def diagonal_swap(value):
        pairs = [
            (b * 4 + i, (b ^ 1) * 4 + (i ^ 2)) for b in range(blocks) for i in range(4)
        ]
        return lax.ppermute(value, ("tm", "tile"), pairs)

    here = (total, block_swap(total, 1))
    there = (tile_swap(total, 2), diagonal_swap(total))
    sums = []
    for pieces in (here, there):
        sums += [*pieces, *(tile_swap(piece, 1) for piece in pieces)]

    own_terms, off_terms, next_terms = call(
        pair_kernel,
        [((share, link + width), F32), ((share, link), F32), ((share, link + width), F32)],
        [((order, 2 * link), BF16)],
        8 * apply_flops,
        info, *p_all, x_top, x_bottom, k_top, k_bottom, k_last, links,
    )
    came = lax.ppermute(next_terms, "tm", [(i + 1, i) for i in range(blocks - 1)])
    start, scaled = call(
        start_kernel,
        [((width, 2 * width), BF16), ((rows, width), F32)],
        [],
        apply_flops,
        info, *s_all, y_own, tile_swap(y_core, 1), tile_swap(y_far, 2), tile_swap(y_cross, 3),
    )
    link_diag, link_cross, global_schur, back_cols = call(
        back_kernel,
        [((share, link), F32), ((share, width), F32), ((group, width), F32),
         ((rows, width), F32)],
        [((8 * size, group), F32), ((width, width), F32)],
        apply_flops,
        info, *sums, start, scaled, own_terms, came,
    )
    return (
        link_diag[None], off_terms[None], link_cross[None], global_schur, back_cols[None],
    )


def solution(mesh):
    return jax.shard_map(
        functools.partial(shards, mesh.shape["tm"]),
        mesh=mesh,
        in_specs=(
            P("tm", "tile", None),
            P("tm", "tile", None),
            P("tm"),
            P("tm", None),
            P("tm", "tile", None),
            P("tm", "tile", None),
            P("tile", None),
            P("tile", None),
        ),
        out_specs=(
            P("tm", "tile", None),
            P("tm", "tile", None),
            P("tm", "tile", None),
            P("tile", None),
            P("tm", "tile", None),
        ),
        check_vma=False,
    )
```

time: 321 us -> 75.4 us (0.23)
  the two profiles are of different devices: /device:TPU:0 before, /device:TPU:9 now
where the time goes in v1:
time: 75.4 us; the launch traced here: 75 us
  starting transfers between devices  25.9 us (34%)
  waiting for transfers between devices  22.7 us (30%)
  Pallas kernels  20.4 us (27%)
  local copies, waits for them, and re-layouts  4.52 us (6%)
  between operations  1.5 us (2%)
    ppermute x23, waiting for transfers between devices, tile_swap(): return lax.ppermute(value, 'tile', [(i, i ^ mask) for i in range(4)])  20.4 us
    pallas_call x5, Pallas kernels, call(): pl.pallas_call(kernel, out_shape=[jax.ShapeDtypeStruct(shape, dtype) for...  20.4 us
    ppermute x23, starting transfers between devices, tile_swap(): return lax.ppermute(value, 'tile', [(i, i ^ mask) for i in range(4)])  17.7 us
    ppermute x5, starting transfers between devices, block_swap(): return lax.ppermute(value, 'tm', [(i, i ^ mask) for i in range(blocks)])  4.13 us
    ppermute x1, starting transfers between devices, shards(): lax.ppermute(next_terms, 'tm', [(i + 1, i) for i in range(blocks - 1)])  3.9 us
    unnamed x18, local copies, waits for them, and re-layouts  2.56 us
    ppermute x5, waiting for transfers between devices, block_swap(): return lax.ppermute(value, 'tm', [(i, i ^ mask) for i in range(blocks)])  2.29 us
  transfers between devices with their start and end apart: 30, of which 8 were waited for; matrix products, arithmetic and copies ran while one was open for 3% of the time, Pallas kernels for 24%

profile of v1, /device:TPU:9, one launch (start us, length us, event | category | flops | bytes accessed | tf_op | source)
XLA Modules:
  0.0 75.0 jit_solution(9664081590291840567)
XLA Ops:
  0.6 0.0 copy-start.1
  0.7 1.3 %collective-permute-start.7 = (bf16[192,512]{1,0:T(8,128)(2,1)}, bf16[192,512]{1,0:T(8,128)(2,1)}, u32[]{:S(2)}, u32[]{:S(2)}) collective-permute-start(bf16[192,512]{1,0:T(8,128)(2,1)} %bitcast.18), channel_id=1, source_target_pairs={{0,2},{1,3},{2,0},{3,1},{4,6},{5,7},{6,4},{7,5},{8,10},{9,11},{10,... | collective-permute-start | bytes 589832 | tf_op jit(solution)/shard_map/ppermute | solution.py:291
  2.0 1.0 %collective-permute-start.6 = (bf16[192,512]{1,0:T(8,128)(2,1)}, bf16[192,512]{1,0:T(8,128)(2,1)S(1)}, u32[]{:S(2)}, u32[]{:S(2)}) collective-permute-start(bf16[192,512]{1,0:T(8,128)(2,1)} %bitcast.19), channel_id=1, source_target_pairs={{0,1},{1,0},{2,3},{3,2},{4,5},{5,4},{6,7},{7,6},{8,9},{9,8},{10,11... | collective-permute-start | bytes 589832 | tf_op jit(solution)/shard_map/ppermute | solution.py:291
  2.9 1.0 %dynamic-slice_bitcast_fusion = f32[192,384]{1,0:T(8,128)S(1)} fusion(f32[1,192,768]{2,1,0:T(8,128)} %param.9, s32[]{:T(128)S(6)} %select_n.10), kind=kLoop, calls=%fused_computation | loop fusion | bytes 589828 | tf_op jit(solution)/shard_map/dynamic_slice | solution.py:302
  3.9 0.3 collective-permute-start.3
  4.2 0.3 collective-permute-start.2
  4.5 0.2 collective-permute-start.5
  4.7 1.0 %dynamic-slice_bitcast_fusion.1 = f32[192,384]{1,0:T(8,128)S(1)} fusion(f32[1,192,768]{2,1,0:T(8,128)} %param.8, s32[]{:T(128)S(6)} %select_n.10), kind=kLoop, calls=%fused_computation.1 | loop fusion | bytes 589828 | tf_op jit(solution)/shard_map/dynamic_slice | solution.py:303
  5.7 1.1 %collective-permute-done.7.g_far = bf16[192,512]{1,0:T(8,128)(2,1)} collective-permute-done((bf16[192,512]{1,0:T(8,128)(2,1)}, bf16[192,512]{1,0:T(8,128)(2,1)}, u32[]{:S(2)}, u32[]{:S(2)}) %collective-permute-start.7) | collective-permute-done | bytes 196640 | tf_op jit(solution)/shard_map/ppermute | solution.py:291
  6.8 1.2 %collective-permute-start = (f32[192,384]{1,0:T(8,128)S(1)}, f32[192,384]{1,0:T(8,128)S(1)}, u32[]{:S(2)}, u32[]{:S(2)}) collective-permute-start(f32[192,384]{1,0:T(8,128)S(1)} %dynamic-slice_bitcast_fusion.1), channel_id=1, source_target_pairs={{0,2},{1,3},{2,0},{3,1},{4,6},{5,7},{6,4},{7,5},{8,10},{9,11},{10,... | collective-permute-start | bytes 884744 | tf_op jit(solution)/shard_map/ppermute | solution.py:291
  8.1 0.7 copy-done.6
  8.7 0.2 collective-permute-start.27
  9.0 4.1 %collective-permute-done.3.x_far = f32[192,384]{1,0:T(8,128)S(1)} collective-permute-done((f32[192,384]{1,0:T(8,128)S(1)}, f32[192,384]{1,0:T(8,128)S(1)}, u32[]{:S(2)}, u32[]{:S(2)}) %collective-permute-start.3) | collective-permute-done | bytes 294944 | tf_op jit(solution)/shard_map/ppermute | solution.py:291
  13.0 2.7 %collective-permute-start.4 = (f32[192,384]{1,0:T(8,128)S(1)}, f32[192,384]{1,0:T(8,128)S(1)}, u32[]{:S(2)}, u32[]{:S(2)}) collective-permute-start(f32[192,384]{1,0:T(8,128)S(1)} %collective-permute-done.3.x_far), channel_id=1, source_target_pairs={{0,1},{1,0},{2,3},{3,2},{4,5},{5,4},{6,7},{7,6},{8,9},{9,8},{10,11... | collective-permute-start | bytes 884744 | tf_op jit(solution)/shard_map/ppermute | solution.py:291
  15.7 7.9 %collective-permute-done.27.p_far = bf16[192,512]{1,0:T(8,128)(2,1)} collective-permute-done((bf16[192,512]{1,0:T(8,128)(2,1)}, bf16[192,512]{1,0:T(8,128)(2,1)}, u32[]{:S(2)}, u32[]{:S(2)}) %collective-permute-start.27) | collective-permute-done | bytes 196640 | tf_op jit(solution)/shard_map/ppermute | solution.py:291
  23.7 1.5 %collective-permute-start.8 = (bf16[192,512]{1,0:T(8,128)(2,1)}, bf16[192,512]{1,0:T(8,128)(2,1)}, u32[]{:S(2)}, u32[]{:S(2)}) collective-permute-start(bf16[192,512]{1,0:T(8,128)(2,1)} %collective-permute-done.7.g_far), channel_id=1, source_target_pairs={{0,1},{1,0},{2,3},{3,2},{4,5},{5,4},{6,7},{7,6},{8,9},{9,8},{10,11... | collective-permute-start | bytes 589832 | tf_op jit(solution)/shard_map/ppermute | solution.py:291
  25.9 0.1 pad_add_fusion.info
  26.0 0.9 %collective-permute-done.8.g_cross = bf16[192,512]{1,0:T(8,128)(2,1)} collective-permute-done((bf16[192,512]{1,0:T(8,128)(2,1)}, bf16[192,512]{1,0:T(8,128)(2,1)}, u32[]{:S(2)}, u32[]{:S(2)}) %collective-permute-start.8) | collective-permute-done | bytes 196640 | tf_op jit(solution)/shard_map/ppermute | solution.py:291
  26.8 0.4 collective-permute-start.26
  27.2 1.2 %collective-permute-start.21 = (f32[128,512]{1,0:T(8,128)}, f32[128,512]{1,0:T(8,128)S(1)}, u32[]{:S(2)}, u32[]{:S(2)}) collective-permute-start(f32[128,512]{1,0:T(8,128)} %s_own.1), channel_id=1, source_target_pairs={{0,2},{1,3},{2,0},{3,1},{4,6},{5,7},{6,4},{7,5},{8,10},{9,11},{10,... | collective-permute-start | bytes 786440 | tf_op jit(solution)/shard_map/ppermute | solution.py:291
  28.4 0.4 collective-permute-start.28
  28.9 0.9 %copy-done.4 = bf16[1,192,512]{2,1,0:T(8,128)(2,1)S(1)} copy-done((bf16[1,192,512]{2,1,0:T(8,128)(2,1)S(1)}, bf16[1,192,512]{2,1,0:T(8,128)(2,1)}, u32[]{:S(2)}) %copy-start.4) | copy-done | bytes 196632
  29.8 0.9 %copy-done.7 = bf16[192,512]{1,0:T(8,128)(2,1)S(1)} copy-done((bf16[192,512]{1,0:T(8,128)(2,1)S(1)}, bf16[192,512]{1,0:T(8,128)(2,1)}, u32[]{:S(2)}) %copy-start.7) | copy-done | bytes 196632
  30.8 2.9 %prepare_kernel.1 = (bf16[768,768]{1,0:T(8,128)(2,1)S(1)}, bf16[768,768]{1,0:T(8,128)(2,1)S(1)}, bf16[768,768]{1,0:T(8,128)(2,1)S(1)}, bf16[768,384]{1,0:T(8,128...) custom-call(s32[3]{0:T(128)S(1)} %pad_add_fusion.info, f32[192,768]{1,0:T(8,128)S(1)} %bitcast.17, ...), custom_call_target="tpu_custom_call" | custom-call | flops 1207959552 | bytes 3737612 | tf_op jit(solution)/shard_map/prepare_kernel/pallas_call | solution.py:264
  33.8 5.9 %global_kernel.1 = (f32[160,128]{1,0:T(8,128)S(1)}, f32[160,128]{1,0:T(8,128)S(1)}, f32[192,128]{1,0:T(8,128)S(1)}, f32[192,128]{1,0:T(8,128)S(1)}, f32[192,128]...) custom-call(s32[3]{0:T(128)S(1)} %pad_add_fusion.info, ...), custom_call_target="tpu_custom_call" | custom-call | flops 4227858432 | bytes 6160396 | tf_op jit(solution)/shard_map/global_kernel/pallas_call | solution.py:264
  39.6 1.3 %collective-permute-start.9 = (f32[160,128]{1,0:T(8,128)S(1)}, f32[160,128]{1,0:T(8,128)S(1)}, u32[]{:S(2)}, u32[]{:S(2)}) collective-permute-start(f32[160,128]{1,0:T(8,128)S(1)} %get-tuple-element.34), channel_id=1, source_target_pairs={{0,4},{4,0},{8,12},{12,8},{16,20},{20,16},{24,28},{28,24},{1,5},{5... | collective-permute-start | bytes 245768 | tf_op jit(solution)/shard_map/ppermute | solution.py:294
  40.9 0.4 collective-permute-start.20
  41.3 0.2 collective-permute-start.22
  41.4 2.3 %collective-permute-done.9 = f32[160,128]{1,0:T(8,128)S(1)} collective-permute-done((f32[160,128]{1,0:T(8,128)S(1)}, f32[160,128]{1,0:T(8,128)S(1)}, u32[]{:S(2)}, u32[]{:S(2)}) %collective-permute-start.9) | collective-permute-done | bytes 81952 | tf_op jit(solution)/shard_map/ppermute | solution.py:294
  43.7 0.2 collective-permute-start.10
  44.0 2.3 %collective-permute-start.11 = (f32[160,128]{1,0:T(8,128)S(1)}, f32[160,128]{1,0:T(8,128)S(1)}, u32[]{:S(2)}, u32[]{:S(2)}) collective-permute-start(f32[160,128]{1,0:T(8,128)S(1)} %add.18), channel_id=1, source_target_pairs={{0,16},{4,20},{8,24},{12,28},{16,0},{20,4},{24,8},{28,12},{1,17},{... | collective-permute-start | bytes 245768 | tf_op jit(solution)/shard_map/ppermute | solution.py:294
  46.3 0.2 collective-permute-start.12
  46.5 7.5 %pair_kernel.1 = (f32[64,768]{1,0:T(8,128)S(1)}, f32[64,256]{1,0:T(8,128)}, f32[64,768]{1,0:T(8,128)S(1)}) custom-call(s32[3]{0:T(128)S(1)} %pad_add_fusion.info, bf16[192,512]{1,0:T(8,128)(2,1)S(1)} %bitcast.23, bf16[192,512]{1,0:T(8,128)(2,1)S(1)} %collective-permute-done.26.p_core, bf16[192,512]{1,0:T(8,128)(2,1)} %collective-permute-done.27.p_far, ...), custom_call_target="tpu_custom_call" | custom-call | flops 4831838208 | bytes 6291468 | tf_op jit(solution)/shard_map/pair_kernel/pallas_call | solution.py:264
  54.0 3.9 %collective-permute-start.29 = (f32[64,768]{1,0:T(8,128)S(1)}, f32[64,768]{1,0:T(8,128)S(1)}, u32[]{:S(2)}, u32[]{:S(2)}) collective-permute-start(f32[64,768]{1,0:T(8,128)S(1)} %get-tuple-element.43), channel_id=1, source_target_pairs={{4,0},{8,4},{12,8},{16,12},{20,16},{24,20},{28,24},{5,1},{9,5},{13... | collective-permute-start | bytes 589832 | tf_op jit(solution)/shard_map/ppermute | solution.py:355
  57.9 2.0 %collective-permute-start.23 = (f32[192,128]{1,0:T(8,128)S(1)}, f32[192,128]{1,0:T(8,128)S(1)}, u32[]{:S(2)}, u32[]{:S(2)}) collective-permute-start(f32[192,128]{1,0:T(8,128)S(1)} %get-tuple-element.36), channel_id=1, source_target_pairs={{0,1},{1,0},{2,3},{3,2},{4,5},{5,4},{6,7},{7,6},{8,9},{9,8},{10,11... | collective-permute-start | bytes 294920 | tf_op jit(solution)/shard_map/ppermute | solution.py:291
  59.9 0.2 collective-permute-start.24
  60.1 1.5 %collective-permute-start.25 = (f32[192,128]{1,0:T(8,128)S(1)}, f32[192,128]{1,0:T(8,128)S(1)}, u32[]{:S(2)}, u32[]{:S(2)}) collective-permute-start(f32[192,128]{1,0:T(8,128)S(1)} %get-tuple-element.38), channel_id=1, source_target_pairs={{0,3},{1,2},{2,1},{3,0},{4,7},{5,6},{6,5},{7,4},{8,11},{9,10},{10,... | collective-permute-start | bytes 294920 | tf_op jit(solution)/shard_map/ppermute | solution.py:291
  61.6 0.1 collective-permute-start.13
  61.7 0.3 collective-permute-start.16
  62.0 2.2 %collective-permute-done.24.y_far = f32[192,128]{1,0:T(8,128)S(1)} collective-permute-done((f32[192,128]{1,0:T(8,128)S(1)}, f32[192,128]{1,0:T(8,128)S(1)}, u32[]{:S(2)}, u32[]{:S(2)}) %collective-permute-start.24) | collective-permute-done | bytes 98336 | tf_op jit(solution)/shard_map/ppermute | solution.py:291
  64.3 0.1 collective-permute-start.17
  64.4 2.6 %collective-permute-done.25.y_cross = f32[192,128]{1,0:T(8,128)S(1)} collective-permute-done((f32[192,128]{1,0:T(8,128)S(1)}, f32[192,128]{1,0:T(8,128)S(1)}, u32[]{:S(2)}, u32[]{:S(2)}) %collective-permute-start.25) | collective-permute-done | bytes 98336 | tf_op jit(solution)/shard_map/ppermute | solution.py:291
  67.0 0.5 collective-permute-start.15
  67.5 1.5 %collective-permute-done.16.refs_4_ = f32[160,128]{1,0:T(8,128)S(1)} collective-permute-done((f32[160,128]{1,0:T(8,128)S(1)}, f32[160,128]{1,0:T(8,128)S(1)}, u32[]{:S(2)}, u32[]{:S(2)}) %collective-permute-start.16) | collective-permute-done | bytes 81952 | tf_op jit(solution)/shard_map/ppermute | solution.py:291
  69.0 0.9 %collective-permute-start.18 = (f32[160,128]{1,0:T(8,128)S(1)}, f32[160,128]{1,0:T(8,128)S(1)}, u32[]{:S(2)}, u32[]{:S(2)}) collective-permute-start(f32[160,128]{1,0:T(8,128)S(1)} %collective-permute-done.16.refs_4_), channel_id=1, source_target_pairs={{0,1},{1,0},{2,3},{3,2},{4,5},{5,4},{6,7},{7,6},{8,9},{9,8},{10,11... | collective-permute-start | bytes 245768 | tf_op jit(solution)/shard_map/ppermute | solution.py:291
  69.9 1.1 %collective-permute-start.19 = (f32[160,128]{1,0:T(8,128)S(1)}, f32[160,128]{1,0:T(8,128)S(1)}, u32[]{:S(2)}, u32[]{:S(2)}) collective-permute-start(f32[160,128]{1,0:T(8,128)S(1)} %collective-permute-done.17.refs_5_), channel_id=1, source_target_pairs={{0,1},{1,0},{2,3},{3,2},{4,5},{5,4},{6,7},{7,6},{8,9},{9,8},{10,11... | collective-permute-start | bytes 245768 | tf_op jit(solution)/shard_map/ppermute | solution.py:291
  70.9 1.5 %start_kernel.1 = (bf16[512,1024]{1,0:T(8,128)(2,1)S(1)}, f32[192,512]{1,0:T(8,128)S(1)}) custom-call(s32[3]{0:T(128)S(1)} %pad_add_fusion.info, f32[128,512]{1,0:T(8,128)S(1)} %copy-done.3, f32[128,512]{1,0:T(8,128)S(1)} %collective-permute-done.20.s_core, f32[128,512]{1,0:T(8,128)S(1)} %collective-permute-done.21.s_far, ...), custom_call_target="tpu_custom_call" | custom-call | flops 603979776 | bytes 1441804 | tf_op jit(solution)/shard_map/start_kernel/pallas_call | solution.py:264
  72.5 2.6 %back_kernel.1 = (f32[64,256]{1,0:T(8,128)}, f32[64,512]{1,0:T(8,128)}, f32[128,512]{1,0:T(8,128)}, f32[192,512]{1,0:T(8,128)}) custom-call(s32[3]{0:T(128)S(1)} %pad_add_fusion.info, f32[160,128]{1,0:T(8,128)S(1)} %add_add_fusion.refs_0_, f32[160,128]{1,0:T(8,128)S(1)} %collective-permute-done.13.refs_1_, f32[160,128]{1,0:T(8,128)S(1)} %collective-permute-done.14.refs_2_, ...), custom_call_target="tpu_custom_call" | custom-call | flops 603979776 | bytes 2490380 | tf_op jit(solution)/shard_map/back_kernel/pallas_call | solution.py:264
  (40 shorter events, 0.1 us)
Async XLA Ops:
  0.6 28.3 %copy-start.1 = (f32[1,192,768]{2,1,0:T(8,128)S(1)}, f32[1,192,768]{2,1,0:T(8,128)}, u32[]{:S(2)}) copy-start(f32[1,192,768]{2,1,0:T(8,128)} %param.9) | copy-start | bytes 1769476
  0.6 28.2 %copy-start = (f32[1,192,768]{2,1,0:T(8,128)S(1)}, f32[1,192,768]{2,1,0:T(8,128)}, u32[]{:S(2)}) copy-start(f32[1,192,768]{2,1,0:T(8,128)} %param.8) | copy-start | bytes 1769476
  0.7 28.2 %copy-start.8 = (s32[1,512]{1,0:T(1,128)S(1)}, s32[1,512]{1,0:T(1,128)}, u32[]{:S(2)}) copy-start(s32[1,512]{1,0:T(1,128)} %index.1) | copy-start | bytes 6148
  0.7 6.2 %collective-permute-start.7 = (bf16[192,512]{1,0:T(8,128)(2,1)}, bf16[192,512]{1,0:T(8,128)(2,1)}, u32[]{:S(2)}, u32[]{:S(2)}) collective-permute-start(bf16[192,512]{1,0:T(8,128)(2,1)} %bitcast.18), channel_id=1, source_target_pairs={{0,2},{1,3},{2,0},{3,1},{4,6},{5,7},{6,4},{7,5},{8,10},{9,11},{10,... | collective-permute-start | bytes 589832 | tf_op jit(solution)/shard_map/ppermute | solution.py:291
  2.0 6.1 %collective-permute-start.6 = (bf16[192,512]{1,0:T(8,128)(2,1)}, bf16[192,512]{1,0:T(8,128)(2,1)S(1)}, u32[]{:S(2)}, u32[]{:S(2)}) collective-permute-start(bf16[192,512]{1,0:T(8,128)(2,1)} %bitcast.19), channel_id=1, source_target_pairs={{0,1},{1,0},{2,3},{3,2},{4,5},{5,4},{6,7},{7,6},{8,9},{9,8},{10,11... | collective-permute-start | bytes 589832 | tf_op jit(solution)/shard_map/ppermute | solution.py:291
  3.9 9.1 %collective-permute-start.3 = (f32[192,384]{1,0:T(8,128)S(1)}, f32[192,384]{1,0:T(8,128)S(1)}, u32[]{:S(2)}, u32[]{:S(2)}) collective-permute-start(f32[192,384]{1,0:T(8,128)S(1)} %dynamic-slice_bitcast_fusion), channel_id=1, source_target_pairs={{0,2},{1,3},{2,0},{3,1},{4,6},{5,7},{6,4},{7,5},{8,10},{9,11},{10,... | collective-permute-start | bytes 884744 | tf_op jit(solution)/shard_map/ppermute | solution.py:291
  4.2 24.2 %collective-permute-start.2 = (f32[192,768]{1,0:T(8,128)}, f32[192,768]{1,0:T(8,128)S(1)}, u32[]{:S(2)}, u32[]{:S(2)}) collective-permute-start(f32[192,768]{1,0:T(8,128)} %bitcast.16), channel_id=1, source_target_pairs={{0,1},{1,0},{2,3},{3,2},{4,5},{5,4},{6,7},{7,6},{8,9},{9,8},{10,11... | collective-permute-start | bytes 1769480 | tf_op jit(solution)/shard_map/ppermute | solution.py:291
  4.5 24.4 %collective-permute-start.5 = (f32[192,768]{1,0:T(8,128)}, f32[192,768]{1,0:T(8,128)S(1)}, u32[]{:S(2)}, u32[]{:S(2)}) collective-permute-start(f32[192,768]{1,0:T(8,128)} %bitcast.14), channel_id=1, source_target_pairs={{0,1},{1,0},{2,3},{3,2},{4,5},{5,4},{6,7},{7,6},{8,9},{9,8},{10,11... | collective-permute-start | bytes 1769480 | tf_op jit(solution)/shard_map/ppermute | solution.py:291
  6.8 18.4 %collective-permute-start = (f32[192,384]{1,0:T(8,128)S(1)}, f32[192,384]{1,0:T(8,128)S(1)}, u32[]{:S(2)}, u32[]{:S(2)}) collective-permute-start(f32[192,384]{1,0:T(8,128)S(1)} %dynamic-slice_bitcast_fusion.1), channel_id=1, source_target_pairs={{0,2},{1,3},{2,0},{3,1},{4,6},{5,7},{6,4},{7,5},{8,10},{9,11},{10,... | collective-permute-start | bytes 884744 | tf_op jit(solution)/shard_map/ppermute | solution.py:291
  8.1 0.7 copy-start.6
  8.7 14.9 %collective-permute-start.27 = (bf16[192,512]{1,0:T(8,128)(2,1)}, bf16[192,512]{1,0:T(8,128)(2,1)}, u32[]{:S(2)}, u32[]{:S(2)}) collective-permute-start(bf16[192,512]{1,0:T(8,128)(2,1)} %bitcast.21), channel_id=1, source_target_pairs={{0,2},{1,3},{2,0},{3,1},{4,6},{5,7},{6,4},{7,5},{8,10},{9,11},{10,... | collective-permute-start | bytes 589832 | tf_op jit(solution)/shard_map/ppermute | solution.py:291
  13.0 14.2 %collective-permute-start.4 = (f32[192,384]{1,0:T(8,128)S(1)}, f32[192,384]{1,0:T(8,128)S(1)}, u32[]{:S(2)}, u32[]{:S(2)}) collective-permute-start(f32[192,384]{1,0:T(8,128)S(1)} %collective-permute-done.3.x_far), channel_id=1, source_target_pairs={{0,1},{1,0},{2,3},{3,2},{4,5},{5,4},{6,7},{7,6},{8,9},{9,8},{10,11... | collective-permute-start | bytes 884744 | tf_op jit(solution)/shard_map/ppermute | solution.py:291
  23.7 3.2 %collective-permute-start.8 = (bf16[192,512]{1,0:T(8,128)(2,1)}, bf16[192,512]{1,0:T(8,128)(2,1)}, u32[]{:S(2)}, u32[]{:S(2)}) collective-permute-start(bf16[192,512]{1,0:T(8,128)(2,1)} %collective-permute-done.7.g_far), channel_id=1, source_target_pairs={{0,1},{1,0},{2,3},{3,2},{4,5},{5,4},{6,7},{7,6},{8,9},{9,8},{10,11... | collective-permute-start | bytes 589832 | tf_op jit(solution)/shard_map/ppermute | solution.py:291
  25.2 8.5 %collective-permute-start.1 = (f32[192,384]{1,0:T(8,128)S(1)}, f32[192,384]{1,0:T(8,128)S(1)}, u32[]{:S(2)}, u32[]{:S(2)}) collective-permute-start(f32[192,384]{1,0:T(8,128)S(1)} %collective-permute-done.k_far), channel_id=1, source_target_pairs={{0,1},{1,0},{2,3},{3,2},{4,5},{5,4},{6,7},{7,6},{8,9},{9,8},{10,11... | collective-permute-start | bytes 884744 | tf_op jit(solution)/shard_map/ppermute | solution.py:291
  26.0 7.8 %copy-start.2 = (f32[128,512]{1,0:T(8,128)S(1)}, f32[128,512]{1,0:T(8,128)}, u32[]{:S(2)}) copy-start(f32[128,512]{1,0:T(8,128)} %base.1) | copy-start | bytes 786436
  26.8 17.1 %collective-permute-start.26 = (bf16[192,512]{1,0:T(8,128)(2,1)}, bf16[192,512]{1,0:T(8,128)(2,1)S(1)}, u32[]{:S(2)}, u32[]{:S(2)}) collective-permute-start(bf16[192,512]{1,0:T(8,128)(2,1)} %bitcast.22), channel_id=1, source_target_pairs={{0,1},{1,0},{2,3},{3,2},{4,5},{5,4},{6,7},{7,6},{8,9},{9,8},{10,11... | collective-permute-start | bytes 589832 | tf_op jit(solution)/shard_map/ppermute | solution.py:291
  27.2 14.1 %collective-permute-start.21 = (f32[128,512]{1,0:T(8,128)}, f32[128,512]{1,0:T(8,128)S(1)}, u32[]{:S(2)}, u32[]{:S(2)}) collective-permute-start(f32[128,512]{1,0:T(8,128)} %s_own.1), channel_id=1, source_target_pairs={{0,2},{1,3},{2,0},{3,1},{4,6},{5,7},{6,4},{7,5},{8,10},{9,11},{10,... | collective-permute-start | bytes 786440 | tf_op jit(solution)/shard_map/ppermute | solution.py:291
  28.4 17.8 %collective-permute-start.28 = (bf16[192,512]{1,0:T(8,128)(2,1)}, bf16[192,512]{1,0:T(8,128)(2,1)S(1)}, u32[]{:S(2)}, u32[]{:S(2)}) collective-permute-start(bf16[192,512]{1,0:T(8,128)(2,1)} %collective-permute-done.27.p_far), channel_id=1, source_target_pairs={{0,1},{1,0},{2,3},{3,2},{4,5},{5,4},{6,7},{7,6},{8,9},{9,8},{10,11... | collective-permute-start | bytes 589832 | tf_op jit(solution)/shard_map/ppermute | solution.py:291
  28.9 0.9 %copy-start.4 = (bf16[1,192,512]{2,1,0:T(8,128)(2,1)S(1)}, bf16[1,192,512]{2,1,0:T(8,128)(2,1)}, u32[]{:S(2)}) copy-start(bf16[1,192,512]{2,1,0:T(8,128)(2,1)} %param.13) | copy-start | bytes 589828
  29.8 0.9 %copy-start.7 = (bf16[192,512]{1,0:T(8,128)(2,1)S(1)}, bf16[192,512]{1,0:T(8,128)(2,1)}, u32[]{:S(2)}) copy-start(bf16[192,512]{1,0:T(8,128)(2,1)} %copy-done.6) | copy-start | bytes 589828
  33.7 7.2 %copy-start.3 = (f32[128,512]{1,0:T(8,128)S(1)}, f32[128,512]{1,0:T(8,128)}, u32[]{:S(2)}) copy-start(f32[128,512]{1,0:T(8,128)} %s_own.1) | copy-start | bytes 786436
  33.7 12.8 %copy-start.5 = (bf16[1,192,512]{2,1,0:T(8,128)(2,1)S(1)}, bf16[1,192,512]{2,1,0:T(8,128)(2,1)}, u32[]{:S(2)}) copy-start(bf16[1,192,512]{2,1,0:T(8,128)(2,1)} %param.12) | copy-start | bytes 589828
  39.6 4.1 %collective-permute-start.9 = (f32[160,128]{1,0:T(8,128)S(1)}, f32[160,128]{1,0:T(8,128)S(1)}, u32[]{:S(2)}, u32[]{:S(2)}) collective-permute-start(f32[160,128]{1,0:T(8,128)S(1)} %get-tuple-element.34), channel_id=1, source_target_pairs={{0,4},{4,0},{8,12},{12,8},{16,20},{20,16},{24,28},{28,24},{1,5},{5... | collective-permute-start | bytes 245768 | tf_op jit(solution)/shard_map/ppermute | solution.py:294
  40.9 13.1 %collective-permute-start.20 = (f32[128,512]{1,0:T(8,128)S(1)}, f32[128,512]{1,0:T(8,128)S(1)}, u32[]{:S(2)}, u32[]{:S(2)}) collective-permute-start(f32[128,512]{1,0:T(8,128)S(1)} %copy-done.3), channel_id=1, source_target_pairs={{0,1},{1,0},{2,3},{3,2},{4,5},{5,4},{6,7},{7,6},{8,9},{9,8},{10,11... | collective-permute-start | bytes 786440 | tf_op jit(solution)/shard_map/ppermute | solution.py:291
  41.3 20.4 %collective-permute-start.22 = (f32[128,512]{1,0:T(8,128)S(1)}, f32[128,512]{1,0:T(8,128)S(1)}, u32[]{:S(2)}, u32[]{:S(2)}) collective-permute-start(f32[128,512]{1,0:T(8,128)S(1)} %collective-permute-done.21.s_far), channel_id=1, source_target_pairs={{0,1},{1,0},{2,3},{3,2},{4,5},{5,4},{6,7},{7,6},{8,9},{9,8},{10,11... | collective-permute-start | bytes 786440 | tf_op jit(solution)/shard_map/ppermute | solution.py:291
  43.7 14.2 %collective-permute-start.10 = (f32[160,128]{1,0:T(8,128)S(1)}, f32[160,128]{1,0:T(8,128)S(1)}, u32[]{:S(2)}, u32[]{:S(2)}) collective-permute-start(f32[160,128]{1,0:T(8,128)S(1)} %add.18), channel_id=1, source_target_pairs={{0,8},{4,12},{8,0},{12,4},{16,24},{20,28},{24,16},{28,20},{1,9},{5... | collective-permute-start | bytes 245768 | tf_op jit(solution)/shard_map/ppermute | solution.py:294
  44.0 15.9 %collective-permute-start.11 = (f32[160,128]{1,0:T(8,128)S(1)}, f32[160,128]{1,0:T(8,128)S(1)}, u32[]{:S(2)}, u32[]{:S(2)}) collective-permute-start(f32[160,128]{1,0:T(8,128)S(1)} %add.18), channel_id=1, source_target_pairs={{0,16},{4,20},{8,24},{12,28},{16,0},{20,4},{24,8},{28,12},{1,17},{... | collective-permute-start | bytes 245768 | tf_op jit(solution)/shard_map/ppermute | solution.py:294
  46.3 13.8 %collective-permute-start.12 = (f32[160,128]{1,0:T(8,128)S(1)}, f32[160,128]{1,0:T(8,128)S(1)}, u32[]{:S(2)}, u32[]{:S(2)}) collective-permute-start(f32[160,128]{1,0:T(8,128)S(1)} %add.18), channel_id=1, source_target_pairs={{0,24},{4,28},{8,16},{12,20},{16,8},{20,12},{24,0},{28,4},{1,25},{... | collective-permute-start | bytes 245768 | tf_op jit(solution)/shard_map/ppermute | solution.py:294
  54.0 18.5 %collective-permute-start.29 = (f32[64,768]{1,0:T(8,128)S(1)}, f32[64,768]{1,0:T(8,128)S(1)}, u32[]{:S(2)}, u32[]{:S(2)}) collective-permute-start(f32[64,768]{1,0:T(8,128)S(1)} %get-tuple-element.43), channel_id=1, source_target_pairs={{4,0},{8,4},{12,8},{16,12},{20,16},{24,20},{28,24},{5,1},{9,5},{13... | collective-permute-start | bytes 589832 | tf_op jit(solution)/shard_map/ppermute | solution.py:355
  57.9 3.8 %collective-permute-start.23 = (f32[192,128]{1,0:T(8,128)S(1)}, f32[192,128]{1,0:T(8,128)S(1)}, u32[]{:S(2)}, u32[]{:S(2)}) collective-permute-start(f32[192,128]{1,0:T(8,128)S(1)} %get-tuple-element.36), channel_id=1, source_target_pairs={{0,1},{1,0},{2,3},{3,2},{4,5},{5,4},{6,7},{7,6},{8,9},{9,8},{10,11... | collective-permute-start | bytes 294920 | tf_op jit(solution)/shard_map/ppermute | solution.py:291
  59.9 4.4 %collective-permute-start.24 = (f32[192,128]{1,0:T(8,128)S(1)}, f32[192,128]{1,0:T(8,128)S(1)}, u32[]{:S(2)}, u32[]{:S(2)}) collective-permute-start(f32[192,128]{1,0:T(8,128)S(1)} %get-tuple-element.37), channel_id=1, source_target_pairs={{0,2},{1,3},{2,0},{3,1},{4,6},{5,7},{6,4},{7,5},{8,10},{9,11},{10,... | collective-permute-start | bytes 294920 | tf_op jit(solution)/shard_map/ppermute | solution.py:291
  60.1 6.9 %collective-permute-start.25 = (f32[192,128]{1,0:T(8,128)S(1)}, f32[192,128]{1,0:T(8,128)S(1)}, u32[]{:S(2)}, u32[]{:S(2)}) collective-permute-start(f32[192,128]{1,0:T(8,128)S(1)} %get-tuple-element.38), channel_id=1, source_target_pairs={{0,3},{1,2},{2,1},{3,0},{4,7},{5,6},{6,5},{7,4},{8,11},{9,10},{10,... | collective-permute-start | bytes 294920 | tf_op jit(solution)/shard_map/ppermute | solution.py:291
  61.6 5.4 %collective-permute-start.13 = (f32[160,128]{1,0:T(8,128)S(1)}, f32[160,128]{1,0:T(8,128)S(1)}, u32[]{:S(2)}, u32[]{:S(2)}) collective-permute-start(f32[160,128]{1,0:T(8,128)S(1)} %add_add_fusion.refs_0_), channel_id=1, source_target_pairs={{0,4},{4,0},{8,12},{12,8},{16,20},{20,16},{24,28},{28,24},{1,5},{5... | collective-permute-start | bytes 245768 | tf_op jit(solution)/shard_map/ppermute | solution.py:294
  61.7 7.3 %collective-permute-start.16 = (f32[160,128]{1,0:T(8,128)S(1)}, f32[160,128]{1,0:T(8,128)S(1)}, u32[]{:S(2)}, u32[]{:S(2)}) collective-permute-start(f32[160,128]{1,0:T(8,128)S(1)} %add_add_fusion.refs_0_), channel_id=1, source_target_pairs={{0,2},{1,3},{2,0},{3,1},{4,6},{5,7},{6,4},{7,5},{8,10},{9,11},{10,... | collective-permute-start | bytes 245768 | tf_op jit(solution)/shard_map/ppermute | solution.py:291
  64.3 5.6 %collective-permute-start.17 = (f32[160,128]{1,0:T(8,128)S(1)}, f32[160,128]{1,0:T(8,128)S(1)}, u32[]{:S(2)}, u32[]{:S(2)}) collective-permute-start(f32[160,128]{1,0:T(8,128)S(1)} %add_add_fusion.refs_0_), channel_id=1, source_target_pairs={{0,6},{1,7},{2,4},{3,5},{4,2},{5,3},{6,0},{7,1},{8,14},{9,15},{10,... | collective-permute-start | bytes 245768 | tf_op jit(solution)/shard_map/ppermute | solution.py:340
  67.0 5.5 %collective-permute-start.14 = (f32[160,128]{1,0:T(8,128)S(1)}, f32[160,128]{1,0:T(8,128)S(1)}, u32[]{:S(2)}, u32[]{:S(2)}) collective-permute-start(f32[160,128]{1,0:T(8,128)S(1)} %add_add_fusion.refs_0_), channel_id=1, source_target_pairs={{0,1},{1,0},{2,3},{3,2},{4,5},{5,4},{6,7},{7,6},{8,9},{9,8},{10,11... | collective-permute-start | bytes 245768 | tf_op jit(solution)/shard_map/ppermute | solution.py:291
  67.0 5.5 %collective-permute-start.15 = (f32[160,128]{1,0:T(8,128)S(1)}, f32[160,128]{1,0:T(8,128)S(1)}, u32[]{:S(2)}, u32[]{:S(2)}) collective-permute-start(f32[160,128]{1,0:T(8,128)S(1)} %collective-permute-done.13.refs_1_), channel_id=1, source_target_pairs={{0,1},{1,0},{2,3},{3,2},{4,5},{5,4},{6,7},{7,6},{8,9},{9,8},{10,11... | collective-permute-start | bytes 245768 | tf_op jit(solution)/shard_map/ppermute | solution.py:291
  69.0 3.5 %collective-permute-start.18 = (f32[160,128]{1,0:T(8,128)S(1)}, f32[160,128]{1,0:T(8,128)S(1)}, u32[]{:S(2)}, u32[]{:S(2)}) collective-permute-start(f32[160,128]{1,0:T(8,128)S(1)} %collective-permute-done.16.refs_4_), channel_id=1, source_target_pairs={{0,1},{1,0},{2,3},{3,2},{4,5},{5,4},{6,7},{7,6},{8,9},{9,8},{10,11... | collective-permute-start | bytes 245768 | tf_op jit(solution)/shard_map/ppermute | solution.py:291
  69.9 2.6 %collective-permute-start.19 = (f32[160,128]{1,0:T(8,128)S(1)}, f32[160,128]{1,0:T(8,128)S(1)}, u32[]{:S(2)}, u32[]{:S(2)}) collective-permute-start(f32[160,128]{1,0:T(8,128)S(1)} %collective-permute-done.17.refs_5_), channel_id=1, source_target_pairs={{0,1},{1,0},{2,3},{3,2},{4,5},{5,4},{6,7},{7,6},{8,9},{9,8},{10,11... | collective-permute-start | bytes 245768 | tf_op jit(solution)/shard_map/ppermute | solution.py:291

commit v2 on v1

v2 whole, which is shorter than its diff:
```python
import functools

import jax
import jax.numpy as jnp
from jax import lax
from jax.experimental import pallas as pl
from jax.experimental.pallas import tpu as pltpu
from jax.sharding import PartitionSpec as P

BF16 = jnp.bfloat16
F32 = jnp.float32
STEPS = 2
TERMS = 2**STEPS - 1
VMEM_BYTES = 32 * 2**20


def halves(value):
    high = value.astype(BF16)
    return high, (value - high.astype(F32)).astype(BF16)


def dot(left_side, right_side):
    return jnp.dot(left_side, right_side, preferred_element_type=F32)


def both(value):
    return jnp.concatenate(halves(value), axis=1)


def stacked(value):
    return jnp.concatenate(halves(value), axis=0)


def quadrants(product):
    rows, cols = product.shape[0] // 2, product.shape[1] // 2
    return (product[:rows, :cols] + product[:rows, cols:]) + (
        product[rows:, :cols] + product[rows:, cols:]
    )


def at_rows(start, size, unit=16):
    return pl.ds(pl.multiple_of(start, unit), size)


def live_rows(info, half):
    near, size = info[0] // 2, info[1]
    ids = lax.broadcasted_iota(jnp.int32, (half, 1), 0)
    return jnp.concatenate(
        [(ids + near * half) < size, (ids + (1 - near) * half) < size], axis=0
    )


def put_rows(info, pieces, target, offset=0):
    rows = pieces[0].shape[0]
    core = info[0] % 2
    target[at_rows(offset + core * rows, rows), :] = pieces[0]
    target[at_rows(offset + (1 - core) * rows, rows), :] = pieces[1]


def pack_kernel(info, x_rows, k_rows, out, x_part, k_part, sems):
    rows, half = x_part.shape
    unit = half // 3
    near, core = info[0] // 2, info[0] % 2
    cols = pl.ds(pl.multiple_of(near * half, 128), half)
    copies = [
        pltpu.make_async_copy(ref.at[:, cols], part, sems.at[i])
        for i, (ref, part) in enumerate(((x_rows, x_part), (k_rows, k_part)))
    ]
    for copy in copies:
        copy.start()
    large = at_rows(core * (rows - unit), unit, 8)
    small = at_rows((1 - core) * unit, rows - unit, 8)
    edge = pl.ds(pl.multiple_of(core * 2 * unit, 128), unit)
    opposite = pl.ds(pl.multiple_of((1 - core) * 2 * unit, 128), unit)
    for i, (copy, part) in enumerate(zip(copies, (x_part, k_part))):
        copy.wait()
        first = i * 3 * unit
        out[first : first + unit, :] = part[large, edge]
        out[first + unit : first + 2 * unit, :] = part[large, unit : 2 * unit]
        out[first + 2 * unit : first + unit + rows, :] = part[small, unit : 2 * unit]
        block = part[large, opposite]
        out[first + unit + rows : first + 3 * unit, :] = jnp.where(
            core == 0, block[: unit // 2, :], block.T[unit // 2 :, :]
        )


def corner(info, far, cross, target, packed, live=None):
    order = target.shape[1]
    half = order // 2
    unit = half // 3
    core = info[0] % 2
    packed[core] = far
    packed[1 - core] = cross
    zero, one = packed.at[0], packed.at[1]

    def put(row, col, value):
        first = half + row * unit
        if live is not None:
            value = jnp.where(live[first : first + unit], value, 0.0)
        high, low = halves(value)
        place = slice(half + col * unit, half + (col + 1) * unit)
        target[first : first + unit, place] = high
        target[order + first : order + first + unit, place] = low

    def joined(first, last):
        return jnp.concatenate([zero[first:last, :], one[first:last, :]], axis=0)

    put(0, 0, zero[0:unit, :])
    put(2, 2, one[0:unit, :])
    side = zero[unit : 2 * unit, :]
    put(0, 1, side)
    put(1, 0, side.T)
    side = one[unit : 2 * unit, :]
    put(2, 1, side)
    put(1, 2, side.T)
    put(1, 1, joined(2 * unit, 2 * unit + unit // 2))
    side = joined(2 * unit + unit // 2, 3 * unit)
    put(0, 2, side)
    put(2, 0, side.T)


def spread(info, own, other, target, whole, live=None):
    rows, order = own.shape
    half = order // 2
    near, core = info[0] // 2, info[0] % 2
    for ref, place in ((own, core), (other, 1 - core)):
        for side in range(2):
            cols = pl.ds(pl.multiple_of((near if side == 0 else 1 - near) * half, 128), half)
            whole[at_rows(place * rows, rows), side * half : (side + 1) * half] = ref[:, cols]
    for rows, cols, value in (
        (slice(0, half), slice(0, order), whole[...]),
        (slice(half, order), slice(0, half), whole[:, half:].T),
    ):
        if live is not None:
            value = jnp.where(live[rows], value, 0.0)
        high, low = halves(value)
        target[rows, cols] = high
        target[order + rows.start : order + rows.stop, cols] = low


def times(matrix, columns):
    return quadrants(dot(matrix[...], both(columns)))


def spread_kernel(
    info, x_own, x_core, k_own, k_core, g_own, g_core, g_far, g_cross, index,
    x, k, links, whole, gathered,
):
    half = x.shape[1] // 2
    width = g_own.shape[1]
    live = live_rows(info, half)
    spread(info, x_own, x_core, x, whole, live)
    spread(info, k_own, k_core, k, whole, live)
    put_rows(info, (g_own[...], g_core[...]), gathered)
    put_rows(info, (g_far[...], g_cross[...]), gathered, half)
    hot = lax.broadcasted_iota(jnp.int32, (width, width), 0) == index[...]
    chosen = dot(gathered[...], hot.astype(F32).astype(BF16))
    links[...] = jnp.where(live, chosen, 0.0).astype(BF16)


def global_kernel(
    info, far, cross, x_in, k_in, links, base,
    keep, send, y_own, y_core, y_far, y_cross, x, k, pack, solved, packed,
):
    del x_in, k_in
    order, width = links.shape
    half = order // 2
    rows = half // 2
    group = width // 4
    part, core = info[0], info[0] % 2
    live = live_rows(info, half)
    corner(info, far[:half, :], cross[:half, :], x, packed, live)
    columns = links[:, pl.ds(pl.multiple_of(part * group, 128), group)].astype(F32)
    value = times(x, columns)
    corner(info, far[half:, :], cross[half:, :], k, packed, live)
    value = 2.0 * columns - times(k, value)
    for step in range(TERMS - 1):
        value = columns + value - times(k, times(x, value))
    result = times(x, value)
    solved[...] = result
    y_own[...] = solved[at_rows(core * rows, rows), :]
    y_core[...] = solved[at_rows((1 - core) * rows, rows), :]
    y_far[...] = solved[at_rows(half + core * rows, rows), :]
    y_cross[...] = solved[at_rows(half + (1 - core) * rows, rows), :]
    left_side = stacked(result.T)

    def block(shift):
        place = pl.ds(pl.multiple_of(((part + shift) % 4) * group, 128), group)
        both_parts = dot(left_side, links[:, place])
        added = jnp.where(info[2] == 0, base[:, place], 0.0)
        return both_parts[:group] + both_parts[group:] + added

    pack[0:group, :] = block(0)
    pack[group : 2 * group, :] = block(1)
    across = block(2)
    pack[2 * group :, :] = jnp.where(
        part < 2, across[: group // 2, :], across.T[group // 2 :, :]
    )
    size = keep.shape[0]
    side = info[2] % 2
    keep[...] = pack[at_rows(side * size, size, 8), :]
    send[...] = pack[at_rows((1 - side) * size, size, 8), :]


def pair_kernel(
    info, p_own, p_core, p_far, p_cross, x, k, masked, columns, state, gathered
):
    half = x.shape[1] // 2
    width = p_own.shape[1]
    link = width // 2
    share = link // 4
    put_rows(info, (p_own[...], p_core[...]), gathered)
    put_rows(info, (p_far[...], p_cross[...]), gathered, half)
    masked[...] = jnp.where(live_rows(info, half), gathered[...], jnp.zeros((), BF16))
    source = lax.broadcasted_iota(jnp.int32, (width, 2 * share), 0)
    place = lax.broadcasted_iota(jnp.int32, (width, 2 * share), 1)
    wanted = info[0] * share + place + jnp.where(place < share, 0, link - share)
    chosen = dot(masked[...], (source == wanted).astype(F32).astype(BF16))
    columns[...] = chosen
    value = chosen
    for step in range(TERMS - 1):
        value = chosen + value - times(k, times(x, value))
    state[...] = value


def terms_kernel(
    info, masked, columns, state, x, k, links, own_terms, off_terms, next_terms
):
    link = masked.shape[1] // 2
    share = link // 4
    value = state[...]
    value = columns[...] + value - times(k, times(x, value))
    left_side = stacked(times(x, value).T)
    terms = dot(left_side, masked[...])
    terms = terms[: 2 * share] + terms[2 * share :]
    cross = dot(left_side, links[...])
    cross = cross[: 2 * share] + cross[2 * share :]
    next_terms[:, :link] = terms[:share, :link]
    next_terms[:, link:] = cross[:share]
    off_terms[...] = terms[:share, link:]
    own_terms[:, :link] = terms[share:, link:]
    own_terms[:, link:] = cross[share:]


def start_kernel(
    info, s_own, s_core, s_far, s_cross, y_own, y_core, y_far, y_cross, start, scaled
):
    part = info[0]
    group = s_own.shape[0]
    width = s_own.shape[1]
    total = None
    for ref, mask, rows in (
        (s_own, 0, y_own), (s_core, 1, y_core), (s_far, 2, y_far), (s_cross, 3, y_cross)
    ):
        value = both(ref[...])
        start[at_rows((part ^ mask) * group, group), :] = value
        product = quadrants(dot(stacked(rows[...]), value))
        total = product if total is None else total + product
    scaled[...] = total


def back_kernel(
    info, *refs
):
    sums, (start, scaled, own_terms, came), outs = refs[:8], refs[8:12], refs[12:]
    link_diag, link_cross, schur, back, whole, full = outs
    part, side = info[0], info[2] % 2
    size = sums[0].shape[0]
    group = schur.shape[0]
    width = schur.shape[1]
    for mask in range(4):
        for half in range(2):
            place = at_rows((part ^ mask) * (2 * size) + (side ^ half) * size, size, 8)
            whole[place, :] = sums[2 * mask + half][...]
    for row in range(4):
        first = row * 2 * size
        diagonal = whole[first : first + group, :]
        after = whole[first + group : first + 2 * group, :]
        nxt = (row + 1) % 4
        full[row * group : (row + 1) * group, row * group : (row + 1) * group] = diagonal
        full[row * group : (row + 1) * group, nxt * group : (nxt + 1) * group] = after
        full[nxt * group : (nxt + 1) * group, row * group : (row + 1) * group] = after.T
        if row < 2:
            other = (row + 2) * 2 * size
            across = jnp.concatenate(
                [whole[first + 2 * group : first + 2 * size, :],
                 whole[other + 2 * group : other + 2 * size, :]], axis=0
            )
            far = row + 2
            full[row * group : (row + 1) * group, far * group : (far + 1) * group] = across
            full[far * group : (far + 1) * group, row * group : (row + 1) * group] = across.T
    schur[...] = full[at_rows(part * group, group, 8), :]
    value = scaled[...]
    product = quadrants(dot(stacked(value), both(full[...])))
    product = quadrants(dot(stacked(product), start[...]))
    back[...] = 2.0 * value - product
    link = link_diag.shape[1]
    link_diag[...] = own_terms[:, :link] + came[:, :link]
    link_cross[...] = own_terms[:, link:] + came[:, link:]


def call(kernel, outs, scratch, info, *args, whole=False, alias={}):
    vmem = pl.BlockSpec(memory_space=pltpu.VMEM)
    return pl.pallas_call(
        kernel,
        out_shape=[jax.ShapeDtypeStruct(shape, dtype) for shape, dtype in outs],
        in_specs=[pl.BlockSpec(memory_space=pltpu.SMEM)]
        + [pl.BlockSpec(memory_space=pltpu.HBM) if whole else vmem] * len(args),
        out_specs=[vmem] * len(outs),
        scratch_shapes=scratch,
        input_output_aliases=alias,
        compiler_params=pltpu.CompilerParams(vmem_limit_bytes=VMEM_BYTES),
        cost_estimate=pl.CostEstimate(flops=0, bytes_accessed=0, transcendentals=0),
        name=kernel.__name__,
    )(info, *args)


def after(value, *others):
    return lax.optimization_barrier((value, *others))[0]


def shards(
    blocks, operator, initial, block_sizes, link_index, link_pair, link_global, schur_base,
    schur_start,
):
    part, block = lax.axis_index("tile"), lax.axis_index("tm")
    info = jnp.stack([part, block_sizes[0], block]).astype(jnp.int32)
    operator, initial = operator[0], initial[0]
    pair, glob = link_pair[0], link_global[0]
    rows, order = operator.shape
    half = order // 2
    unit = half // 3
    link, width = pair.shape[1] // 2, glob.shape[1]
    group, share = width // 4, link // 4
    size = group + group // 4

    def tile_swap(value, mask):
        return lax.ppermute(value, "tile", [(i, i ^ mask) for i in range(4)])

    def block_swap(value, mask):
        return lax.ppermute(value, "tm", [(i, i ^ mask) for i in range(blocks)])

    def diagonal_swap(value):
        pairs = [
            (b * 4 + i, (b ^ 1) * 4 + (i ^ 2)) for b in range(blocks) for i in range(4)
        ]
        return lax.ppermute(value, ("tm", "tile"), pairs)

    vmem, matrix = pltpu.VMEM, ((2 * order, order), BF16)

    g_far = tile_swap(glob, 2)
    sent = call(
        pack_kernel,
        [((6 * unit, unit), F32)],
        [vmem((rows, half), F32), vmem((rows, half), F32), pltpu.SemaphoreType.DMA((2,))],
        info, initial, operator, whole=True,
    )[0]
    far = tile_swap(sent, 2)
    x_core, k_core, g_core = (tile_swap(v, 1) for v in (initial, operator, glob))
    g_far = after(g_far, sent)
    x, k, links = call(
        spread_kernel,
        [matrix, matrix, ((order, width), BF16)],
        [vmem((half, order), F32), vmem((order, width), BF16)],
        info, initial, x_core, operator, k_core, glob, g_core, g_far, tile_swap(g_far, 1),
        link_index,
    )
    far = after(far, links)
    keep, send, y_own, y_core, y_far, y_cross, x, k = call(
        global_kernel,
        [((size, group), F32)] * 2 + [((rows, group), F32)] * 4 + [matrix, matrix],
        [vmem((2 * size, group), F32), vmem((order, group), F32),
         vmem((2, 3 * unit, unit), F32)],
        info, far, tile_swap(far, 1), x, k, links, schur_base, alias={3: 6, 4: 7},
    )
    p_far, s_far = tile_swap(after(pair, far), 2), tile_swap(after(schur_start, far), 2)

    p_far = after(p_far, keep)
    p_all = (pair, tile_swap(pair, 1), p_far, tile_swap(p_far, 1))
    masked, columns, state = call(
        pair_kernel,
        [((order, 2 * link), BF16), ((order, 2 * share), F32), ((order, 2 * share), F32)],
        [vmem((order, 2 * link), BF16)],
        info, *p_all, x, k,
    )
    y_all = (y_own, tile_swap(y_core, 1), tile_swap(y_far, 2), tile_swap(y_cross, 3))
    came = [block_swap(send, 1)]
    if blocks > 2:
        came += [block_swap(keep, 2), block_swap(send, 3)]
        came[0], state = lax.optimization_barrier((came[0], state))
        total = (keep + came[1]) + (came[0] + came[2])
    else:
        total = keep + came[0]
    s_far = after(s_far, total)
    s_all = (schur_start, tile_swap(schur_start, 1), s_far, tile_swap(s_far, 1))
    own_terms, off_terms, next_terms = call(
        terms_kernel,
        [((share, link + width), F32), ((share, link), F32), ((share, link + width), F32)],
        [],
        info, masked, columns, after(state, total), x, k, links,
    )
    step = 4
    while step < blocks:
        other = block_swap(total, step)
        if step == 4:
            other = after(other, off_terms)
        total = total + other
        step *= 2
    total, *y_all = lax.optimization_barrier((total, *y_all))
    start, scaled = call(
        start_kernel,
        [((width, 2 * width), BF16), ((rows, width), F32)],
        [],
        info, *s_all, *y_all,
    )

    here = (total, block_swap(total, 1))
    there = (tile_swap(total, 2), diagonal_swap(total))
    sums = []
    for pieces in (here, there):
        sums += [*pieces, *(tile_swap(piece, 1) for piece in pieces)]
    came = lax.ppermute(next_terms, "tm", [(i + 1, i) for i in range(blocks - 1)])
    link_diag, link_cross, global_schur, back_cols = call(
        back_kernel,
        [((share, link), F32), ((share, width), F32), ((group, width), F32),
         ((rows, width), F32)],
        [vmem((8 * size, group), F32), vmem((width, width), F32)],
        info, *sums, start, scaled, own_terms, came,
    )
    return (
        link_diag[None], off_terms[None], link_cross[None], global_schur, back_cols[None],
    )


def solution(mesh):
    return jax.shard_map(
        functools.partial(shards, mesh.shape["tm"]),
        mesh=mesh,
        in_specs=(
            P("tm", "tile", None),
            P("tm", "tile", None),
            P("tm"),
            P("tm", None),
            P("tm", "tile", None),
            P("tm", "tile", None),
            P("tile", None),
            P("tile", None),
        ),
        out_specs=(
            P("tm", "tile", None),
            P("tm", "tile", None),
            P("tm", "tile", None),
            P("tile", None),
            P("tm", "tile", None),
        ),
        check_vma=False,
    )
```

time: 75.4 us -> 69.7 us (0.924)
  the two profiles are of different devices: /device:TPU:9 before, /device:TPU:0 now
where the time goes in v2:
time: 69.7 us; the launch traced here: 69.4 us
  Pallas kernels  28.4 us (41%)
  starting transfers between devices  20.8 us (30%)
  waiting for transfers between devices  14.9 us (21%)
  local copies, waits for them, and re-layouts  3.75 us (5%)
  between operations  1.46 us (2%)
    pallas_call x7, Pallas kernels, call(): pl.pallas_call(kernel, out_shape=[jax.ShapeDtypeStruct(shape, dtype) for...  28.4 us
    ppermute x21, starting transfers between devices, tile_swap(): return lax.ppermute(value, 'tile', [(i, i ^ mask) for i in range(4)])  10.2 us
    ppermute x5, starting transfers between devices, block_swap(): return lax.ppermute(value, 'tm', [(i, i ^ mask) for i in range(blocks)])  8.85 us
    ppermute x21, waiting for transfers between devices, tile_swap(): return lax.ppermute(value, 'tile', [(i, i ^ mask) for i in range(4)])  7.68 us
    ppermute x5, waiting for transfers between devices, block_swap(): return lax.ppermute(value, 'tm', [(i, i ^ mask) for i in range(blocks)])  5.75 us
    unnamed x14, local copies, waits for them, and re-layouts  3.75 us
    ppermute x1, waiting for transfers between devices, diagonal_swap(): return lax.ppermute(value, ('tm', 'tile'), pairs)  1.51 us
  transfers between devices with their start and end apart: 28, of which 8 were waited for; matrix products, arithmetic and copies ran while one was open for 0% of the time, Pallas kernels for 37%

profile of v2, /device:TPU:0, one launch (start us, length us, event | category | flops | bytes accessed | tf_op | source)
XLA Modules:
  0.0 69.4 jit_solution(11118391910735976975)
XLA Ops:
  0.6 0.5 collective-permute-start.1
  1.1 0.1 collective-permute-start.2
  1.2 2.9 %collective-permute-start.4 = (bf16[192,512]{1,0:T(8,128)(2,1)}, bf16[192,512]{1,0:T(8,128)(2,1)S(1)}, u32[]{:S(2)}, u32[]{:S(2)}) collective-permute-start(bf16[192,512]{1,0:T(8,128)(2,1)} %bitcast.19), channel_id=1, source_target_pairs={{0,2},{1,3},{2,0},{3,1},{4,6},{5,7},{6,4},{7,5},{8,10},{9,11},{10,... | collective-permute-start | bytes 589832 | tf_op jit(solution)/shard_map/ppermute | solution.py:338
  4.8 0.1 pad_add_fusion.info
  4.9 1.1 %copy-done = f32[1,192,768]{2,1,0:T(8,128)S(1)} copy-done((f32[1,192,768]{2,1,0:T(8,128)S(1)}, f32[1,192,768]{2,1,0:T(8,128)}, u32[]{:S(2)}) %copy-start) | copy-done | bytes 589848
  6.0 1.1 %copy-done.1 = f32[1,192,768]{2,1,0:T(8,128)S(1)} copy-done((f32[1,192,768]{2,1,0:T(8,128)S(1)}, f32[1,192,768]{2,1,0:T(8,128)}, u32[]{:S(2)}) %copy-start.1) | copy-done | bytes 589848
  7.0 0.8 %pack_kernel.1 = f32[768,128]{1,0:T(8,128)S(1)} custom-call(s32[3]{0:T(128)S(1)} %pad_add_fusion.info, f32[192,768]{1,0:T(8,128)S(1)} %bitcast.11, f32[192,768]{1,0:T(8,128)S(1)} %bitcast.14), custom_call_target="tpu_custom_call" | custom-call | tf_op jit(solution)/shard_map/pack_kernel/pallas_call | solution.py:304
  7.9 0.1 collective-permute-start
  8.0 0.1 collective-permute-start.3
  8.0 1.5 %collective-permute-done.4.g_far = bf16[192,512]{1,0:T(8,128)(2,1)S(1)} collective-permute-done((bf16[192,512]{1,0:T(8,128)(2,1)}, bf16[192,512]{1,0:T(8,128)(2,1)S(1)}, u32[]{:S(2)}, u32[]{:S(2)}) %collective-permute-start.4) | collective-permute-done | bytes 196640 | tf_op jit(solution)/shard_map/ppermute | solution.py:338
  9.5 0.0 collective-permute-start.5
  9.5 0.1 collective-permute-done.3.g_core
  9.7 1.3 %collective-permute-done.5.g_cross = bf16[192,512]{1,0:T(8,128)(2,1)S(1)} collective-permute-done((bf16[192,512]{1,0:T(8,128)(2,1)S(1)}, bf16[192,512]{1,0:T(8,128)(2,1)S(1)}, u32[]{:S(2)}, u32[]{:S(2)}) %collective-permute-start.5) | collective-permute-done | bytes 196640 | tf_op jit(solution)/shard_map/ppermute | solution.py:338
  11.0 0.9 %copy-done.5 = bf16[1,192,512]{2,1,0:T(8,128)(2,1)S(1)} copy-done((bf16[1,192,512]{2,1,0:T(8,128)(2,1)S(1)}, bf16[1,192,512]{2,1,0:T(8,128)(2,1)}, u32[]{:S(2)}) %copy-start.5) | copy-done | bytes 196632
  11.9 0.7 copy-done.6
  12.6 2.1 %spread_kernel.1 = (bf16[1536,768]{1,0:T(8,128)(2,1)S(1)}, bf16[1536,768]{1,0:T(8,128)(2,1)S(1)}, bf16[768,512]{1,0:T(8,128)(2,1)S(1)}) custom-call(s32[3]{0:T(128)S(1)} %pad_add_fusion.info, f32[192,768]{1,0:T(8,128)S(1)} %bitcast.12, f32[192,768]{1,0:T(8,128)S(1)} %collective-permute-done.1.x_core, f32[192,768]{1,0:T(8,128)S(1)} %bitcast.15, ...), custom_call_target="tpu_custom_call" | custom-call | tf_op jit(solution)/shard_map/spread_kernel/pallas_call | solution.py:304
  14.7 4.1 %collective-permute-done.far = f32[768,128]{1,0:T(8,128)S(1)} collective-permute-done((f32[768,128]{1,0:T(8,128)S(1)}, f32[768,128]{1,0:T(8,128)S(1)}, u32[]{:S(2)}, u32[]{:S(2)}) %collective-permute-start) | collective-permute-done | bytes 393248 | tf_op jit(solution)/shard_map/ppermute | solution.py:338
  18.8 0.0 collective-permute-start.6
  18.8 0.9 %collective-permute-start.10 = (bf16[192,512]{1,0:T(8,128)(2,1)S(1)}, bf16[192,512]{1,0:T(8,128)(2,1)S(1)}, u32[]{:S(2)}, u32[]{:S(2)}) collective-permute-start(bf16[192,512]{1,0:T(8,128)(2,1)S(1)} %bitcast.16), channel_id=1, source_target_pairs={{0,2},{1,3},{2,0},{3,1},{4,6},{5,7},{6,4},{7,5},{8,10},{9,11},{10,... | collective-permute-start | bytes 589832 | tf_op jit(solution)/shard_map/ppermute | solution.py:338
  19.7 0.2 collective-permute-start.9
  19.9 0.6 collective-permute-done.6.cross
  20.5 10.1 %global_kernel.1 = (f32[160,128]{1,0:T(8,128)S(1)}, f32[160,128]{1,0:T(8,128)S(1)}, f32[192,128]{1,0:T(8,128)S(1)}, f32[192,128]{1,0:T(8,128)S(1)}, f32[192,128]...) custom-call(s32[3]{0:T(128)S(1)} %pad_add_fusion.info, ...), custom_call_target="tpu_custom_call", output_to_operand_aliasing={{6}: (3, {}), {7}: (4, {})} | custom-call | tf_op jit(solution)/shard_map/global_kernel/pallas_call | solution.py:304
  30.6 0.0 collective-permute-done.10.p_far
  30.6 0.2 collective-permute-start.11
  30.8 1.5 %collective-permute-start.8 = (f32[160,128]{1,0:T(8,128)S(1)}, f32[160,128]{1,0:T(8,128)S(1)}, u32[]{:S(2)}, u32[]{:S(2)}) collective-permute-start(f32[160,128]{1,0:T(8,128)S(1)} %get-tuple-element.49), channel_id=1, source_target_pairs={{0,4},{4,0},{8,12},{12,8},{16,20},{20,16},{24,28},{28,24},{1,5},{5... | collective-permute-start | bytes 245768 | tf_op jit(solution)/shard_map/ppermute | solution.py:341
  32.3 1.5 %collective-permute-start.12 = (f32[160,128]{1,0:T(8,128)S(1)}, f32[160,128]{1,0:T(8,128)S(1)}, u32[]{:S(2)}, u32[]{:S(2)}) collective-permute-start(f32[160,128]{1,0:T(8,128)S(1)} %get-tuple-element.49), channel_id=1, source_target_pairs={{0,12},{4,8},{8,4},{12,0},{16,28},{20,24},{24,20},{28,16},{1,13},{... | collective-permute-start | bytes 245768 | tf_op jit(solution)/shard_map/ppermute | solution.py:341
  33.8 0.5 collective-permute-start.7
  34.3 0.9 %collective-permute-start.25 = (f32[128,512]{1,0:T(8,128)S(1)}, f32[128,512]{1,0:T(8,128)S(1)}, u32[]{:S(2)}, u32[]{:S(2)}) collective-permute-start(f32[128,512]{1,0:T(8,128)S(1)} %copy-done.2), channel_id=1, source_target_pairs={{0,2},{1,3},{2,0},{3,1},{4,6},{5,7},{6,4},{7,5},{8,10},{9,11},{10,... | collective-permute-start | bytes 786440 | tf_op jit(solution)/shard_map/ppermute | solution.py:338
  35.2 0.0 collective-permute-done.11.p_cross
  35.2 0.0 collective-permute-start.24
  35.2 6.1 %pair_kernel.1 = (bf16[768,512]{1,0:T(8,128)(2,1)S(1)}, f32[768,128]{1,0:T(8,128)S(1)}, f32[768,128]{1,0:T(8,128)S(1)}) custom-call(s32[3]{0:T(128)S(1)} %pad_add_fusion.info, bf16[192,512]{1,0:T(8,128)(2,1)S(1)} %bitcast.18, bf16[192,512]{1,0:T(8,128)(2,1)S(1)} %collective-permute-done.9.p_core, bf16[192,512]{1,0:T(8,128)(2,1)S(1)} %collective-permute-done.10.p_far, ...), custom_call_target="tpu_custom_call" | custom-call | tf_op jit(solution)/shard_map/pair_kernel/pallas_call | solution.py:304
  41.3 0.6 collective-permute-start.14
  41.9 0.1 collective-permute-done.25.s_far
  42.0 0.0 collective-permute-start.26
  42.0 2.6 %collective-permute-start.13 = (f32[160,128]{1,0:T(8,128)S(1)}, f32[160,128]{1,0:T(8,128)S(1)}, u32[]{:S(2)}, u32[]{:S(2)}) collective-permute-start(f32[160,128]{1,0:T(8,128)S(1)} %add_add_fusion), channel_id=1, source_target_pairs={{0,16},{4,20},{8,24},{12,28},{16,0},{20,4},{24,8},{28,12},{1,17},{... | collective-permute-start | bytes 245768 | tf_op jit(solution)/shard_map/ppermute | solution.py:341
  44.6 1.1 %collective-permute-start.15 = (f32[192,128]{1,0:T(8,128)S(1)}, f32[192,128]{1,0:T(8,128)S(1)}, u32[]{:S(2)}, u32[]{:S(2)}) collective-permute-start(f32[192,128]{1,0:T(8,128)S(1)} %get-tuple-element.64), channel_id=1, source_target_pairs={{0,2},{1,3},{2,0},{3,1},{4,6},{5,7},{6,4},{7,5},{8,10},{9,11},{10,... | collective-permute-start | bytes 294920 | tf_op jit(solution)/shard_map/ppermute | solution.py:338
  45.7 0.4 collective-permute-start.16
  46.2 5.2 %terms_kernel.1 = (f32[64,768]{1,0:T(8,128)S(1)}, f32[64,256]{1,0:T(8,128)}, f32[64,768]{1,0:T(8,128)S(1)}) custom-call(s32[3]{0:T(128)S(1)} %pad_add_fusion.info, bf16[768,512]{1,0:T(8,128)(2,1)S(1)} %get-tuple-element.56.masked, f32[768,128]{1,0:T(8,128)S(1)} %get-tuple-element.57.columns, f32[768,128]{1,0:T(8,128)S(1)} %get-tuple-element.59.state, ...), custom_call_target="tpu_custom_call" | custom-call | tf_op jit(solution)/shard_map/terms_kernel/pallas_call | solution.py:304
  51.4 1.3 %collective-permute-start.27 = (f32[64,768]{1,0:T(8,128)S(1)}, f32[64,768]{1,0:T(8,128)S(1)}, u32[]{:S(2)}, u32[]{:S(2)}) collective-permute-start(f32[64,768]{1,0:T(8,128)S(1)} %get-tuple-element.76), channel_id=1, source_target_pairs={{4,0},{8,4},{12,8},{16,12},{20,16},{24,20},{28,24},{5,1},{9,5},{13... | collective-permute-start | bytes 589832 | tf_op jit(solution)/shard_map/ppermute | solution.py:422
  52.8 2.7 %collective-permute-start.17 = (f32[160,128]{1,0:T(8,128)S(1)}, f32[160,128]{1,0:T(8,128)S(1)}, u32[]{:S(2)}, u32[]{:S(2)}) collective-permute-start(f32[160,128]{1,0:T(8,128)S(1)} %add.15.refs_0_), channel_id=1, source_target_pairs={{0,4},{4,0},{8,12},{12,8},{16,20},{20,16},{24,28},{28,24},{1,5},{5... | collective-permute-start | bytes 245768 | tf_op jit(solution)/shard_map/ppermute | solution.py:341
  55.5 1.1 %collective-permute-start.20 = (f32[160,128]{1,0:T(8,128)S(1)}, f32[160,128]{1,0:T(8,128)S(1)}, u32[]{:S(2)}, u32[]{:S(2)}) collective-permute-start(f32[160,128]{1,0:T(8,128)S(1)} %add.15.refs_0_), channel_id=1, source_target_pairs={{0,2},{1,3},{2,0},{3,1},{4,6},{5,7},{6,4},{7,5},{8,10},{9,11},{10,... | collective-permute-start | bytes 245768 | tf_op jit(solution)/shard_map/ppermute | solution.py:338
  56.6 0.5 collective-permute-start.21
  57.0 5.7 %collective-permute-done.17.refs_1_ = f32[160,128]{1,0:T(8,128)S(1)} collective-permute-done((f32[160,128]{1,0:T(8,128)S(1)}, f32[160,128]{1,0:T(8,128)S(1)}, u32[]{:S(2)}, u32[]{:S(2)}) %collective-permute-start.17) | collective-permute-done | bytes 81952 | tf_op jit(solution)/shard_map/ppermute | solution.py:341
  62.8 0.5 collective-permute-start.19
  63.3 1.5 %collective-permute-done.21.refs_5_ = f32[160,128]{1,0:T(8,128)S(1)} collective-permute-done((f32[160,128]{1,0:T(8,128)S(1)}, f32[160,128]{1,0:T(8,128)S(1)}, u32[]{:S(2)}, u32[]{:S(2)}) %collective-permute-start.21) | collective-permute-done | bytes 81952 | tf_op jit(solution)/shard_map/ppermute | solution.py:347
  64.8 0.5 collective-permute-start.23
  65.3 1.5 %start_kernel.1 = (bf16[512,1024]{1,0:T(8,128)(2,1)S(1)}, f32[192,512]{1,0:T(8,128)S(1)}) custom-call(s32[3]{0:T(128)S(1)} %pad_add_fusion.info, f32[128,512]{1,0:T(8,128)S(1)} %copy-done.2, f32[128,512]{1,0:T(8,128)S(1)} %collective-permute-done.24.s_core, f32[128,512]{1,0:T(8,128)S(1)} %collective-permute-done.25.s_far, ...), custom_call_target="tpu_custom_call" | custom-call | tf_op jit(solution)/shard_map/start_kernel/pallas_call | solution.py:304
  66.9 2.5 %back_kernel.1 = (f32[64,256]{1,0:T(8,128)}, f32[64,512]{1,0:T(8,128)}, f32[128,512]{1,0:T(8,128)}, f32[192,512]{1,0:T(8,128)}) custom-call(s32[3]{0:T(128)S(1)} %pad_add_fusion.info, f32[160,128]{1,0:T(8,128)S(1)} %add.15.refs_0_, f32[160,128]{1,0:T(8,128)S(1)} %collective-permute-done.17.refs_1_, f32[160,128]{1,0:T(8,128)S(1)} %collective-permute-done.18.refs_2_, ...), custom_call_target="tpu_custom_call" | custom-call | tf_op jit(solution)/shard_map/back_kernel/pallas_call | solution.py:304
  (32 shorter events, 0.1 us)
Async XLA Ops:
  0.6 10.3 %collective-permute-start.1 = (f32[192,768]{1,0:T(8,128)}, f32[192,768]{1,0:T(8,128)S(1)}, u32[]{:S(2)}, u32[]{:S(2)}) collective-permute-start(f32[192,768]{1,0:T(8,128)} %bitcast.10), channel_id=1, source_target_pairs={{0,1},{1,0},{2,3},{3,2},{4,5},{5,4},{6,7},{7,6},{8,9},{9,8},{10,11... | collective-permute-start | bytes 1769480 | tf_op jit(solution)/shard_map/ppermute | solution.py:338
  1.1 9.8 %collective-permute-start.2 = (f32[192,768]{1,0:T(8,128)}, f32[192,768]{1,0:T(8,128)S(1)}, u32[]{:S(2)}, u32[]{:S(2)}) collective-permute-start(f32[192,768]{1,0:T(8,128)} %bitcast.13), channel_id=1, source_target_pairs={{0,1},{1,0},{2,3},{3,2},{4,5},{5,4},{6,7},{7,6},{8,9},{9,8},{10,11... | collective-permute-start | bytes 1769480 | tf_op jit(solution)/shard_map/ppermute | solution.py:338
  1.2 8.3 %collective-permute-start.4 = (bf16[192,512]{1,0:T(8,128)(2,1)}, bf16[192,512]{1,0:T(8,128)(2,1)S(1)}, u32[]{:S(2)}, u32[]{:S(2)}) collective-permute-start(bf16[192,512]{1,0:T(8,128)(2,1)} %bitcast.19), channel_id=1, source_target_pairs={{0,2},{1,3},{2,0},{3,1},{4,6},{5,7},{6,4},{7,5},{8,10},{9,11},{10,... | collective-permute-start | bytes 589832 | tf_op jit(solution)/shard_map/ppermute | solution.py:338
  4.9 1.1 %copy-start = (f32[1,192,768]{2,1,0:T(8,128)S(1)}, f32[1,192,768]{2,1,0:T(8,128)}, u32[]{:S(2)}) copy-start(f32[1,192,768]{2,1,0:T(8,128)} %param.9) | copy-start | bytes 1769476
  6.0 1.1 %copy-start.1 = (f32[1,192,768]{2,1,0:T(8,128)S(1)}, f32[1,192,768]{2,1,0:T(8,128)}, u32[]{:S(2)}) copy-start(f32[1,192,768]{2,1,0:T(8,128)} %param.8) | copy-start | bytes 1769476
  7.0 11.7 %copy-start.4 = (bf16[1,192,512]{2,1,0:T(8,128)(2,1)S(1)}, bf16[1,192,512]{2,1,0:T(8,128)(2,1)}, u32[]{:S(2)}) copy-start(bf16[1,192,512]{2,1,0:T(8,128)(2,1)} %param.12) | copy-start | bytes 589828
  7.0 13.5 %copy-start.3 = (f32[128,512]{1,0:T(8,128)S(1)}, f32[128,512]{1,0:T(8,128)}, u32[]{:S(2)}) copy-start(f32[128,512]{1,0:T(8,128)} %base.1) | copy-start | bytes 786436
  7.9 10.9 %collective-permute-start = (f32[768,128]{1,0:T(8,128)S(1)}, f32[768,128]{1,0:T(8,128)S(1)}, u32[]{:S(2)}, u32[]{:S(2)}) collective-permute-start(f32[768,128]{1,0:T(8,128)S(1)} %pack_kernel.1), channel_id=1, source_target_pairs={{0,2},{1,3},{2,0},{3,1},{4,6},{5,7},{6,4},{7,5},{8,10},{9,11},{10,... | collective-permute-start | bytes 1179656 | tf_op jit(solution)/shard_map/ppermute | solution.py:338
  8.0 1.7 %collective-permute-start.3 = (bf16[192,512]{1,0:T(8,128)(2,1)}, bf16[192,512]{1,0:T(8,128)(2,1)S(1)}, u32[]{:S(2)}, u32[]{:S(2)}) collective-permute-start(bf16[192,512]{1,0:T(8,128)(2,1)} %bitcast.20), channel_id=1, source_target_pairs={{0,1},{1,0},{2,3},{3,2},{4,5},{5,4},{6,7},{7,6},{8,9},{9,8},{10,11... | collective-permute-start | bytes 589832 | tf_op jit(solution)/shard_map/ppermute | solution.py:338
  9.5 1.4 %collective-permute-start.5 = (bf16[192,512]{1,0:T(8,128)(2,1)S(1)}, bf16[192,512]{1,0:T(8,128)(2,1)S(1)}, u32[]{:S(2)}, u32[]{:S(2)}) collective-permute-start(bf16[192,512]{1,0:T(8,128)(2,1)S(1)} %collective-permute-done.4.g_far), channel_id=1, source_target_pairs={{0,1},{1,0},{2,3},{3,2},{4,5},{5,4},{6,7},{7,6},{8,9},{9,8},{10,11... | collective-permute-start | bytes 589832 | tf_op jit(solution)/shard_map/ppermute | solution.py:338
  11.0 0.9 %copy-start.5 = (bf16[1,192,512]{2,1,0:T(8,128)(2,1)S(1)}, bf16[1,192,512]{2,1,0:T(8,128)(2,1)}, u32[]{:S(2)}) copy-start(bf16[1,192,512]{2,1,0:T(8,128)(2,1)} %param.13) | copy-start | bytes 589828
  11.9 0.7 copy-start.6
  18.8 1.7 %collective-permute-start.6 = (f32[768,128]{1,0:T(8,128)S(1)}, f32[768,128]{1,0:T(8,128)S(1)}, u32[]{:S(2)}, u32[]{:S(2)}) collective-permute-start(f32[768,128]{1,0:T(8,128)S(1)} %collective-permute-done.far), channel_id=1, source_target_pairs={{0,1},{1,0},{2,3},{3,2},{4,5},{5,4},{6,7},{7,6},{8,9},{9,8},{10,11... | collective-permute-start | bytes 1179656 | tf_op jit(solution)/shard_map/ppermute | solution.py:338
  18.8 11.8 %collective-permute-start.10 = (bf16[192,512]{1,0:T(8,128)(2,1)S(1)}, bf16[192,512]{1,0:T(8,128)(2,1)S(1)}, u32[]{:S(2)}, u32[]{:S(2)}) collective-permute-start(bf16[192,512]{1,0:T(8,128)(2,1)S(1)} %bitcast.16), channel_id=1, source_target_pairs={{0,2},{1,3},{2,0},{3,1},{4,6},{5,7},{6,4},{7,5},{8,10},{9,11},{10,... | collective-permute-start | bytes 589832 | tf_op jit(solution)/shard_map/ppermute | solution.py:338
  19.7 14.6 %collective-permute-start.9 = (bf16[192,512]{1,0:T(8,128)(2,1)S(1)}, bf16[192,512]{1,0:T(8,128)(2,1)S(1)}, u32[]{:S(2)}, u32[]{:S(2)}) collective-permute-start(bf16[192,512]{1,0:T(8,128)(2,1)S(1)} %bitcast.17), channel_id=1, source_target_pairs={{0,1},{1,0},{2,3},{3,2},{4,5},{5,4},{6,7},{7,6},{8,9},{9,8},{10,11... | collective-permute-start | bytes 589832 | tf_op jit(solution)/shard_map/ppermute | solution.py:338
  20.5 13.8 %copy-start.2 = (f32[128,512]{1,0:T(8,128)S(1)}, f32[128,512]{1,0:T(8,128)}, u32[]{:S(2)}) copy-start(f32[128,512]{1,0:T(8,128)} %s_own.1) | copy-start | bytes 786436
  30.6 4.6 %collective-permute-start.11 = (bf16[192,512]{1,0:T(8,128)(2,1)S(1)}, bf16[192,512]{1,0:T(8,128)(2,1)S(1)}, u32[]{:S(2)}, u32[]{:S(2)}) collective-permute-start(bf16[192,512]{1,0:T(8,128)(2,1)S(1)} %collective-permute-done.10.p_far), channel_id=1, source_target_pairs={{0,1},{1,0},{2,3},{3,2},{4,5},{5,4},{6,7},{7,6},{8,9},{9,8},{10,11... | collective-permute-start | bytes 589832 | tf_op jit(solution)/shard_map/ppermute | solution.py:338
  30.8 10.5 %collective-permute-start.8 = (f32[160,128]{1,0:T(8,128)S(1)}, f32[160,128]{1,0:T(8,128)S(1)}, u32[]{:S(2)}, u32[]{:S(2)}) collective-permute-start(f32[160,128]{1,0:T(8,128)S(1)} %get-tuple-element.49), channel_id=1, source_target_pairs={{0,4},{4,0},{8,12},{12,8},{16,20},{20,16},{24,28},{28,24},{1,5},{5... | collective-permute-start | bytes 245768 | tf_op jit(solution)/shard_map/ppermute | solution.py:341
  32.3 9.6 %collective-permute-start.12 = (f32[160,128]{1,0:T(8,128)S(1)}, f32[160,128]{1,0:T(8,128)S(1)}, u32[]{:S(2)}, u32[]{:S(2)}) collective-permute-start(f32[160,128]{1,0:T(8,128)S(1)} %get-tuple-element.49), channel_id=1, source_target_pairs={{0,12},{4,8},{8,4},{12,0},{16,28},{20,24},{24,20},{28,16},{1,13},{... | collective-permute-start | bytes 245768 | tf_op jit(solution)/shard_map/ppermute | solution.py:341
  33.8 8.1 %collective-permute-start.7 = (f32[160,128]{1,0:T(8,128)S(1)}, f32[160,128]{1,0:T(8,128)S(1)}, u32[]{:S(2)}, u32[]{:S(2)}) collective-permute-start(f32[160,128]{1,0:T(8,128)S(1)} %get-tuple-element.48), channel_id=1, source_target_pairs={{0,8},{4,12},{8,0},{12,4},{16,24},{20,28},{24,16},{28,20},{1,9},{5... | collective-permute-start | bytes 245768 | tf_op jit(solution)/shard_map/ppermute | solution.py:341
  34.3 7.7 %collective-permute-start.25 = (f32[128,512]{1,0:T(8,128)S(1)}, f32[128,512]{1,0:T(8,128)S(1)}, u32[]{:S(2)}, u32[]{:S(2)}) collective-permute-start(f32[128,512]{1,0:T(8,128)S(1)} %copy-done.2), channel_id=1, source_target_pairs={{0,2},{1,3},{2,0},{3,1},{4,6},{5,7},{6,4},{7,5},{8,10},{9,11},{10,... | collective-permute-start | bytes 786440 | tf_op jit(solution)/shard_map/ppermute | solution.py:338
  35.2 21.3 %collective-permute-start.24 = (f32[128,512]{1,0:T(8,128)S(1)}, f32[128,512]{1,0:T(8,128)S(1)}, u32[]{:S(2)}, u32[]{:S(2)}) collective-permute-start(f32[128,512]{1,0:T(8,128)S(1)} %copy-done.2), channel_id=1, source_target_pairs={{0,1},{1,0},{2,3},{3,2},{4,5},{5,4},{6,7},{7,6},{8,9},{9,8},{10,11... | collective-permute-start | bytes 786440 | tf_op jit(solution)/shard_map/ppermute | solution.py:338
  41.3 4.5 %collective-permute-start.14 = (f32[192,128]{1,0:T(8,128)S(1)}, f32[192,128]{1,0:T(8,128)S(1)}, u32[]{:S(2)}, u32[]{:S(2)}) collective-permute-start(f32[192,128]{1,0:T(8,128)S(1)} %get-tuple-element.63), channel_id=1, source_target_pairs={{0,1},{1,0},{2,3},{3,2},{4,5},{5,4},{6,7},{7,6},{8,9},{9,8},{10,11... | collective-permute-start | bytes 294920 | tf_op jit(solution)/shard_map/ppermute | solution.py:338
  42.0 22.8 %collective-permute-start.26 = (f32[128,512]{1,0:T(8,128)S(1)}, f32[128,512]{1,0:T(8,128)S(1)}, u32[]{:S(2)}, u32[]{:S(2)}) collective-permute-start(f32[128,512]{1,0:T(8,128)S(1)} %collective-permute-done.25.s_far), channel_id=1, source_target_pairs={{0,1},{1,0},{2,3},{3,2},{4,5},{5,4},{6,7},{7,6},{8,9},{9,8},{10,11... | collective-permute-start | bytes 786440 | tf_op jit(solution)/shard_map/ppermute | solution.py:338
  42.0 9.4 %collective-permute-start.13 = (f32[160,128]{1,0:T(8,128)S(1)}, f32[160,128]{1,0:T(8,128)S(1)}, u32[]{:S(2)}, u32[]{:S(2)}) collective-permute-start(f32[160,128]{1,0:T(8,128)S(1)} %add_add_fusion), channel_id=1, source_target_pairs={{0,16},{4,20},{8,24},{12,28},{16,0},{20,4},{24,8},{28,12},{1,17},{... | collective-permute-start | bytes 245768 | tf_op jit(solution)/shard_map/ppermute | solution.py:341
  44.6 8.1 %collective-permute-start.15 = (f32[192,128]{1,0:T(8,128)S(1)}, f32[192,128]{1,0:T(8,128)S(1)}, u32[]{:S(2)}, u32[]{:S(2)}) collective-permute-start(f32[192,128]{1,0:T(8,128)S(1)} %get-tuple-element.64), channel_id=1, source_target_pairs={{0,2},{1,3},{2,0},{3,1},{4,6},{5,7},{6,4},{7,5},{8,10},{9,11},{10,... | collective-permute-start | bytes 294920 | tf_op jit(solution)/shard_map/ppermute | solution.py:338
  45.7 7.0 %collective-permute-start.16 = (f32[192,128]{1,0:T(8,128)S(1)}, f32[192,128]{1,0:T(8,128)S(1)}, u32[]{:S(2)}, u32[]{:S(2)}) collective-permute-start(f32[192,128]{1,0:T(8,128)S(1)} %get-tuple-element.65), channel_id=1, source_target_pairs={{0,3},{1,2},{2,1},{3,0},{4,7},{5,6},{6,5},{7,4},{8,11},{9,10},{10,... | collective-permute-start | bytes 294920 | tf_op jit(solution)/shard_map/ppermute | solution.py:338
  51.4 15.4 %collective-permute-start.27 = (f32[64,768]{1,0:T(8,128)S(1)}, f32[64,768]{1,0:T(8,128)S(1)}, u32[]{:S(2)}, u32[]{:S(2)}) collective-permute-start(f32[64,768]{1,0:T(8,128)S(1)} %get-tuple-element.76), channel_id=1, source_target_pairs={{4,0},{8,4},{12,8},{16,12},{20,16},{24,20},{28,24},{5,1},{9,5},{13... | collective-permute-start | bytes 589832 | tf_op jit(solution)/shard_map/ppermute | solution.py:422
  52.8 10.0 %collective-permute-start.17 = (f32[160,128]{1,0:T(8,128)S(1)}, f32[160,128]{1,0:T(8,128)S(1)}, u32[]{:S(2)}, u32[]{:S(2)}) collective-permute-start(f32[160,128]{1,0:T(8,128)S(1)} %add.15.refs_0_), channel_id=1, source_target_pairs={{0,4},{4,0},{8,12},{12,8},{16,20},{20,16},{24,28},{28,24},{1,5},{5... | collective-permute-start | bytes 245768 | tf_op jit(solution)/shard_map/ppermute | solution.py:341
  55.5 7.3 %collective-permute-start.20 = (f32[160,128]{1,0:T(8,128)S(1)}, f32[160,128]{1,0:T(8,128)S(1)}, u32[]{:S(2)}, u32[]{:S(2)}) collective-permute-start(f32[160,128]{1,0:T(8,128)S(1)} %add.15.refs_0_), channel_id=1, source_target_pairs={{0,2},{1,3},{2,0},{3,1},{4,6},{5,7},{6,4},{7,5},{8,10},{9,11},{10,... | collective-permute-start | bytes 245768 | tf_op jit(solution)/shard_map/ppermute | solution.py:338
  56.6 8.2 %collective-permute-start.21 = (f32[160,128]{1,0:T(8,128)S(1)}, f32[160,128]{1,0:T(8,128)S(1)}, u32[]{:S(2)}, u32[]{:S(2)}) collective-permute-start(f32[160,128]{1,0:T(8,128)S(1)} %add.15.refs_0_), channel_id=1, source_target_pairs={{0,6},{1,7},{2,4},{3,5},{4,2},{5,3},{6,0},{7,1},{8,14},{9,15},{10,... | collective-permute-start | bytes 245768 | tf_op jit(solution)/shard_map/ppermute | solution.py:347
  62.8 4.1 %collective-permute-start.18 = (f32[160,128]{1,0:T(8,128)S(1)}, f32[160,128]{1,0:T(8,128)S(1)}, u32[]{:S(2)}, u32[]{:S(2)}) collective-permute-start(f32[160,128]{1,0:T(8,128)S(1)} %add.15.refs_0_), channel_id=1, source_target_pairs={{0,1},{1,0},{2,3},{3,2},{4,5},{5,4},{6,7},{7,6},{8,9},{9,8},{10,11... | collective-permute-start | bytes 245768 | tf_op jit(solution)/shard_map/ppermute | solution.py:338
  62.8 4.1 %collective-permute-start.19 = (f32[160,128]{1,0:T(8,128)S(1)}, f32[160,128]{1,0:T(8,128)S(1)}, u32[]{:S(2)}, u32[]{:S(2)}) collective-permute-start(f32[160,128]{1,0:T(8,128)S(1)} %collective-permute-done.17.refs_1_), channel_id=1, source_target_pairs={{0,1},{1,0},{2,3},{3,2},{4,5},{5,4},{6,7},{7,6},{8,9},{9,8},{10,11... | collective-permute-start | bytes 245768 | tf_op jit(solution)/shard_map/ppermute | solution.py:338
  64.8 2.1 %collective-permute-start.22 = (f32[160,128]{1,0:T(8,128)S(1)}, f32[160,128]{1,0:T(8,128)S(1)}, u32[]{:S(2)}, u32[]{:S(2)}) collective-permute-start(f32[160,128]{1,0:T(8,128)S(1)} %collective-permute-done.20.refs_4_), channel_id=1, source_target_pairs={{0,1},{1,0},{2,3},{3,2},{4,5},{5,4},{6,7},{7,6},{8,9},{9,8},{10,11... | collective-permute-start | bytes 245768 | tf_op jit(solution)/shard_map/ppermute | solution.py:338
  64.8 2.1 %collective-permute-start.23 = (f32[160,128]{1,0:T(8,128)S(1)}, f32[160,128]{1,0:T(8,128)S(1)}, u32[]{:S(2)}, u32[]{:S(2)}) collective-permute-start(f32[160,128]{1,0:T(8,128)S(1)} %collective-permute-done.21.refs_5_), channel_id=1, source_target_pairs={{0,1},{1,0},{2,3},{3,2},{4,5},{5,4},{6,7},{7,6},{8,9},{9,8},{10,11... | collective-permute-start | bytes 245768 | tf_op jit(solution)/shard_map/ppermute | solution.py:338

commit v3 on v2

v3 whole, which is shorter than its diff:
```python
import functools

import jax
import jax.numpy as jnp
from jax import lax
from jax.experimental import pallas as pl
from jax.experimental.pallas import tpu as pltpu
from jax.sharding import PartitionSpec as P

BF16 = jnp.bfloat16
F32 = jnp.float32
STEPS = 2
TERMS = 2**STEPS - 1
SPARE = 8
VMEM_BYTES = 32 * 2**20


def halves(value):
    high = value.astype(BF16)
    return high, (value - high.astype(F32)).astype(BF16)


def dot(left_side, right_side):
    return jnp.dot(left_side, right_side, preferred_element_type=F32)


def both(value):
    return jnp.concatenate(halves(value), axis=1)


def stacked(value):
    return jnp.concatenate(halves(value), axis=0)


def at(start, size, unit=16):
    return pl.ds(pl.multiple_of(start, unit), size)


def place():
    part = lax.axis_index("tile")
    return part, part // 2, part % 2


def live_rows(sizes, half):
    near, size = place()[1], sizes[0]
    ids = lax.broadcasted_iota(jnp.int32, (half, 1), 0)
    return jnp.concatenate(
        [(ids + near * half) < size, (ids + (1 - near) * half) < size], axis=0
    )


def put_rows(own, other, target, offset=0):
    rows = own.shape[0]
    core = place()[2]
    target[at(offset + core * rows, rows), :] = own[...]
    target[at(offset + (1 - core) * rows, rows), :] = other[...]


def started(*pairs, sems):
    copies = [
        pltpu.make_async_copy(source, target, sems.at[i])
        for i, (source, target) in enumerate(pairs)
    ]
    for copy in copies:
        copy.start()
    return copies


def pack_kernel(x_rows, k_rows, s_rows, x_out, k_out, s_out, x_part, k_part, sems):
    rows, half = x_part.shape
    unit = half // 3
    _, near, core = place()
    cols = at(near * half, half, 128)
    copies = started(
        (x_rows.at[:, cols], x_part),
        (k_rows.at[:, cols], k_part),
        (s_rows.at[:, at(near * s_out.shape[1], s_out.shape[1], 128)], s_out),
        sems=sems,
    )
    large = at(core * (rows - unit), unit, 8)
    small = at((1 - core) * unit, rows - unit, 8)
    edge = at(core * 2 * unit, unit, 128)
    opposite = at((1 - core) * 2 * unit, unit, 128)
    for copy, part, out in zip(copies, (x_part, k_part), (x_out, k_out)):
        copy.wait()
        out[0:unit, :] = part[large, edge]
        out[unit : 2 * unit, :] = part[large, unit : 2 * unit]
        out[2 * unit : unit + rows, :] = part[small, unit : 2 * unit]
        block = part[large, opposite]
        out[unit + rows : 3 * unit, :] = jnp.where(
            core == 0, block[: unit // 2, :], block.T[unit // 2 :, :]
        )
        out[3 * unit :, :] = jnp.zeros((out.shape[0] - 3 * unit, unit), F32)
    copies[2].wait()


def corner(far, cross, target, live):
    order = target.shape[1]
    half = order // 2
    unit = half // 3
    core = place()[2]

    def joined(first, last):
        mine, theirs = far[first:last, :], cross[first:last, :]
        return jnp.where(core == 0, mine, theirs), jnp.where(core == 0, theirs, mine)

    def put(row, col, value):
        first = half + row * unit
        high, low = halves(jnp.where(live[first : first + unit], value, 0.0))
        cols = slice(half + col * unit, half + (col + 1) * unit)
        target[first : first + unit, cols] = high
        target[order + first : order + first + unit, cols] = low

    zero, one = joined(0, unit)
    put(0, 0, zero)
    put(2, 2, one)
    zero, one = joined(unit, 2 * unit)
    put(0, 1, zero)
    put(1, 0, zero.T)
    put(2, 1, one)
    put(1, 2, one.T)
    put(1, 1, jnp.concatenate(joined(2 * unit, 2 * unit + unit // 2), axis=0))
    side = jnp.concatenate(joined(2 * unit + unit // 2, 3 * unit), axis=0)
    put(0, 2, side)
    put(2, 0, side.T)


def spread(whole, target, live):
    half, order = whole.shape
    for rows, cols, value in (
        (slice(0, half), slice(0, order), whole[...]),
        (slice(half, order), slice(0, half), whole[:, half:].T),
    ):
        high, low = halves(jnp.where(live[rows], value, 0.0))
        target[rows, cols] = high
        target[order + rows.start : order + rows.stop, cols] = low


def times(matrix, columns):
    order, width = columns.shape
    columns = both(columns)
    step = order // 2
    result = []
    for first in range(0, order, step):
        high = dot(matrix[first : first + step, :], columns)
        low = dot(matrix[order + first : order + first + step, :], columns)
        result.append((high[:, :width] + high[:, width:]) + (low[:, :width] + low[:, width:]))
    return jnp.concatenate(result, axis=0)


def times_wide(left_side, right_side):
    width = right_side.shape[1] // 2
    high, low = halves(left_side)
    product = dot(high, right_side[...])
    return (product[:, :width] + product[:, width:]) + dot(low, right_side[:, :width])


def spread_kernel(
    sizes, x_own, k_own, g_own, index, x_core, k_core, g_core, g_far, g_cross,
    x, k, links, x_whole, k_whole, gathered, g_rows, index_here, sems,
):
    half, order = x_whole.shape
    rows = half // 2
    width = links.shape[1]
    _, near, core = place()
    sides = [at(near * half, half, 128), at((1 - near) * half, half, 128)]
    pairs = [
        (own.at[:, cols], whole.at[at(core * rows, rows), side * half : (side + 1) * half])
        for own, whole in ((x_own, x_whole), (k_own, k_whole))
        for side, cols in enumerate(sides)
    ]
    copies = started(*pairs, (g_own, g_rows), (index, index_here), sems=sems)
    for other, whole in ((x_core, x_whole), (k_core, k_whole)):
        for side, cols in enumerate(sides):
            whole[at((1 - core) * rows, rows), side * half : (side + 1) * half] = other[:, cols]
    put_rows(g_far, g_cross, gathered, half)
    for copy in copies:
        copy.wait()
    put_rows(g_rows, g_core, gathered)
    live = live_rows(sizes, half)
    spread(x_whole, x, live)
    spread(k_whole, k, live)
    hot = lax.broadcasted_iota(jnp.int32, (width, width), 0) == index_here[...]
    chosen = dot(gathered[...], hot.astype(F32).astype(BF16))
    links[...] = jnp.where(live, chosen, 0.0).astype(BF16)


def first_kernel(sizes, far, cross, x_in, links, x, first):
    del x_in
    corner(far, cross, x, live_rows(sizes, x.shape[1] // 2))
    group = links.shape[1] // 4
    columns = links[:, at(place()[0] * group, group, 128)]
    product = dot(x[...], columns)
    first[...] = product[: first.shape[0]] + product[first.shape[0] :]


def global_kernel(
    sizes, far, cross, x, k_in, links, first, base,
    keep, send, y_own, y_core, y_far, y_cross, k, pack, solved,
):
    del k_in
    order, width = links.shape
    half = order // 2
    rows = half // 2
    group = width // 4
    part, _, core = place()
    block = lax.axis_index("tm")
    corner(far, cross, k, live_rows(sizes, half))
    columns = links[:, at(part * group, group, 128)].astype(F32)
    value = 2.0 * columns - times(k, first[...])
    for step in range(TERMS - 1):
        value = columns + value - times(k, times(x, value))
    result = times(x, value)
    solved[...] = result
    y_own[...] = solved[at(core * rows, rows), :]
    y_core[...] = solved[at((1 - core) * rows, rows), :]
    y_far[...] = solved[at(half + core * rows, rows), :]
    y_cross[...] = solved[at(half + (1 - core) * rows, rows), :]
    left_side = stacked(result.T)

    def square(shift):
        cols = at(((part + shift) % 4) * group, group, 128)
        parts = dot(left_side, links[:, cols])
        added = jnp.where(block == 0, base[:, cols], 0.0)
        return parts[:group] + parts[group:] + added

    pack[0:group, :] = square(0)
    pack[group : 2 * group, :] = square(1)
    across = square(2)
    pack[2 * group :, :] = jnp.where(
        part < 2, across[: group // 2, :], across.T[group // 2 :, :]
    )
    size = keep.shape[0]
    side = block % 2
    keep[...] = pack[at(side * size, size, 8), :]
    send[...] = pack[at((1 - side) * size, size, 8), :]


def pair_kernel(
    sizes, p_own, p_core, p_far, p_cross, x, k, links, own_terms, off_terms, next_terms, gathered
):
    half = x.shape[1] // 2
    width = p_own.shape[1]
    link = width // 2
    share = link // 4
    put_rows(p_own, p_core, gathered)
    put_rows(p_far, p_cross, gathered, half)
    masked = jnp.where(live_rows(sizes, half), gathered[...], jnp.zeros((), BF16))
    source = lax.broadcasted_iota(jnp.int32, (width, 2 * share), 0)
    target = lax.broadcasted_iota(jnp.int32, (width, 2 * share), 1)
    wanted = place()[0] * share + target + jnp.where(target < share, 0, link - share)
    columns = dot(masked, (source == wanted).astype(F32).astype(BF16))
    value = columns
    for step in range(TERMS):
        value = columns + value - times(k, times(x, value))
    left_side = stacked(times(x, value).T)
    terms = dot(left_side, masked)
    terms = terms[: 2 * share] + terms[2 * share :]
    cross = dot(left_side, links[...])
    cross = cross[: 2 * share] + cross[2 * share :]
    next_terms[:share, :link] = terms[:share, :link]
    next_terms[:share, link:] = cross[:share]
    next_terms[share:, :] = jnp.zeros((next_terms.shape[0] - share, next_terms.shape[1]), F32)
    off_terms[...] = terms[:share, link:]
    own_terms[:, :link] = terms[share:, link:]
    own_terms[:, link:] = cross[share:]


def start_kernel(
    s_own, s_core, s_far, s_cross, y_own, y_core, y_far, y_cross, start, scaled, s_rows, y_rows
):
    group, width = s_own.shape
    half = width // 2
    part, near, core = place()
    put_rows(s_own, s_core, s_rows)
    top, bottom = at(near * half, half), at((1 - near) * half, half)
    left, right = at(near * half, half, 128), at((1 - near) * half, half, 128)
    low_left, low_right = (at(width + v * half, half, 128) for v in (near, 1 - near))

    def put(rows, cols, low_cols, value):
        start[rows, cols], start[rows, low_cols] = halves(value)

    put(top, left, low_left, s_rows[:, left])
    side = s_rows[:, right]
    put(top, right, low_right, side)
    put(bottom, left, low_left, side.T)
    put_rows(s_far, s_cross, s_rows.at[:, :half])
    put(bottom, right, low_right, s_rows[:, :half])
    for ref, mask in ((y_own, 0), (y_core, 1), (y_far, 2), (y_cross, 3)):
        y_rows[:, at((part ^ mask) * group, group, 128)] = ref[...]
    scaled[...] = times_wide(y_rows[...], start)


def back_kernel(*refs):
    sums, (start, scaled, own_terms, came), outs = refs[:8], refs[8:12], refs[12:]
    link_diag, link_cross, schur, back, whole, full, full_parts = outs
    part = place()[0]
    side = lax.axis_index("tm") % 2
    size = sums[0].shape[0]
    group = schur.shape[0]
    for mask in range(4):
        for half in range(2):
            rows = at((part ^ mask) * (2 * size) + (side ^ half) * size, size, 8)
            whole[rows, :] = sums[2 * mask + half][...]

    def put(row, col, value):
        full[row * group : (row + 1) * group, col * group : (col + 1) * group] = value

    for row in range(4):
        first = row * 2 * size
        put(row, row, whole[first : first + group, :])
        after_it = whole[first + group : first + 2 * group, :]
        put(row, (row + 1) % 4, after_it)
        put((row + 1) % 4, row, after_it.T)
        if row < 2:
            other = (row + 2) * 2 * size
            across = jnp.concatenate(
                [whole[first + 2 * group : first + 2 * size, :],
                 whole[other + 2 * group : other + 2 * size, :]], axis=0
            )
            put(row, row + 2, across)
            put(row + 2, row, across.T)
    schur[...] = full[at(part * group, group, 8), :]
    full_parts[...] = both(full[...])
    value = scaled[...]
    back[...] = 2.0 * value - times_wide(times_wide(value, full_parts), start)
    share, link = link_diag.shape
    link_diag[...] = own_terms[:, :link] + came[:share, :link]
    link_cross[...] = own_terms[:, link:] + came[:share, link:]


def call(kernel, outs, scratch, *args, sizes=None, whole=0, alias={}):
    vmem = pl.BlockSpec(memory_space=pltpu.VMEM)
    specs = [pl.BlockSpec(memory_space=pltpu.HBM)] * whole + [vmem] * (len(args) - whole)
    if sizes is not None:
        specs, args = [pl.BlockSpec(memory_space=pltpu.SMEM), *specs], (sizes, *args)
    return pl.pallas_call(
        kernel,
        out_shape=[jax.ShapeDtypeStruct(shape, dtype) for shape, dtype in outs],
        in_specs=specs,
        out_specs=[vmem] * len(outs),
        scratch_shapes=scratch,
        input_output_aliases=alias,
        compiler_params=pltpu.CompilerParams(vmem_limit_bytes=VMEM_BYTES),
        cost_estimate=pl.CostEstimate(flops=0, bytes_accessed=0, transcendentals=0),
        name=kernel.__name__,
    )(*args)


def after(value, *others):
    return lax.optimization_barrier((value, *others))[0]


def shards(
    blocks, operator, initial, block_sizes, link_index, link_pair, link_global, schur_base,
    schur_start,
):
    operator, initial = operator[0], initial[0]
    pair, glob = link_pair[0], link_global[0]
    rows, order = operator.shape
    half = order // 2
    unit = half // 3
    link, width = pair.shape[1] // 2, glob.shape[1]
    group, share = width // 4, link // 4
    size = group + group // 4

    def tile_swap(value, mask):
        return lax.ppermute(value, "tile", [(i, i ^ mask) for i in range(4)])

    def block_swap(value, mask):
        return lax.ppermute(value, "tm", [(i, i ^ mask) for i in range(blocks)])

    def diagonal_swap(value):
        pairs = [
            (b * 4 + i, (b ^ 1) * 4 + (i ^ 2)) for b in range(blocks) for i in range(4)
        ]
        return lax.ppermute(value, ("tm", "tile"), pairs)

    vmem, dma, matrix = pltpu.VMEM, pltpu.SemaphoreType.DMA, ((2 * order, order), BF16)

    g_far = tile_swap(glob, 2)
    x_sent, k_sent, s_sent = call(
        pack_kernel,
        [((3 * unit + SPARE, unit), F32), ((3 * unit + 2 * SPARE, unit), F32),
         ((group, width // 2), F32)],
        [vmem((rows, half), F32), vmem((rows, half), F32), dma((3,))],
        initial, operator, schur_start, whole=3,
    )
    x_far, k_far = tile_swap(x_sent, 2), tile_swap(k_sent, 2)
    x_core, k_core, g_core = (tile_swap(v, 1) for v in (initial, operator, glob))
    p_core, s_core = tile_swap(pair, 1), tile_swap(schur_start, 1)
    g_far = after(g_far, x_sent)
    x, k, links = call(
        spread_kernel,
        [matrix, matrix, ((order, width), BF16)],
        [vmem((half, order), F32), vmem((half, order), F32), vmem((order, width), BF16),
         vmem((rows, width), BF16), vmem((1, width), jnp.int32), dma((6,))],
        initial, operator, glob, link_index, x_core, k_core, g_core, g_far,
        tile_swap(g_far, 1), sizes=block_sizes, whole=4,
    )
    x_far = after(x_far, x)
    x, first = call(
        first_kernel,
        [matrix, ((order, group), F32)],
        [],
        x_far, tile_swap(x_far, 1), x, links, sizes=block_sizes, alias={3: 0},
    )
    k_far, first, p_core, s_core = lax.optimization_barrier((k_far, first, p_core, s_core))
    p_far, s_far = tile_swap(after(pair, first), 2), tile_swap(after(s_sent, first), 2)
    keep, send, y_own, y_core, y_far, y_cross, k = call(
        global_kernel,
        [((size, group), F32)] * 2 + [((rows, group), F32)] * 4 + [matrix],
        [vmem((2 * size, group), F32), vmem((order, group), F32)],
        k_far, tile_swap(k_far, 1), x, k, links, first, schur_base,
        sizes=block_sizes, alias={4: 6},
    )

    p_far = after(p_far, keep)
    own_terms, off_terms, next_terms = call(
        pair_kernel,
        [((share, link + width), F32), ((share, link), F32),
         ((share + 2 * SPARE, link + width), F32)],
        [vmem((order, 2 * link), BF16)],
        pair, p_core, p_far, tile_swap(p_far, 1), x, k, links, sizes=block_sizes,
    )
    came = lax.ppermute(next_terms, "tm", [(i + 1, i) for i in range(blocks - 1)])
    y_all = (y_own, tile_swap(y_core, 1), tile_swap(y_far, 2), tile_swap(y_cross, 3))
    if blocks > 2:
        parts = [block_swap(send, 1), block_swap(keep, 2), block_swap(send, 3)]
        *parts, off_terms = lax.optimization_barrier((*parts, off_terms))
        total = (keep + parts[1]) + (parts[0] + parts[2])
    else:
        total = keep + block_swap(send, 1)
    s_far = after(s_far, total)
    s_all = (schur_start, s_core, s_far, tile_swap(s_far, 1))
    step = 4
    while step < blocks:
        total = total + block_swap(total, step)
        step *= 2
    total, *y_all = lax.optimization_barrier((total, *y_all))
    start, scaled = call(
        start_kernel,
        [((width, 2 * width), BF16), ((rows, width), F32)],
        [vmem((2 * group, width), F32), vmem((rows, width), F32)],
        *s_all, *y_all,
    )

    here = (total, block_swap(total, 1))
    there = (tile_swap(total, 2), diagonal_swap(total))
    sums = []
    for pieces in (here, there):
        sums += [*pieces, *(tile_swap(piece, 1) for piece in pieces)]
    link_diag, link_cross, global_schur, back_cols = call(
        back_kernel,
        [((share, link), F32), ((share, width), F32), ((group, width), F32),
         ((rows, width), F32)],
        [vmem((8 * size, group), F32), vmem((width, width), F32),
         vmem((width, 2 * width), BF16)],
        *sums, start, scaled, own_terms, came,
    )
    return (
        link_diag[None], off_terms[None], link_cross[None], global_schur, back_cols[None],
    )


def solution(mesh):
    return jax.shard_map(
        functools.partial(shards, mesh.shape["tm"]),
        mesh=mesh,
        in_specs=(
            P("tm", "tile", None),
            P("tm", "tile", None),
            P("tm"),
            P("tm", None),
            P("tm", "tile", None),
            P("tm", "tile", None),
            P("tile", None),
            P("tile", None),
        ),
        out_specs=(
            P("tm", "tile", None),
            P("tm", "tile", None),
            P("tm", "tile", None),
            P("tile", None),
            P("tm", "tile", None),
        ),
        check_vma=False,
    )
```

time: 69.7 us -> 60.2 us (0.86)
  Pallas kernels: 28.4 us -> 17.9 us
  starting transfers between devices: 20.8 us -> 21.9 us
    pallas_call x7, Pallas kernels: 28.4 us -> 17.9 us  [call(): pl.pallas_call(kernel, out_shape=[jax.ShapeDtypeStruct(shape, dtype) for...]
    ppermute x21 -> x23, starting transfers between devices: 10.2 us -> 12.3 us  [tile_swap(): return lax.ppermute(value, 'tile', [(i, i ^ mask) for i in range(4)])]
    ppermute x5, starting transfers between devices: 8.85 us -> 7.42 us  [block_swap(): return lax.ppermute(value, 'tm', [(i, i ^ mask) for i in range(blocks)])]
    ppermute x21 -> x23, waiting for transfers between devices: 7.68 us -> 8.84 us  [tile_swap(): return lax.ppermute(value, 'tile', [(i, i ^ mask) for i in range(4)])]
    ppermute x5, waiting for transfers between devices: 5.75 us -> 4.74 us  [block_swap(): return lax.ppermute(value, 'tm', [(i, i ^ mask) for i in range(blocks)])]
    unnamed x14 -> x12, local copies, waits for them, and re-layouts: 3.75 us -> 3.74 us
  transfers between devices with their start and end apart: 28 -> 30, of which waited for: 8 -> 10; matrix products, arithmetic and copies ran while one was open for 0% -> 0% of each run, Pallas kernels for 37% -> 27%
where the time goes in v3:
time: 60.2 us; the launch traced here: 59.7 us
  starting transfers between devices  21.9 us (36%)
  Pallas kernels  17.9 us (30%)
  waiting for transfers between devices  14.7 us (24%)
  local copies, waits for them, and re-layouts  3.74 us (6%)
  between operations  1.49 us (2%)
    pallas_call x7, Pallas kernels, call(): pl.pallas_call(kernel, out_shape=[jax.ShapeDtypeStruct(shape, dtype) for...  17.9 us
    ppermute x23, starting transfers between devices, tile_swap(): return lax.ppermute(value, 'tile', [(i, i ^ mask) for i in range(4)])  12.3 us
    ppermute x23, waiting for transfers between devices, tile_swap(): return lax.ppermute(value, 'tile', [(i, i ^ mask) for i in range(4)])  8.84 us
    ppermute x5, starting transfers between devices, block_swap(): return lax.ppermute(value, 'tm', [(i, i ^ mask) for i in range(blocks)])  7.42 us
    ppermute x5, waiting for transfers between devices, block_swap(): return lax.ppermute(value, 'tm', [(i, i ^ mask) for i in range(blocks)])  4.74 us
    unnamed x12, local copies, waits for them, and re-layouts  3.74 us
    ppermute x1, starting transfers between devices, shards(): lax.ppermute(next_terms, 'tm', [(i + 1, i) for i in range(blocks - 1)])  1.28 us
  transfers between devices with their start and end apart: 30, of which 10 were waited for; matrix products, arithmetic and copies ran while one was open for 0% of the time, Pallas kernels for 27%

profile of v3, /device:TPU:0, one launch (start us, length us, event | category | flops | bytes accessed | tf_op | source)
XLA Modules:
  0.0 59.7 jit_solution(2202741929945894647)
XLA Ops:
  0.6 0.5 collective-permute-start.2
  1.1 0.1 collective-permute-start.3
  1.2 2.9 %collective-permute-start.5 = (bf16[192,512]{1,0:T(8,128)(2,1)}, bf16[192,512]{1,0:T(8,128)(2,1)S(1)}, u32[]{:S(2)}, u32[]{:S(2)}) collective-permute-start(bf16[192,512]{1,0:T(8,128)(2,1)} %bitcast.17), channel_id=1, source_target_pairs={{0,2},{1,3},{2,0},{3,1},{4,6},{5,7},{6,4},{7,5},{8,10},{9,11},{10,... | collective-permute-start | bytes 589832 | tf_op jit(solution)/shard_map/ppermute | solution.py:368
  4.2 0.0 collective-permute-start.4
  4.2 1.1 %copy-done = f32[1,192,768]{2,1,0:T(8,128)S(1)} copy-done((f32[1,192,768]{2,1,0:T(8,128)S(1)}, f32[1,192,768]{2,1,0:T(8,128)}, u32[]{:S(2)}) %copy-start) | copy-done | bytes 589848
  5.2 1.1 %copy-done.1 = f32[1,192,768]{2,1,0:T(8,128)S(1)} copy-done((f32[1,192,768]{2,1,0:T(8,128)S(1)}, f32[1,192,768]{2,1,0:T(8,128)}, u32[]{:S(2)}) %copy-start.1) | copy-done | bytes 589848
  6.3 1.0 %pack_kernel.1 = (f32[392,128]{1,0:T(8,128)S(1)}, f32[400,128]{1,0:T(8,128)S(1)}, f32[128,256]{1,0:T(8,128)S(1)}) custom-call(f32[192,768]{1,0:T(8,128)S(1)} %bitcast.9, f32[192,768]{1,0:T(8,128)S(1)} %bitcast.12, f32[128,512]{1,0:T(8,128)} %s_own.1), custom_call_target="tpu_custom_call" | custom-call | tf_op jit(solution)/shard_map/pack_kernel/pallas_call | solution.py:337
  7.3 0.1 collective-permute-start.1
  7.5 2.0 %collective-permute-done.5.g_far = bf16[192,512]{1,0:T(8,128)(2,1)S(1)} collective-permute-done((bf16[192,512]{1,0:T(8,128)(2,1)}, bf16[192,512]{1,0:T(8,128)(2,1)S(1)}, u32[]{:S(2)}, u32[]{:S(2)}) %collective-permute-start.5) | collective-permute-done | bytes 196640 | tf_op jit(solution)/shard_map/ppermute | solution.py:368
  9.5 0.5 collective-permute-start.9
  10.0 1.1 %collective-permute-done.6.g_cross = bf16[192,512]{1,0:T(8,128)(2,1)S(1)} collective-permute-done((bf16[192,512]{1,0:T(8,128)(2,1)S(1)}, bf16[192,512]{1,0:T(8,128)(2,1)S(1)}, u32[]{:S(2)}, u32[]{:S(2)}) %collective-permute-start.6) | collective-permute-done | bytes 196640 | tf_op jit(solution)/shard_map/ppermute | solution.py:368
  11.2 2.2 %collective-permute-start = (f32[400,128]{1,0:T(8,128)S(1)}, f32[400,128]{1,0:T(8,128)S(1)}, u32[]{:S(2)}, u32[]{:S(2)}) collective-permute-start(f32[400,128]{1,0:T(8,128)S(1)} %get-tuple-element.48), channel_id=1, source_target_pairs={{0,2},{1,3},{2,0},{3,1},{4,6},{5,7},{6,4},{7,5},{8,10},{9,11},{10,... | collective-permute-start | bytes 614408 | tf_op jit(solution)/shard_map/ppermute | solution.py:368
  14.0 0.0 collective-permute-done.3.k_core
  14.0 0.0 copy-start.4
  14.0 0.9 %copy-done.4 = bf16[1,192,512]{2,1,0:T(8,128)(2,1)S(1)} copy-done((bf16[1,192,512]{2,1,0:T(8,128)(2,1)S(1)}, bf16[1,192,512]{2,1,0:T(8,128)(2,1)}, u32[]{:S(2)}) %copy-start.4) | copy-done | bytes 196632
  14.9 0.7 %copy-done.5 = s32[1,512]{1,0:T(1,128)S(1)} copy-done((s32[1,512]{1,0:T(1,128)S(1)}, s32[1,512]{1,0:T(1,128)}, u32[]{:S(2)}) %copy-start.5) | copy-done | bytes 2072
  15.6 1.5 %spread_kernel.1 = (bf16[1536,768]{1,0:T(8,128)(2,1)S(1)}, bf16[1536,768]{1,0:T(8,128)(2,1)S(1)}, bf16[768,512]{1,0:T(8,128)(2,1)S(1)}) custom-call(s32[1]{0:T(128)S(6)} %copy.17.sizes, f32[192,768]{1,0:T(8,128)S(1)} %bitcast.10, f32[192,768]{1,0:T(8,128)S(1)} %bitcast.13, bf16[192,512]{1,0:T(8,128)(2,1)S(1)} %bitcast.19, s32[1,512]{1,0:T(1,128)S(1)} %copy-done.5, ...), custom_call_target="tpu_custom_call" | custom-call | tf_op jit(solution)/shard_map/spread_kernel/pallas_call | solution.py:337
  17.1 0.0 copy-start.2
  17.1 0.1 collective-permute-start.7
  17.2 0.5 collective-permute-start.8
  17.7 0.9 %collective-permute-done.7.cross = f32[392,128]{1,0:T(8,128)S(1)} collective-permute-done((f32[392,128]{1,0:T(8,128)S(1)}, f32[392,128]{1,0:T(8,128)S(1)}, u32[]{:S(2)}, u32[]{:S(2)}) %collective-permute-start.7) | collective-permute-done | bytes 200736 | tf_op jit(solution)/shard_map/ppermute | solution.py:368
  18.6 0.8 %first_kernel.1 = (bf16[1536,768]{1,0:T(8,128)(2,1)S(1)}, f32[768,128]{1,0:T(8,128)S(1)}) custom-call(s32[1]{0:T(128)S(6)} %copy.17.sizes, f32[392,128]{1,0:T(8,128)S(1)} %collective-permute-done.1.far, f32[392,128]{1,0:T(8,128)S(1)} %collective-permute-done.7.cross, bf16[1536,768]{1,0:T(8,128)(2,1)S(1)} %get-tuple-element.51.x_in, ...), custom_call_target="tpu_custom_call", output_to_operand_aliasing={{0}: (3, {})} | custom-call | tf_op jit(solution)/shard_map/first_kernel/pallas_call | solution.py:337
  19.4 0.0 collective-permute-done.8.p_core
  19.5 0.2 collective-permute-start.10
  19.7 0.8 %collective-permute-start.14 = (bf16[192,512]{1,0:T(8,128)(2,1)S(1)}, bf16[192,512]{1,0:T(8,128)(2,1)S(1)}, u32[]{:S(2)}, u32[]{:S(2)}) collective-permute-start(bf16[192,512]{1,0:T(8,128)(2,1)S(1)} %bitcast.15), channel_id=1, source_target_pairs={{0,2},{1,3},{2,0},{3,1},{4,6},{5,7},{6,4},{7,5},{8,10},{9,11},{10,... | collective-permute-start | bytes 589832 | tf_op jit(solution)/shard_map/ppermute | solution.py:368
  20.5 0.5 collective-permute-done.10.cross
  21.0 4.6 %global_kernel.1 = (f32[160,128]{1,0:T(8,128)S(1)}, f32[160,128]{1,0:T(8,128)S(1)}, f32[192,128]{1,0:T(8,128)S(1)}, f32[192,128]{1,0:T(8,128)S(1)}, f32[192,128]...) custom-call(s32[1]{0:T(128)S(6)} %copy.17.sizes, ...), custom_call_target="tpu_custom_call", output_to_operand_aliasing={{6}: (4, {})} | custom-call | tf_op jit(solution)/shard_map/global_kernel/pallas_call | solution.py:337
  25.6 1.3 %collective-permute-done.14.p_far = bf16[192,512]{1,0:T(8,128)(2,1)S(1)} collective-permute-done((bf16[192,512]{1,0:T(8,128)(2,1)S(1)}, bf16[192,512]{1,0:T(8,128)(2,1)S(1)}, u32[]{:S(2)}, u32[]{:S(2)}) %collective-permute-start.14) | collective-permute-done | bytes 196640 | tf_op jit(solution)/shard_map/ppermute | solution.py:368
  26.9 1.3 %collective-permute-start.11 = (f32[160,128]{1,0:T(8,128)S(1)}, f32[160,128]{1,0:T(8,128)S(1)}, u32[]{:S(2)}, u32[]{:S(2)}) collective-permute-start(f32[160,128]{1,0:T(8,128)S(1)} %get-tuple-element.60), channel_id=1, source_target_pairs={{0,4},{4,0},{8,12},{12,8},{16,20},{20,16},{24,28},{28,24},{1,5},{5... | collective-permute-start | bytes 245768 | tf_op jit(solution)/shard_map/ppermute | solution.py:371
  28.1 1.6 %collective-permute-start.12 = (f32[160,128]{1,0:T(8,128)S(1)}, f32[160,128]{1,0:T(8,128)S(1)}, u32[]{:S(2)}, u32[]{:S(2)}) collective-permute-start(f32[160,128]{1,0:T(8,128)S(1)} %get-tuple-element.59), channel_id=1, source_target_pairs={{0,8},{4,12},{8,0},{12,4},{16,24},{20,28},{24,16},{28,20},{1,9},{5... | collective-permute-start | bytes 245768 | tf_op jit(solution)/shard_map/ppermute | solution.py:371
  29.7 0.6 %collective-permute-start.13 = (f32[160,128]{1,0:T(8,128)S(1)}, f32[160,128]{1,0:T(8,128)S(1)}, u32[]{:S(2)}, u32[]{:S(2)}) collective-permute-start(f32[160,128]{1,0:T(8,128)S(1)} %get-tuple-element.60), channel_id=1, source_target_pairs={{0,12},{4,8},{8,4},{12,0},{16,28},{20,24},{24,20},{28,16},{1,13},{... | collective-permute-start | bytes 245768 | tf_op jit(solution)/shard_map/ppermute | solution.py:371
  30.3 0.9 %collective-permute-start.27 = (f32[128,256]{1,0:T(8,128)S(1)}, f32[128,256]{1,0:T(8,128)S(1)}, u32[]{:S(2)}, u32[]{:S(2)}) collective-permute-start(f32[128,256]{1,0:T(8,128)S(1)} %get-tuple-element.76), channel_id=1, source_target_pairs={{0,2},{1,3},{2,0},{3,1},{4,6},{5,7},{6,4},{7,5},{8,10},{9,11},{10,... | collective-permute-start | bytes 393224 | tf_op jit(solution)/shard_map/ppermute | solution.py:368
  31.3 6.2 %pair_kernel.1 = (f32[64,768]{1,0:T(8,128)S(1)}, f32[64,256]{1,0:T(8,128)}, f32[80,768]{1,0:T(8,128)S(1)}) custom-call(s32[1]{0:T(128)S(6)} %copy.17.sizes, bf16[192,512]{1,0:T(8,128)(2,1)S(1)} %bitcast.16, bf16[192,512]{1,0:T(8,128)(2,1)S(1)} %collective-permute-done.8.p_core, bf16[192,512]{1,0:T(8,128)(2,1)S(1)} %collective-permute-done.14.p_far, ...), custom_call_target="tpu_custom_call" | custom-call | tf_op jit(solution)/shard_map/pair_kernel/pallas_call | solution.py:337
  37.5 2.4 %collective-permute-start.16 = (f32[160,128]{1,0:T(8,128)S(1)}, f32[160,128]{1,0:T(8,128)S(1)}, u32[]{:S(2)}, u32[]{:S(2)}) collective-permute-start(f32[160,128]{1,0:T(8,128)S(1)} %add_add_fusion), channel_id=1, source_target_pairs={{0,16},{4,20},{8,24},{12,28},{16,0},{20,4},{24,8},{28,12},{1,17},{... | collective-permute-start | bytes 245768 | tf_op jit(solution)/shard_map/ppermute | solution.py:371
  39.9 1.1 %collective-permute-start.18 = (f32[192,128]{1,0:T(8,128)S(1)}, f32[192,128]{1,0:T(8,128)S(1)}, u32[]{:S(2)}, u32[]{:S(2)}) collective-permute-start(f32[192,128]{1,0:T(8,128)S(1)} %get-tuple-element.71), channel_id=1, source_target_pairs={{0,2},{1,3},{2,0},{3,1},{4,6},{5,7},{6,4},{7,5},{8,10},{9,11},{10,... | collective-permute-start | bytes 294920 | tf_op jit(solution)/shard_map/ppermute | solution.py:368
  41.1 0.7 %collective-permute-start.19 = (f32[192,128]{1,0:T(8,128)S(1)}, f32[192,128]{1,0:T(8,128)S(1)}, u32[]{:S(2)}, u32[]{:S(2)}) collective-permute-start(f32[192,128]{1,0:T(8,128)S(1)} %get-tuple-element.72), channel_id=1, source_target_pairs={{0,3},{1,2},{2,1},{3,0},{4,7},{5,6},{6,5},{7,4},{8,11},{9,10},{10,... | collective-permute-start | bytes 294920 | tf_op jit(solution)/shard_map/ppermute | solution.py:368
  41.8 1.3 %collective-permute-start.29 = (f32[80,768]{1,0:T(8,128)S(1)}, f32[80,768]{1,0:T(8,128)S(1)}, u32[]{:S(2)}, u32[]{:S(2)}) collective-permute-start(f32[80,768]{1,0:T(8,128)S(1)} %get-tuple-element.85), channel_id=1, source_target_pairs={{4,0},{8,4},{12,8},{16,12},{20,16},{24,20},{28,24},{5,1},{9,5},{13... | collective-permute-start | bytes 737288 | tf_op jit(solution)/shard_map/ppermute | solution.py:426
  43.1 0.9 %collective-permute-done.16 = f32[160,128]{1,0:T(8,128)S(1)} collective-permute-done((f32[160,128]{1,0:T(8,128)S(1)}, f32[160,128]{1,0:T(8,128)S(1)}, u32[]{:S(2)}, u32[]{:S(2)}) %collective-permute-start.16) | collective-permute-done | bytes 81952 | tf_op jit(solution)/shard_map/ppermute | solution.py:371
  44.0 1.5 %collective-permute-done.18.y_far = f32[192,128]{1,0:T(8,128)S(1)} collective-permute-done((f32[192,128]{1,0:T(8,128)S(1)}, f32[192,128]{1,0:T(8,128)S(1)}, u32[]{:S(2)}, u32[]{:S(2)}) %collective-permute-start.18) | collective-permute-done | bytes 98336 | tf_op jit(solution)/shard_map/ppermute | solution.py:368
  45.5 1.3 %collective-permute-done.19.y_cross = f32[192,128]{1,0:T(8,128)S(1)} collective-permute-done((f32[192,128]{1,0:T(8,128)S(1)}, f32[192,128]{1,0:T(8,128)S(1)}, u32[]{:S(2)}, u32[]{:S(2)}) %collective-permute-start.19) | collective-permute-done | bytes 98336 | tf_op jit(solution)/shard_map/ppermute | solution.py:368
  46.9 1.5 %collective-permute-start.20 = (f32[160,128]{1,0:T(8,128)S(1)}, f32[160,128]{1,0:T(8,128)S(1)}, u32[]{:S(2)}, u32[]{:S(2)}) collective-permute-start(f32[160,128]{1,0:T(8,128)S(1)} %add.15.refs_0_), channel_id=1, source_target_pairs={{0,4},{4,0},{8,12},{12,8},{16,20},{20,16},{24,28},{28,24},{1,5},{5... | collective-permute-start | bytes 245768 | tf_op jit(solution)/shard_map/ppermute | solution.py:371
  48.4 1.1 %collective-permute-start.23 = (f32[160,128]{1,0:T(8,128)S(1)}, f32[160,128]{1,0:T(8,128)S(1)}, u32[]{:S(2)}, u32[]{:S(2)}) collective-permute-start(f32[160,128]{1,0:T(8,128)S(1)} %add.15.refs_0_), channel_id=1, source_target_pairs={{0,2},{1,3},{2,0},{3,1},{4,6},{5,7},{6,4},{7,5},{8,10},{9,11},{10,... | collective-permute-start | bytes 245768 | tf_op jit(solution)/shard_map/ppermute | solution.py:368
  49.5 0.9 %collective-permute-start.24 = (f32[160,128]{1,0:T(8,128)S(1)}, f32[160,128]{1,0:T(8,128)S(1)}, u32[]{:S(2)}, u32[]{:S(2)}) collective-permute-start(f32[160,128]{1,0:T(8,128)S(1)} %add.15.refs_0_), channel_id=1, source_target_pairs={{0,6},{1,7},{2,4},{3,5},{4,2},{5,3},{6,0},{7,1},{8,14},{9,15},{10,... | collective-permute-start | bytes 245768 | tf_op jit(solution)/shard_map/ppermute | solution.py:377
  50.4 3.9 %collective-permute-done.20.refs_1_ = f32[160,128]{1,0:T(8,128)S(1)} collective-permute-done((f32[160,128]{1,0:T(8,128)S(1)}, f32[160,128]{1,0:T(8,128)S(1)}, u32[]{:S(2)}, u32[]{:S(2)}) %collective-permute-start.20) | collective-permute-done | bytes 81952 | tf_op jit(solution)/shard_map/ppermute | solution.py:371
  54.2 0.5 collective-permute-start.25
  54.7 1.1 %collective-permute-done.24.refs_5_ = f32[160,128]{1,0:T(8,128)S(1)} collective-permute-done((f32[160,128]{1,0:T(8,128)S(1)}, f32[160,128]{1,0:T(8,128)S(1)}, u32[]{:S(2)}, u32[]{:S(2)}) %collective-permute-start.24) | collective-permute-done | bytes 81952 | tf_op jit(solution)/shard_map/ppermute | solution.py:377
  55.9 1.8 %start_kernel.1 = (bf16[512,1024]{1,0:T(8,128)(2,1)S(1)}, f32[192,512]{1,0:T(8,128)S(1)}) custom-call(f32[128,512]{1,0:T(8,128)} %s_own.1, f32[128,512]{1,0:T(8,128)S(1)} %collective-permute-done.9.s_core, f32[128,256]{1,0:T(8,128)S(1)} %collective-permute-done.27.s_far, f32[128,256]{1,0:T(8,128)S(1)} %collective-permute-done.28.s_cross, ...), custom_call_target="tpu_custom_call" | custom-call | tf_op jit(solution)/shard_map/start_kernel/pallas_call | solution.py:337
  57.8 2.0 %back_kernel.1 = (f32[64,256]{1,0:T(8,128)}, f32[64,512]{1,0:T(8,128)}, f32[128,512]{1,0:T(8,128)}, f32[192,512]{1,0:T(8,128)}) custom-call(f32[160,128]{1,0:T(8,128)S(1)} %add.15.refs_0_, f32[160,128]{1,0:T(8,128)S(1)} %collective-permute-done.20.refs_1_, f32[160,128]{1,0:T(8,128)S(1)} %collective-permute-done.21.refs_2_, ...), custom_call_target="tpu_custom_call" | custom-call | tf_op jit(solution)/shard_map/back_kernel/pallas_call | solution.py:337
  (33 shorter events, 0.1 us)
Async XLA Ops:
  0.6 13.3 %collective-permute-start.2 = (f32[192,768]{1,0:T(8,128)}, f32[192,768]{1,0:T(8,128)S(1)}, u32[]{:S(2)}, u32[]{:S(2)}) collective-permute-start(f32[192,768]{1,0:T(8,128)} %bitcast.8), channel_id=1, source_target_pairs={{0,1},{1,0},{2,3},{3,2},{4,5},{5,4},{6,7},{7,6},{8,9},{9,8},{10,11... | collective-permute-start | bytes 1769480 | tf_op jit(solution)/shard_map/ppermute | solution.py:368
  1.1 12.8 %collective-permute-start.3 = (f32[192,768]{1,0:T(8,128)}, f32[192,768]{1,0:T(8,128)S(1)}, u32[]{:S(2)}, u32[]{:S(2)}) collective-permute-start(f32[192,768]{1,0:T(8,128)} %bitcast.11), channel_id=1, source_target_pairs={{0,1},{1,0},{2,3},{3,2},{4,5},{5,4},{6,7},{7,6},{8,9},{9,8},{10,11... | collective-permute-start | bytes 1769480 | tf_op jit(solution)/shard_map/ppermute | solution.py:368
  1.2 8.3 %collective-permute-start.5 = (bf16[192,512]{1,0:T(8,128)(2,1)}, bf16[192,512]{1,0:T(8,128)(2,1)S(1)}, u32[]{:S(2)}, u32[]{:S(2)}) collective-permute-start(bf16[192,512]{1,0:T(8,128)(2,1)} %bitcast.17), channel_id=1, source_target_pairs={{0,2},{1,3},{2,0},{3,1},{4,6},{5,7},{6,4},{7,5},{8,10},{9,11},{10,... | collective-permute-start | bytes 589832 | tf_op jit(solution)/shard_map/ppermute | solution.py:368
  4.2 5.4 %collective-permute-start.4 = (bf16[192,512]{1,0:T(8,128)(2,1)}, bf16[192,512]{1,0:T(8,128)(2,1)S(1)}, u32[]{:S(2)}, u32[]{:S(2)}) collective-permute-start(bf16[192,512]{1,0:T(8,128)(2,1)} %bitcast.18), channel_id=1, source_target_pairs={{0,1},{1,0},{2,3},{3,2},{4,5},{5,4},{6,7},{7,6},{8,9},{9,8},{10,11... | collective-permute-start | bytes 589832 | tf_op jit(solution)/shard_map/ppermute | solution.py:368
  4.2 1.1 %copy-start = (f32[1,192,768]{2,1,0:T(8,128)S(1)}, f32[1,192,768]{2,1,0:T(8,128)}, u32[]{:S(2)}) copy-start(f32[1,192,768]{2,1,0:T(8,128)} %param.9) | copy-start | bytes 1769476
  5.2 1.1 %copy-start.1 = (f32[1,192,768]{2,1,0:T(8,128)S(1)}, f32[1,192,768]{2,1,0:T(8,128)}, u32[]{:S(2)}) copy-start(f32[1,192,768]{2,1,0:T(8,128)} %param.8) | copy-start | bytes 1769476
  6.3 10.9 %copy-start.3 = (bf16[1,192,512]{2,1,0:T(8,128)(2,1)S(1)}, bf16[1,192,512]{2,1,0:T(8,128)(2,1)}, u32[]{:S(2)}) copy-start(bf16[1,192,512]{2,1,0:T(8,128)(2,1)} %param.12) | copy-start | bytes 589828
  7.3 9.8 %collective-permute-start.1 = (f32[392,128]{1,0:T(8,128)S(1)}, f32[392,128]{1,0:T(8,128)S(1)}, u32[]{:S(2)}, u32[]{:S(2)}) collective-permute-start(f32[392,128]{1,0:T(8,128)S(1)} %get-tuple-element.49), channel_id=1, source_target_pairs={{0,2},{1,3},{2,0},{3,1},{4,6},{5,7},{6,4},{7,5},{8,10},{9,11},{10,... | collective-permute-start | bytes 602120 | tf_op jit(solution)/shard_map/ppermute | solution.py:368
  9.5 1.6 %collective-permute-start.6 = (bf16[192,512]{1,0:T(8,128)(2,1)S(1)}, bf16[192,512]{1,0:T(8,128)(2,1)S(1)}, u32[]{:S(2)}, u32[]{:S(2)}) collective-permute-start(bf16[192,512]{1,0:T(8,128)(2,1)S(1)} %collective-permute-done.5.g_far), channel_id=1, source_target_pairs={{0,1},{1,0},{2,3},{3,2},{4,5},{5,4},{6,7},{7,6},{8,9},{9,8},{10,11... | collective-permute-start | bytes 589832 | tf_op jit(solution)/shard_map/ppermute | solution.py:368
  9.5 9.9 %collective-permute-start.9 = (f32[128,512]{1,0:T(8,128)}, f32[128,512]{1,0:T(8,128)S(1)}, u32[]{:S(2)}, u32[]{:S(2)}) collective-permute-start(f32[128,512]{1,0:T(8,128)} %s_own.1), channel_id=1, source_target_pairs={{0,1},{1,0},{2,3},{3,2},{4,5},{5,4},{6,7},{7,6},{8,9},{9,8},{10,11... | collective-permute-start | bytes 786440 | tf_op jit(solution)/shard_map/ppermute | solution.py:368
  11.2 8.3 %collective-permute-start = (f32[400,128]{1,0:T(8,128)S(1)}, f32[400,128]{1,0:T(8,128)S(1)}, u32[]{:S(2)}, u32[]{:S(2)}) collective-permute-start(f32[400,128]{1,0:T(8,128)S(1)} %get-tuple-element.48), channel_id=1, source_target_pairs={{0,2},{1,3},{2,0},{3,1},{4,6},{5,7},{6,4},{7,5},{8,10},{9,11},{10,... | collective-permute-start | bytes 614408 | tf_op jit(solution)/shard_map/ppermute | solution.py:368
  14.0 0.9 %copy-start.4 = (bf16[1,192,512]{2,1,0:T(8,128)(2,1)S(1)}, bf16[1,192,512]{2,1,0:T(8,128)(2,1)}, u32[]{:S(2)}) copy-start(bf16[1,192,512]{2,1,0:T(8,128)(2,1)} %param.13) | copy-start | bytes 589828
  14.9 0.7 %copy-start.5 = (s32[1,512]{1,0:T(1,128)S(1)}, s32[1,512]{1,0:T(1,128)}, u32[]{:S(2)}) copy-start(s32[1,512]{1,0:T(1,128)} %index.1) | copy-start | bytes 6148
  17.1 3.9 %copy-start.2 = (f32[128,512]{1,0:T(8,128)S(1)}, f32[128,512]{1,0:T(8,128)}, u32[]{:S(2)}) copy-start(f32[128,512]{1,0:T(8,128)} %base.1) | copy-start | bytes 786436
  17.1 1.5 %collective-permute-start.7 = (f32[392,128]{1,0:T(8,128)S(1)}, f32[392,128]{1,0:T(8,128)S(1)}, u32[]{:S(2)}, u32[]{:S(2)}) collective-permute-start(f32[392,128]{1,0:T(8,128)S(1)} %collective-permute-done.1.far), channel_id=1, source_target_pairs={{0,1},{1,0},{2,3},{3,2},{4,5},{5,4},{6,7},{7,6},{8,9},{9,8},{10,11... | collective-permute-start | bytes 602120 | tf_op jit(solution)/shard_map/ppermute | solution.py:368
  17.2 2.2 %collective-permute-start.8 = (bf16[192,512]{1,0:T(8,128)(2,1)S(1)}, bf16[192,512]{1,0:T(8,128)(2,1)S(1)}, u32[]{:S(2)}, u32[]{:S(2)}) collective-permute-start(bf16[192,512]{1,0:T(8,128)(2,1)S(1)} %bitcast.14), channel_id=1, source_target_pairs={{0,1},{1,0},{2,3},{3,2},{4,5},{5,4},{6,7},{7,6},{8,9},{9,8},{10,11... | collective-permute-start | bytes 589832 | tf_op jit(solution)/shard_map/ppermute | solution.py:368
  19.5 1.5 %collective-permute-start.10 = (f32[400,128]{1,0:T(8,128)S(1)}, f32[400,128]{1,0:T(8,128)S(1)}, u32[]{:S(2)}, u32[]{:S(2)}) collective-permute-start(f32[400,128]{1,0:T(8,128)S(1)} %collective-permute-done.far), channel_id=1, source_target_pairs={{0,1},{1,0},{2,3},{3,2},{4,5},{5,4},{6,7},{7,6},{8,9},{9,8},{10,11... | collective-permute-start | bytes 614408 | tf_op jit(solution)/shard_map/ppermute | solution.py:368
  19.7 7.2 %collective-permute-start.14 = (bf16[192,512]{1,0:T(8,128)(2,1)S(1)}, bf16[192,512]{1,0:T(8,128)(2,1)S(1)}, u32[]{:S(2)}, u32[]{:S(2)}) collective-permute-start(bf16[192,512]{1,0:T(8,128)(2,1)S(1)} %bitcast.15), channel_id=1, source_target_pairs={{0,2},{1,3},{2,0},{3,1},{4,6},{5,7},{6,4},{7,5},{8,10},{9,11},{10,... | collective-permute-start | bytes 589832 | tf_op jit(solution)/shard_map/ppermute | solution.py:368
  26.9 4.4 %collective-permute-start.15 = (bf16[192,512]{1,0:T(8,128)(2,1)S(1)}, bf16[192,512]{1,0:T(8,128)(2,1)S(1)}, u32[]{:S(2)}, u32[]{:S(2)}) collective-permute-start(bf16[192,512]{1,0:T(8,128)(2,1)S(1)} %collective-permute-done.14.p_far), channel_id=1, source_target_pairs={{0,1},{1,0},{2,3},{3,2},{4,5},{5,4},{6,7},{7,6},{8,9},{9,8},{10,11... | collective-permute-start | bytes 589832 | tf_op jit(solution)/shard_map/ppermute | solution.py:368
  26.9 10.6 %collective-permute-start.11 = (f32[160,128]{1,0:T(8,128)S(1)}, f32[160,128]{1,0:T(8,128)S(1)}, u32[]{:S(2)}, u32[]{:S(2)}) collective-permute-start(f32[160,128]{1,0:T(8,128)S(1)} %get-tuple-element.60), channel_id=1, source_target_pairs={{0,4},{4,0},{8,12},{12,8},{16,20},{20,16},{24,28},{28,24},{1,5},{5... | collective-permute-start | bytes 245768 | tf_op jit(solution)/shard_map/ppermute | solution.py:371
  28.1 9.3 %collective-permute-start.12 = (f32[160,128]{1,0:T(8,128)S(1)}, f32[160,128]{1,0:T(8,128)S(1)}, u32[]{:S(2)}, u32[]{:S(2)}) collective-permute-start(f32[160,128]{1,0:T(8,128)S(1)} %get-tuple-element.59), channel_id=1, source_target_pairs={{0,8},{4,12},{8,0},{12,4},{16,24},{20,28},{24,16},{28,20},{1,9},{5... | collective-permute-start | bytes 245768 | tf_op jit(solution)/shard_map/ppermute | solution.py:371
  29.7 7.8 %collective-permute-start.13 = (f32[160,128]{1,0:T(8,128)S(1)}, f32[160,128]{1,0:T(8,128)S(1)}, u32[]{:S(2)}, u32[]{:S(2)}) collective-permute-start(f32[160,128]{1,0:T(8,128)S(1)} %get-tuple-element.60), channel_id=1, source_target_pairs={{0,12},{4,8},{8,4},{12,0},{16,28},{20,24},{24,20},{28,16},{1,13},{... | collective-permute-start | bytes 245768 | tf_op jit(solution)/shard_map/ppermute | solution.py:371
  30.3 11.5 %collective-permute-start.27 = (f32[128,256]{1,0:T(8,128)S(1)}, f32[128,256]{1,0:T(8,128)S(1)}, u32[]{:S(2)}, u32[]{:S(2)}) collective-permute-start(f32[128,256]{1,0:T(8,128)S(1)} %get-tuple-element.76), channel_id=1, source_target_pairs={{0,2},{1,3},{2,0},{3,1},{4,6},{5,7},{6,4},{7,5},{8,10},{9,11},{10,... | collective-permute-start | bytes 393224 | tf_op jit(solution)/shard_map/ppermute | solution.py:368
  37.5 6.5 %collective-permute-start.16 = (f32[160,128]{1,0:T(8,128)S(1)}, f32[160,128]{1,0:T(8,128)S(1)}, u32[]{:S(2)}, u32[]{:S(2)}) collective-permute-start(f32[160,128]{1,0:T(8,128)S(1)} %add_add_fusion), channel_id=1, source_target_pairs={{0,16},{4,20},{8,24},{12,28},{16,0},{20,4},{24,8},{28,12},{1,17},{... | collective-permute-start | bytes 245768 | tf_op jit(solution)/shard_map/ppermute | solution.py:371
  39.9 4.0 %collective-permute-start.17 = (f32[192,128]{1,0:T(8,128)S(1)}, f32[192,128]{1,0:T(8,128)S(1)}, u32[]{:S(2)}, u32[]{:S(2)}) collective-permute-start(f32[192,128]{1,0:T(8,128)S(1)} %get-tuple-element.70), channel_id=1, source_target_pairs={{0,1},{1,0},{2,3},{3,2},{4,5},{5,4},{6,7},{7,6},{8,9},{9,8},{10,11... | collective-permute-start | bytes 294920 | tf_op jit(solution)/shard_map/ppermute | solution.py:368
  39.9 5.6 %collective-permute-start.18 = (f32[192,128]{1,0:T(8,128)S(1)}, f32[192,128]{1,0:T(8,128)S(1)}, u32[]{:S(2)}, u32[]{:S(2)}) collective-permute-start(f32[192,128]{1,0:T(8,128)S(1)} %get-tuple-element.71), channel_id=1, source_target_pairs={{0,2},{1,3},{2,0},{3,1},{4,6},{5,7},{6,4},{7,5},{8,10},{9,11},{10,... | collective-permute-start | bytes 294920 | tf_op jit(solution)/shard_map/ppermute | solution.py:368
  41.1 5.8 %collective-permute-start.19 = (f32[192,128]{1,0:T(8,128)S(1)}, f32[192,128]{1,0:T(8,128)S(1)}, u32[]{:S(2)}, u32[]{:S(2)}) collective-permute-start(f32[192,128]{1,0:T(8,128)S(1)} %get-tuple-element.72), channel_id=1, source_target_pairs={{0,3},{1,2},{2,1},{3,0},{4,7},{5,6},{6,5},{7,4},{8,11},{9,10},{10,... | collective-permute-start | bytes 294920 | tf_op jit(solution)/shard_map/ppermute | solution.py:368
  41.8 15.9 %collective-permute-start.29 = (f32[80,768]{1,0:T(8,128)S(1)}, f32[80,768]{1,0:T(8,128)S(1)}, u32[]{:S(2)}, u32[]{:S(2)}) collective-permute-start(f32[80,768]{1,0:T(8,128)S(1)} %get-tuple-element.85), channel_id=1, source_target_pairs={{4,0},{8,4},{12,8},{16,12},{20,16},{24,20},{28,24},{5,1},{9,5},{13... | collective-permute-start | bytes 737288 | tf_op jit(solution)/shard_map/ppermute | solution.py:426
  44.0 6.4 %collective-permute-start.28 = (f32[128,256]{1,0:T(8,128)S(1)}, f32[128,256]{1,0:T(8,128)S(1)}, u32[]{:S(2)}, u32[]{:S(2)}) collective-permute-start(f32[128,256]{1,0:T(8,128)S(1)} %collective-permute-done.27.s_far), channel_id=1, source_target_pairs={{0,1},{1,0},{2,3},{3,2},{4,5},{5,4},{6,7},{7,6},{8,9},{9,8},{10,11... | collective-permute-start | bytes 393224 | tf_op jit(solution)/shard_map/ppermute | solution.py:368
  46.9 7.4 %collective-permute-start.20 = (f32[160,128]{1,0:T(8,128)S(1)}, f32[160,128]{1,0:T(8,128)S(1)}, u32[]{:S(2)}, u32[]{:S(2)}) collective-permute-start(f32[160,128]{1,0:T(8,128)S(1)} %add.15.refs_0_), channel_id=1, source_target_pairs={{0,4},{4,0},{8,12},{12,8},{16,20},{20,16},{24,28},{28,24},{1,5},{5... | collective-permute-start | bytes 245768 | tf_op jit(solution)/shard_map/ppermute | solution.py:371
  48.4 5.9 %collective-permute-start.23 = (f32[160,128]{1,0:T(8,128)S(1)}, f32[160,128]{1,0:T(8,128)S(1)}, u32[]{:S(2)}, u32[]{:S(2)}) collective-permute-start(f32[160,128]{1,0:T(8,128)S(1)} %add.15.refs_0_), channel_id=1, source_target_pairs={{0,2},{1,3},{2,0},{3,1},{4,6},{5,7},{6,4},{7,5},{8,10},{9,11},{10,... | collective-permute-start | bytes 245768 | tf_op jit(solution)/shard_map/ppermute | solution.py:368
  49.5 6.4 %collective-permute-start.24 = (f32[160,128]{1,0:T(8,128)S(1)}, f32[160,128]{1,0:T(8,128)S(1)}, u32[]{:S(2)}, u32[]{:S(2)}) collective-permute-start(f32[160,128]{1,0:T(8,128)S(1)} %add.15.refs_0_), channel_id=1, source_target_pairs={{0,6},{1,7},{2,4},{3,5},{4,2},{5,3},{6,0},{7,1},{8,14},{9,15},{10,... | collective-permute-start | bytes 245768 | tf_op jit(solution)/shard_map/ppermute | solution.py:377
  50.4 7.4 %collective-permute-start.21 = (f32[160,128]{1,0:T(8,128)S(1)}, f32[160,128]{1,0:T(8,128)S(1)}, u32[]{:S(2)}, u32[]{:S(2)}) collective-permute-start(f32[160,128]{1,0:T(8,128)S(1)} %add.15.refs_0_), channel_id=1, source_target_pairs={{0,1},{1,0},{2,3},{3,2},{4,5},{5,4},{6,7},{7,6},{8,9},{9,8},{10,11... | collective-permute-start | bytes 245768 | tf_op jit(solution)/shard_map/ppermute | solution.py:368
  54.2 3.5 %collective-permute-start.22 = (f32[160,128]{1,0:T(8,128)S(1)}, f32[160,128]{1,0:T(8,128)S(1)}, u32[]{:S(2)}, u32[]{:S(2)}) collective-permute-start(f32[160,128]{1,0:T(8,128)S(1)} %collective-permute-done.20.refs_1_), channel_id=1, source_target_pairs={{0,1},{1,0},{2,3},{3,2},{4,5},{5,4},{6,7},{7,6},{8,9},{9,8},{10,11... | collective-permute-start | bytes 245768 | tf_op jit(solution)/shard_map/ppermute | solution.py:368
  54.2 3.5 %collective-permute-start.25 = (f32[160,128]{1,0:T(8,128)S(1)}, f32[160,128]{1,0:T(8,128)S(1)}, u32[]{:S(2)}, u32[]{:S(2)}) collective-permute-start(f32[160,128]{1,0:T(8,128)S(1)} %collective-permute-done.23.refs_4_), channel_id=1, source_target_pairs={{0,1},{1,0},{2,3},{3,2},{4,5},{5,4},{6,7},{7,6},{8,9},{9,8},{10,11... | collective-permute-start | bytes 245768 | tf_op jit(solution)/shard_map/ppermute | solution.py:368
  55.9 1.9 %collective-permute-start.26 = (f32[160,128]{1,0:T(8,128)S(1)}, f32[160,128]{1,0:T(8,128)S(1)}, u32[]{:S(2)}, u32[]{:S(2)}) collective-permute-start(f32[160,128]{1,0:T(8,128)S(1)} %collective-permute-done.24.refs_5_), channel_id=1, source_target_pairs={{0,1},{1,0},{2,3},{3,2},{4,5},{5,4},{6,7},{7,6},{8,9},{9,8},{10,11... | collective-permute-start | bytes 245768 | tf_op jit(solution)/shard_map/ppermute | solution.py:368

commit v4 on v3

--- a/solution.py
+++ b/solution.py
@@ -41,12 +41,8 @@
     return part, part // 2, part % 2
 
 
-def live_rows(sizes, half):
-    near, size = place()[1], sizes[0]
-    ids = lax.broadcasted_iota(jnp.int32, (half, 1), 0)
-    return jnp.concatenate(
-        [(ids + near * half) < size, (ids + (1 - near) * half) < size], axis=0
-    )
+def live_rows(live):
+    return live[...] > 0.0
 
 
 def put_rows(own, other, target, offset=0):
@@ -66,32 +62,43 @@
     return copies
 
 
-def pack_kernel(x_rows, k_rows, s_rows, x_out, k_out, s_out, x_part, k_part, sems):
-    rows, half = x_part.shape
+def pack_kernel(
+    x_rows, k_rows, g_rows, s_rows, index,
+    x_out, k_out, x_own, k_own, g_own, s_out, index_out, sems,
+):
+    rows, order = x_own.shape
+    half = order // 2
     unit = half // 3
+    group = s_rows.shape[0]
     _, near, core = place()
-    cols = at(near * half, half, 128)
     copies = started(
-        (x_rows.at[:, cols], x_part),
-        (k_rows.at[:, cols], k_part),
-        (s_rows.at[:, at(near * s_out.shape[1], s_out.shape[1], 128)], s_out),
+        (x_rows, x_own),
+        (k_rows, k_own),
+        (g_rows, g_own),
+        (index, index_out),
+        *[
+            (s_rows.at[:, at((2 * near + i) * group, group, 128)], s_out.at[first : first + group, :])
+            for i, first in enumerate(range(0, s_out.shape[0], group))
+        ],
         sems=sems,
     )
     large = at(core * (rows - unit), unit, 8)
     small = at((1 - core) * unit, rows - unit, 8)
-    edge = at(core * 2 * unit, unit, 128)
-    opposite = at((1 - core) * 2 * unit, unit, 128)
-    for copy, part, out in zip(copies, (x_part, k_part), (x_out, k_out)):
+    edge = at(near * half + core * 2 * unit, unit, 128)
+    middle = at(near * half + unit, unit, 128)
+    opposite = at(near * half + (1 - core) * 2 * unit, unit, 128)
+    for copy, own, out in zip(copies, (x_own, k_own), (x_out, k_out)):
         copy.wait()
-        out[0:unit, :] = part[large, edge]
-        out[unit : 2 * unit, :] = part[large, unit : 2 * unit]
-        out[2 * unit : unit + rows, :] = part[small, unit : 2 * unit]
-        block = part[large, opposite]
+        out[0:unit, :] = own[large, edge]
+        out[unit : 2 * unit, :] = own[large, middle]
+        out[2 * unit : unit + rows, :] = own[small, middle]
+        block = own[large, opposite]
         out[unit + rows : 3 * unit, :] = jnp.where(
             core == 0, block[: unit // 2, :], block.T[unit // 2 :, :]
         )
         out[3 * unit :, :] = jnp.zeros((out.shape[0] - 3 * unit, unit), F32)
-    copies[2].wait()
+    for copy in copies[2:]:
+        copy.wait()
 
 
 def corner(far, cross, target, live):
@@ -155,47 +162,41 @@
     return (product[:, :width] + product[:, width:]) + dot(low, right_side[:, :width])
 
 
-def spread_kernel(
-    sizes, x_own, k_own, g_own, index, x_core, k_core, g_core, g_far, g_cross,
-    x, k, links, x_whole, k_whole, gathered, g_rows, index_here, sems,
+def spread_kernel(sizes, x_own, k_own, x_core, k_core, x, k, live_out, whole):
+    half, order = whole.shape
+    rows = half // 2
+    _, near, core = place()
+    ids = lax.broadcasted_iota(jnp.int32, (half, 1), 0)
+    live = jnp.concatenate([ids + near * half, ids + (1 - near) * half], axis=0) < sizes[0]
+    live_out[...] = jnp.where(live, 1.0, 0.0)
+    for own, other, target in ((x_own, x_core, x), (k_own, k_core, k)):
+        for side, first in enumerate((near * half, (1 - near) * half)):
+            cols = slice(side * half, (side + 1) * half)
+            whole[at(core * rows, rows), cols] = own[:, at(first, half, 128)]
+            whole[at((1 - core) * rows, rows), cols] = other[:, at(first, half, 128)]
+        spread(whole, target, live)
+
+
+def first_kernel(
+    live_in, far, cross, x_in, g_own, g_core, g_far, g_cross, index, x, first, links, gathered
 ):
-    half, order = x_whole.shape
-    rows = half // 2
-    width = links.shape[1]
-    _, near, core = place()
-    sides = [at(near * half, half, 128), at((1 - near) * half, half, 128)]
-    pairs = [
-        (own.at[:, cols], whole.at[at(core * rows, rows), side * half : (side + 1) * half])
-        for own, whole in ((x_own, x_whole), (k_own, k_whole))
-        for side, cols in enumerate(sides)
-    ]
-    copies = started(*pairs, (g_own, g_rows), (index, index_here), sems=sems)
-    for other, whole in ((x_core, x_whole), (k_core, k_whole)):
-        for side, cols in enumerate(sides):
-            whole[at((1 - core) * rows, rows), side * half : (side + 1) * half] = other[:, cols]
-    put_rows(g_far, g_cross, gathered, half)
-    for copy in copies:
-        copy.wait()
-    put_rows(g_rows, g_core, gathered)
-    live = live_rows(sizes, half)
-    spread(x_whole, x, live)
-    spread(k_whole, k, live)
-    hot = lax.broadcasted_iota(jnp.int32, (width, width), 0) == index_here[...]
+    del x_in
+    order, width = links.shape
+    group = width // 4
+    live = live_rows(live_in)
+    put_rows(g_own, g_core, gathered)
+    put_rows(g_far, g_cross, gathered, order // 2)
+    hot = lax.broadcasted_iota(jnp.int32, (width, width), 0) == index[...]
     chosen = dot(gathered[...], hot.astype(F32).astype(BF16))
     links[...] = jnp.where(live, chosen, 0.0).astype(BF16)
-
-
-def first_kernel(sizes, far, cross, x_in, links, x, first):
-    del x_in
-    corner(far, cross, x, live_rows(sizes, x.shape[1] // 2))
-    group = links.shape[1] // 4
+    corner(far, cross, x, live)
     columns = links[:, at(place()[0] * group, group, 128)]
     product = dot(x[...], columns)
-    first[...] = product[: first.shape[0]] + product[first.shape[0] :]
+    first[...] = product[:order] + product[order:]
 
 
 def global_kernel(
-    sizes, far, cross, x, k_in, links, first, base,
+    live, far, cross, x, k_in, links, first, base, s_sent,
     keep, send, y_own, y_core, y_far, y_cross, k, pack, solved,
 ):
     del k_in
@@ -205,7 +206,7 @@
     group = width // 4
     part, _, core = place()
     block = lax.axis_index("tm")
-    corner(far, cross, k, live_rows(sizes, half))
+    corner(far, cross, k, live_rows(live))
     columns = links[:, at(part * group, group, 128)].astype(F32)
     value = 2.0 * columns - times(k, first[...])
     for step in range(TERMS - 1):
@@ -214,8 +215,10 @@
     solved[...] = result
     y_own[...] = solved[at(core * rows, rows), :]
     y_core[...] = solved[at((1 - core) * rows, rows), :]
-    y_far[...] = solved[at(half + core * rows, rows), :]
-    y_cross[...] = solved[at(half + (1 - core) * rows, rows), :]
+    y_far[:rows, :] = solved[at(half + core * rows, rows), :]
+    y_cross[:rows, :] = solved[at(half + (1 - core) * rows, rows), :]
+    y_far[rows:, :] = s_sent[...]
+    y_cross[rows:, :] = s_sent[...]
     left_side = stacked(result.T)
 
     def square(shift):
@@ -237,7 +240,7 @@
 
 
 def pair_kernel(
-    sizes, p_own, p_core, p_far, p_cross, x, k, links, own_terms, off_terms, next_terms, gathered
+    live, p_own, p_core, p_far, p_cross, x, k, links, own_terms, off_terms, next_terms, gathered
 ):
     half = x.shape[1] // 2
     width = p_own.shape[1]
@@ -245,7 +248,7 @@
     share = link // 4
     put_rows(p_own, p_core, gathered)
     put_rows(p_far, p_cross, gathered, half)
-    masked = jnp.where(live_rows(sizes, half), gathered[...], jnp.zeros((), BF16))
+    masked = jnp.where(live_rows(live), gathered[...], jnp.zeros((), BF16))
     source = lax.broadcasted_iota(jnp.int32, (width, 2 * share), 0)
     target = lax.broadcasted_iota(jnp.int32, (width, 2 * share), 1)
     wanted = place()[0] * share + target + jnp.where(target < share, 0, link - share)
@@ -266,11 +269,10 @@
     own_terms[:, link:] = cross[share:]
 
 
-def start_kernel(
-    s_own, s_core, s_far, s_cross, y_own, y_core, y_far, y_cross, start, scaled, s_rows, y_rows
-):
+def start_kernel(s_own, s_core, y_own, y_core, far, cross, start, scaled, s_rows, y_rows):
     group, width = s_own.shape
     half = width // 2
+    rows = y_own.shape[0]
     part, near, core = place()
     put_rows(s_own, s_core, s_rows)
     top, bottom = at(near * half, half), at((1 - near) * half, half)
@@ -284,10 +286,12 @@
     side = s_rows[:, right]
     put(top, right, low_right, side)
     put(bottom, left, low_left, side.T)
-    put_rows(s_far, s_cross, s_rows.at[:, :half])
+    for i in range(2):
+        first = slice(rows + i * group, rows + (i + 1) * group)
+        put_rows(far.at[first, :], cross.at[first, :], s_rows.at[:, i * group : (i + 1) * group])
     put(bottom, right, low_right, s_rows[:, :half])
-    for ref, mask in ((y_own, 0), (y_core, 1), (y_far, 2), (y_cross, 3)):
-        y_rows[:, at((part ^ mask) * group, group, 128)] = ref[...]
+    for ref, mask in ((y_own, 0), (y_core, 1), (far, 2), (cross, 3)):
+        y_rows[:, at((part ^ mask) * group, group, 128)] = ref[:rows, :]
     scaled[...] = times_wide(y_rows[...], start)
 
 
@@ -329,9 +333,11 @@
     link_cross[...] = own_terms[:, link:] + came[:share, link:]
 
 
-def call(kernel, outs, scratch, *args, sizes=None, whole=0, alias={}):
+def call(kernel, outs, scratch, *args, sizes=None, whole=False, alias={}):
     vmem = pl.BlockSpec(memory_space=pltpu.VMEM)
-    specs = [pl.BlockSpec(memory_space=pltpu.HBM)] * whole + [vmem] * (len(args) - whole)
+    specs = [pl.BlockSpec(memory_space=pltpu.HBM) if whole else vmem] * len(args)
+    if whole:
+        args = [pltpu.with_memory_space_constraint(arg, pltpu.HBM) for arg in args]
     if sizes is not None:
         specs, args = [pl.BlockSpec(memory_space=pltpu.SMEM), *specs], (sizes, *args)
     return pl.pallas_call(
@@ -376,52 +382,54 @@
         ]
         return lax.ppermute(value, ("tm", "tile"), pairs)
 
-    vmem, dma, matrix = pltpu.VMEM, pltpu.SemaphoreType.DMA, ((2 * order, order), BF16)
+    vmem, matrix = pltpu.VMEM, ((2 * order, order), BF16)
 
     g_far = tile_swap(glob, 2)
-    x_sent, k_sent, s_sent = call(
+    x_sent, k_sent, x_own, k_own, g_own, s_sent, index = call(
         pack_kernel,
-        [((3 * unit + SPARE, unit), F32), ((3 * unit + 2 * SPARE, unit), F32),
-         ((group, width // 2), F32)],
-        [vmem((rows, half), F32), vmem((rows, half), F32), dma((3,))],
-        initial, operator, schur_start, whole=3,
+        [((3 * unit + SPARE, unit), F32), ((3 * unit + 4 * SPARE, unit), F32),
+         ((rows, order), F32), ((rows, order), F32), ((rows, width), BF16),
+         ((2 * group, group), F32), (link_index.shape, jnp.int32)],
+        [pltpu.SemaphoreType.DMA((6,))],
+        initial, operator, glob, schur_start, link_index, whole=True,
     )
     x_far, k_far = tile_swap(x_sent, 2), tile_swap(k_sent, 2)
-    x_core, k_core, g_core = (tile_swap(v, 1) for v in (initial, operator, glob))
-    p_core, s_core = tile_swap(pair, 1), tile_swap(schur_start, 1)
-    g_far = after(g_far, x_sent)
-    x, k, links = call(
+    initial, operator, x_sent = lax.optimization_barrier((initial, operator, x_sent))
+    x_core, k_core = tile_swap(initial, 1), tile_swap(operator, 1)
+    x, k, live = call(
         spread_kernel,
-        [matrix, matrix, ((order, width), BF16)],
-        [vmem((half, order), F32), vmem((half, order), F32), vmem((order, width), BF16),
-         vmem((rows, width), BF16), vmem((1, width), jnp.int32), dma((6,))],
-        initial, operator, glob, link_index, x_core, k_core, g_core, g_far,
-        tile_swap(g_far, 1), sizes=block_sizes, whole=4,
-    )
-    x_far = after(x_far, x)
-    x, first = call(
+        [matrix, matrix, ((order, 1), F32)],
+        [vmem((half, order), F32)],
+        x_own, k_own, x_core, k_core, sizes=block_sizes,
+    )
+    x_far, g_far = after(x_far, x), after(g_far, x)
+    g_core, p_core, s_core = (tile_swap(after(v, x), 1) for v in (glob, pair, schur_start))
+    x, first, links = call(
         first_kernel,
-        [matrix, ((order, group), F32)],
-        [],
-        x_far, tile_swap(x_far, 1), x, links, sizes=block_sizes, alias={3: 0},
-    )
+        [matrix, ((order, group), F32), ((order, width), BF16)],
+        [vmem((order, width), BF16)],
+        live, x_far, tile_swap(x_far, 1), x, g_own, g_core, g_far, tile_swap(g_far, 1), index,
+        alias={3: 0},
+    )
+    pair = after(pair, x)
+    p_far, p_cross = tile_swap(pair, 2), tile_swap(pair, 3)
     k_far, first, p_core, s_core = lax.optimization_barrier((k_far, first, p_core, s_core))
-    p_far, s_far = tile_swap(after(pair, first), 2), tile_swap(after(s_sent, first), 2)
     keep, send, y_own, y_core, y_far, y_cross, k = call(
         global_kernel,
-        [((size, group), F32)] * 2 + [((rows, group), F32)] * 4 + [matrix],
+        [((size, group), F32)] * 2 + [((rows, group), F32)] * 2
+        + [((rows + 2 * group, group), F32)] * 2 + [matrix],
         [vmem((2 * size, group), F32), vmem((order, group), F32)],
-        k_far, tile_swap(k_far, 1), x, k, links, first, schur_base,
-        sizes=block_sizes, alias={4: 6},
-    )
-
-    p_far = after(p_far, keep)
+        live, k_far, tile_swap(k_far, 1), x, k, links, first, schur_base, s_sent,
+        alias={4: 6},
+    )
+
+    p_far, p_cross, keep = lax.optimization_barrier((p_far, p_cross, keep))
     own_terms, off_terms, next_terms = call(
         pair_kernel,
         [((share, link + width), F32), ((share, link), F32),
-         ((share + 2 * SPARE, link + width), F32)],
+         ((share + 3 * SPARE, link + width), F32)],
         [vmem((order, 2 * link), BF16)],
-        pair, p_core, p_far, tile_swap(p_far, 1), x, k, links, sizes=block_sizes,
+        live, pair, p_core, p_far, p_cross, x, k, links,
     )
     came = lax.ppermute(next_terms, "tm", [(i + 1, i) for i in range(blocks - 1)])
     y_all = (y_own, tile_swap(y_core, 1), tile_swap(y_far, 2), tile_swap(y_cross, 3))
@@ -431,22 +439,22 @@
         total = (keep + parts[1]) + (parts[0] + parts[2])
     else:
         total = keep + block_swap(send, 1)
-    s_far = after(s_far, total)
-    s_all = (schur_start, s_core, s_far, tile_swap(s_far, 1))
     step = 4
     while step < blocks:
-        total = total + block_swap(total, step)
+        other = block_swap(total, step)
+        if step == 4:
+            other, *y_all = lax.optimization_barrier((other, *y_all))
+        total = total + other
         step *= 2
-    total, *y_all = lax.optimization_barrier((total, *y_all))
     start, scaled = call(
         start_kernel,
         [((width, 2 * width), BF16), ((rows, width), F32)],
         [vmem((2 * group, width), F32), vmem((rows, width), F32)],
-        *s_all, *y_all,
-    )
-
-    here = (total, block_swap(total, 1))
-    there = (tile_swap(total, 2), diagonal_swap(total))
+        schur_start, s_core, *y_all,
+    )
+
+    here = (total, after(block_swap(total, 1), scaled))
+    there = (after(tile_swap(total, 2), scaled), after(diagonal_swap(total), scaled))
     sums = []
     for pieces in (here, there):
         sums += [*pieces, *(tile_swap(piece, 1) for piece in pieces)]

time: 60.2 us -> 68.7 us (1.14)
  waiting for transfers between devices: 14.7 us -> 24.5 us
  local copies, waits for them, and re-layouts: 3.74 us -> 0.02 us
  starting transfers between devices: 21.9 us -> 24.5 us
    ppermute x5, waiting for transfers between devices: 4.74 us -> 10.1 us  [block_swap(): return lax.ppermute(value, 'tm', [(i, i ^ mask) for i in range(blocks)])]
    ppermute x23 -> x21, waiting for transfers between devices: 8.84 us -> 13.3 us  [tile_swap(): return lax.ppermute(value, 'tile', [(i, i ^ mask) for i in range(4)])]
    unnamed x12 -> x8, local copies, waits for them, and re-layouts: 3.74 us -> 0.02 us
    ppermute x5, starting transfers between devices: 7.42 us -> 10.2 us  [block_swap(): return lax.ppermute(value, 'tm', [(i, i ^ mask) for i in range(blocks)])]
    ppermute x1, starting transfers between devices: 0.88 us -> 0.07 us  [diagonal_swap(): return lax.ppermute(value, ('tm', 'tile'), pairs)]
    ppermute x23 -> x21, starting transfers between devices: 12.3 us -> 12.9 us  [tile_swap(): return lax.ppermute(value, 'tile', [(i, i ^ mask) for i in range(4)])]
  transfers between devices with their start and end apart: 30 -> 28, of which waited for: 10 -> 12; matrix products, arithmetic and copies ran while one was open for 0% -> 0% of each run, Pallas kernels for 27% -> 21%
where the time goes in v4:
time: 68.7 us; the launch traced here: 68.5 us
  starting transfers between devices  24.5 us (36%)
  waiting for transfers between devices  24.5 us (36%)
  Pallas kernels  18.1 us (26%)
  between operations  1.43 us (2%)
    pallas_call x7, Pallas kernels, call(): pl.pallas_call(kernel, out_shape=[jax.ShapeDtypeStruct(shape, dtype) for...  18.1 us
    ppermute x21, waiting for transfers between devices, tile_swap(): return lax.ppermute(value, 'tile', [(i, i ^ mask) for i in range(4)])  13.3 us
    ppermute x21, starting transfers between devices, tile_swap(): return lax.ppermute(value, 'tile', [(i, i ^ mask) for i in range(4)])  12.9 us
    ppermute x5, starting transfers between devices, block_swap(): return lax.ppermute(value, 'tm', [(i, i ^ mask) for i in range(blocks)])  10.2 us
    ppermute x5, waiting for transfers between devices, block_swap(): return lax.ppermute(value, 'tm', [(i, i ^ mask) for i in range(blocks)])  10.1 us
  transfers between devices with their start and end apart: 28, of which 12 were waited for; matrix products, arithmetic and copies ran while one was open for 0% of the time, Pallas kernels for 21%

profile of v4, /device:TPU:0, one launch (start us, length us, event | category | flops | bytes accessed | tf_op | source)
XLA Modules:
  0.0 68.5 jit_solution(17262341007826630709)
XLA Ops:
  0.6 0.0 copy-start.3
  0.7 1.5 %pack_kernel.1 = (f32[392,128]{1,0:T(8,128)S(1)}, f32[416,128]{1,0:T(8,128)S(1)}, f32[192,768]{1,0:T(8,128)S(1)}, f32[192,768]{1,0:T(8,128)S(1)}, bf16[192,512]{...) custom-call(f32[192,768]{1,0:T(8,128)} %bitcast.12, f32[192,768]{1,0:T(8,128)} %bitcast.14, ...), custom_call_target="tpu_custom_call" | custom-call | tf_op jit(solution)/shard_map/pack_kernel/pallas_call | solution.py:343
  2.2 0.5 collective-permute-start
  2.7 0.1 collective-permute-start.1
  2.8 2.9 %collective-permute-start.5 = (bf16[192,512]{1,0:T(8,128)(2,1)}, bf16[192,512]{1,0:T(8,128)(2,1)S(1)}, u32[]{:S(2)}, u32[]{:S(2)}) collective-permute-start(bf16[192,512]{1,0:T(8,128)(2,1)} %bitcast.17), channel_id=1, source_target_pairs={{0,2},{1,3},{2,0},{3,1},{4,6},{5,7},{6,4},{7,5},{8,10},{9,11},{10,... | collective-permute-start | bytes 589832 | tf_op jit(solution)/shard_map/ppermute | solution.py:374
  5.7 0.0 collective-permute-start.2
  6.4 0.0 collective-permute-done.x_core
  6.4 0.0 collective-permute-done.1.k_core
  6.4 1.2 %spread_kernel.1 = (bf16[1536,768]{1,0:T(8,128)(2,1)S(1)}, bf16[1536,768]{1,0:T(8,128)(2,1)S(1)}, f32[768,1]{1,0:T(8,128)S(1)}) custom-call(s32[1]{0:T(128)S(6)} %copy.17.sizes, f32[192,768]{1,0:T(8,128)S(1)} %get-tuple-element.61.x_own, f32[192,768]{1,0:T(8,128)S(1)} %get-tuple-element.62.k_own, f32[192,768]{1,0:T(8,128)S(1)} %collective-permute-done.x_core, ...), custom_call_target="tpu_custom_call" | custom-call | tf_op jit(solution)/shard_map/spread_kernel/pallas_call | solution.py:343
  7.6 0.0 copy-start.1
  7.6 4.0 %collective-permute-done.5.g_far = bf16[192,512]{1,0:T(8,128)(2,1)S(1)} collective-permute-done((bf16[192,512]{1,0:T(8,128)(2,1)}, bf16[192,512]{1,0:T(8,128)(2,1)S(1)}, u32[]{:S(2)}, u32[]{:S(2)}) %collective-permute-start.5) | collective-permute-done | bytes 196640 | tf_op jit(solution)/shard_map/ppermute | solution.py:374
  11.6 0.0 collective-permute-start.6
  11.6 0.5 collective-permute-start.11
  12.1 2.1 %collective-permute-start.9 = (f32[416,128]{1,0:T(8,128)S(1)}, f32[416,128]{1,0:T(8,128)S(1)}, u32[]{:S(2)}, u32[]{:S(2)}) collective-permute-start(f32[416,128]{1,0:T(8,128)S(1)} %get-tuple-element.75), channel_id=1, source_target_pairs={{0,2},{1,3},{2,0},{3,1},{4,6},{5,7},{6,4},{7,5},{8,10},{9,11},{10,... | collective-permute-start | bytes 638984 | tf_op jit(solution)/shard_map/ppermute | solution.py:374
  14.2 1.4 %collective-permute-done.2.far = f32[392,128]{1,0:T(8,128)S(1)} collective-permute-done((f32[392,128]{1,0:T(8,128)S(1)}, f32[392,128]{1,0:T(8,128)S(1)}, u32[]{:S(2)}, u32[]{:S(2)}) %collective-permute-start.2) | collective-permute-done | bytes 200736 | tf_op jit(solution)/shard_map/ppermute | solution.py:374
  15.6 0.5 collective-permute-start.4
  16.1 0.1 collective-permute-start.10
  16.2 1.1 %collective-permute-done.4.g_core = bf16[192,512]{1,0:T(8,128)(2,1)S(1)} collective-permute-done((bf16[192,512]{1,0:T(8,128)(2,1)S(1)}, bf16[192,512]{1,0:T(8,128)(2,1)S(1)}, u32[]{:S(2)}, u32[]{:S(2)}) %collective-permute-start.4) | collective-permute-done | bytes 196640 | tf_op jit(solution)/shard_map/ppermute | solution.py:374
  17.3 0.0 collective-permute-done.3.cross
  17.3 1.7 %first_kernel.1 = (bf16[1536,768]{1,0:T(8,128)(2,1)S(1)}, f32[768,128]{1,0:T(8,128)S(1)}, bf16[768,512]{1,0:T(8,128)(2,1)S(1)}) custom-call(f32[768,1]{1,0:T(8,128)S(1)} %get-tuple-element.66.live_in.live, f32[392,128]{1,0:T(8,128)S(1)} %collective-permute-done.2.far, f32[392,128]{1,0:T(8,128)S(1)} %collective-permute-done.3.cross, ...), custom_call_target="tpu_custom_call", output_to_operand_aliasing={{0}: (3, {})} | custom-call | tf_op jit(solution)/shard_map/first_kernel/pallas_call | solution.py:343
  19.1 0.8 %collective-permute-done.9.far = f32[416,128]{1,0:T(8,128)S(1)} collective-permute-done((f32[416,128]{1,0:T(8,128)S(1)}, f32[416,128]{1,0:T(8,128)S(1)}, u32[]{:S(2)}, u32[]{:S(2)}) %collective-permute-start.9) | collective-permute-done | bytes 213024 | tf_op jit(solution)/shard_map/ppermute | solution.py:374
  19.9 0.0 collective-permute-done.10.p_core
  19.9 0.0 collective-permute-done.11.s_core
  19.9 1.8 %collective-permute-start.7 = (bf16[192,512]{1,0:T(8,128)(2,1)S(1)}, bf16[192,512]{1,0:T(8,128)(2,1)S(1)}, u32[]{:S(2)}, u32[]{:S(2)}) collective-permute-start(bf16[192,512]{1,0:T(8,128)(2,1)S(1)} %bitcast.9), channel_id=1, source_target_pairs={{0,2},{1,3},{2,0},{3,1},{4,6},{5,7},{6,4},{7,5},{8,10},{9,11},{10,... | collective-permute-start | bytes 589832 | tf_op jit(solution)/shard_map/ppermute | solution.py:374
  21.7 0.1 collective-permute-start.8
  21.8 4.5 %global_kernel.1 = (f32[160,128]{1,0:T(8,128)S(1)}, f32[160,128]{1,0:T(8,128)S(1)}, f32[192,128]{1,0:T(8,128)S(1)}, f32[192,128]{1,0:T(8,128)S(1)}, f32[448,128]...) custom-call(f32[768,1]{1,0:T(8,128)S(1)} %get-tuple-element.66.live_in.l, ...), custom_call_target="tpu_custom_call", output_to_operand_aliasing={{6}: (4, {})} | custom-call | tf_op jit(solution)/shard_map/global_kernel/pallas_call | solution.py:343
  26.3 1.4 %collective-permute-done.7.p_far = bf16[192,512]{1,0:T(8,128)(2,1)S(1)} collective-permute-done((bf16[192,512]{1,0:T(8,128)(2,1)S(1)}, bf16[192,512]{1,0:T(8,128)(2,1)S(1)}, u32[]{:S(2)}, u32[]{:S(2)}) %collective-permute-start.7) | collective-permute-done | bytes 196640 | tf_op jit(solution)/shard_map/ppermute | solution.py:374
  27.7 3.3 %collective-permute-done.8.p_cross = bf16[192,512]{1,0:T(8,128)(2,1)S(1)} collective-permute-done((bf16[192,512]{1,0:T(8,128)(2,1)S(1)}, bf16[192,512]{1,0:T(8,128)(2,1)S(1)}, u32[]{:S(2)}, u32[]{:S(2)}) %collective-permute-start.8) | collective-permute-done | bytes 196640 | tf_op jit(solution)/shard_map/ppermute | solution.py:374
  31.0 1.8 %collective-permute-start.14 = (f32[160,128]{1,0:T(8,128)S(1)}, f32[160,128]{1,0:T(8,128)S(1)}, u32[]{:S(2)}, u32[]{:S(2)}) collective-permute-start(f32[160,128]{1,0:T(8,128)S(1)} %get-tuple-element.85), channel_id=1, source_target_pairs={{0,8},{4,12},{8,0},{12,4},{16,24},{20,28},{24,16},{28,20},{1,9},{5... | collective-permute-start | bytes 245768 | tf_op jit(solution)/shard_map/ppermute | solution.py:377
  32.8 1.5 %collective-permute-start.13 = (f32[160,128]{1,0:T(8,128)S(1)}, f32[160,128]{1,0:T(8,128)S(1)}, u32[]{:S(2)}, u32[]{:S(2)}) collective-permute-start(f32[160,128]{1,0:T(8,128)S(1)} %get-tuple-element.86), channel_id=1, source_target_pairs={{0,4},{4,0},{8,12},{12,8},{16,20},{20,16},{24,28},{28,24},{1,5},{5... | collective-permute-start | bytes 245768 | tf_op jit(solution)/shard_map/ppermute | solution.py:377
  34.3 0.2 collective-permute-start.15
  34.5 1.7 %collective-permute-start.18 = (f32[448,128]{1,0:T(8,128)S(1)}, f32[448,128]{1,0:T(8,128)S(1)}, u32[]{:S(2)}, u32[]{:S(2)}) collective-permute-start(f32[448,128]{1,0:T(8,128)S(1)} %get-tuple-element.97), channel_id=1, source_target_pairs={{0,2},{1,3},{2,0},{3,1},{4,6},{5,7},{6,4},{7,5},{8,10},{9,11},{10,... | collective-permute-start | bytes 688136 | tf_op jit(solution)/shard_map/ppermute | solution.py:374
  36.2 6.3 %pair_kernel.1 = (f32[64,768]{1,0:T(8,128)S(1)}, f32[64,256]{1,0:T(8,128)}, f32[88,768]{1,0:T(8,128)S(1)}) custom-call(f32[768,1]{1,0:T(8,128)S(1)} %get-tuple-element.66.live_in.live, bf16[192,512]{1,0:T(8,128)(2,1)S(1)} %bitcast.11, bf16[192,512]{1,0:T(8,128)(2,1)S(1)} %collective-permute-done.10.p_core, ...), custom_call_target="tpu_custom_call" | custom-call | tf_op jit(solution)/shard_map/pair_kernel/pallas_call | solution.py:343
  42.6 0.4 collective-permute-start.17
  43.0 1.3 %collective-permute-start.27 = (f32[88,768]{1,0:T(8,128)S(1)}, f32[88,768]{1,0:T(8,128)S(1)}, u32[]{:S(2)}, u32[]{:S(2)}) collective-permute-start(f32[88,768]{1,0:T(8,128)S(1)} %get-tuple-element.111), channel_id=1, source_target_pairs={{4,0},{8,4},{12,8},{16,12},{20,16},{24,20},{28,24},{5,1},{9,5},{13... | collective-permute-start | bytes 811016 | tf_op jit(solution)/shard_map/ppermute | solution.py:434
  44.3 4.9 %collective-permute-start.16 = (f32[160,128]{1,0:T(8,128)S(1)}, f32[160,128]{1,0:T(8,128)S(1)}, u32[]{:S(2)}, u32[]{:S(2)}) collective-permute-start(f32[160,128]{1,0:T(8,128)S(1)} %add_add_fusion), channel_id=1, source_target_pairs={{0,16},{4,20},{8,24},{12,28},{16,0},{20,4},{24,8},{28,12},{1,17},{... | collective-permute-start | bytes 245768 | tf_op jit(solution)/shard_map/ppermute | solution.py:377
  49.2 9.8 %collective-permute-done.16 = f32[160,128]{1,0:T(8,128)S(1)} collective-permute-done((f32[160,128]{1,0:T(8,128)S(1)}, f32[160,128]{1,0:T(8,128)S(1)}, u32[]{:S(2)}, u32[]{:S(2)}) %collective-permute-start.16) | collective-permute-done | bytes 81952 | tf_op jit(solution)/shard_map/ppermute | solution.py:377
  58.9 0.1 collective-permute-start.24
  59.0 1.6 %collective-permute-start.23 = (f32[160,128]{1,0:T(8,128)S(1)}, f32[160,128]{1,0:T(8,128)S(1)}, u32[]{:S(2)}, u32[]{:S(2)}) collective-permute-start(f32[160,128]{1,0:T(8,128)S(1)} %add.15.refs_0_), channel_id=1, source_target_pairs={{0,2},{1,3},{2,0},{3,1},{4,6},{5,7},{6,4},{7,5},{8,10},{9,11},{10,... | collective-permute-start | bytes 245768 | tf_op jit(solution)/shard_map/ppermute | solution.py:374
  60.6 1.9 %collective-permute-start.20 = (f32[160,128]{1,0:T(8,128)S(1)}, f32[160,128]{1,0:T(8,128)S(1)}, u32[]{:S(2)}, u32[]{:S(2)}) collective-permute-start(f32[160,128]{1,0:T(8,128)S(1)} %add.15.refs_0_), channel_id=1, source_target_pairs={{0,4},{4,0},{8,12},{12,8},{16,20},{20,16},{24,28},{28,24},{1,5},{5... | collective-permute-start | bytes 245768 | tf_op jit(solution)/shard_map/ppermute | solution.py:377
  62.5 0.9 %start_kernel.1 = (bf16[512,1024]{1,0:T(8,128)(2,1)S(1)}, f32[192,512]{1,0:T(8,128)S(1)}) custom-call(f32[128,512]{1,0:T(8,128)S(1)} %copy-done, f32[128,512]{1,0:T(8,128)S(1)} %collective-permute-done.11.s_core, f32[192,128]{1,0:T(8,128)S(1)} %get-tuple-element.101.y_own, f32[192,128]{1,0:T(8,128)S(1)} %collective-permute-done.17.y_core, ...), custom_call_target="tpu_custom_call" | custom-call | tf_op jit(solution)/shard_map/start_kernel/pallas_call | solution.py:343
  63.4 1.0 %collective-permute-done.24.refs_5_ = f32[160,128]{1,0:T(8,128)S(1)} collective-permute-done((f32[160,128]{1,0:T(8,128)S(1)}, f32[160,128]{1,0:T(8,128)S(1)}, u32[]{:S(2)}, u32[]{:S(2)}) %collective-permute-start.24) | collective-permute-done | bytes 81952 | tf_op jit(solution)/shard_map/ppermute | solution.py:383
  64.4 0.5 collective-permute-start.25
  64.9 0.4 collective-permute-done.20.refs_1_
  65.3 0.4 collective-permute-done.26.refs_7_
  65.7 0.2 collective-permute-done.25.refs_6_
  65.8 0.7 %collective-permute-done.22.refs_3_ = f32[160,128]{1,0:T(8,128)S(1)} collective-permute-done((f32[160,128]{1,0:T(8,128)S(1)}, f32[160,128]{1,0:T(8,128)S(1)}, u32[]{:S(2)}, u32[]{:S(2)}) %collective-permute-start.22) | collective-permute-done | bytes 81952 | tf_op jit(solution)/shard_map/ppermute | solution.py:374
  66.6 1.9 %back_kernel.1 = (f32[64,256]{1,0:T(8,128)}, f32[64,512]{1,0:T(8,128)}, f32[128,512]{1,0:T(8,128)}, f32[192,512]{1,0:T(8,128)}) custom-call(f32[160,128]{1,0:T(8,128)S(1)} %add.15.refs_0_, f32[160,128]{1,0:T(8,128)S(1)} %collective-permute-done.20.refs_1_, f32[160,128]{1,0:T(8,128)S(1)} %collective-permute-done.21.refs_2_, ...), custom_call_target="tpu_custom_call" | custom-call | tf_op jit(solution)/shard_map/back_kernel/pallas_call | solution.py:343
  (25 shorter events, 0.1 us)
Async XLA Ops:
  0.6 15.0 %copy-start.3 = (bf16[1,192,512]{2,1,0:T(8,128)(2,1)S(1)}, bf16[1,192,512]{2,1,0:T(8,128)(2,1)}, u32[]{:S(2)}) copy-start(bf16[1,192,512]{2,1,0:T(8,128)(2,1)} %param.13) | copy-start | bytes 589828
  0.6 11.0 %copy-start = (f32[128,512]{1,0:T(8,128)S(1)}, f32[128,512]{1,0:T(8,128)}, u32[]{:S(2)}) copy-start(f32[128,512]{1,0:T(8,128)} %s_own.1) | copy-start | bytes 786436
  0.7 15.5 %copy-start.2 = (bf16[1,192,512]{2,1,0:T(8,128)(2,1)S(1)}, bf16[1,192,512]{2,1,0:T(8,128)(2,1)}, u32[]{:S(2)}) copy-start(bf16[1,192,512]{2,1,0:T(8,128)(2,1)} %param.12) | copy-start | bytes 589828
  2.2 4.2 %collective-permute-start = (f32[192,768]{1,0:T(8,128)}, f32[192,768]{1,0:T(8,128)S(1)}, u32[]{:S(2)}, u32[]{:S(2)}) collective-permute-start(f32[192,768]{1,0:T(8,128)} %bitcast.13), channel_id=1, source_target_pairs={{0,1},{1,0},{2,3},{3,2},{4,5},{5,4},{6,7},{7,6},{8,9},{9,8},{10,11... | collective-permute-start | bytes 1769480 | tf_op jit(solution)/shard_map/ppermute | solution.py:374
  2.7 3.7 %collective-permute-start.1 = (f32[192,768]{1,0:T(8,128)}, f32[192,768]{1,0:T(8,128)S(1)}, u32[]{:S(2)}, u32[]{:S(2)}) collective-permute-start(f32[192,768]{1,0:T(8,128)} %bitcast.15), channel_id=1, source_target_pairs={{0,1},{1,0},{2,3},{3,2},{4,5},{5,4},{6,7},{7,6},{8,9},{9,8},{10,11... | collective-permute-start | bytes 1769480 | tf_op jit(solution)/shard_map/ppermute | solution.py:374
  2.8 8.9 %collective-permute-start.5 = (bf16[192,512]{1,0:T(8,128)(2,1)}, bf16[192,512]{1,0:T(8,128)(2,1)S(1)}, u32[]{:S(2)}, u32[]{:S(2)}) collective-permute-start(bf16[192,512]{1,0:T(8,128)(2,1)} %bitcast.17), channel_id=1, source_target_pairs={{0,2},{1,3},{2,0},{3,1},{4,6},{5,7},{6,4},{7,5},{8,10},{9,11},{10,... | collective-permute-start | bytes 589832 | tf_op jit(solution)/shard_map/ppermute | solution.py:374
  5.7 9.9 %collective-permute-start.2 = (f32[392,128]{1,0:T(8,128)S(1)}, f32[392,128]{1,0:T(8,128)S(1)}, u32[]{:S(2)}, u32[]{:S(2)}) collective-permute-start(f32[392,128]{1,0:T(8,128)S(1)} %get-tuple-element.63), channel_id=1, source_target_pairs={{0,2},{1,3},{2,0},{3,1},{4,6},{5,7},{6,4},{7,5},{8,10},{9,11},{10,... | collective-permute-start | bytes 602120 | tf_op jit(solution)/shard_map/ppermute | solution.py:374
  7.6 14.2 %copy-start.1 = (f32[128,512]{1,0:T(8,128)S(1)}, f32[128,512]{1,0:T(8,128)}, u32[]{:S(2)}) copy-start(f32[128,512]{1,0:T(8,128)} %base.1) | copy-start | bytes 786436
  11.6 4.5 %collective-permute-start.6 = (bf16[192,512]{1,0:T(8,128)(2,1)S(1)}, bf16[192,512]{1,0:T(8,128)(2,1)S(1)}, u32[]{:S(2)}, u32[]{:S(2)}) collective-permute-start(bf16[192,512]{1,0:T(8,128)(2,1)S(1)} %collective-permute-done.5.g_far), channel_id=1, source_target_pairs={{0,1},{1,0},{2,3},{3,2},{4,5},{5,4},{6,7},{7,6},{8,9},{9,8},{10,11... | collective-permute-start | bytes 589832 | tf_op jit(solution)/shard_map/ppermute | solution.py:374
  11.6 8.3 %collective-permute-start.11 = (f32[128,512]{1,0:T(8,128)S(1)}, f32[128,512]{1,0:T(8,128)S(1)}, u32[]{:S(2)}, u32[]{:S(2)}) collective-permute-start(f32[128,512]{1,0:T(8,128)S(1)} %copy-done), channel_id=1, source_target_pairs={{0,1},{1,0},{2,3},{3,2},{4,5},{5,4},{6,7},{7,6},{8,9},{9,8},{10,11... | collective-permute-start | bytes 786440 | tf_op jit(solution)/shard_map/ppermute | solution.py:374
  12.1 7.8 %collective-permute-start.9 = (f32[416,128]{1,0:T(8,128)S(1)}, f32[416,128]{1,0:T(8,128)S(1)}, u32[]{:S(2)}, u32[]{:S(2)}) collective-permute-start(f32[416,128]{1,0:T(8,128)S(1)} %get-tuple-element.75), channel_id=1, source_target_pairs={{0,2},{1,3},{2,0},{3,1},{4,6},{5,7},{6,4},{7,5},{8,10},{9,11},{10,... | collective-permute-start | bytes 638984 | tf_op jit(solution)/shard_map/ppermute | solution.py:374
  15.6 1.7 %collective-permute-start.3 = (f32[392,128]{1,0:T(8,128)S(1)}, f32[392,128]{1,0:T(8,128)S(1)}, u32[]{:S(2)}, u32[]{:S(2)}) collective-permute-start(f32[392,128]{1,0:T(8,128)S(1)} %collective-permute-done.2.far), channel_id=1, source_target_pairs={{0,1},{1,0},{2,3},{3,2},{4,5},{5,4},{6,7},{7,6},{8,9},{9,8},{10,11... | collective-permute-start | bytes 602120 | tf_op jit(solution)/shard_map/ppermute | solution.py:374
  15.6 1.7 %collective-permute-start.4 = (bf16[192,512]{1,0:T(8,128)(2,1)S(1)}, bf16[192,512]{1,0:T(8,128)(2,1)S(1)}, u32[]{:S(2)}, u32[]{:S(2)}) collective-permute-start(bf16[192,512]{1,0:T(8,128)(2,1)S(1)} %bitcast.18), channel_id=1, source_target_pairs={{0,1},{1,0},{2,3},{3,2},{4,5},{5,4},{6,7},{7,6},{8,9},{9,8},{10,11... | collective-permute-start | bytes 589832 | tf_op jit(solution)/shard_map/ppermute | solution.py:374
  16.1 3.8 %collective-permute-start.10 = (bf16[192,512]{1,0:T(8,128)(2,1)S(1)}, bf16[192,512]{1,0:T(8,128)(2,1)S(1)}, u32[]{:S(2)}, u32[]{:S(2)}) collective-permute-start(bf16[192,512]{1,0:T(8,128)(2,1)S(1)} %bitcast.8), channel_id=1, source_target_pairs={{0,1},{1,0},{2,3},{3,2},{4,5},{5,4},{6,7},{7,6},{8,9},{9,8},{10,11... | collective-permute-start | bytes 589832 | tf_op jit(solution)/shard_map/ppermute | solution.py:374
  19.9 1.9 %collective-permute-start.12 = (f32[416,128]{1,0:T(8,128)S(1)}, f32[416,128]{1,0:T(8,128)S(1)}, u32[]{:S(2)}, u32[]{:S(2)}) collective-permute-start(f32[416,128]{1,0:T(8,128)S(1)} %collective-permute-done.9.far), channel_id=1, source_target_pairs={{0,1},{1,0},{2,3},{3,2},{4,5},{5,4},{6,7},{7,6},{8,9},{9,8},{10,11... | collective-permute-start | bytes 638984 | tf_op jit(solution)/shard_map/ppermute | solution.py:374
  19.9 7.8 %collective-permute-start.7 = (bf16[192,512]{1,0:T(8,128)(2,1)S(1)}, bf16[192,512]{1,0:T(8,128)(2,1)S(1)}, u32[]{:S(2)}, u32[]{:S(2)}) collective-permute-start(bf16[192,512]{1,0:T(8,128)(2,1)S(1)} %bitcast.9), channel_id=1, source_target_pairs={{0,2},{1,3},{2,0},{3,1},{4,6},{5,7},{6,4},{7,5},{8,10},{9,11},{10,... | collective-permute-start | bytes 589832 | tf_op jit(solution)/shard_map/ppermute | solution.py:374
  21.7 9.2 %collective-permute-start.8 = (bf16[192,512]{1,0:T(8,128)(2,1)S(1)}, bf16[192,512]{1,0:T(8,128)(2,1)S(1)}, u32[]{:S(2)}, u32[]{:S(2)}) collective-permute-start(bf16[192,512]{1,0:T(8,128)(2,1)S(1)} %bitcast.10), channel_id=1, source_target_pairs={{0,3},{1,2},{2,1},{3,0},{4,7},{5,6},{6,5},{7,4},{8,11},{9,10},{10,... | collective-permute-start | bytes 589832 | tf_op jit(solution)/shard_map/ppermute | solution.py:374
  31.0 11.6 %collective-permute-start.14 = (f32[160,128]{1,0:T(8,128)S(1)}, f32[160,128]{1,0:T(8,128)S(1)}, u32[]{:S(2)}, u32[]{:S(2)}) collective-permute-start(f32[160,128]{1,0:T(8,128)S(1)} %get-tuple-element.85), channel_id=1, source_target_pairs={{0,8},{4,12},{8,0},{12,4},{16,24},{20,28},{24,16},{28,20},{1,9},{5... | collective-permute-start | bytes 245768 | tf_op jit(solution)/shard_map/ppermute | solution.py:377
  32.8 10.2 %collective-permute-start.13 = (f32[160,128]{1,0:T(8,128)S(1)}, f32[160,128]{1,0:T(8,128)S(1)}, u32[]{:S(2)}, u32[]{:S(2)}) collective-permute-start(f32[160,128]{1,0:T(8,128)S(1)} %get-tuple-element.86), channel_id=1, source_target_pairs={{0,4},{4,0},{8,12},{12,8},{16,20},{20,16},{24,28},{28,24},{1,5},{5... | collective-permute-start | bytes 245768 | tf_op jit(solution)/shard_map/ppermute | solution.py:377
  34.3 10.0 %collective-permute-start.15 = (f32[160,128]{1,0:T(8,128)S(1)}, f32[160,128]{1,0:T(8,128)S(1)}, u32[]{:S(2)}, u32[]{:S(2)}) collective-permute-start(f32[160,128]{1,0:T(8,128)S(1)} %get-tuple-element.86), channel_id=1, source_target_pairs={{0,12},{4,8},{8,4},{12,0},{16,28},{20,24},{24,20},{28,16},{1,13},{... | collective-permute-start | bytes 245768 | tf_op jit(solution)/shard_map/ppermute | solution.py:377
  34.5 24.4 %collective-permute-start.18 = (f32[448,128]{1,0:T(8,128)S(1)}, f32[448,128]{1,0:T(8,128)S(1)}, u32[]{:S(2)}, u32[]{:S(2)}) collective-permute-start(f32[448,128]{1,0:T(8,128)S(1)} %get-tuple-element.97), channel_id=1, source_target_pairs={{0,2},{1,3},{2,0},{3,1},{4,6},{5,7},{6,4},{7,5},{8,10},{9,11},{10,... | collective-permute-start | bytes 688136 | tf_op jit(solution)/shard_map/ppermute | solution.py:374
  36.2 22.7 %collective-permute-start.19 = (f32[448,128]{1,0:T(8,128)S(1)}, f32[448,128]{1,0:T(8,128)S(1)}, u32[]{:S(2)}, u32[]{:S(2)}) collective-permute-start(f32[448,128]{1,0:T(8,128)S(1)} %get-tuple-element.98), channel_id=1, source_target_pairs={{0,3},{1,2},{2,1},{3,0},{4,7},{5,6},{6,5},{7,4},{8,11},{9,10},{10,... | collective-permute-start | bytes 688136 | tf_op jit(solution)/shard_map/ppermute | solution.py:374
  42.6 6.6 %collective-permute-start.17 = (f32[192,128]{1,0:T(8,128)S(1)}, f32[192,128]{1,0:T(8,128)S(1)}, u32[]{:S(2)}, u32[]{:S(2)}) collective-permute-start(f32[192,128]{1,0:T(8,128)S(1)} %get-tuple-element.96), channel_id=1, source_target_pairs={{0,1},{1,0},{2,3},{3,2},{4,5},{5,4},{6,7},{7,6},{8,9},{9,8},{10,11... | collective-permute-start | bytes 294920 | tf_op jit(solution)/shard_map/ppermute | solution.py:374
  43.0 22.3 %collective-permute-start.27 = (f32[88,768]{1,0:T(8,128)S(1)}, f32[88,768]{1,0:T(8,128)S(1)}, u32[]{:S(2)}, u32[]{:S(2)}) collective-permute-start(f32[88,768]{1,0:T(8,128)S(1)} %get-tuple-element.111), channel_id=1, source_target_pairs={{4,0},{8,4},{12,8},{16,12},{20,16},{24,20},{28,24},{5,1},{9,5},{13... | collective-permute-start | bytes 811016 | tf_op jit(solution)/shard_map/ppermute | solution.py:434
  44.3 14.6 %collective-permute-start.16 = (f32[160,128]{1,0:T(8,128)S(1)}, f32[160,128]{1,0:T(8,128)S(1)}, u32[]{:S(2)}, u32[]{:S(2)}) collective-permute-start(f32[160,128]{1,0:T(8,128)S(1)} %add_add_fusion), channel_id=1, source_target_pairs={{0,16},{4,20},{8,24},{12,28},{16,0},{20,4},{24,8},{28,12},{1,17},{... | collective-permute-start | bytes 245768 | tf_op jit(solution)/shard_map/ppermute | solution.py:377
  58.9 5.5 %collective-permute-start.24 = (f32[160,128]{1,0:T(8,128)S(1)}, f32[160,128]{1,0:T(8,128)S(1)}, u32[]{:S(2)}, u32[]{:S(2)}) collective-permute-start(f32[160,128]{1,0:T(8,128)S(1)} %add.15.refs_0_), channel_id=1, source_target_pairs={{0,6},{1,7},{2,4},{3,5},{4,2},{5,3},{6,0},{7,1},{8,14},{9,15},{10,... | collective-permute-start | bytes 245768 | tf_op jit(solution)/shard_map/ppermute | solution.py:383
  59.0 5.4 %collective-permute-start.23 = (f32[160,128]{1,0:T(8,128)S(1)}, f32[160,128]{1,0:T(8,128)S(1)}, u32[]{:S(2)}, u32[]{:S(2)}) collective-permute-start(f32[160,128]{1,0:T(8,128)S(1)} %add.15.refs_0_), channel_id=1, source_target_pairs={{0,2},{1,3},{2,0},{3,1},{4,6},{5,7},{6,4},{7,5},{8,10},{9,11},{10,... | collective-permute-start | bytes 245768 | tf_op jit(solution)/shard_map/ppermute | solution.py:374
  60.6 4.7 %collective-permute-start.20 = (f32[160,128]{1,0:T(8,128)S(1)}, f32[160,128]{1,0:T(8,128)S(1)}, u32[]{:S(2)}, u32[]{:S(2)}) collective-permute-start(f32[160,128]{1,0:T(8,128)S(1)} %add.15.refs_0_), channel_id=1, source_target_pairs={{0,4},{4,0},{8,12},{12,8},{16,20},{20,16},{24,28},{28,24},{1,5},{5... | collective-permute-start | bytes 245768 | tf_op jit(solution)/shard_map/ppermute | solution.py:377
  62.5 2.8 %collective-permute-start.21 = (f32[160,128]{1,0:T(8,128)S(1)}, f32[160,128]{1,0:T(8,128)S(1)}, u32[]{:S(2)}, u32[]{:S(2)}) collective-permute-start(f32[160,128]{1,0:T(8,128)S(1)} %add.15.refs_0_), channel_id=1, source_target_pairs={{0,1},{1,0},{2,3},{3,2},{4,5},{5,4},{6,7},{7,6},{8,9},{9,8},{10,11... | collective-permute-start | bytes 245768 | tf_op jit(solution)/shard_map/ppermute | solution.py:374
  64.4 1.3 %collective-permute-start.26 = (f32[160,128]{1,0:T(8,128)S(1)}, f32[160,128]{1,0:T(8,128)S(1)}, u32[]{:S(2)}, u32[]{:S(2)}) collective-permute-start(f32[160,128]{1,0:T(8,128)S(1)} %collective-permute-done.24.refs_5_), channel_id=1, source_target_pairs={{0,1},{1,0},{2,3},{3,2},{4,5},{5,4},{6,7},{7,6},{8,9},{9,8},{10,11... | collective-permute-start | bytes 245768 | tf_op jit(solution)/shard_map/ppermute | solution.py:374
  64.4 1.4 %collective-permute-start.25 = (f32[160,128]{1,0:T(8,128)S(1)}, f32[160,128]{1,0:T(8,128)S(1)}, u32[]{:S(2)}, u32[]{:S(2)}) collective-permute-start(f32[160,128]{1,0:T(8,128)S(1)} %collective-permute-done.23.refs_4_), channel_id=1, source_target_pairs={{0,1},{1,0},{2,3},{3,2},{4,5},{5,4},{6,7},{7,6},{8,9},{9,8},{10,11... | collective-permute-start | bytes 245768 | tf_op jit(solution)/shard_map/ppermute | solution.py:374
  65.3 1.3 %collective-permute-start.22 = (f32[160,128]{1,0:T(8,128)S(1)}, f32[160,128]{1,0:T(8,128)S(1)}, u32[]{:S(2)}, u32[]{:S(2)}) collective-permute-start(f32[160,128]{1,0:T(8,128)S(1)} %collective-permute-done.20.refs_1_), channel_id=1, source_target_pairs={{0,1},{1,0},{2,3},{3,2},{4,5},{5,4},{6,7},{7,6},{8,9},{9,8},{10,11... | collective-permute-start | bytes 245768 | tf_op jit(solution)/shard_map/ppermute | solution.py:374

commit v5 on v4

--- a/solution.py
+++ b/solution.py
@@ -66,7 +66,7 @@
     x_rows, k_rows, g_rows, s_rows, index,
     x_out, k_out, x_own, k_own, g_own, s_out, index_out, sems,
 ):
-    rows, order = x_own.shape
+    rows, order = x_rows.shape
     half = order // 2
     unit = half // 3
     group = s_rows.shape[0]
@@ -82,11 +82,11 @@
         ],
         sems=sems,
     )
-    large = at(core * (rows - unit), unit, 8)
-    small = at((1 - core) * unit, rows - unit, 8)
     edge = at(near * half + core * 2 * unit, unit, 128)
     middle = at(near * half + unit, unit, 128)
     opposite = at(near * half + (1 - core) * 2 * unit, unit, 128)
+    large = at(core * (rows - unit), unit, 8)
+    small = at((1 - core) * unit, rows - unit, 8)
     for copy, own, out in zip(copies, (x_own, k_own), (x_out, k_out)):
         copy.wait()
         out[0:unit, :] = own[large, edge]
@@ -162,36 +162,31 @@
     return (product[:, :width] + product[:, width:]) + dot(low, right_side[:, :width])
 
 
-def spread_kernel(sizes, x_own, k_own, x_core, k_core, x, k, live_out, whole):
+def prepare_kernel(
+    sizes, x_own, k_own, x_core, k_core, g_own, g_core, g_far, g_cross, index, far, cross,
+    x, k, links, live_out, first, whole, gathered,
+):
     half, order = whole.shape
     rows = half // 2
-    _, near, core = place()
+    width = links.shape[1]
+    group = width // 4
+    part, near, core = place()
     ids = lax.broadcasted_iota(jnp.int32, (half, 1), 0)
     live = jnp.concatenate([ids + near * half, ids + (1 - near) * half], axis=0) < sizes[0]
     live_out[...] = jnp.where(live, 1.0, 0.0)
     for own, other, target in ((x_own, x_core, x), (k_own, k_core, k)):
-        for side, first in enumerate((near * half, (1 - near) * half)):
+        for side, col in enumerate((near * half, (1 - near) * half)):
             cols = slice(side * half, (side + 1) * half)
-            whole[at(core * rows, rows), cols] = own[:, at(first, half, 128)]
-            whole[at((1 - core) * rows, rows), cols] = other[:, at(first, half, 128)]
+            whole[at(core * rows, rows), cols] = own[:, at(col, half, 128)]
+            whole[at((1 - core) * rows, rows), cols] = other[:, at(col, half, 128)]
         spread(whole, target, live)
-
-
-def first_kernel(
-    live_in, far, cross, x_in, g_own, g_core, g_far, g_cross, index, x, first, links, gathered
-):
-    del x_in
-    order, width = links.shape
-    group = width // 4
-    live = live_rows(live_in)
     put_rows(g_own, g_core, gathered)
-    put_rows(g_far, g_cross, gathered, order // 2)
+    put_rows(g_far, g_cross, gathered, half)
     hot = lax.broadcasted_iota(jnp.int32, (width, width), 0) == index[...]
     chosen = dot(gathered[...], hot.astype(F32).astype(BF16))
     links[...] = jnp.where(live, chosen, 0.0).astype(BF16)
     corner(far, cross, x, live)
-    columns = links[:, at(place()[0] * group, group, 128)]
-    product = dot(x[...], columns)
+    product = dot(x[...], links[:, at(part * group, group, 128)])
     first[...] = product[:order] + product[order:]
 
 
@@ -216,9 +211,8 @@
     y_own[...] = solved[at(core * rows, rows), :]
     y_core[...] = solved[at((1 - core) * rows, rows), :]
     y_far[:rows, :] = solved[at(half + core * rows, rows), :]
-    y_cross[:rows, :] = solved[at(half + (1 - core) * rows, rows), :]
+    y_cross[...] = solved[at(half + (1 - core) * rows, rows), :]
     y_far[rows:, :] = s_sent[...]
-    y_cross[rows:, :] = s_sent[...]
     left_side = stacked(result.T)
 
     def square(shift):
@@ -261,15 +255,16 @@
     terms = terms[: 2 * share] + terms[2 * share :]
     cross = dot(left_side, links[...])
     cross = cross[: 2 * share] + cross[2 * share :]
-    next_terms[:share, :link] = terms[:share, :link]
-    next_terms[:share, link:] = cross[:share]
-    next_terms[share:, :] = jnp.zeros((next_terms.shape[0] - share, next_terms.shape[1]), F32)
+    next_terms[:, :link] = terms[:share, :link]
+    next_terms[:, link:] = cross[:share]
     off_terms[...] = terms[:share, link:]
     own_terms[:, :link] = terms[share:, link:]
     own_terms[:, link:] = cross[share:]
 
 
-def start_kernel(s_own, s_core, y_own, y_core, far, cross, start, scaled, s_rows, y_rows):
+def start_kernel(
+    s_own, s_core, y_own, y_core, far, y_cross, s_cross, start, scaled, s_rows, y_rows
+):
     group, width = s_own.shape
     half = width // 2
     rows = y_own.shape[0]
@@ -288,16 +283,15 @@
     put(bottom, left, low_left, side.T)
     for i in range(2):
         first = slice(rows + i * group, rows + (i + 1) * group)
-        put_rows(far.at[first, :], cross.at[first, :], s_rows.at[:, i * group : (i + 1) * group])
+        put_rows(far.at[first, :], s_cross.at[first, :], s_rows.at[:, i * group : (i + 1) * group])
     put(bottom, right, low_right, s_rows[:, :half])
-    for ref, mask in ((y_own, 0), (y_core, 1), (far, 2), (cross, 3)):
+    for ref, mask in ((y_own, 0), (y_core, 1), (far, 2), (y_cross, 3)):
         y_rows[:, at((part ^ mask) * group, group, 128)] = ref[:rows, :]
     scaled[...] = times_wide(y_rows[...], start)
 
 
 def back_kernel(*refs):
-    sums, (start, scaled, own_terms, came), outs = refs[:8], refs[8:12], refs[12:]
-    link_diag, link_cross, schur, back, whole, full, full_parts = outs
+    sums, (start, scaled, schur, back, whole, full, full_parts) = refs[:8], refs[8:]
     part = place()[0]
     side = lax.axis_index("tm") % 2
     size = sums[0].shape[0]
@@ -328,12 +322,15 @@
     full_parts[...] = both(full[...])
     value = scaled[...]
     back[...] = 2.0 * value - times_wide(times_wide(value, full_parts), start)
-    share, link = link_diag.shape
-    link_diag[...] = own_terms[:, :link] + came[:share, :link]
-    link_cross[...] = own_terms[:, link:] + came[:share, link:]
-
-
-def call(kernel, outs, scratch, *args, sizes=None, whole=False, alias={}):
+
+
+def finish_kernel(own_terms, came, link_diag, link_cross):
+    link = link_diag.shape[1]
+    link_diag[...] = own_terms[:, :link] + came[:, :link]
+    link_cross[...] = own_terms[:, link:] + came[:, link:]
+
+
+def call(kernel, outs, scratch, *args, sizes=None, whole=False, alias={}, flops=0):
     vmem = pl.BlockSpec(memory_space=pltpu.VMEM)
     specs = [pl.BlockSpec(memory_space=pltpu.HBM) if whole else vmem] * len(args)
     if whole:
@@ -348,7 +345,7 @@
         scratch_shapes=scratch,
         input_output_aliases=alias,
         compiler_params=pltpu.CompilerParams(vmem_limit_bytes=VMEM_BYTES),
-        cost_estimate=pl.CostEstimate(flops=0, bytes_accessed=0, transcendentals=0),
+        cost_estimate=pl.CostEstimate(flops=flops, bytes_accessed=0, transcendentals=0),
         name=kernel.__name__,
     )(*args)
 
@@ -388,69 +385,60 @@
     x_sent, k_sent, x_own, k_own, g_own, s_sent, index = call(
         pack_kernel,
         [((3 * unit + SPARE, unit), F32), ((3 * unit + 4 * SPARE, unit), F32),
-         ((rows, order), F32), ((rows, order), F32), ((rows, width), BF16),
-         ((2 * group, group), F32), (link_index.shape, jnp.int32)],
+         ((rows, order), F32), ((rows, order), F32), ((rows, width), BF16), ((2 * group, group), F32),
+         (link_index.shape, jnp.int32)],
         [pltpu.SemaphoreType.DMA((6,))],
         initial, operator, glob, schur_start, link_index, whole=True,
     )
     x_far, k_far = tile_swap(x_sent, 2), tile_swap(k_sent, 2)
-    initial, operator, x_sent = lax.optimization_barrier((initial, operator, x_sent))
-    x_core, k_core = tile_swap(initial, 1), tile_swap(operator, 1)
-    x, k, live = call(
-        spread_kernel,
-        [matrix, matrix, ((order, 1), F32)],
-        [vmem((half, order), F32)],
-        x_own, k_own, x_core, k_core, sizes=block_sizes,
-    )
-    x_far, g_far = after(x_far, x), after(g_far, x)
-    g_core, p_core, s_core = (tile_swap(after(v, x), 1) for v in (glob, pair, schur_start))
-    x, first, links = call(
-        first_kernel,
-        [matrix, ((order, group), F32), ((order, width), BF16)],
-        [vmem((order, width), BF16)],
-        live, x_far, tile_swap(x_far, 1), x, g_own, g_core, g_far, tile_swap(g_far, 1), index,
-        alias={3: 0},
-    )
-    pair = after(pair, x)
-    p_far, p_cross = tile_swap(pair, 2), tile_swap(pair, 3)
-    k_far, first, p_core, s_core = lax.optimization_barrier((k_far, first, p_core, s_core))
+    g_far = after(g_far, x_sent)
+    g_cross = tile_swap(g_far, 1)
+    x_far, g_cross = lax.optimization_barrier((x_far, g_cross))
+    x, k, links, live, first = call(
+        prepare_kernel,
+        [matrix, matrix, ((order, width), BF16), ((order, 1), F32), ((order, group), F32)],
+        [vmem((half, order), F32), vmem((order, width), BF16)],
+        x_own, k_own, tile_swap(x_own, 1), tile_swap(k_own, 1), g_own, tile_swap(g_own, 1), g_far, g_cross, index,
+        x_far, tile_swap(x_far, 1), sizes=block_sizes,
+    )
+    k_far = after(k_far, first)
+    p_core, p_far, s_core = (
+        tile_swap(after(v, first), m) for v, m in ((pair, 1), (pair, 2), (schur_start, 1))
+    )
     keep, send, y_own, y_core, y_far, y_cross, k = call(
         global_kernel,
         [((size, group), F32)] * 2 + [((rows, group), F32)] * 2
-        + [((rows + 2 * group, group), F32)] * 2 + [matrix],
+        + [((rows + 2 * group, group), F32), ((rows, group), F32), matrix],
         [vmem((2 * size, group), F32), vmem((order, group), F32)],
         live, k_far, tile_swap(k_far, 1), x, k, links, first, schur_base, s_sent,
         alias={4: 6},
     )
 
-    p_far, p_cross, keep = lax.optimization_barrier((p_far, p_cross, keep))
-    own_terms, off_terms, next_terms = call(
-        pair_kernel,
-        [((share, link + width), F32), ((share, link), F32),
-         ((share + 3 * SPARE, link + width), F32)],
-        [vmem((order, 2 * link), BF16)],
-        live, pair, p_core, p_far, p_cross, x, k, links,
-    )
-    came = lax.ppermute(next_terms, "tm", [(i + 1, i) for i in range(blocks - 1)])
     y_all = (y_own, tile_swap(y_core, 1), tile_swap(y_far, 2), tile_swap(y_cross, 3))
     if blocks > 2:
         parts = [block_swap(send, 1), block_swap(keep, 2), block_swap(send, 3)]
-        *parts, off_terms = lax.optimization_barrier((*parts, off_terms))
         total = (keep + parts[1]) + (parts[0] + parts[2])
     else:
         total = keep + block_swap(send, 1)
+    p_far = after(p_far, keep)
+    own_terms, off_terms, next_terms = call(
+        pair_kernel,
+        [((share, link + width), F32), ((share, link), F32), ((share, link + width), F32)],
+        [vmem((order, 2 * link), BF16)],
+        live, pair, p_core, p_far, tile_swap(p_far, 1), x, k, after(links, total),
+    )
     step = 4
     while step < blocks:
         other = block_swap(total, step)
         if step == 4:
-            other, *y_all = lax.optimization_barrier((other, *y_all))
+            other, off_terms, *y_all = lax.optimization_barrier((other, off_terms, *y_all))
         total = total + other
         step *= 2
     start, scaled = call(
         start_kernel,
         [((width, 2 * width), BF16), ((rows, width), F32)],
         [vmem((2 * group, width), F32), vmem((rows, width), F32)],
-        schur_start, s_core, *y_all,
+        schur_start, s_core, *y_all, tile_swap(after(y_all[2], total), 1),
     )
 
     here = (total, after(block_swap(total, 1), scaled))
@@ -458,13 +446,20 @@
     sums = []
     for pieces in (here, there):
         sums += [*pieces, *(tile_swap(piece, 1) for piece in pieces)]
-    link_diag, link_cross, global_schur, back_cols = call(
+    global_schur, back_cols = call(
         back_kernel,
-        [((share, link), F32), ((share, width), F32), ((group, width), F32),
-         ((rows, width), F32)],
+        [((group, width), F32), ((rows, width), F32)],
         [vmem((8 * size, group), F32), vmem((width, width), F32),
          vmem((width, 2 * width), BF16)],
-        *sums, start, scaled, own_terms, came,
+        *sums, start, scaled, flops=2 * rows * order * order * 2,
+    )
+    next_terms = after(next_terms, scaled)
+    came = lax.ppermute(next_terms, "tm", [(i + 1, i) for i in range(blocks - 1)])
+    link_diag, link_cross = call(
+        finish_kernel,
+        [((share, link), F32), ((share, width), F32)],
+        [],
+        own_terms, came,
     )
     return (
         link_diag[None], off_terms[None], link_cross[None], global_schur, back_cols[None],

time: 68.7 us -> 56.6 us (0.82)
  waiting for transfers between devices: 24.5 us -> 13.3 us
  starting transfers between devices: 24.5 us -> 23.3 us
    ppermute x5, waiting for transfers between devices: 10.1 us -> 3.03 us  [block_swap(): return lax.ppermute(value, 'tm', [(i, i ^ mask) for i in range(blocks)])]
    ppermute x21 -> x22, waiting for transfers between devices: 13.3 us -> 8 us  [tile_swap(): return lax.ppermute(value, 'tile', [(i, i ^ mask) for i in range(4)])]
    ppermute x5, starting transfers between devices: 10.2 us -> 6.67 us  [block_swap(): return lax.ppermute(value, 'tm', [(i, i ^ mask) for i in range(blocks)])]
    ppermute x1, waiting for transfers between devices: 0.01 us -> 1.91 us  [shards(): lax.ppermute(next_terms, 'tm', [(i + 1, i) for i in range(blocks - 1)])]
    ppermute x1, starting transfers between devices: 0.07 us -> 1.64 us  [diagonal_swap(): return lax.ppermute(value, ('tm', 'tile'), pairs)]
    ppermute x21 -> x22, starting transfers between devices: 12.9 us -> 13.7 us  [tile_swap(): return lax.ppermute(value, 'tile', [(i, i ^ mask) for i in range(4)])]
  transfers between devices with their start and end apart: 28 -> 29, of which waited for: 12 -> 12; matrix products, arithmetic and copies ran while one was open for 0% -> 0% of each run, Pallas kernels for 21% -> 31%
where the time goes in v5:
time: 56.6 us; the launch traced here: 56.4 us
  starting transfers between devices  23.3 us (41%)
  Pallas kernels  18.4 us (33%)
  waiting for transfers between devices  13.3 us (23%)
  between operations  1.4 us (2%)
    pallas_call x7, Pallas kernels, call(): pl.pallas_call(kernel, out_shape=[jax.ShapeDtypeStruct(shape, dtype) for...  18.4 us
    ppermute x22, starting transfers between devices, tile_swap(): return lax.ppermute(value, 'tile', [(i, i ^ mask) for i in range(4)])  13.7 us
    ppermute x22, waiting for transfers between devices, tile_swap(): return lax.ppermute(value, 'tile', [(i, i ^ mask) for i in range(4)])  8 us
    ppermute x5, starting transfers between devices, block_swap(): return lax.ppermute(value, 'tm', [(i, i ^ mask) for i in range(blocks)])  6.67 us
    ppermute x5, waiting for transfers between devices, block_swap(): return lax.ppermute(value, 'tm', [(i, i ^ mask) for i in range(blocks)])  3.03 us
    ppermute x1, waiting for transfers between devices, shards(): lax.ppermute(next_terms, 'tm', [(i + 1, i) for i in range(blocks - 1)])  1.91 us
    ppermute x1, starting transfers between devices, diagonal_swap(): return lax.ppermute(value, ('tm', 'tile'), pairs)  1.64 us
    ppermute x1, starting transfers between devices, shards(): lax.ppermute(next_terms, 'tm', [(i + 1, i) for i in range(blocks - 1)])  1.29 us
  transfers between devices with their start and end apart: 29, of which 12 were waited for; matrix products, arithmetic and copies ran while one was open for 0% of the time, Pallas kernels for 31%

profile of v5, /device:TPU:0, one launch (start us, length us, event | category | flops | bytes accessed | tf_op | source)
XLA Modules:
  0.0 56.4 jit_solution(15530925913793584812)
XLA Ops:
  0.6 3.0 %collective-permute-start.3 = (bf16[192,512]{1,0:T(8,128)(2,1)}, bf16[192,512]{1,0:T(8,128)(2,1)S(1)}, u32[]{:S(2)}, u32[]{:S(2)}) collective-permute-start(bf16[192,512]{1,0:T(8,128)(2,1)} %bitcast.13), channel_id=1, source_target_pairs={{0,2},{1,3},{2,0},{3,1},{4,6},{5,7},{6,4},{7,5},{8,10},{9,11},{10,... | collective-permute-start | bytes 589832 | tf_op jit(solution)/shard_map/ppermute | solution.py:371
  3.7 1.5 %pack_kernel.1 = (f32[392,128]{1,0:T(8,128)S(1)}, f32[416,128]{1,0:T(8,128)S(1)}, f32[192,768]{1,0:T(8,128)S(1)}, f32[192,768]{1,0:T(8,128)S(1)}, bf16[192,512]{...) custom-call(f32[192,768]{1,0:T(8,128)} %bitcast.11, f32[192,768]{1,0:T(8,128)} %bitcast.12, ...), custom_call_target="tpu_custom_call" | custom-call | tf_op jit(solution)/shard_map/pack_kernel/pallas_call | solution.py:340
  5.1 0.1 collective-permute-start
  5.2 0.5 collective-permute-start.1
  5.7 0.0 collective-permute-start.4
  5.8 3.5 %collective-permute-done.3.g_far = bf16[192,512]{1,0:T(8,128)(2,1)S(1)} collective-permute-done((bf16[192,512]{1,0:T(8,128)(2,1)}, bf16[192,512]{1,0:T(8,128)(2,1)S(1)}, u32[]{:S(2)}, u32[]{:S(2)}) %collective-permute-start.3) | collective-permute-done | bytes 196640 | tf_op jit(solution)/shard_map/ppermute | solution.py:371
  9.3 0.0 collective-permute-start.5
  9.3 2.4 %collective-permute-start.9 = (f32[416,128]{1,0:T(8,128)S(1)}, f32[416,128]{1,0:T(8,128)S(1)}, u32[]{:S(2)}, u32[]{:S(2)}) collective-permute-start(f32[416,128]{1,0:T(8,128)S(1)} %get-tuple-element.63), channel_id=1, source_target_pairs={{0,2},{1,3},{2,0},{3,1},{4,6},{5,7},{6,4},{7,5},{8,10},{9,11},{10,... | collective-permute-start | bytes 638984 | tf_op jit(solution)/shard_map/ppermute | solution.py:371
  11.7 1.4 %collective-permute-done.4.far = f32[392,128]{1,0:T(8,128)S(1)} collective-permute-done((f32[392,128]{1,0:T(8,128)S(1)}, f32[392,128]{1,0:T(8,128)S(1)}, u32[]{:S(2)}, u32[]{:S(2)}) %collective-permute-start.4) | collective-permute-done | bytes 200736 | tf_op jit(solution)/shard_map/ppermute | solution.py:371
  13.1 0.0 collective-permute-done.5.g_cross
  13.1 0.0 collective-permute-start.6
  13.1 0.5 collective-permute-start.2
  14.2 0.6 %collective-permute-done.2.g_core = bf16[192,512]{1,0:T(8,128)(2,1)S(1)} collective-permute-done((bf16[192,512]{1,0:T(8,128)(2,1)S(1)}, bf16[192,512]{1,0:T(8,128)(2,1)S(1)}, u32[]{:S(2)}, u32[]{:S(2)}) %collective-permute-start.2) | collective-permute-done | bytes 196640 | tf_op jit(solution)/shard_map/ppermute | solution.py:371
  14.8 0.0 collective-permute-done.x_core
  14.8 0.0 collective-permute-done.1.k_core
  14.8 0.0 collective-permute-done.6.cross
  14.8 2.5 %prepare_kernel.1 = (bf16[1536,768]{1,0:T(8,128)(2,1)S(1)}, bf16[1536,768]{1,0:T(8,128)(2,1)S(1)}, bf16[768,512]{1,0:T(8,128)(2,1)S(1)}, f32[768,1]{1,0:T(8,128)S(1)}, f32[768,128]{1,0:T(8,128)S(1)}) custom-call(s32[1]{0:T(128)S(6)} %copy.15.sizes, f32[192,768]{1,0:T(8,128)S(1)} %get-tuple-element.52.x_own, f32[192,768]{1,0:T(8,128)S(1)} %get-tuple-element.53.k_own, ...), custom_call_target="tpu_custom_call" | custom-call | tf_op jit(solution)/shard_map/prepare_kernel/pallas_call | solution.py:340
  17.3 0.4 collective-permute-done.9.far
  17.6 1.7 %collective-permute-start.8 = (bf16[192,512]{1,0:T(8,128)(2,1)S(1)}, bf16[192,512]{1,0:T(8,128)(2,1)S(1)}, u32[]{:S(2)}, u32[]{:S(2)}) collective-permute-start(bf16[192,512]{1,0:T(8,128)(2,1)S(1)} %bitcast.8), channel_id=1, source_target_pairs={{0,2},{1,3},{2,0},{3,1},{4,6},{5,7},{6,4},{7,5},{8,10},{9,11},{10,... | collective-permute-start | bytes 589832 | tf_op jit(solution)/shard_map/ppermute | solution.py:371
  19.4 4.6 %global_kernel.1 = (f32[160,128]{1,0:T(8,128)S(1)}, f32[160,128]{1,0:T(8,128)S(1)}, f32[192,128]{1,0:T(8,128)S(1)}, f32[192,128]{1,0:T(8,128)S(1)}, f32[448,128]...) custom-call(f32[768,1]{1,0:T(8,128)S(1)} %get-tuple-element.60.live, ...), custom_call_target="tpu_custom_call", output_to_operand_aliasing={{6}: (4, {})} | custom-call | tf_op jit(solution)/shard_map/global_kernel/pallas_call | solution.py:340
  24.0 1.6 %collective-permute-start.12 = (f32[160,128]{1,0:T(8,128)S(1)}, f32[160,128]{1,0:T(8,128)S(1)}, u32[]{:S(2)}, u32[]{:S(2)}) collective-permute-start(f32[160,128]{1,0:T(8,128)S(1)} %get-tuple-element.69), channel_id=1, source_target_pairs={{0,8},{4,12},{8,0},{12,4},{16,24},{20,28},{24,16},{28,20},{1,9},{5... | collective-permute-start | bytes 245768 | tf_op jit(solution)/shard_map/ppermute | solution.py:374
  25.6 1.5 %collective-permute-start.13 = (f32[160,128]{1,0:T(8,128)S(1)}, f32[160,128]{1,0:T(8,128)S(1)}, u32[]{:S(2)}, u32[]{:S(2)}) collective-permute-start(f32[160,128]{1,0:T(8,128)S(1)} %get-tuple-element.72), channel_id=1, source_target_pairs={{0,4},{4,0},{8,12},{12,8},{16,20},{20,16},{24,28},{28,24},{1,5},{5... | collective-permute-start | bytes 245768 | tf_op jit(solution)/shard_map/ppermute | solution.py:374
  27.1 0.4 collective-permute-start.14
  27.5 0.5 collective-permute-start.11
  28.0 0.6 %collective-permute-done.12 = f32[160,128]{1,0:T(8,128)S(1)} collective-permute-done((f32[160,128]{1,0:T(8,128)S(1)}, f32[160,128]{1,0:T(8,128)S(1)}, u32[]{:S(2)}, u32[]{:S(2)}) %collective-permute-start.12) | collective-permute-done | bytes 81952 | tf_op jit(solution)/shard_map/ppermute | solution.py:374
  28.6 1.4 %collective-permute-start.18 = (f32[448,128]{1,0:T(8,128)S(1)}, f32[448,128]{1,0:T(8,128)S(1)}, u32[]{:S(2)}, u32[]{:S(2)}) collective-permute-start(f32[448,128]{1,0:T(8,128)S(1)} %get-tuple-element.80), channel_id=1, source_target_pairs={{0,2},{1,3},{2,0},{3,1},{4,6},{5,7},{6,4},{7,5},{8,10},{9,11},{10,... | collective-permute-start | bytes 688136 | tf_op jit(solution)/shard_map/ppermute | solution.py:371
  30.0 0.9 %collective-permute-done.13 = f32[160,128]{1,0:T(8,128)S(1)} collective-permute-done((f32[160,128]{1,0:T(8,128)S(1)}, f32[160,128]{1,0:T(8,128)S(1)}, u32[]{:S(2)}, u32[]{:S(2)}) %collective-permute-start.13) | collective-permute-done | bytes 81952 | tf_op jit(solution)/shard_map/ppermute | solution.py:374
  30.9 1.6 %collective-permute-done.14 = f32[160,128]{1,0:T(8,128)S(1)} collective-permute-done((f32[160,128]{1,0:T(8,128)S(1)}, f32[160,128]{1,0:T(8,128)S(1)}, u32[]{:S(2)}, u32[]{:S(2)}) %collective-permute-start.14) | collective-permute-done | bytes 81952 | tf_op jit(solution)/shard_map/ppermute | solution.py:374
  32.5 2.7 %collective-permute-start.16 = (f32[160,128]{1,0:T(8,128)S(1)}, f32[160,128]{1,0:T(8,128)S(1)}, u32[]{:S(2)}, u32[]{:S(2)}) collective-permute-start(f32[160,128]{1,0:T(8,128)S(1)} %add_add_fusion), channel_id=1, source_target_pairs={{0,16},{4,20},{8,24},{12,28},{16,0},{20,4},{24,8},{28,12},{1,17},{... | collective-permute-start | bytes 245768 | tf_op jit(solution)/shard_map/ppermute | solution.py:374
  35.1 1.3 %collective-permute-start.15 = (f32[128,512]{1,0:T(8,128)S(1)}, f32[128,512]{1,0:T(8,128)S(1)}, u32[]{:S(2)}, u32[]{:S(2)}) collective-permute-start(f32[128,512]{1,0:T(8,128)S(1)} %copy-done), channel_id=1, source_target_pairs={{0,1},{1,0},{2,3},{3,2},{4,5},{5,4},{6,7},{7,6},{8,9},{9,8},{10,11... | collective-permute-start | bytes 786440 | tf_op jit(solution)/shard_map/ppermute | solution.py:371
  36.4 6.4 %pair_kernel.1 = (f32[64,768]{1,0:T(8,128)S(1)}, f32[64,256]{1,0:T(8,128)}, f32[64,768]{1,0:T(8,128)S(1)}) custom-call(f32[768,1]{1,0:T(8,128)S(1)} %get-tuple-element.60.live, bf16[192,512]{1,0:T(8,128)(2,1)S(1)} %bitcast.10, bf16[192,512]{1,0:T(8,128)(2,1)S(1)} %collective-permute-done.7.p_core, bf16[192,512]{1,0:T(8,128)(2,1)S(1)} %collective-permute-done.8.p_far, ...), custom_call_target="tpu_custom_call" | custom-call | tf_op jit(solution)/shard_map/pair_kernel/pallas_call | solution.py:340
  42.9 0.1 collective-permute-start.20
  43.0 1.6 %collective-permute-start.26 = (f32[160,128]{1,0:T(8,128)S(1)}, f32[160,128]{1,0:T(8,128)S(1)}, u32[]{:S(2)}, u32[]{:S(2)}) collective-permute-start(f32[160,128]{1,0:T(8,128)S(1)} %add.15.refs_0_), channel_id=1, source_target_pairs={{0,6},{1,7},{2,4},{3,5},{4,2},{5,3},{6,0},{7,1},{8,14},{9,15},{10,... | collective-permute-start | bytes 245768 | tf_op jit(solution)/shard_map/ppermute | solution.py:380
  44.6 1.5 %collective-permute-start.25 = (f32[160,128]{1,0:T(8,128)S(1)}, f32[160,128]{1,0:T(8,128)S(1)}, u32[]{:S(2)}, u32[]{:S(2)}) collective-permute-start(f32[160,128]{1,0:T(8,128)S(1)} %add.15.refs_0_), channel_id=1, source_target_pairs={{0,2},{1,3},{2,0},{3,1},{4,6},{5,7},{6,4},{7,5},{8,10},{9,11},{10,... | collective-permute-start | bytes 245768 | tf_op jit(solution)/shard_map/ppermute | solution.py:371
  46.1 0.5 collective-permute-start.22
  46.5 0.9 %start_kernel.1 = (bf16[512,1024]{1,0:T(8,128)(2,1)S(1)}, f32[192,512]{1,0:T(8,128)S(1)}) custom-call(f32[128,512]{1,0:T(8,128)S(1)} %copy-done, f32[128,512]{1,0:T(8,128)S(1)} %collective-permute-done.15.s_core, f32[192,128]{1,0:T(8,128)S(1)} %get-tuple-element.82.y_own, f32[192,128]{1,0:T(8,128)S(1)} %collective-permute-done.17.y_core, ...), custom_call_target="tpu_custom_call" | custom-call | tf_op jit(solution)/shard_map/start_kernel/pallas_call | solution.py:340
  47.4 1.3 %collective-permute-start.21 = (f32[64,768]{1,0:T(8,128)S(1)}, f32[64,768]{1,0:T(8,128)S(1)}, u32[]{:S(2)}, u32[]{:S(2)}) collective-permute-start(f32[64,768]{1,0:T(8,128)S(1)} %get-tuple-element.89), channel_id=1, source_target_pairs={{4,0},{8,4},{12,8},{16,12},{20,16},{24,20},{28,24},{5,1},{9,5},{13... | collective-permute-start | bytes 589832 | tf_op jit(solution)/shard_map/ppermute | solution.py:457
  48.7 0.1 collective-permute-start.23
  48.8 0.4 collective-permute-done.26.refs_5_
  49.2 0.1 collective-permute-start.28
  49.3 1.2 %collective-permute-done.25.refs_4_ = f32[160,128]{1,0:T(8,128)S(1)} collective-permute-done((f32[160,128]{1,0:T(8,128)S(1)}, f32[160,128]{1,0:T(8,128)S(1)}, u32[]{:S(2)}, u32[]{:S(2)}) %collective-permute-start.25) | collective-permute-done | bytes 81952 | tf_op jit(solution)/shard_map/ppermute | solution.py:371
  50.5 0.0 collective-permute-start.27
  50.5 0.5 collective-permute-start.24
  51.0 0.8 %collective-permute-done.27.refs_6_ = f32[160,128]{1,0:T(8,128)S(1)} collective-permute-done((f32[160,128]{1,0:T(8,128)S(1)}, f32[160,128]{1,0:T(8,128)S(1)}, u32[]{:S(2)}, u32[]{:S(2)}) %collective-permute-start.27) | collective-permute-done | bytes 81952 | tf_op jit(solution)/shard_map/ppermute | solution.py:371
  51.8 0.2 collective-permute-done.24.refs_3_
  51.9 1.9 %back_kernel.1 = (f32[128,512]{1,0:T(8,128)}, f32[192,512]{1,0:T(8,128)}) custom-call(f32[160,128]{1,0:T(8,128)S(1)} %add.15.refs_0_, f32[160,128]{1,0:T(8,128)S(1)} %collective-permute-done.22.refs_1_, f32[160,128]{1,0:T(8,128)S(1)} %collective-permute-done.23.refs_2_, f32[160,128]{1,0:T(8,128)S(1)} %collective-permute-done.24.refs_3_, ...), custom_call_target="tpu_custom_call" | custom-call | flops 452984832 | tf_op jit(solution)/shard_map/back_kernel/pallas_call | solution.py:340
  53.8 1.9 %collective-permute-done.21.came = f32[64,768]{1,0:T(8,128)S(1)} collective-permute-done((f32[64,768]{1,0:T(8,128)S(1)}, f32[64,768]{1,0:T(8,128)S(1)}, u32[]{:S(2)}, u32[]{:S(2)}) %collective-permute-start.21) | collective-permute-done | bytes 196640 | tf_op jit(solution)/shard_map/ppermute | solution.py:457
  55.7 0.7 %finish_kernel.1 = (f32[64,256]{1,0:T(8,128)}, f32[64,512]{1,0:T(8,128)}) custom-call(f32[64,768]{1,0:T(8,128)S(1)} %get-tuple-element.74.own_terms, f32[64,768]{1,0:T(8,128)S(1)} %collective-permute-done.21.came), custom_call_target="tpu_custom_call" | custom-call | tf_op jit(solution)/shard_map/finish_kernel/pallas_call | solution.py:340
  (25 shorter events, 0.1 us)
Async XLA Ops:
  0.6 8.7 %collective-permute-start.3 = (bf16[192,512]{1,0:T(8,128)(2,1)}, bf16[192,512]{1,0:T(8,128)(2,1)S(1)}, u32[]{:S(2)}, u32[]{:S(2)}) collective-permute-start(bf16[192,512]{1,0:T(8,128)(2,1)} %bitcast.13), channel_id=1, source_target_pairs={{0,2},{1,3},{2,0},{3,1},{4,6},{5,7},{6,4},{7,5},{8,10},{9,11},{10,... | collective-permute-start | bytes 589832 | tf_op jit(solution)/shard_map/ppermute | solution.py:371
  3.7 14.0 %copy-start.2 = (bf16[1,192,512]{2,1,0:T(8,128)(2,1)S(1)}, bf16[1,192,512]{2,1,0:T(8,128)(2,1)}, u32[]{:S(2)}) copy-start(bf16[1,192,512]{2,1,0:T(8,128)(2,1)} %param.12) | copy-start | bytes 589828
  3.7 15.7 %copy-start.1 = (f32[128,512]{1,0:T(8,128)S(1)}, f32[128,512]{1,0:T(8,128)}, u32[]{:S(2)}) copy-start(f32[128,512]{1,0:T(8,128)} %base.1) | copy-start | bytes 786436
  5.1 9.7 %collective-permute-start = (f32[192,768]{1,0:T(8,128)S(1)}, f32[192,768]{1,0:T(8,128)S(1)}, u32[]{:S(2)}, u32[]{:S(2)}) collective-permute-start(f32[192,768]{1,0:T(8,128)S(1)} %get-tuple-element.52.x_own), channel_id=1, source_target_pairs={{0,1},{1,0},{2,3},{3,2},{4,5},{5,4},{6,7},{7,6},{8,9},{9,8},{10,11... | collective-permute-start | bytes 1769480 | tf_op jit(solution)/shard_map/ppermute | solution.py:371
  5.2 9.6 %collective-permute-start.1 = (f32[192,768]{1,0:T(8,128)S(1)}, f32[192,768]{1,0:T(8,128)S(1)}, u32[]{:S(2)}, u32[]{:S(2)}) collective-permute-start(f32[192,768]{1,0:T(8,128)S(1)} %get-tuple-element.53.k_own), channel_id=1, source_target_pairs={{0,1},{1,0},{2,3},{3,2},{4,5},{5,4},{6,7},{7,6},{8,9},{9,8},{10,11... | collective-permute-start | bytes 1769480 | tf_op jit(solution)/shard_map/ppermute | solution.py:371
  5.7 7.4 %collective-permute-start.4 = (f32[392,128]{1,0:T(8,128)S(1)}, f32[392,128]{1,0:T(8,128)S(1)}, u32[]{:S(2)}, u32[]{:S(2)}) collective-permute-start(f32[392,128]{1,0:T(8,128)S(1)} %get-tuple-element.55), channel_id=1, source_target_pairs={{0,2},{1,3},{2,0},{3,1},{4,6},{5,7},{6,4},{7,5},{8,10},{9,11},{10,... | collective-permute-start | bytes 602120 | tf_op jit(solution)/shard_map/ppermute | solution.py:371
  9.3 3.8 %collective-permute-start.5 = (bf16[192,512]{1,0:T(8,128)(2,1)S(1)}, bf16[192,512]{1,0:T(8,128)(2,1)S(1)}, u32[]{:S(2)}, u32[]{:S(2)}) collective-permute-start(bf16[192,512]{1,0:T(8,128)(2,1)S(1)} %collective-permute-done.3.g_far), channel_id=1, source_target_pairs={{0,1},{1,0},{2,3},{3,2},{4,5},{5,4},{6,7},{7,6},{8,9},{9,8},{10,11... | collective-permute-start | bytes 589832 | tf_op jit(solution)/shard_map/ppermute | solution.py:371
  9.3 8.4 %collective-permute-start.9 = (f32[416,128]{1,0:T(8,128)S(1)}, f32[416,128]{1,0:T(8,128)S(1)}, u32[]{:S(2)}, u32[]{:S(2)}) collective-permute-start(f32[416,128]{1,0:T(8,128)S(1)} %get-tuple-element.63), channel_id=1, source_target_pairs={{0,2},{1,3},{2,0},{3,1},{4,6},{5,7},{6,4},{7,5},{8,10},{9,11},{10,... | collective-permute-start | bytes 638984 | tf_op jit(solution)/shard_map/ppermute | solution.py:371
  13.1 1.7 %collective-permute-start.6 = (f32[392,128]{1,0:T(8,128)S(1)}, f32[392,128]{1,0:T(8,128)S(1)}, u32[]{:S(2)}, u32[]{:S(2)}) collective-permute-start(f32[392,128]{1,0:T(8,128)S(1)} %collective-permute-done.4.far), channel_id=1, source_target_pairs={{0,1},{1,0},{2,3},{3,2},{4,5},{5,4},{6,7},{7,6},{8,9},{9,8},{10,11... | collective-permute-start | bytes 602120 | tf_op jit(solution)/shard_map/ppermute | solution.py:371
  13.1 1.7 %collective-permute-start.2 = (bf16[192,512]{1,0:T(8,128)(2,1)S(1)}, bf16[192,512]{1,0:T(8,128)(2,1)S(1)}, u32[]{:S(2)}, u32[]{:S(2)}) collective-permute-start(bf16[192,512]{1,0:T(8,128)(2,1)S(1)} %get-tuple-element.54.g_own), channel_id=1, source_target_pairs={{0,1},{1,0},{2,3},{3,2},{4,5},{5,4},{6,7},{7,6},{8,9},{9,8},{10,11... | collective-permute-start | bytes 589832 | tf_op jit(solution)/shard_map/ppermute | solution.py:371
  17.6 1.8 %collective-permute-start.10 = (f32[416,128]{1,0:T(8,128)S(1)}, f32[416,128]{1,0:T(8,128)S(1)}, u32[]{:S(2)}, u32[]{:S(2)}) collective-permute-start(f32[416,128]{1,0:T(8,128)S(1)} %collective-permute-done.9.far), channel_id=1, source_target_pairs={{0,1},{1,0},{2,3},{3,2},{4,5},{5,4},{6,7},{7,6},{8,9},{9,8},{10,11... | collective-permute-start | bytes 638984 | tf_op jit(solution)/shard_map/ppermute | solution.py:371
  17.6 9.9 %collective-permute-start.8 = (bf16[192,512]{1,0:T(8,128)(2,1)S(1)}, bf16[192,512]{1,0:T(8,128)(2,1)S(1)}, u32[]{:S(2)}, u32[]{:S(2)}) collective-permute-start(bf16[192,512]{1,0:T(8,128)(2,1)S(1)} %bitcast.8), channel_id=1, source_target_pairs={{0,2},{1,3},{2,0},{3,1},{4,6},{5,7},{6,4},{7,5},{8,10},{9,11},{10,... | collective-permute-start | bytes 589832 | tf_op jit(solution)/shard_map/ppermute | solution.py:371
  19.4 15.8 %copy-start = (f32[128,512]{1,0:T(8,128)S(1)}, f32[128,512]{1,0:T(8,128)}, u32[]{:S(2)}) copy-start(f32[128,512]{1,0:T(8,128)} %s_own.1) | copy-start | bytes 786436
  24.0 4.6 %collective-permute-start.12 = (f32[160,128]{1,0:T(8,128)S(1)}, f32[160,128]{1,0:T(8,128)S(1)}, u32[]{:S(2)}, u32[]{:S(2)}) collective-permute-start(f32[160,128]{1,0:T(8,128)S(1)} %get-tuple-element.69), channel_id=1, source_target_pairs={{0,8},{4,12},{8,0},{12,4},{16,24},{20,28},{24,16},{28,20},{1,9},{5... | collective-permute-start | bytes 245768 | tf_op jit(solution)/shard_map/ppermute | solution.py:374
  25.6 5.2 %collective-permute-start.13 = (f32[160,128]{1,0:T(8,128)S(1)}, f32[160,128]{1,0:T(8,128)S(1)}, u32[]{:S(2)}, u32[]{:S(2)}) collective-permute-start(f32[160,128]{1,0:T(8,128)S(1)} %get-tuple-element.72), channel_id=1, source_target_pairs={{0,4},{4,0},{8,12},{12,8},{16,20},{20,16},{24,28},{28,24},{1,5},{5... | collective-permute-start | bytes 245768 | tf_op jit(solution)/shard_map/ppermute | solution.py:374
  27.1 5.3 %collective-permute-start.14 = (f32[160,128]{1,0:T(8,128)S(1)}, f32[160,128]{1,0:T(8,128)S(1)}, u32[]{:S(2)}, u32[]{:S(2)}) collective-permute-start(f32[160,128]{1,0:T(8,128)S(1)} %get-tuple-element.72), channel_id=1, source_target_pairs={{0,12},{4,8},{8,4},{12,0},{16,28},{20,24},{24,20},{28,16},{1,13},{... | collective-permute-start | bytes 245768 | tf_op jit(solution)/shard_map/ppermute | solution.py:374
  27.5 5.0 %collective-permute-start.7 = (bf16[192,512]{1,0:T(8,128)(2,1)S(1)}, bf16[192,512]{1,0:T(8,128)(2,1)S(1)}, u32[]{:S(2)}, u32[]{:S(2)}) collective-permute-start(bf16[192,512]{1,0:T(8,128)(2,1)S(1)} %bitcast.9), channel_id=1, source_target_pairs={{0,1},{1,0},{2,3},{3,2},{4,5},{5,4},{6,7},{7,6},{8,9},{9,8},{10,11... | collective-permute-start | bytes 589832 | tf_op jit(solution)/shard_map/ppermute | solution.py:371
  27.5 7.6 %collective-permute-start.11 = (bf16[192,512]{1,0:T(8,128)(2,1)S(1)}, bf16[192,512]{1,0:T(8,128)(2,1)S(1)}, u32[]{:S(2)}, u32[]{:S(2)}) collective-permute-start(bf16[192,512]{1,0:T(8,128)(2,1)S(1)} %collective-permute-done.8.p_far), channel_id=1, source_target_pairs={{0,1},{1,0},{2,3},{3,2},{4,5},{5,4},{6,7},{7,6},{8,9},{9,8},{10,11... | collective-permute-start | bytes 589832 | tf_op jit(solution)/shard_map/ppermute | solution.py:371
  28.6 14.2 %collective-permute-start.18 = (f32[448,128]{1,0:T(8,128)S(1)}, f32[448,128]{1,0:T(8,128)S(1)}, u32[]{:S(2)}, u32[]{:S(2)}) collective-permute-start(f32[448,128]{1,0:T(8,128)S(1)} %get-tuple-element.80), channel_id=1, source_target_pairs={{0,2},{1,3},{2,0},{3,1},{4,6},{5,7},{6,4},{7,5},{8,10},{9,11},{10,... | collective-permute-start | bytes 688136 | tf_op jit(solution)/shard_map/ppermute | solution.py:371
  30.9 12.0 %collective-permute-start.17 = (f32[192,128]{1,0:T(8,128)S(1)}, f32[192,128]{1,0:T(8,128)S(1)}, u32[]{:S(2)}, u32[]{:S(2)}) collective-permute-start(f32[192,128]{1,0:T(8,128)S(1)} %get-tuple-element.79), channel_id=1, source_target_pairs={{0,1},{1,0},{2,3},{3,2},{4,5},{5,4},{6,7},{7,6},{8,9},{9,8},{10,11... | collective-permute-start | bytes 294920 | tf_op jit(solution)/shard_map/ppermute | solution.py:371
  32.5 10.4 %collective-permute-start.19 = (f32[192,128]{1,0:T(8,128)S(1)}, f32[192,128]{1,0:T(8,128)S(1)}, u32[]{:S(2)}, u32[]{:S(2)}) collective-permute-start(f32[192,128]{1,0:T(8,128)S(1)} %get-tuple-element.81), channel_id=1, source_target_pairs={{0,3},{1,2},{2,1},{3,0},{4,7},{5,6},{6,5},{7,4},{8,11},{9,10},{10,... | collective-permute-start | bytes 294920 | tf_op jit(solution)/shard_map/ppermute | solution.py:371
  32.5 10.4 %collective-permute-start.16 = (f32[160,128]{1,0:T(8,128)S(1)}, f32[160,128]{1,0:T(8,128)S(1)}, u32[]{:S(2)}, u32[]{:S(2)}) collective-permute-start(f32[160,128]{1,0:T(8,128)S(1)} %add_add_fusion), channel_id=1, source_target_pairs={{0,16},{4,20},{8,24},{12,28},{16,0},{20,4},{24,8},{28,12},{1,17},{... | collective-permute-start | bytes 245768 | tf_op jit(solution)/shard_map/ppermute | solution.py:374
  35.1 11.4 %collective-permute-start.15 = (f32[128,512]{1,0:T(8,128)S(1)}, f32[128,512]{1,0:T(8,128)S(1)}, u32[]{:S(2)}, u32[]{:S(2)}) collective-permute-start(f32[128,512]{1,0:T(8,128)S(1)} %copy-done), channel_id=1, source_target_pairs={{0,1},{1,0},{2,3},{3,2},{4,5},{5,4},{6,7},{7,6},{8,9},{9,8},{10,11... | collective-permute-start | bytes 786440 | tf_op jit(solution)/shard_map/ppermute | solution.py:371
  42.9 3.6 %collective-permute-start.20 = (f32[448,128]{1,0:T(8,128)S(1)}, f32[448,128]{1,0:T(8,128)S(1)}, u32[]{:S(2)}, u32[]{:S(2)}) collective-permute-start(f32[448,128]{1,0:T(8,128)S(1)} %collective-permute-done.18.far), channel_id=1, source_target_pairs={{0,1},{1,0},{2,3},{3,2},{4,5},{5,4},{6,7},{7,6},{8,9},{9,8},{10,11... | collective-permute-start | bytes 688136 | tf_op jit(solution)/shard_map/ppermute | solution.py:371
  43.0 6.2 %collective-permute-start.26 = (f32[160,128]{1,0:T(8,128)S(1)}, f32[160,128]{1,0:T(8,128)S(1)}, u32[]{:S(2)}, u32[]{:S(2)}) collective-permute-start(f32[160,128]{1,0:T(8,128)S(1)} %add.15.refs_0_), channel_id=1, source_target_pairs={{0,6},{1,7},{2,4},{3,5},{4,2},{5,3},{6,0},{7,1},{8,14},{9,15},{10,... | collective-permute-start | bytes 245768 | tf_op jit(solution)/shard_map/ppermute | solution.py:380
  44.6 5.9 %collective-permute-start.25 = (f32[160,128]{1,0:T(8,128)S(1)}, f32[160,128]{1,0:T(8,128)S(1)}, u32[]{:S(2)}, u32[]{:S(2)}) collective-permute-start(f32[160,128]{1,0:T(8,128)S(1)} %add.15.refs_0_), channel_id=1, source_target_pairs={{0,2},{1,3},{2,0},{3,1},{4,6},{5,7},{6,4},{7,5},{8,10},{9,11},{10,... | collective-permute-start | bytes 245768 | tf_op jit(solution)/shard_map/ppermute | solution.py:371
  46.1 4.4 %collective-permute-start.22 = (f32[160,128]{1,0:T(8,128)S(1)}, f32[160,128]{1,0:T(8,128)S(1)}, u32[]{:S(2)}, u32[]{:S(2)}) collective-permute-start(f32[160,128]{1,0:T(8,128)S(1)} %add.15.refs_0_), channel_id=1, source_target_pairs={{0,4},{4,0},{8,12},{12,8},{16,20},{20,16},{24,28},{28,24},{1,5},{5... | collective-permute-start | bytes 245768 | tf_op jit(solution)/shard_map/ppermute | solution.py:374
  47.4 8.3 %collective-permute-start.21 = (f32[64,768]{1,0:T(8,128)S(1)}, f32[64,768]{1,0:T(8,128)S(1)}, u32[]{:S(2)}, u32[]{:S(2)}) collective-permute-start(f32[64,768]{1,0:T(8,128)S(1)} %get-tuple-element.89), channel_id=1, source_target_pairs={{4,0},{8,4},{12,8},{16,12},{20,16},{24,20},{28,24},{5,1},{9,5},{13... | collective-permute-start | bytes 589832 | tf_op jit(solution)/shard_map/ppermute | solution.py:457
  48.7 2.3 %collective-permute-start.23 = (f32[160,128]{1,0:T(8,128)S(1)}, f32[160,128]{1,0:T(8,128)S(1)}, u32[]{:S(2)}, u32[]{:S(2)}) collective-permute-start(f32[160,128]{1,0:T(8,128)S(1)} %add.15.refs_0_), channel_id=1, source_target_pairs={{0,1},{1,0},{2,3},{3,2},{4,5},{5,4},{6,7},{7,6},{8,9},{9,8},{10,11... | collective-permute-start | bytes 245768 | tf_op jit(solution)/shard_map/ppermute | solution.py:371
  49.2 1.8 %collective-permute-start.28 = (f32[160,128]{1,0:T(8,128)S(1)}, f32[160,128]{1,0:T(8,128)S(1)}, u32[]{:S(2)}, u32[]{:S(2)}) collective-permute-start(f32[160,128]{1,0:T(8,128)S(1)} %collective-permute-done.26.refs_5_), channel_id=1, source_target_pairs={{0,1},{1,0},{2,3},{3,2},{4,5},{5,4},{6,7},{7,6},{8,9},{9,8},{10,11... | collective-permute-start | bytes 245768 | tf_op jit(solution)/shard_map/ppermute | solution.py:371
  50.5 1.3 %collective-permute-start.27 = (f32[160,128]{1,0:T(8,128)S(1)}, f32[160,128]{1,0:T(8,128)S(1)}, u32[]{:S(2)}, u32[]{:S(2)}) collective-permute-start(f32[160,128]{1,0:T(8,128)S(1)} %collective-permute-done.25.refs_4_), channel_id=1, source_target_pairs={{0,1},{1,0},{2,3},{3,2},{4,5},{5,4},{6,7},{7,6},{8,9},{9,8},{10,11... | collective-permute-start | bytes 245768 | tf_op jit(solution)/shard_map/ppermute | solution.py:371
  50.5 1.4 %collective-permute-start.24 = (f32[160,128]{1,0:T(8,128)S(1)}, f32[160,128]{1,0:T(8,128)S(1)}, u32[]{:S(2)}, u32[]{:S(2)}) collective-permute-start(f32[160,128]{1,0:T(8,128)S(1)} %collective-permute-done.22.refs_1_), channel_id=1, source_target_pairs={{0,1},{1,0},{2,3},{3,2},{4,5},{5,4},{6,7},{7,6},{8,9},{9,8},{10,11... | collective-permute-start | bytes 245768 | tf_op jit(solution)/shard_map/ppermute | solution.py:371

commit v6 on v5

--- a/solution.py
+++ b/solution.py
@@ -39,10 +39,6 @@
 def place():
     part = lax.axis_index("tile")
     return part, part // 2, part % 2
-
-
-def live_rows(live):
-    return live[...] > 0.0
 
 
 def put_rows(own, other, target, offset=0):
@@ -113,8 +109,8 @@
 
     def put(row, col, value):
         first = half + row * unit
-        high, low = halves(jnp.where(live[first : first + unit], value, 0.0))
         cols = slice(half + col * unit, half + (col + 1) * unit)
+        high, low = halves(value * live[:, cols])
         target[first : first + unit, cols] = high
         target[order + first : order + first + unit, cols] = low
 
@@ -138,21 +134,21 @@
         (slice(0, half), slice(0, order), whole[...]),
         (slice(half, order), slice(0, half), whole[:, half:].T),
     ):
-        high, low = halves(jnp.where(live[rows], value, 0.0))
+        high, low = halves(value * live[:, cols])
         target[rows, cols] = high
         target[order + rows.start : order + rows.stop, cols] = low
 
 
-def times(matrix, columns):
-    order, width = columns.shape
-    columns = both(columns)
-    step = order // 2
+def times(rows, matrix):
+    count, order = rows.shape
+    high = rows.astype(BF16)
+    parts = stacked(rows)
     result = []
-    for first in range(0, order, step):
-        high = dot(matrix[first : first + step, :], columns)
-        low = dot(matrix[order + first : order + first + step, :], columns)
-        result.append((high[:, :width] + high[:, width:]) + (low[:, :width] + low[:, width:]))
-    return jnp.concatenate(result, axis=0)
+    for first in range(0, order, 256):
+        cols = slice(first, min(first + 256, order))
+        product = dot(parts, matrix[:order, cols])
+        result.append((product[:count] + product[count:]) + dot(high, matrix[order:, cols]))
+    return jnp.concatenate(result, axis=1)
 
 
 def times_wide(left_side, right_side):
@@ -164,35 +160,38 @@
 
 def prepare_kernel(
     sizes, x_own, k_own, x_core, k_core, g_own, g_core, g_far, g_cross, index, far, cross,
-    x, k, links, live_out, first, whole, gathered,
+    x, k, links, live_rows, live_cols, columns, first, whole, gathered,
 ):
     half, order = whole.shape
     rows = half // 2
     width = links.shape[1]
     group = width // 4
     part, near, core = place()
-    ids = lax.broadcasted_iota(jnp.int32, (half, 1), 0)
-    live = jnp.concatenate([ids + near * half, ids + (1 - near) * half], axis=0) < sizes[0]
-    live_out[...] = jnp.where(live, 1.0, 0.0)
+    for out, axis in ((live_rows, 0), (live_cols, 1)):
+        ids = lax.broadcasted_iota(jnp.int32, out.shape, axis)
+        ids = jnp.where(ids < half, ids + near * half, ids - near * half)
+        out[...] = jnp.where(ids < sizes[0], 1.0, 0.0)
     for own, other, target in ((x_own, x_core, x), (k_own, k_core, k)):
         for side, col in enumerate((near * half, (1 - near) * half)):
             cols = slice(side * half, (side + 1) * half)
             whole[at(core * rows, rows), cols] = own[:, at(col, half, 128)]
             whole[at((1 - core) * rows, rows), cols] = other[:, at(col, half, 128)]
-        spread(whole, target, live)
+        spread(whole, target, live_cols)
     put_rows(g_own, g_core, gathered)
     put_rows(g_far, g_cross, gathered, half)
     hot = lax.broadcasted_iota(jnp.int32, (width, width), 0) == index[...]
     chosen = dot(gathered[...], hot.astype(F32).astype(BF16))
-    links[...] = jnp.where(live, chosen, 0.0).astype(BF16)
-    corner(far, cross, x, live)
-    product = dot(x[...], links[:, at(part * group, group, 128)])
-    first[...] = product[:order] + product[order:]
+    links[...] = (chosen * live_rows[...]).astype(BF16)
+    corner(far, cross, x, live_cols)
+    value = links[:, at(part * group, group, 128)].astype(F32).T
+    columns[...] = value
+    high = value.astype(BF16)
+    first[...] = dot(high, x[:order, :]) + dot(high, x[order:, :])
 
 
 def global_kernel(
-    live, far, cross, x, k_in, links, first, base, s_sent,
-    keep, send, y_own, y_core, y_far, y_cross, k, pack, solved,
+    live, far, cross, x, k_in, links, columns, first, base, s_sent,
+    keep, send, y_own, y_core, y_far, k, pack, solved,
 ):
     del k_in
     order, width = links.shape
@@ -201,19 +200,18 @@
     group = width // 4
     part, _, core = place()
     block = lax.axis_index("tm")
-    corner(far, cross, k, live_rows(live))
-    columns = links[:, at(part * group, group, 128)].astype(F32)
-    value = 2.0 * columns - times(k, first[...])
+    corner(far, cross, k, live)
+    value = 2.0 * columns[...] - times(first[...], k)
     for step in range(TERMS - 1):
-        value = columns + value - times(k, times(x, value))
-    result = times(x, value)
-    solved[...] = result
+        value = columns[...] + value - times(times(value, x), k)
+    result = times(value, x)
+    left_side = stacked(result)
+    solved[...] = result.T
     y_own[...] = solved[at(core * rows, rows), :]
     y_core[...] = solved[at((1 - core) * rows, rows), :]
     y_far[:rows, :] = solved[at(half + core * rows, rows), :]
-    y_cross[...] = solved[at(half + (1 - core) * rows, rows), :]
-    y_far[rows:, :] = s_sent[...]
-    left_side = stacked(result.T)
+    y_far[rows : 2 * rows, :] = solved[at(half + (1 - core) * rows, rows), :]
+    y_far[2 * rows :, :] = s_sent[...]
 
     def square(shift):
         cols = at(((part + shift) % 4) * group, group, 128)
@@ -242,15 +240,15 @@
     share = link // 4
     put_rows(p_own, p_core, gathered)
     put_rows(p_far, p_cross, gathered, half)
-    masked = jnp.where(live_rows(live), gathered[...], jnp.zeros((), BF16))
+    masked = gathered[...] * live[...].astype(BF16)
     source = lax.broadcasted_iota(jnp.int32, (width, 2 * share), 0)
     target = lax.broadcasted_iota(jnp.int32, (width, 2 * share), 1)
     wanted = place()[0] * share + target + jnp.where(target < share, 0, link - share)
-    columns = dot(masked, (source == wanted).astype(F32).astype(BF16))
+    columns = dot(masked, (source == wanted).astype(F32).astype(BF16)).T
     value = columns
     for step in range(TERMS):
-        value = columns + value - times(k, times(x, value))
-    left_side = stacked(times(x, value).T)
+        value = columns + value - times(times(value, x), k)
+    left_side = stacked(times(value, x))
     terms = dot(left_side, masked)
     terms = terms[: 2 * share] + terms[2 * share :]
     cross = dot(left_side, links[...])
@@ -263,7 +261,7 @@
 
 
 def start_kernel(
-    s_own, s_core, y_own, y_core, far, y_cross, s_cross, start, scaled, s_rows, y_rows
+    s_own, s_core, y_own, y_core, far, cross, start, scaled, s_rows, y_rows
 ):
     group, width = s_own.shape
     half = width // 2
@@ -282,10 +280,10 @@
     put(top, right, low_right, side)
     put(bottom, left, low_left, side.T)
     for i in range(2):
-        first = slice(rows + i * group, rows + (i + 1) * group)
-        put_rows(far.at[first, :], s_cross.at[first, :], s_rows.at[:, i * group : (i + 1) * group])
+        first = slice(2 * rows + i * group, 2 * rows + (i + 1) * group)
+        put_rows(far.at[first, :], cross.at[first, :], s_rows.at[:, i * group : (i + 1) * group])
     put(bottom, right, low_right, s_rows[:, :half])
-    for ref, mask in ((y_own, 0), (y_core, 1), (far, 2), (y_cross, 3)):
+    for ref, mask in ((y_own, 0), (y_core, 1), (far, 2), (cross.at[rows:, :], 3)):
         y_rows[:, at((part ^ mask) * group, group, 128)] = ref[:rows, :]
     scaled[...] = times_wide(y_rows[...], start)
 
@@ -326,8 +324,9 @@
 
 def finish_kernel(own_terms, came, link_diag, link_cross):
     link = link_diag.shape[1]
-    link_diag[...] = own_terms[:, :link] + came[:, :link]
-    link_cross[...] = own_terms[:, link:] + came[:, link:]
+    there = lax.axis_index("tm") + 1 < lax.axis_size("tm")
+    link_diag[...] = own_terms[:, :link] + jnp.where(there, came[:, :link], 0.0)
+    link_cross[...] = own_terms[:, link:] + jnp.where(there, came[:, link:], 0.0)
 
 
 def call(kernel, outs, scratch, *args, sizes=None, whole=False, alias={}, flops=0):
@@ -394,9 +393,10 @@
     g_far = after(g_far, x_sent)
     g_cross = tile_swap(g_far, 1)
     x_far, g_cross = lax.optimization_barrier((x_far, g_cross))
-    x, k, links, live, first = call(
+    x, k, links, live_rows, live_cols, columns, first = call(
         prepare_kernel,
-        [matrix, matrix, ((order, width), BF16), ((order, 1), F32), ((order, group), F32)],
+        [matrix, matrix, ((order, width), BF16), ((order, 1), F32), ((1, order), F32),
+         ((group, order), F32), ((group, order), F32)],
         [vmem((half, order), F32), vmem((order, width), BF16)],
         x_own, k_own, tile_swap(x_own, 1), tile_swap(k_own, 1), g_own, tile_swap(g_own, 1), g_far, g_cross, index,
         x_far, tile_swap(x_far, 1), sizes=block_sizes,
@@ -405,16 +405,16 @@
     p_core, p_far, s_core = (
         tile_swap(after(v, first), m) for v, m in ((pair, 1), (pair, 2), (schur_start, 1))
     )
-    keep, send, y_own, y_core, y_far, y_cross, k = call(
+    keep, send, y_own, y_core, y_far, k = call(
         global_kernel,
         [((size, group), F32)] * 2 + [((rows, group), F32)] * 2
-        + [((rows + 2 * group, group), F32), ((rows, group), F32), matrix],
+        + [((2 * rows + 2 * group, group), F32), matrix],
         [vmem((2 * size, group), F32), vmem((order, group), F32)],
-        live, k_far, tile_swap(k_far, 1), x, k, links, first, schur_base, s_sent,
-        alias={4: 6},
-    )
-
-    y_all = (y_own, tile_swap(y_core, 1), tile_swap(y_far, 2), tile_swap(y_cross, 3))
+        live_cols, k_far, tile_swap(k_far, 1), x, k, links, columns, first, schur_base, s_sent,
+        alias={4: 5},
+    )
+
+    y_all = (y_own, tile_swap(y_core, 1), tile_swap(y_far, 2))
     if blocks > 2:
         parts = [block_swap(send, 1), block_swap(keep, 2), block_swap(send, 3)]
         total = (keep + parts[1]) + (parts[0] + parts[2])
@@ -425,7 +425,7 @@
         pair_kernel,
         [((share, link + width), F32), ((share, link), F32), ((share, link + width), F32)],
         [vmem((order, 2 * link), BF16)],
-        live, pair, p_core, p_far, tile_swap(p_far, 1), x, k, after(links, total),
+        live_rows, pair, p_core, p_far, tile_swap(p_far, 1), x, k, after(links, total),
     )
     step = 4
     while step < blocks:
@@ -454,7 +454,7 @@
         *sums, start, scaled, flops=2 * rows * order * order * 2,
     )
     next_terms = after(next_terms, scaled)
-    came = lax.ppermute(next_terms, "tm", [(i + 1, i) for i in range(blocks - 1)])
+    came = lax.ppermute(next_terms, "tm", [(i, (i - 1) % blocks) for i in range(blocks)])
     link_diag, link_cross = call(
         finish_kernel,
         [((share, link), F32), ((share, width), F32)],

time: 56.6 us -> 53 us (0.936)
  Pallas kernels: 18.4 us -> 16.6 us
  waiting for transfers between devices: 13.3 us -> 11.6 us
    pallas_call x7, Pallas kernels: 18.4 us -> 16.6 us  [call(): pl.pallas_call(kernel, out_shape=[jax.ShapeDtypeStruct(shape, dtype) for...]
    ppermute x22 -> x21, starting transfers between devices: 13.7 us -> 11.9 us  [tile_swap(): return lax.ppermute(value, 'tile', [(i, i ^ mask) for i in range(4)])]
    ppermute x1, waiting for transfers between devices: 1.91 us -> 0.24 us  [shards(): lax.ppermute(next_terms, 'tm', [(i, (i - 1) % blocks) for i in range(bloc...]
    ppermute x1, starting transfers between devices: 1.29 us -> 2.17 us  [shards(): lax.ppermute(next_terms, 'tm', [(i, (i - 1) % blocks) for i in range(bloc...]
    ppermute x5, starting transfers between devices: 6.67 us -> 7.37 us  [block_swap(): return lax.ppermute(value, 'tm', [(i, i ^ mask) for i in range(blocks)])]
    ppermute x5, waiting for transfers between devices: 3.03 us -> 3.71 us  [block_swap(): return lax.ppermute(value, 'tm', [(i, i ^ mask) for i in range(blocks)])]
    ppermute x22 -> x21, waiting for transfers between devices: 8 us -> 7.66 us  [tile_swap(): return lax.ppermute(value, 'tile', [(i, i ^ mask) for i in range(4)])]
  transfers between devices with their start and end apart: 29 -> 28, of which waited for: 12 -> 11; matrix products, arithmetic and copies ran while one was open for 0% -> 0% of each run, Pallas kernels for 31% -> 30%
where the time goes in v6:
time: 53 us; the launch traced here: 52.9 us
  starting transfers between devices  23.2 us (44%)
  Pallas kernels  16.6 us (31%)
  waiting for transfers between devices  11.6 us (22%)
  between operations  1.38 us (3%)
    pallas_call x7, Pallas kernels, call(): pl.pallas_call(kernel, out_shape=[jax.ShapeDtypeStruct(shape, dtype) for...  16.6 us
    ppermute x21, starting transfers between devices, tile_swap(): return lax.ppermute(value, 'tile', [(i, i ^ mask) for i in range(4)])  11.9 us
    ppermute x21, waiting for transfers between devices, tile_swap(): return lax.ppermute(value, 'tile', [(i, i ^ mask) for i in range(4)])  7.66 us
    ppermute x5, starting transfers between devices, block_swap(): return lax.ppermute(value, 'tm', [(i, i ^ mask) for i in range(blocks)])  7.37 us
    ppermute x5, waiting for transfers between devices, block_swap(): return lax.ppermute(value, 'tm', [(i, i ^ mask) for i in range(blocks)])  3.71 us
    ppermute x1, starting transfers between devices, shards(): lax.ppermute(next_terms, 'tm', [(i, (i - 1) % blocks) for i in range(bloc...  2.17 us
    ppermute x1, starting transfers between devices, diagonal_swap(): return lax.ppermute(value, ('tm', 'tile'), pairs)  1.75 us
  transfers between devices with their start and end apart: 28, of which 11 were waited for; matrix products, arithmetic and copies ran while one was open for 0% of the time, Pallas kernels for 30%

profile of v6, /device:TPU:0, one launch (start us, length us, event | category | flops | bytes accessed | tf_op | source)
XLA Modules:
  0.0 52.9 jit_solution(5866307643713033113)
XLA Ops:
  0.6 3.0 %collective-permute-start.3 = (bf16[192,512]{1,0:T(8,128)(2,1)}, bf16[192,512]{1,0:T(8,128)(2,1)S(1)}, u32[]{:S(2)}, u32[]{:S(2)}) collective-permute-start(bf16[192,512]{1,0:T(8,128)(2,1)} %bitcast.13), channel_id=1, source_target_pairs={{0,2},{1,3},{2,0},{3,1},{4,6},{5,7},{6,4},{7,5},{8,10},{9,11},{10,... | collective-permute-start | bytes 589832 | tf_op jit(solution)/shard_map/ppermute | solution.py:370
  3.7 1.5 %pack_kernel.1 = (f32[392,128]{1,0:T(8,128)S(1)}, f32[416,128]{1,0:T(8,128)S(1)}, f32[192,768]{1,0:T(8,128)S(1)}, f32[192,768]{1,0:T(8,128)S(1)}, bf16[192,512]{...) custom-call(f32[192,768]{1,0:T(8,128)} %bitcast.11, f32[192,768]{1,0:T(8,128)} %bitcast.12, ...), custom_call_target="tpu_custom_call" | custom-call | tf_op jit(solution)/shard_map/pack_kernel/pallas_call | solution.py:339
  5.1 0.1 collective-permute-start
  5.2 0.5 collective-permute-start.1
  5.7 0.0 collective-permute-start.4
  5.8 3.5 %collective-permute-done.3.g_far = bf16[192,512]{1,0:T(8,128)(2,1)S(1)} collective-permute-done((bf16[192,512]{1,0:T(8,128)(2,1)}, bf16[192,512]{1,0:T(8,128)(2,1)S(1)}, u32[]{:S(2)}, u32[]{:S(2)}) %collective-permute-start.3) | collective-permute-done | bytes 196640 | tf_op jit(solution)/shard_map/ppermute | solution.py:370
  9.3 0.0 collective-permute-start.5
  9.3 2.4 %collective-permute-start.9 = (f32[416,128]{1,0:T(8,128)S(1)}, f32[416,128]{1,0:T(8,128)S(1)}, u32[]{:S(2)}, u32[]{:S(2)}) collective-permute-start(f32[416,128]{1,0:T(8,128)S(1)} %get-tuple-element.64), channel_id=1, source_target_pairs={{0,2},{1,3},{2,0},{3,1},{4,6},{5,7},{6,4},{7,5},{8,10},{9,11},{10,... | collective-permute-start | bytes 638984 | tf_op jit(solution)/shard_map/ppermute | solution.py:370
  11.7 1.4 %collective-permute-done.4.far = f32[392,128]{1,0:T(8,128)S(1)} collective-permute-done((f32[392,128]{1,0:T(8,128)S(1)}, f32[392,128]{1,0:T(8,128)S(1)}, u32[]{:S(2)}, u32[]{:S(2)}) %collective-permute-start.4) | collective-permute-done | bytes 200736 | tf_op jit(solution)/shard_map/ppermute | solution.py:370
  13.1 0.0 collective-permute-done.5.g_cross
  13.1 0.0 collective-permute-start.6
  13.1 0.5 collective-permute-start.2
  14.2 0.6 %collective-permute-done.2.g_core = bf16[192,512]{1,0:T(8,128)(2,1)S(1)} collective-permute-done((bf16[192,512]{1,0:T(8,128)(2,1)S(1)}, bf16[192,512]{1,0:T(8,128)(2,1)S(1)}, u32[]{:S(2)}, u32[]{:S(2)}) %collective-permute-start.2) | collective-permute-done | bytes 196640 | tf_op jit(solution)/shard_map/ppermute | solution.py:370
  14.8 0.0 collective-permute-done.x_core
  14.8 0.0 collective-permute-done.1.k_core
  14.8 0.0 collective-permute-done.6.cross
  14.8 2.0 %prepare_kernel.1 = (bf16[1536,768]{1,0:T(8,128)(2,1)S(1)}, bf16[1536,768]{1,0:T(8,128)(2,1)S(1)}, bf16[768,512]{1,0:T(8,128)(2,1)S(1)}, f32[768,1]{1,0:T(8,128)...) custom-call(s32[1]{0:T(128)S(6)} %copy.15.sizes, ...), custom_call_target="tpu_custom_call" | custom-call | tf_op jit(solution)/shard_map/prepare_kernel/pallas_call | solution.py:339
  16.8 0.8 %collective-permute-done.9.far = f32[416,128]{1,0:T(8,128)S(1)} collective-permute-done((f32[416,128]{1,0:T(8,128)S(1)}, f32[416,128]{1,0:T(8,128)S(1)}, u32[]{:S(2)}, u32[]{:S(2)}) %collective-permute-start.9) | collective-permute-done | bytes 213024 | tf_op jit(solution)/shard_map/ppermute | solution.py:370
  17.6 1.7 %collective-permute-start.8 = (bf16[192,512]{1,0:T(8,128)(2,1)S(1)}, bf16[192,512]{1,0:T(8,128)(2,1)S(1)}, u32[]{:S(2)}, u32[]{:S(2)}) collective-permute-start(bf16[192,512]{1,0:T(8,128)(2,1)S(1)} %bitcast.8), channel_id=1, source_target_pairs={{0,2},{1,3},{2,0},{3,1},{4,6},{5,7},{6,4},{7,5},{8,10},{9,11},{10,... | collective-permute-start | bytes 589832 | tf_op jit(solution)/shard_map/ppermute | solution.py:370
  19.4 0.0 collective-permute-done.10.cross
  19.4 4.1 %global_kernel.1 = (f32[160,128]{1,0:T(8,128)S(1)}, f32[160,128]{1,0:T(8,128)S(1)}, f32[192,128]{1,0:T(8,128)S(1)}, f32[192,128]{1,0:T(8,128)S(1)}, f32[640,128]...) custom-call(f32[1,768]{1,0:T(1,128)S(1)} %get-tuple-element.63.live, ...), custom_call_target="tpu_custom_call", output_to_operand_aliasing={{5}: (4, {})} | custom-call | tf_op jit(solution)/shard_map/global_kernel/pallas_call | solution.py:339
  23.5 1.6 %collective-permute-start.12 = (f32[160,128]{1,0:T(8,128)S(1)}, f32[160,128]{1,0:T(8,128)S(1)}, u32[]{:S(2)}, u32[]{:S(2)}) collective-permute-start(f32[160,128]{1,0:T(8,128)S(1)} %get-tuple-element.71), channel_id=1, source_target_pairs={{0,8},{4,12},{8,0},{12,4},{16,24},{20,28},{24,16},{28,20},{1,9},{5... | collective-permute-start | bytes 245768 | tf_op jit(solution)/shard_map/ppermute | solution.py:373
  25.2 1.5 %collective-permute-start.13 = (f32[160,128]{1,0:T(8,128)S(1)}, f32[160,128]{1,0:T(8,128)S(1)}, u32[]{:S(2)}, u32[]{:S(2)}) collective-permute-start(f32[160,128]{1,0:T(8,128)S(1)} %get-tuple-element.74), channel_id=1, source_target_pairs={{0,4},{4,0},{8,12},{12,8},{16,20},{20,16},{24,28},{28,24},{1,5},{5... | collective-permute-start | bytes 245768 | tf_op jit(solution)/shard_map/ppermute | solution.py:373
  26.7 0.4 collective-permute-start.14
  27.1 1.5 %collective-permute-start.18 = (f32[640,128]{1,0:T(8,128)S(1)}, f32[640,128]{1,0:T(8,128)S(1)}, u32[]{:S(2)}, u32[]{:S(2)}) collective-permute-start(f32[640,128]{1,0:T(8,128)S(1)} %get-tuple-element.82), channel_id=1, source_target_pairs={{0,2},{1,3},{2,0},{3,1},{4,6},{5,7},{6,4},{7,5},{8,10},{9,11},{10,... | collective-permute-start | bytes 983048 | tf_op jit(solution)/shard_map/ppermute | solution.py:370
  28.5 0.0 collective-permute-done.8.p_far
  28.6 0.5 collective-permute-start.11
  29.1 1.3 %collective-permute-done.13 = f32[160,128]{1,0:T(8,128)S(1)} collective-permute-done((f32[160,128]{1,0:T(8,128)S(1)}, f32[160,128]{1,0:T(8,128)S(1)}, u32[]{:S(2)}, u32[]{:S(2)}) %collective-permute-start.13) | collective-permute-done | bytes 81952 | tf_op jit(solution)/shard_map/ppermute | solution.py:373
  30.4 1.6 %collective-permute-done.14 = f32[160,128]{1,0:T(8,128)S(1)} collective-permute-done((f32[160,128]{1,0:T(8,128)S(1)}, f32[160,128]{1,0:T(8,128)S(1)}, u32[]{:S(2)}, u32[]{:S(2)}) %collective-permute-start.14) | collective-permute-done | bytes 81952 | tf_op jit(solution)/shard_map/ppermute | solution.py:373
  32.0 2.6 %collective-permute-start.16 = (f32[160,128]{1,0:T(8,128)S(1)}, f32[160,128]{1,0:T(8,128)S(1)}, u32[]{:S(2)}, u32[]{:S(2)}) collective-permute-start(f32[160,128]{1,0:T(8,128)S(1)} %add_add_fusion), channel_id=1, source_target_pairs={{0,16},{4,20},{8,24},{12,28},{16,0},{20,4},{24,8},{28,12},{1,17},{... | collective-permute-start | bytes 245768 | tf_op jit(solution)/shard_map/ppermute | solution.py:373
  34.7 5.6 %pair_kernel.1 = (f32[64,768]{1,0:T(8,128)S(1)}, f32[64,256]{1,0:T(8,128)}, f32[64,768]{1,0:T(8,128)S(1)}) custom-call(f32[768,1]{1,0:T(8,128)S(1)} %get-tuple-element.60.live, bf16[192,512]{1,0:T(8,128)(2,1)S(1)} %bitcast.10, bf16[192,512]{1,0:T(8,128)(2,1)S(1)} %collective-permute-done.7.p_core, bf16[192,512]{1,0:T(8,128)(2,1)S(1)} %collective-permute-done.8.p_far, ...), custom_call_target="tpu_custom_call" | custom-call | tf_op jit(solution)/shard_map/pair_kernel/pallas_call | solution.py:339
  40.3 0.1 collective-permute-start.19
  40.4 0.5 collective-permute-start.15
  40.9 1.8 %collective-permute-start.25 = (f32[160,128]{1,0:T(8,128)S(1)}, f32[160,128]{1,0:T(8,128)S(1)}, u32[]{:S(2)}, u32[]{:S(2)}) collective-permute-start(f32[160,128]{1,0:T(8,128)S(1)} %add.15.refs_0_), channel_id=1, source_target_pairs={{0,6},{1,7},{2,4},{3,5},{4,2},{5,3},{6,0},{7,1},{8,14},{9,15},{10,... | collective-permute-start | bytes 245768 | tf_op jit(solution)/shard_map/ppermute | solution.py:379
  42.6 0.6 %collective-permute-start.24 = (f32[160,128]{1,0:T(8,128)S(1)}, f32[160,128]{1,0:T(8,128)S(1)}, u32[]{:S(2)}, u32[]{:S(2)}) collective-permute-start(f32[160,128]{1,0:T(8,128)S(1)} %add.15.refs_0_), channel_id=1, source_target_pairs={{0,2},{1,3},{2,0},{3,1},{4,6},{5,7},{6,4},{7,5},{8,10},{9,11},{10,... | collective-permute-start | bytes 245768 | tf_op jit(solution)/shard_map/ppermute | solution.py:370
  43.2 1.2 %collective-permute-start.21 = (f32[160,128]{1,0:T(8,128)S(1)}, f32[160,128]{1,0:T(8,128)S(1)}, u32[]{:S(2)}, u32[]{:S(2)}) collective-permute-start(f32[160,128]{1,0:T(8,128)S(1)} %add.15.refs_0_), channel_id=1, source_target_pairs={{0,4},{4,0},{8,12},{12,8},{16,20},{20,16},{24,28},{28,24},{1,5},{5... | collective-permute-start | bytes 245768 | tf_op jit(solution)/shard_map/ppermute | solution.py:373
  44.4 0.9 %start_kernel.1 = (bf16[512,1024]{1,0:T(8,128)(2,1)S(1)}, f32[192,512]{1,0:T(8,128)S(1)}) custom-call(f32[128,512]{1,0:T(8,128)S(1)} %copy-done, f32[128,512]{1,0:T(8,128)S(1)} %collective-permute-done.15.s_core, f32[192,128]{1,0:T(8,128)S(1)} %get-tuple-element.83.y_own, f32[192,128]{1,0:T(8,128)S(1)} %collective-permute-done.17.y_core, ...), custom_call_target="tpu_custom_call" | custom-call | tf_op jit(solution)/shard_map/start_kernel/pallas_call | solution.py:339
  45.2 2.2 %collective-permute-start.20 = (f32[64,768]{1,0:T(8,128)S(1)}, f32[64,768]{1,0:T(8,128)S(1)}, u32[]{:S(2)}, u32[]{:S(2)}) collective-permute-start(f32[64,768]{1,0:T(8,128)S(1)} %get-tuple-element.89), channel_id=1, source_target_pairs={{0,28},{4,0},{8,4},{12,8},{16,12},{20,16},{24,20},{28,24},{1,29},{... | collective-permute-start | bytes 589832 | tf_op jit(solution)/shard_map/ppermute | solution.py:457
  47.4 0.5 collective-permute-start.27
  47.9 0.0 collective-permute-done.24.refs_4_
  47.9 0.1 collective-permute-start.26
  48.0 0.8 %collective-permute-done.21.refs_1_ = f32[160,128]{1,0:T(8,128)S(1)} collective-permute-done((f32[160,128]{1,0:T(8,128)S(1)}, f32[160,128]{1,0:T(8,128)S(1)}, u32[]{:S(2)}, u32[]{:S(2)}) %collective-permute-start.21) | collective-permute-done | bytes 81952 | tf_op jit(solution)/shard_map/ppermute | solution.py:373
  48.8 0.1 collective-permute-done.27.refs_7_
  48.9 0.4 collective-permute-done.26.refs_6_
  49.2 0.8 %collective-permute-done.23.refs_3_ = f32[160,128]{1,0:T(8,128)S(1)} collective-permute-done((f32[160,128]{1,0:T(8,128)S(1)}, f32[160,128]{1,0:T(8,128)S(1)}, u32[]{:S(2)}, u32[]{:S(2)}) %collective-permute-start.23) | collective-permute-done | bytes 81952 | tf_op jit(solution)/shard_map/ppermute | solution.py:370
  50.1 1.9 %back_kernel.1 = (f32[128,512]{1,0:T(8,128)}, f32[192,512]{1,0:T(8,128)}) custom-call(f32[160,128]{1,0:T(8,128)S(1)} %add.15.refs_0_, f32[160,128]{1,0:T(8,128)S(1)} %collective-permute-done.21.refs_1_, f32[160,128]{1,0:T(8,128)S(1)} %collective-permute-done.22.refs_2_, f32[160,128]{1,0:T(8,128)S(1)} %collective-permute-done.23.refs_3_, ...), custom_call_target="tpu_custom_call" | custom-call | flops 452984832 | tf_op jit(solution)/shard_map/back_kernel/pallas_call | solution.py:339
  52.0 0.2 collective-permute-done.20.came
  52.2 0.7 %finish_kernel.1 = (f32[64,256]{1,0:T(8,128)}, f32[64,512]{1,0:T(8,128)}) custom-call(f32[64,768]{1,0:T(8,128)S(1)} %get-tuple-element.76.own_terms, f32[64,768]{1,0:T(8,128)S(1)} %collective-permute-done.20.came), custom_call_target="tpu_custom_call" | custom-call | tf_op jit(solution)/shard_map/finish_kernel/pallas_call | solution.py:339
  (23 shorter events, 0.1 us)
Async XLA Ops:
  0.6 8.7 %collective-permute-start.3 = (bf16[192,512]{1,0:T(8,128)(2,1)}, bf16[192,512]{1,0:T(8,128)(2,1)S(1)}, u32[]{:S(2)}, u32[]{:S(2)}) collective-permute-start(bf16[192,512]{1,0:T(8,128)(2,1)} %bitcast.13), channel_id=1, source_target_pairs={{0,2},{1,3},{2,0},{3,1},{4,6},{5,7},{6,4},{7,5},{8,10},{9,11},{10,... | collective-permute-start | bytes 589832 | tf_op jit(solution)/shard_map/ppermute | solution.py:370
  3.7 14.0 %copy-start.2 = (bf16[1,192,512]{2,1,0:T(8,128)(2,1)S(1)}, bf16[1,192,512]{2,1,0:T(8,128)(2,1)}, u32[]{:S(2)}) copy-start(bf16[1,192,512]{2,1,0:T(8,128)(2,1)} %param.12) | copy-start | bytes 589828
  3.7 15.7 %copy-start.1 = (f32[128,512]{1,0:T(8,128)S(1)}, f32[128,512]{1,0:T(8,128)}, u32[]{:S(2)}) copy-start(f32[128,512]{1,0:T(8,128)} %base.1) | copy-start | bytes 786436
  5.1 9.7 %collective-permute-start = (f32[192,768]{1,0:T(8,128)S(1)}, f32[192,768]{1,0:T(8,128)S(1)}, u32[]{:S(2)}, u32[]{:S(2)}) collective-permute-start(f32[192,768]{1,0:T(8,128)S(1)} %get-tuple-element.52.x_own), channel_id=1, source_target_pairs={{0,1},{1,0},{2,3},{3,2},{4,5},{5,4},{6,7},{7,6},{8,9},{9,8},{10,11... | collective-permute-start | bytes 1769480 | tf_op jit(solution)/shard_map/ppermute | solution.py:370
  5.2 9.6 %collective-permute-start.1 = (f32[192,768]{1,0:T(8,128)S(1)}, f32[192,768]{1,0:T(8,128)S(1)}, u32[]{:S(2)}, u32[]{:S(2)}) collective-permute-start(f32[192,768]{1,0:T(8,128)S(1)} %get-tuple-element.53.k_own), channel_id=1, source_target_pairs={{0,1},{1,0},{2,3},{3,2},{4,5},{5,4},{6,7},{7,6},{8,9},{9,8},{10,11... | collective-permute-start | bytes 1769480 | tf_op jit(solution)/shard_map/ppermute | solution.py:370
  5.7 7.4 %collective-permute-start.4 = (f32[392,128]{1,0:T(8,128)S(1)}, f32[392,128]{1,0:T(8,128)S(1)}, u32[]{:S(2)}, u32[]{:S(2)}) collective-permute-start(f32[392,128]{1,0:T(8,128)S(1)} %get-tuple-element.55), channel_id=1, source_target_pairs={{0,2},{1,3},{2,0},{3,1},{4,6},{5,7},{6,4},{7,5},{8,10},{9,11},{10,... | collective-permute-start | bytes 602120 | tf_op jit(solution)/shard_map/ppermute | solution.py:370
  9.3 3.8 %collective-permute-start.5 = (bf16[192,512]{1,0:T(8,128)(2,1)S(1)}, bf16[192,512]{1,0:T(8,128)(2,1)S(1)}, u32[]{:S(2)}, u32[]{:S(2)}) collective-permute-start(bf16[192,512]{1,0:T(8,128)(2,1)S(1)} %collective-permute-done.3.g_far), channel_id=1, source_target_pairs={{0,1},{1,0},{2,3},{3,2},{4,5},{5,4},{6,7},{7,6},{8,9},{9,8},{10,11... | collective-permute-start | bytes 589832 | tf_op jit(solution)/shard_map/ppermute | solution.py:370
  9.3 8.4 %collective-permute-start.9 = (f32[416,128]{1,0:T(8,128)S(1)}, f32[416,128]{1,0:T(8,128)S(1)}, u32[]{:S(2)}, u32[]{:S(2)}) collective-permute-start(f32[416,128]{1,0:T(8,128)S(1)} %get-tuple-element.64), channel_id=1, source_target_pairs={{0,2},{1,3},{2,0},{3,1},{4,6},{5,7},{6,4},{7,5},{8,10},{9,11},{10,... | collective-permute-start | bytes 638984 | tf_op jit(solution)/shard_map/ppermute | solution.py:370
  13.1 1.7 %collective-permute-start.6 = (f32[392,128]{1,0:T(8,128)S(1)}, f32[392,128]{1,0:T(8,128)S(1)}, u32[]{:S(2)}, u32[]{:S(2)}) collective-permute-start(f32[392,128]{1,0:T(8,128)S(1)} %collective-permute-done.4.far), channel_id=1, source_target_pairs={{0,1},{1,0},{2,3},{3,2},{4,5},{5,4},{6,7},{7,6},{8,9},{9,8},{10,11... | collective-permute-start | bytes 602120 | tf_op jit(solution)/shard_map/ppermute | solution.py:370
  13.1 1.7 %collective-permute-start.2 = (bf16[192,512]{1,0:T(8,128)(2,1)S(1)}, bf16[192,512]{1,0:T(8,128)(2,1)S(1)}, u32[]{:S(2)}, u32[]{:S(2)}) collective-permute-start(bf16[192,512]{1,0:T(8,128)(2,1)S(1)} %get-tuple-element.54.g_own), channel_id=1, source_target_pairs={{0,1},{1,0},{2,3},{3,2},{4,5},{5,4},{6,7},{7,6},{8,9},{9,8},{10,11... | collective-permute-start | bytes 589832 | tf_op jit(solution)/shard_map/ppermute | solution.py:370
  17.6 1.8 %collective-permute-start.10 = (f32[416,128]{1,0:T(8,128)S(1)}, f32[416,128]{1,0:T(8,128)S(1)}, u32[]{:S(2)}, u32[]{:S(2)}) collective-permute-start(f32[416,128]{1,0:T(8,128)S(1)} %collective-permute-done.9.far), channel_id=1, source_target_pairs={{0,1},{1,0},{2,3},{3,2},{4,5},{5,4},{6,7},{7,6},{8,9},{9,8},{10,11... | collective-permute-start | bytes 638984 | tf_op jit(solution)/shard_map/ppermute | solution.py:370
  17.6 10.9 %collective-permute-start.8 = (bf16[192,512]{1,0:T(8,128)(2,1)S(1)}, bf16[192,512]{1,0:T(8,128)(2,1)S(1)}, u32[]{:S(2)}, u32[]{:S(2)}) collective-permute-start(bf16[192,512]{1,0:T(8,128)(2,1)S(1)} %bitcast.8), channel_id=1, source_target_pairs={{0,2},{1,3},{2,0},{3,1},{4,6},{5,7},{6,4},{7,5},{8,10},{9,11},{10,... | collective-permute-start | bytes 589832 | tf_op jit(solution)/shard_map/ppermute | solution.py:370
  23.5 5.0 %collective-permute-start.12 = (f32[160,128]{1,0:T(8,128)S(1)}, f32[160,128]{1,0:T(8,128)S(1)}, u32[]{:S(2)}, u32[]{:S(2)}) collective-permute-start(f32[160,128]{1,0:T(8,128)S(1)} %get-tuple-element.71), channel_id=1, source_target_pairs={{0,8},{4,12},{8,0},{12,4},{16,24},{20,28},{24,16},{28,20},{1,9},{5... | collective-permute-start | bytes 245768 | tf_op jit(solution)/shard_map/ppermute | solution.py:373
  25.2 5.2 %collective-permute-start.13 = (f32[160,128]{1,0:T(8,128)S(1)}, f32[160,128]{1,0:T(8,128)S(1)}, u32[]{:S(2)}, u32[]{:S(2)}) collective-permute-start(f32[160,128]{1,0:T(8,128)S(1)} %get-tuple-element.74), channel_id=1, source_target_pairs={{0,4},{4,0},{8,12},{12,8},{16,20},{20,16},{24,28},{28,24},{1,5},{5... | collective-permute-start | bytes 245768 | tf_op jit(solution)/shard_map/ppermute | solution.py:373
  26.7 5.3 %collective-permute-start.14 = (f32[160,128]{1,0:T(8,128)S(1)}, f32[160,128]{1,0:T(8,128)S(1)}, u32[]{:S(2)}, u32[]{:S(2)}) collective-permute-start(f32[160,128]{1,0:T(8,128)S(1)} %get-tuple-element.74), channel_id=1, source_target_pairs={{0,12},{4,8},{8,4},{12,0},{16,28},{20,24},{24,20},{28,16},{1,13},{... | collective-permute-start | bytes 245768 | tf_op jit(solution)/shard_map/ppermute | solution.py:373
  27.1 13.2 %collective-permute-start.18 = (f32[640,128]{1,0:T(8,128)S(1)}, f32[640,128]{1,0:T(8,128)S(1)}, u32[]{:S(2)}, u32[]{:S(2)}) collective-permute-start(f32[640,128]{1,0:T(8,128)S(1)} %get-tuple-element.82), channel_id=1, source_target_pairs={{0,2},{1,3},{2,0},{3,1},{4,6},{5,7},{6,4},{7,5},{8,10},{9,11},{10,... | collective-permute-start | bytes 983048 | tf_op jit(solution)/shard_map/ppermute | solution.py:370
  28.5 6.1 %collective-permute-start.7 = (bf16[192,512]{1,0:T(8,128)(2,1)S(1)}, bf16[192,512]{1,0:T(8,128)(2,1)S(1)}, u32[]{:S(2)}, u32[]{:S(2)}) collective-permute-start(bf16[192,512]{1,0:T(8,128)(2,1)S(1)} %bitcast.9), channel_id=1, source_target_pairs={{0,1},{1,0},{2,3},{3,2},{4,5},{5,4},{6,7},{7,6},{8,9},{9,8},{10,11... | collective-permute-start | bytes 589832 | tf_op jit(solution)/shard_map/ppermute | solution.py:370
  28.6 6.1 %collective-permute-start.11 = (bf16[192,512]{1,0:T(8,128)(2,1)S(1)}, bf16[192,512]{1,0:T(8,128)(2,1)S(1)}, u32[]{:S(2)}, u32[]{:S(2)}) collective-permute-start(bf16[192,512]{1,0:T(8,128)(2,1)S(1)} %collective-permute-done.8.p_far), channel_id=1, source_target_pairs={{0,1},{1,0},{2,3},{3,2},{4,5},{5,4},{6,7},{7,6},{8,9},{9,8},{10,11... | collective-permute-start | bytes 589832 | tf_op jit(solution)/shard_map/ppermute | solution.py:370
  30.4 9.8 %collective-permute-start.17 = (f32[192,128]{1,0:T(8,128)S(1)}, f32[192,128]{1,0:T(8,128)S(1)}, u32[]{:S(2)}, u32[]{:S(2)}) collective-permute-start(f32[192,128]{1,0:T(8,128)S(1)} %get-tuple-element.81), channel_id=1, source_target_pairs={{0,1},{1,0},{2,3},{3,2},{4,5},{5,4},{6,7},{7,6},{8,9},{9,8},{10,11... | collective-permute-start | bytes 294920 | tf_op jit(solution)/shard_map/ppermute | solution.py:370
  32.0 8.2 %collective-permute-start.16 = (f32[160,128]{1,0:T(8,128)S(1)}, f32[160,128]{1,0:T(8,128)S(1)}, u32[]{:S(2)}, u32[]{:S(2)}) collective-permute-start(f32[160,128]{1,0:T(8,128)S(1)} %add_add_fusion), channel_id=1, source_target_pairs={{0,16},{4,20},{8,24},{12,28},{16,0},{20,4},{24,8},{28,12},{1,17},{... | collective-permute-start | bytes 245768 | tf_op jit(solution)/shard_map/ppermute | solution.py:373
  34.7 5.7 %copy-start = (f32[128,512]{1,0:T(8,128)S(1)}, f32[128,512]{1,0:T(8,128)}, u32[]{:S(2)}) copy-start(f32[128,512]{1,0:T(8,128)} %s_own.1) | copy-start | bytes 786436
  40.3 4.1 %collective-permute-start.19 = (f32[640,128]{1,0:T(8,128)S(1)}, f32[640,128]{1,0:T(8,128)S(1)}, u32[]{:S(2)}, u32[]{:S(2)}) collective-permute-start(f32[640,128]{1,0:T(8,128)S(1)} %collective-permute-done.18.far), channel_id=1, source_target_pairs={{0,1},{1,0},{2,3},{3,2},{4,5},{5,4},{6,7},{7,6},{8,9},{9,8},{10,11... | collective-permute-start | bytes 983048 | tf_op jit(solution)/shard_map/ppermute | solution.py:370
  40.4 4.0 %collective-permute-start.15 = (f32[128,512]{1,0:T(8,128)S(1)}, f32[128,512]{1,0:T(8,128)S(1)}, u32[]{:S(2)}, u32[]{:S(2)}) collective-permute-start(f32[128,512]{1,0:T(8,128)S(1)} %copy-done), channel_id=1, source_target_pairs={{0,1},{1,0},{2,3},{3,2},{4,5},{5,4},{6,7},{7,6},{8,9},{9,8},{10,11... | collective-permute-start | bytes 786440 | tf_op jit(solution)/shard_map/ppermute | solution.py:370
  40.9 6.6 %collective-permute-start.25 = (f32[160,128]{1,0:T(8,128)S(1)}, f32[160,128]{1,0:T(8,128)S(1)}, u32[]{:S(2)}, u32[]{:S(2)}) collective-permute-start(f32[160,128]{1,0:T(8,128)S(1)} %add.15.refs_0_), channel_id=1, source_target_pairs={{0,6},{1,7},{2,4},{3,5},{4,2},{5,3},{6,0},{7,1},{8,14},{9,15},{10,... | collective-permute-start | bytes 245768 | tf_op jit(solution)/shard_map/ppermute | solution.py:379
  42.6 5.3 %collective-permute-start.24 = (f32[160,128]{1,0:T(8,128)S(1)}, f32[160,128]{1,0:T(8,128)S(1)}, u32[]{:S(2)}, u32[]{:S(2)}) collective-permute-start(f32[160,128]{1,0:T(8,128)S(1)} %add.15.refs_0_), channel_id=1, source_target_pairs={{0,2},{1,3},{2,0},{3,1},{4,6},{5,7},{6,4},{7,5},{8,10},{9,11},{10,... | collective-permute-start | bytes 245768 | tf_op jit(solution)/shard_map/ppermute | solution.py:370
  43.2 5.6 %collective-permute-start.21 = (f32[160,128]{1,0:T(8,128)S(1)}, f32[160,128]{1,0:T(8,128)S(1)}, u32[]{:S(2)}, u32[]{:S(2)}) collective-permute-start(f32[160,128]{1,0:T(8,128)S(1)} %add.15.refs_0_), channel_id=1, source_target_pairs={{0,4},{4,0},{8,12},{12,8},{16,20},{20,16},{24,28},{28,24},{1,5},{5... | collective-permute-start | bytes 245768 | tf_op jit(solution)/shard_map/ppermute | solution.py:373
  45.2 6.9 %collective-permute-start.20 = (f32[64,768]{1,0:T(8,128)S(1)}, f32[64,768]{1,0:T(8,128)S(1)}, u32[]{:S(2)}, u32[]{:S(2)}) collective-permute-start(f32[64,768]{1,0:T(8,128)S(1)} %get-tuple-element.89), channel_id=1, source_target_pairs={{0,28},{4,0},{8,4},{12,8},{16,12},{20,16},{24,20},{28,24},{1,29},{... | collective-permute-start | bytes 589832 | tf_op jit(solution)/shard_map/ppermute | solution.py:457
  47.4 1.4 %collective-permute-start.22 = (f32[160,128]{1,0:T(8,128)S(1)}, f32[160,128]{1,0:T(8,128)S(1)}, u32[]{:S(2)}, u32[]{:S(2)}) collective-permute-start(f32[160,128]{1,0:T(8,128)S(1)} %add.15.refs_0_), channel_id=1, source_target_pairs={{0,1},{1,0},{2,3},{3,2},{4,5},{5,4},{6,7},{7,6},{8,9},{9,8},{10,11... | collective-permute-start | bytes 245768 | tf_op jit(solution)/shard_map/ppermute | solution.py:370
  47.4 1.4 %collective-permute-start.27 = (f32[160,128]{1,0:T(8,128)S(1)}, f32[160,128]{1,0:T(8,128)S(1)}, u32[]{:S(2)}, u32[]{:S(2)}) collective-permute-start(f32[160,128]{1,0:T(8,128)S(1)} %collective-permute-done.25.refs_5_), channel_id=1, source_target_pairs={{0,1},{1,0},{2,3},{3,2},{4,5},{5,4},{6,7},{7,6},{8,9},{9,8},{10,11... | collective-permute-start | bytes 245768 | tf_op jit(solution)/shard_map/ppermute | solution.py:370
  47.9 1.3 %collective-permute-start.26 = (f32[160,128]{1,0:T(8,128)S(1)}, f32[160,128]{1,0:T(8,128)S(1)}, u32[]{:S(2)}, u32[]{:S(2)}) collective-permute-start(f32[160,128]{1,0:T(8,128)S(1)} %collective-permute-done.24.refs_4_), channel_id=1, source_target_pairs={{0,1},{1,0},{2,3},{3,2},{4,5},{5,4},{6,7},{7,6},{8,9},{9,8},{10,11... | collective-permute-start | bytes 245768 | tf_op jit(solution)/shard_map/ppermute | solution.py:370
  48.8 1.3 %collective-permute-start.23 = (f32[160,128]{1,0:T(8,128)S(1)}, f32[160,128]{1,0:T(8,128)S(1)}, u32[]{:S(2)}, u32[]{:S(2)}) collective-permute-start(f32[160,128]{1,0:T(8,128)S(1)} %collective-permute-done.21.refs_1_), channel_id=1, source_target_pairs={{0,1},{1,0},{2,3},{3,2},{4,5},{5,4},{6,7},{7,6},{8,9},{9,8},{10,11... | collective-permute-start | bytes 245768 | tf_op jit(solution)/shard_map/ppermute | solution.py:370

commit v7 on v6

--- a/solution.py
+++ b/solution.py
@@ -73,8 +73,8 @@
         (g_rows, g_own),
         (index, index_out),
         *[
-            (s_rows.at[:, at((2 * near + i) * group, group, 128)], s_out.at[first : first + group, :])
-            for i, first in enumerate(range(0, s_out.shape[0], group))
+            (s_rows.at[:, first : first + group], s_out.at[first : first + group, :])
+            for first in range(0, s_out.shape[0], group)
         ],
         sems=sems,
     )
@@ -190,7 +190,7 @@
 
 
 def global_kernel(
-    live, far, cross, x, k_in, links, columns, first, base, s_sent,
+    live, far, cross, x, k_in, links, columns, first, base, s_own,
     keep, send, y_own, y_core, y_far, k, pack, solved,
 ):
     del k_in
@@ -198,7 +198,7 @@
     half = order // 2
     rows = half // 2
     group = width // 4
-    part, _, core = place()
+    part, near, core = place()
     block = lax.axis_index("tm")
     corner(far, cross, k, live)
     value = 2.0 * columns[...] - times(first[...], k)
@@ -208,10 +208,11 @@
     left_side = stacked(result)
     solved[...] = result.T
     y_own[...] = solved[at(core * rows, rows), :]
-    y_core[...] = solved[at((1 - core) * rows, rows), :]
+    y_core[:rows, :] = solved[at((1 - core) * rows, rows), :]
+    y_core[rows:, :] = s_own[...]
     y_far[:rows, :] = solved[at(half + core * rows, rows), :]
     y_far[rows : 2 * rows, :] = solved[at(half + (1 - core) * rows, rows), :]
-    y_far[2 * rows :, :] = s_sent[...]
+    y_far[2 * rows :, :] = s_own[at(2 * near * group, 2 * group, 8), :]
 
     def square(shift):
         cols = at(((part + shift) % 4) * group, group, 128)
@@ -232,10 +233,11 @@
 
 
 def pair_kernel(
-    live, p_own, p_core, p_far, p_cross, x, k, links, own_terms, off_terms, next_terms, gathered
+    live, p_own, p_core, p_far, p_cross, x, k, links,
+    own_terms, off_terms, next_terms, gathered,
 ):
     half = x.shape[1] // 2
-    width = p_own.shape[1]
+    rows, width = p_far.shape
     link = width // 2
     share = link // 4
     put_rows(p_own, p_core, gathered)
@@ -261,13 +263,13 @@
 
 
 def start_kernel(
-    s_own, s_core, y_own, y_core, far, cross, start, scaled, s_rows, y_rows
+    s_own, y_own, y_core, far, cross, own_terms, came,
+    start, scaled, link_diag, link_cross, s_rows, y_rows,
 ):
-    group, width = s_own.shape
+    rows, group = y_own.shape
+    width = s_rows.shape[1]
     half = width // 2
-    rows = y_own.shape[0]
     part, near, core = place()
-    put_rows(s_own, s_core, s_rows)
     top, bottom = at(near * half, half), at((1 - near) * half, half)
     left, right = at(near * half, half, 128), at((1 - near) * half, half, 128)
     low_left, low_right = (at(width + v * half, half, 128) for v in (near, 1 - near))
@@ -275,58 +277,79 @@
     def put(rows, cols, low_cols, value):
         start[rows, cols], start[rows, low_cols] = halves(value)
 
+    for i in range(width // group):
+        first, cols = i * group, slice(i * group, (i + 1) * group)
+        put_rows(
+            s_own.at[first : first + group, :],
+            y_core.at[rows + first : rows + first + group, :],
+            s_rows.at[:, cols],
+        )
     put(top, left, low_left, s_rows[:, left])
     side = s_rows[:, right]
     put(top, right, low_right, side)
     put(bottom, left, low_left, side.T)
-    for i in range(2):
+    for i in range(half // group):
         first = slice(2 * rows + i * group, 2 * rows + (i + 1) * group)
         put_rows(far.at[first, :], cross.at[first, :], s_rows.at[:, i * group : (i + 1) * group])
     put(bottom, right, low_right, s_rows[:, :half])
     for ref, mask in ((y_own, 0), (y_core, 1), (far, 2), (cross.at[rows:, :], 3)):
         y_rows[:, at((part ^ mask) * group, group, 128)] = ref[:rows, :]
     scaled[...] = times_wide(y_rows[...], start)
-
-
-def back_kernel(*refs):
-    sums, (start, scaled, schur, back, whole, full, full_parts) = refs[:8], refs[8:]
-    part = place()[0]
-    side = lax.axis_index("tm") % 2
-    size = sums[0].shape[0]
-    group = schur.shape[0]
-    for mask in range(4):
-        for half in range(2):
-            rows = at((part ^ mask) * (2 * size) + (side ^ half) * size, size, 8)
-            whole[rows, :] = sums[2 * mask + half][...]
-
-    def put(row, col, value):
-        full[row * group : (row + 1) * group, col * group : (col + 1) * group] = value
-
-    for row in range(4):
-        first = row * 2 * size
-        put(row, row, whole[first : first + group, :])
-        after_it = whole[first + group : first + 2 * group, :]
-        put(row, (row + 1) % 4, after_it)
-        put((row + 1) % 4, row, after_it.T)
-        if row < 2:
-            other = (row + 2) * 2 * size
-            across = jnp.concatenate(
-                [whole[first + 2 * group : first + 2 * size, :],
-                 whole[other + 2 * group : other + 2 * size, :]], axis=0
-            )
-            put(row, row + 2, across)
-            put(row + 2, row, across.T)
-    schur[...] = full[at(part * group, group, 8), :]
-    full_parts[...] = both(full[...])
-    value = scaled[...]
-    back[...] = 2.0 * value - times_wide(times_wide(value, full_parts), start)
-
-
-def finish_kernel(own_terms, came, link_diag, link_cross):
     link = link_diag.shape[1]
     there = lax.axis_index("tm") + 1 < lax.axis_size("tm")
     link_diag[...] = own_terms[:, :link] + jnp.where(there, came[:, :link], 0.0)
     link_cross[...] = own_terms[:, link:] + jnp.where(there, came[:, link:], 0.0)
+
+
+def sum_kernel(mine, came, total):
+    total[...] = mine[...] + came[...]
+
+
+def back_kernel(*refs):
+    sums, (start, scaled, schur, back, whole, parts) = refs[:8], refs[8:]
+    part = place()[0]
+    side = lax.axis_index("tm") % 2
+    size = sums[0].shape[0]
+    group, width = schur.shape
+    span = 2 * size
+    for mask in range(4):
+        for half in range(2):
+            rows = at((part ^ mask) * span + (side ^ half) * size, size, 8)
+            whole[rows, :] = sums[2 * mask + half][...]
+
+    def put(row, col, value):
+        rows = slice(row * group, (row + 1) * group)
+        high, low = halves(value)
+        parts[rows, col * group : (col + 1) * group] = high
+        parts[rows, width + col * group : width + (col + 1) * group] = low
+
+    def across(row):
+        first, other = row * span + 2 * group, (row + 2) * span + 2 * group
+        return jnp.concatenate(
+            [whole[at(first, group // 2, 8), :], whole[at(other, group // 2, 8), :]], axis=0
+        )
+
+    for row in range(4):
+        first = row * span
+        put(row, row, whole[first : first + group, :])
+        value = whole[first + group : first + 2 * group, :]
+        put(row, (row + 1) % 4, value)
+        put((row + 1) % 4, row, value.T)
+        if row < 2:
+            value = across(row)
+            put(row, row + 2, value)
+            put(row + 2, row, value.T)
+    before = (part + 3) % 4
+    value = across(part % 2)
+    for col, value in (
+        (part, whole[at(part * span, group, 8), :]),
+        ((part + 1) % 4, whole[at(part * span + group, group, 8), :]),
+        ((part + 2) % 4, jnp.where(part < 2, value, value.T)),
+        (before, whole[at(before * span + group, group, 8), :].T),
+    ):
+        schur[:, at(col * group, group, 128)] = value
+    value = scaled[...]
+    back[...] = 2.0 * value - times_wide(times_wide(value, parts), start)
 
 
 def call(kernel, outs, scratch, *args, sizes=None, whole=False, alias={}, flops=0):
@@ -381,12 +404,12 @@
     vmem, matrix = pltpu.VMEM, ((2 * order, order), BF16)
 
     g_far = tile_swap(glob, 2)
-    x_sent, k_sent, x_own, k_own, g_own, s_sent, index = call(
+    x_sent, k_sent, x_own, k_own, g_own, s_own, index = call(
         pack_kernel,
-        [((3 * unit + SPARE, unit), F32), ((3 * unit + 4 * SPARE, unit), F32),
-         ((rows, order), F32), ((rows, order), F32), ((rows, width), BF16), ((2 * group, group), F32),
-         (link_index.shape, jnp.int32)],
-        [pltpu.SemaphoreType.DMA((6,))],
+        [((3 * unit + SPARE, unit), F32), ((3 * unit + 2 * SPARE, unit), F32),
+         ((rows, order), F32), ((rows, order), F32), ((rows, width), BF16),
+         ((width, group), F32), (link_index.shape, jnp.int32)],
+        [pltpu.SemaphoreType.DMA((8,))],
         initial, operator, glob, schur_start, link_index, whole=True,
     )
     x_far, k_far = tile_swap(x_sent, 2), tile_swap(k_sent, 2)
@@ -398,47 +421,50 @@
         [matrix, matrix, ((order, width), BF16), ((order, 1), F32), ((1, order), F32),
          ((group, order), F32), ((group, order), F32)],
         [vmem((half, order), F32), vmem((order, width), BF16)],
-        x_own, k_own, tile_swap(x_own, 1), tile_swap(k_own, 1), g_own, tile_swap(g_own, 1), g_far, g_cross, index,
+        x_own, k_own, tile_swap(x_own, 1), tile_swap(k_own, 1), g_own, tile_swap(g_own, 1),
+        g_far, g_cross, index,
         x_far, tile_swap(x_far, 1), sizes=block_sizes,
     )
     k_far = after(k_far, first)
-    p_core, p_far, s_core = (
-        tile_swap(after(v, first), m) for v, m in ((pair, 1), (pair, 2), (schur_start, 1))
-    )
+    p_core, p_far = (tile_swap(after(pair, first), m) for m in (1, 2))
     keep, send, y_own, y_core, y_far, k = call(
         global_kernel,
-        [((size, group), F32)] * 2 + [((rows, group), F32)] * 2
+        [((size, group), F32)] * 2 + [((rows, group), F32), ((rows + width, group), F32)]
         + [((2 * rows + 2 * group, group), F32), matrix],
         [vmem((2 * size, group), F32), vmem((order, group), F32)],
-        live_cols, k_far, tile_swap(k_far, 1), x, k, links, columns, first, schur_base, s_sent,
+        live_cols, k_far, tile_swap(k_far, 1), x, k, links, columns, first, schur_base, s_own,
         alias={4: 5},
     )
 
     y_all = (y_own, tile_swap(y_core, 1), tile_swap(y_far, 2))
-    if blocks > 2:
-        parts = [block_swap(send, 1), block_swap(keep, 2), block_swap(send, 3)]
-        total = (keep + parts[1]) + (parts[0] + parts[2])
-    else:
-        total = keep + block_swap(send, 1)
     p_far = after(p_far, keep)
     own_terms, off_terms, next_terms = call(
         pair_kernel,
         [((share, link + width), F32), ((share, link), F32), ((share, link + width), F32)],
         [vmem((order, 2 * link), BF16)],
-        live_rows, pair, p_core, p_far, tile_swap(p_far, 1), x, k, after(links, total),
-    )
+        live_rows, pair, p_core, p_far, tile_swap(p_far, 1), x, k, links,
+    )
+    came = lax.ppermute(next_terms, "tm", [(i, (i - 1) % blocks) for i in range(blocks)])
+    parts = [block_swap(send, 1)]
+    if blocks > 2:
+        parts += [block_swap(keep, 2), block_swap(send, 3)]
+        *parts, off_terms = lax.optimization_barrier((*parts, off_terms))
+        total = (keep + parts[1]) + (parts[0] + parts[2])
+    else:
+        total = keep + parts[0]
     step = 4
     while step < blocks:
-        other = block_swap(total, step)
-        if step == 4:
-            other, off_terms, *y_all = lax.optimization_barrier((other, off_terms, *y_all))
-        total = total + other
+        total = call(
+            sum_kernel, [(total.shape, F32)], [], total, block_swap(total, step),
+            flops=32 * rows * order * order,
+        )[0]
         step *= 2
-    start, scaled = call(
+    start, scaled, link_diag, link_cross = call(
         start_kernel,
-        [((width, 2 * width), BF16), ((rows, width), F32)],
+        [((width, 2 * width), BF16), ((rows, width), F32), ((share, link), F32),
+         ((share, width), F32)],
         [vmem((2 * group, width), F32), vmem((rows, width), F32)],
-        schur_start, s_core, *y_all, tile_swap(after(y_all[2], total), 1),
+        s_own, *y_all, tile_swap(y_all[2], 1), own_terms, came,
     )
 
     here = (total, after(block_swap(total, 1), scaled))
@@ -449,17 +475,8 @@
     global_schur, back_cols = call(
         back_kernel,
         [((group, width), F32), ((rows, width), F32)],
-        [vmem((8 * size, group), F32), vmem((width, width), F32),
-         vmem((width, 2 * width), BF16)],
-        *sums, start, scaled, flops=2 * rows * order * order * 2,
-    )
-    next_terms = after(next_terms, scaled)
-    came = lax.ppermute(next_terms, "tm", [(i, (i - 1) % blocks) for i in range(blocks)])
-    link_diag, link_cross = call(
-        finish_kernel,
-        [((share, link), F32), ((share, width), F32)],
-        [],
-        own_terms, came,
+        [vmem((8 * size, group), F32), vmem((width, 2 * width), BF16)],
+        *sums, start, scaled,
     )
     return (
         link_diag[None], off_terms[None], link_cross[None], global_schur, back_cols[None],

time: 53 us -> 54.9 us (1.036)
  the two profiles are of different devices: /device:TPU:0 before, /device:TPU:27 now
where the time goes in v7:
time: 54.9 us; the launch traced here: 54.7 us
  starting transfers between devices  26.4 us (48%)
  Pallas kernels  16.6 us (30%)
  waiting for transfers between devices  10.4 us (19%)
  between operations  1.34 us (2%)
    ppermute x20, starting transfers between devices, tile_swap(): return lax.ppermute(value, 'tile', [(i, i ^ mask) for i in range(4)])  22.2 us
    pallas_call x7, Pallas kernels, call(): pl.pallas_call(kernel, out_shape=[jax.ShapeDtypeStruct(shape, dtype) for...  16.6 us
    ppermute x20, waiting for transfers between devices, tile_swap(): return lax.ppermute(value, 'tile', [(i, i ^ mask) for i in range(4)])  5.63 us
    ppermute x5, starting transfers between devices, block_swap(): return lax.ppermute(value, 'tm', [(i, i ^ mask) for i in range(blocks)])  3.64 us
    ppermute x5, waiting for transfers between devices, block_swap(): return lax.ppermute(value, 'tm', [(i, i ^ mask) for i in range(blocks)])  2.61 us
    ppermute x1, waiting for transfers between devices, shards(): lax.ppermute(next_terms, 'tm', [(i, (i - 1) % blocks) for i in range(bloc...  2.17 us
  transfers between devices with their start and end apart: 27, of which 8 were waited for; matrix products, arithmetic and copies ran while one was open for 0% of the time, Pallas kernels for 27%

profile of v7, /device:TPU:27, one launch (start us, length us, event | category | flops | bytes accessed | tf_op | source)
XLA Modules:
  0.0 54.7 jit_solution(13660739142010961725)
XLA Ops:
  0.6 1.3 %collective-permute-start.3 = (bf16[192,512]{1,0:T(8,128)(2,1)}, bf16[192,512]{1,0:T(8,128)(2,1)S(1)}, u32[]{:S(2)}, u32[]{:S(2)}) collective-permute-start(bf16[192,512]{1,0:T(8,128)(2,1)} %bitcast.13), channel_id=1, source_target_pairs={{0,2},{1,3},{2,0},{3,1},{4,6},{5,7},{6,4},{7,5},{8,10},{9,11},{10,... | collective-permute-start | bytes 589832 | tf_op jit(solution)/shard_map/ppermute | solution.py:393
  1.9 1.5 %pack_kernel.1 = (f32[392,128]{1,0:T(8,128)S(1)}, f32[400,128]{1,0:T(8,128)S(1)}, f32[192,768]{1,0:T(8,128)S(1)}, f32[192,768]{1,0:T(8,128)S(1)}, bf16[192,512]{...) custom-call(f32[192,768]{1,0:T(8,128)} %bitcast.11, f32[192,768]{1,0:T(8,128)} %bitcast.12, ...), custom_call_target="tpu_custom_call" | custom-call | tf_op jit(solution)/shard_map/pack_kernel/pallas_call | solution.py:362
  3.4 1.0 %collective-permute-start = (f32[192,768]{1,0:T(8,128)S(1)}, f32[192,768]{1,0:T(8,128)S(1)}, u32[]{:S(2)}, u32[]{:S(2)}) collective-permute-start(f32[192,768]{1,0:T(8,128)S(1)} %get-tuple-element.48.x_own), channel_id=1, source_target_pairs={{0,1},{1,0},{2,3},{3,2},{4,5},{5,4},{6,7},{7,6},{8,9},{9,8},{10,11... | collective-permute-start | bytes 1769480 | tf_op jit(solution)/shard_map/ppermute | solution.py:393
  4.5 0.1 collective-permute-start.1
  4.5 0.2 collective-permute-start.4
  4.8 1.9 %collective-permute-done.3.g_far = bf16[192,512]{1,0:T(8,128)(2,1)S(1)} collective-permute-done((bf16[192,512]{1,0:T(8,128)(2,1)}, bf16[192,512]{1,0:T(8,128)(2,1)S(1)}, u32[]{:S(2)}, u32[]{:S(2)}) %collective-permute-start.3) | collective-permute-done | bytes 196640 | tf_op jit(solution)/shard_map/ppermute | solution.py:393
  6.7 2.1 %collective-permute-start.5 = (bf16[192,512]{1,0:T(8,128)(2,1)S(1)}, bf16[192,512]{1,0:T(8,128)(2,1)S(1)}, u32[]{:S(2)}, u32[]{:S(2)}) collective-permute-start(bf16[192,512]{1,0:T(8,128)(2,1)S(1)} %collective-permute-done.3.g_far), channel_id=1, source_target_pairs={{0,1},{1,0},{2,3},{3,2},{4,5},{5,4},{6,7},{7,6},{8,9},{9,8},{10,11... | collective-permute-start | bytes 589832 | tf_op jit(solution)/shard_map/ppermute | solution.py:393
  8.7 1.9 %collective-permute-start.7 = (f32[400,128]{1,0:T(8,128)S(1)}, f32[400,128]{1,0:T(8,128)S(1)}, u32[]{:S(2)}, u32[]{:S(2)}) collective-permute-start(f32[400,128]{1,0:T(8,128)S(1)} %get-tuple-element.57), channel_id=1, source_target_pairs={{0,2},{1,3},{2,0},{3,1},{4,6},{5,7},{6,4},{7,5},{8,10},{9,11},{10,... | collective-permute-start | bytes 614408 | tf_op jit(solution)/shard_map/ppermute | solution.py:393
  10.6 1.0 %collective-permute-done.4.far = f32[392,128]{1,0:T(8,128)S(1)} collective-permute-done((f32[392,128]{1,0:T(8,128)S(1)}, f32[392,128]{1,0:T(8,128)S(1)}, u32[]{:S(2)}, u32[]{:S(2)}) %collective-permute-start.4) | collective-permute-done | bytes 200736 | tf_op jit(solution)/shard_map/ppermute | solution.py:393
  11.6 1.1 %collective-permute-start.6 = (f32[392,128]{1,0:T(8,128)S(1)}, f32[392,128]{1,0:T(8,128)S(1)}, u32[]{:S(2)}, u32[]{:S(2)}) collective-permute-start(f32[392,128]{1,0:T(8,128)S(1)} %collective-permute-done.4.far), channel_id=1, source_target_pairs={{0,1},{1,0},{2,3},{3,2},{4,5},{5,4},{6,7},{7,6},{8,9},{9,8},{10,11... | collective-permute-start | bytes 602120 | tf_op jit(solution)/shard_map/ppermute | solution.py:393
  12.7 0.0 collective-permute-start.2
  13.4 0.8 %collective-permute-done.2.g_core = bf16[192,512]{1,0:T(8,128)(2,1)S(1)} collective-permute-done((bf16[192,512]{1,0:T(8,128)(2,1)S(1)}, bf16[192,512]{1,0:T(8,128)(2,1)S(1)}, u32[]{:S(2)}, u32[]{:S(2)}) %collective-permute-start.2) | collective-permute-done | bytes 196640 | tf_op jit(solution)/shard_map/ppermute | solution.py:393
  14.2 0.0 collective-permute-done.1.k_core
  14.2 0.0 collective-permute-done.6.cross
  14.2 2.0 %prepare_kernel.1 = (bf16[1536,768]{1,0:T(8,128)(2,1)S(1)}, bf16[1536,768]{1,0:T(8,128)(2,1)S(1)}, bf16[768,512]{1,0:T(8,128)(2,1)S(1)}, f32[768,1]{1,0:T(8,128)...) custom-call(s32[1]{0:T(128)S(6)} %copy.15.sizes, ...), custom_call_target="tpu_custom_call" | custom-call | tf_op jit(solution)/shard_map/prepare_kernel/pallas_call | solution.py:362
  16.2 0.1 collective-permute-done.7.far
  16.3 0.6 %collective-permute-start.8 = (f32[400,128]{1,0:T(8,128)S(1)}, f32[400,128]{1,0:T(8,128)S(1)}, u32[]{:S(2)}, u32[]{:S(2)}) collective-permute-start(f32[400,128]{1,0:T(8,128)S(1)} %collective-permute-done.7.far), channel_id=1, source_target_pairs={{0,1},{1,0},{2,3},{3,2},{4,5},{5,4},{6,7},{7,6},{8,9},{9,8},{10,11... | collective-permute-start | bytes 614408 | tf_op jit(solution)/shard_map/ppermute | solution.py:393
  16.9 1.2 %collective-permute-start.13 = (bf16[192,512]{1,0:T(8,128)(2,1)S(1)}, bf16[192,512]{1,0:T(8,128)(2,1)S(1)}, u32[]{:S(2)}, u32[]{:S(2)}) collective-permute-start(bf16[192,512]{1,0:T(8,128)(2,1)S(1)} %bitcast.8), channel_id=1, source_target_pairs={{0,2},{1,3},{2,0},{3,1},{4,6},{5,7},{6,4},{7,5},{8,10},{9,11},{10,... | collective-permute-start | bytes 589832 | tf_op jit(solution)/shard_map/ppermute | solution.py:393
  18.2 0.3 collective-permute-start.12
  18.4 0.0 collective-permute-done.8.cross
  18.4 4.1 %global_kernel.1 = (f32[160,128]{1,0:T(8,128)S(1)}, f32[160,128]{1,0:T(8,128)S(1)}, f32[192,128]{1,0:T(8,128)S(1)}, f32[704,128]{1,0:T(8,128)S(1)}, f32[640,128]...) custom-call(f32[1,768]{1,0:T(1,128)S(1)} %get-tuple-element.56.live, ...), custom_call_target="tpu_custom_call", output_to_operand_aliasing={{5}: (4, {})} | custom-call | tf_op jit(solution)/shard_map/global_kernel/pallas_call | solution.py:362
  22.6 0.9 %collective-permute-done.13.p_far = bf16[192,512]{1,0:T(8,128)(2,1)S(1)} collective-permute-done((bf16[192,512]{1,0:T(8,128)(2,1)S(1)}, bf16[192,512]{1,0:T(8,128)(2,1)S(1)}, u32[]{:S(2)}, u32[]{:S(2)}) %collective-permute-start.13) | collective-permute-done | bytes 196640 | tf_op jit(solution)/shard_map/ppermute | solution.py:393
  23.5 0.8 %collective-permute-start.14 = (bf16[192,512]{1,0:T(8,128)(2,1)S(1)}, bf16[192,512]{1,0:T(8,128)(2,1)S(1)}, u32[]{:S(2)}, u32[]{:S(2)}) collective-permute-start(bf16[192,512]{1,0:T(8,128)(2,1)S(1)} %collective-permute-done.13.p_far), channel_id=1, source_target_pairs={{0,1},{1,0},{2,3},{3,2},{4,5},{5,4},{6,7},{7,6},{8,9},{9,8},{10,11... | collective-permute-start | bytes 589832 | tf_op jit(solution)/shard_map/ppermute | solution.py:393
  24.2 0.3 collective-permute-start.16
  24.5 0.2 collective-permute-start.17
  24.7 2.2 %collective-permute-start.18 = (f32[160,128]{1,0:T(8,128)S(1)}, f32[160,128]{1,0:T(8,128)S(1)}, u32[]{:S(2)}, u32[]{:S(2)}) collective-permute-start(f32[160,128]{1,0:T(8,128)S(1)} %get-tuple-element.75), channel_id=1, source_target_pairs={{0,12},{4,8},{8,4},{12,0},{16,28},{20,24},{24,20},{28,16},{1,13},{... | collective-permute-start | bytes 245768 | tf_op jit(solution)/shard_map/ppermute | solution.py:396
  26.9 0.0 collective-permute-done.12.p_core
  26.9 1.2 %collective-permute-start.10 = (f32[640,128]{1,0:T(8,128)S(1)}, f32[640,128]{1,0:T(8,128)S(1)}, u32[]{:S(2)}, u32[]{:S(2)}) collective-permute-start(f32[640,128]{1,0:T(8,128)S(1)} %get-tuple-element.66), channel_id=1, source_target_pairs={{0,2},{1,3},{2,0},{3,1},{4,6},{5,7},{6,4},{7,5},{8,10},{9,11},{10,... | collective-permute-start | bytes 983048 | tf_op jit(solution)/shard_map/ppermute | solution.py:393
  28.1 0.0 collective-permute-done.14.p_cross
  28.1 5.6 %pair_kernel.1 = (f32[64,768]{1,0:T(8,128)S(1)}, f32[64,256]{1,0:T(8,128)}, f32[64,768]{1,0:T(8,128)S(1)}) custom-call(f32[768,1]{1,0:T(8,128)S(1)} %get-tuple-element.67.live, bf16[192,512]{1,0:T(8,128)(2,1)S(1)} %bitcast.10, bf16[192,512]{1,0:T(8,128)(2,1)S(1)} %collective-permute-done.12.p_core, bf16[192,512]{1,0:T(8,128)(2,1)S(1)} %collective-permute-done.13.p_far, ...), custom_call_target="tpu_custom_call" | custom-call | tf_op jit(solution)/shard_map/pair_kernel/pallas_call | solution.py:362
  33.7 0.1 collective-permute-start.19
  33.8 1.4 %collective-permute-start.9 = (f32[704,128]{1,0:T(8,128)S(1)}, f32[704,128]{1,0:T(8,128)S(1)}, u32[]{:S(2)}, u32[]{:S(2)}) collective-permute-start(f32[704,128]{1,0:T(8,128)S(1)} %get-tuple-element.65), channel_id=1, source_target_pairs={{0,1},{1,0},{2,3},{3,2},{4,5},{5,4},{6,7},{7,6},{8,9},{9,8},{10,11... | collective-permute-start | bytes 1081352 | tf_op jit(solution)/shard_map/ppermute | solution.py:393
  35.2 0.2 collective-permute-start.15
  35.5 1.5 %collective-permute-start.11 = (f32[640,128]{1,0:T(8,128)S(1)}, f32[640,128]{1,0:T(8,128)S(1)}, u32[]{:S(2)}, u32[]{:S(2)}) collective-permute-start(f32[640,128]{1,0:T(8,128)S(1)} %collective-permute-done.10.far), channel_id=1, source_target_pairs={{0,1},{1,0},{2,3},{3,2},{4,5},{5,4},{6,7},{7,6},{8,9},{9,8},{10,11... | collective-permute-start | bytes 983048 | tf_op jit(solution)/shard_map/ppermute | solution.py:393
  37.0 2.6 %collective-permute-done.19.came = f32[160,128]{1,0:T(8,128)S(1)} collective-permute-done((f32[160,128]{1,0:T(8,128)S(1)}, f32[160,128]{1,0:T(8,128)S(1)}, u32[]{:S(2)}, u32[]{:S(2)}) %collective-permute-start.19) | collective-permute-done | bytes 81952 | tf_op jit(solution)/shard_map/ppermute | solution.py:396
  39.6 0.3 collective-permute-start.24
  39.9 1.6 %collective-permute-start.23 = (f32[160,128]{1,0:T(8,128)S(1)}, f32[160,128]{1,0:T(8,128)S(1)}, u32[]{:S(2)}, u32[]{:S(2)}) collective-permute-start(f32[160,128]{1,0:T(8,128)S(1)} %sum_kernel.1.refs_0_), channel_id=1, source_target_pairs={{0,2},{1,3},{2,0},{3,1},{4,6},{5,7},{6,4},{7,5},{8,10},{9,11},{10,... | collective-permute-start | bytes 245768 | tf_op jit(solution)/shard_map/ppermute | solution.py:393
  41.5 0.0 collective-permute-done.9.y_core
  41.5 0.9 %collective-permute-start.20 = (f32[160,128]{1,0:T(8,128)S(1)}, f32[160,128]{1,0:T(8,128)S(1)}, u32[]{:S(2)}, u32[]{:S(2)}) collective-permute-start(f32[160,128]{1,0:T(8,128)S(1)} %sum_kernel.1.refs_0_), channel_id=1, source_target_pairs={{0,4},{4,0},{8,12},{12,8},{16,20},{20,16},{24,28},{28,24},{1,5},{5... | collective-permute-start | bytes 245768 | tf_op jit(solution)/shard_map/ppermute | solution.py:396
  42.3 2.2 %collective-permute-done.15.came = f32[64,768]{1,0:T(8,128)S(1)} collective-permute-done((f32[64,768]{1,0:T(8,128)S(1)}, f32[64,768]{1,0:T(8,128)S(1)}, u32[]{:S(2)}, u32[]{:S(2)}) %collective-permute-start.15) | collective-permute-done | bytes 196640 | tf_op jit(solution)/shard_map/ppermute | solution.py:447
  44.5 3.1 %collective-permute-start.21 = (f32[160,128]{1,0:T(8,128)S(1)}, f32[160,128]{1,0:T(8,128)S(1)}, u32[]{:S(2)}, u32[]{:S(2)}) collective-permute-start(f32[160,128]{1,0:T(8,128)S(1)} %sum_kernel.1.refs_0_), channel_id=1, source_target_pairs={{0,1},{1,0},{2,3},{3,2},{4,5},{5,4},{6,7},{7,6},{8,9},{9,8},{10,11... | collective-permute-start | bytes 245768 | tf_op jit(solution)/shard_map/ppermute | solution.py:393
  47.6 1.5 %start_kernel.1 = (bf16[512,1024]{1,0:T(8,128)(2,1)S(1)}, f32[192,512]{1,0:T(8,128)S(1)}, f32[64,256]{1,0:T(8,128)}, f32[64,512]{1,0:T(8,128)}) custom-call(f32[512,128]{1,0:T(8,128)S(1)} %get-tuple-element.47.s_own, f32[192,128]{1,0:T(8,128)S(1)} %get-tuple-element.64.y_own, f32[704,128]{1,0:T(8,128)S(1)} %collective-permute-done.9.y_core, ...), custom_call_target="tpu_custom_call" | custom-call | tf_op jit(solution)/shard_map/start_kernel/pallas_call | solution.py:362
  49.2 0.0 collective-permute-start.26
  49.2 1.2 %collective-permute-start.25 = (f32[160,128]{1,0:T(8,128)S(1)}, f32[160,128]{1,0:T(8,128)S(1)}, u32[]{:S(2)}, u32[]{:S(2)}) collective-permute-start(f32[160,128]{1,0:T(8,128)S(1)} %collective-permute-done.23.refs_4_), channel_id=1, source_target_pairs={{0,1},{1,0},{2,3},{3,2},{4,5},{5,4},{6,7},{7,6},{8,9},{9,8},{10,11... | collective-permute-start | bytes 245768 | tf_op jit(solution)/shard_map/ppermute | solution.py:393
  50.4 1.6 %collective-permute-start.22 = (f32[160,128]{1,0:T(8,128)S(1)}, f32[160,128]{1,0:T(8,128)S(1)}, u32[]{:S(2)}, u32[]{:S(2)}) collective-permute-start(f32[160,128]{1,0:T(8,128)S(1)} %collective-permute-done.20.refs_1_), channel_id=1, source_target_pairs={{0,1},{1,0},{2,3},{3,2},{4,5},{5,4},{6,7},{7,6},{8,9},{9,8},{10,11... | collective-permute-start | bytes 245768 | tf_op jit(solution)/shard_map/ppermute | solution.py:393
  52.0 0.0 collective-permute-done.21.refs_2_
  52.0 0.9 %collective-permute-done.22.refs_3_ = f32[160,128]{1,0:T(8,128)S(1)} collective-permute-done((f32[160,128]{1,0:T(8,128)S(1)}, f32[160,128]{1,0:T(8,128)S(1)}, u32[]{:S(2)}, u32[]{:S(2)}) %collective-permute-start.22) | collective-permute-done | bytes 81952 | tf_op jit(solution)/shard_map/ppermute | solution.py:393
  52.9 1.8 %back_kernel.1 = (f32[128,512]{1,0:T(8,128)}, f32[192,512]{1,0:T(8,128)}) custom-call(f32[160,128]{1,0:T(8,128)S(1)} %sum_kernel.1.refs_0_, f32[160,128]{1,0:T(8,128)S(1)} %collective-permute-done.20.refs_1_, f32[160,128]{1,0:T(8,128)S(1)} %collective-permute-done.21.refs_2_, f32[160,128]{1,0:T(8,128)S(1)} %collective-permute-done.22.refs_3_, ...), custom_call_target="tpu_custom_call" | custom-call | tf_op jit(solution)/shard_map/back_kernel/pallas_call | solution.py:362
  (18 shorter events, 0.1 us)
Async XLA Ops:
  0.6 6.0 %collective-permute-start.3 = (bf16[192,512]{1,0:T(8,128)(2,1)}, bf16[192,512]{1,0:T(8,128)(2,1)S(1)}, u32[]{:S(2)}, u32[]{:S(2)}) collective-permute-start(bf16[192,512]{1,0:T(8,128)(2,1)} %bitcast.13), channel_id=1, source_target_pairs={{0,2},{1,3},{2,0},{3,1},{4,6},{5,7},{6,4},{7,5},{8,10},{9,11},{10,... | collective-permute-start | bytes 589832 | tf_op jit(solution)/shard_map/ppermute | solution.py:393
  1.9 15.0 %copy-start.1 = (bf16[1,192,512]{2,1,0:T(8,128)(2,1)S(1)}, bf16[1,192,512]{2,1,0:T(8,128)(2,1)}, u32[]{:S(2)}) copy-start(bf16[1,192,512]{2,1,0:T(8,128)(2,1)} %param.12) | copy-start | bytes 589828
  1.9 16.5 %copy-start = (f32[128,512]{1,0:T(8,128)S(1)}, f32[128,512]{1,0:T(8,128)}, u32[]{:S(2)}) copy-start(f32[128,512]{1,0:T(8,128)} %base.1) | copy-start | bytes 786436
  3.4 10.7 %collective-permute-start = (f32[192,768]{1,0:T(8,128)S(1)}, f32[192,768]{1,0:T(8,128)S(1)}, u32[]{:S(2)}, u32[]{:S(2)}) collective-permute-start(f32[192,768]{1,0:T(8,128)S(1)} %get-tuple-element.48.x_own), channel_id=1, source_target_pairs={{0,1},{1,0},{2,3},{3,2},{4,5},{5,4},{6,7},{7,6},{8,9},{9,8},{10,11... | collective-permute-start | bytes 1769480 | tf_op jit(solution)/shard_map/ppermute | solution.py:393
  4.5 9.7 %collective-permute-start.1 = (f32[192,768]{1,0:T(8,128)S(1)}, f32[192,768]{1,0:T(8,128)S(1)}, u32[]{:S(2)}, u32[]{:S(2)}) collective-permute-start(f32[192,768]{1,0:T(8,128)S(1)} %get-tuple-element.49.k_own), channel_id=1, source_target_pairs={{0,1},{1,0},{2,3},{3,2},{4,5},{5,4},{6,7},{7,6},{8,9},{9,8},{10,11... | collective-permute-start | bytes 1769480 | tf_op jit(solution)/shard_map/ppermute | solution.py:393
  4.5 7.1 %collective-permute-start.4 = (f32[392,128]{1,0:T(8,128)S(1)}, f32[392,128]{1,0:T(8,128)S(1)}, u32[]{:S(2)}, u32[]{:S(2)}) collective-permute-start(f32[392,128]{1,0:T(8,128)S(1)} %get-tuple-element.51), channel_id=1, source_target_pairs={{0,2},{1,3},{2,0},{3,1},{4,6},{5,7},{6,4},{7,5},{8,10},{9,11},{10,... | collective-permute-start | bytes 602120 | tf_op jit(solution)/shard_map/ppermute | solution.py:393
  6.7 4.9 %collective-permute-start.5 = (bf16[192,512]{1,0:T(8,128)(2,1)S(1)}, bf16[192,512]{1,0:T(8,128)(2,1)S(1)}, u32[]{:S(2)}, u32[]{:S(2)}) collective-permute-start(bf16[192,512]{1,0:T(8,128)(2,1)S(1)} %collective-permute-done.3.g_far), channel_id=1, source_target_pairs={{0,1},{1,0},{2,3},{3,2},{4,5},{5,4},{6,7},{7,6},{8,9},{9,8},{10,11... | collective-permute-start | bytes 589832 | tf_op jit(solution)/shard_map/ppermute | solution.py:393
  8.7 7.6 %collective-permute-start.7 = (f32[400,128]{1,0:T(8,128)S(1)}, f32[400,128]{1,0:T(8,128)S(1)}, u32[]{:S(2)}, u32[]{:S(2)}) collective-permute-start(f32[400,128]{1,0:T(8,128)S(1)} %get-tuple-element.57), channel_id=1, source_target_pairs={{0,2},{1,3},{2,0},{3,1},{4,6},{5,7},{6,4},{7,5},{8,10},{9,11},{10,... | collective-permute-start | bytes 614408 | tf_op jit(solution)/shard_map/ppermute | solution.py:393
  11.6 2.6 %collective-permute-start.6 = (f32[392,128]{1,0:T(8,128)S(1)}, f32[392,128]{1,0:T(8,128)S(1)}, u32[]{:S(2)}, u32[]{:S(2)}) collective-permute-start(f32[392,128]{1,0:T(8,128)S(1)} %collective-permute-done.4.far), channel_id=1, source_target_pairs={{0,1},{1,0},{2,3},{3,2},{4,5},{5,4},{6,7},{7,6},{8,9},{9,8},{10,11... | collective-permute-start | bytes 602120 | tf_op jit(solution)/shard_map/ppermute | solution.py:393
  12.7 1.4 %collective-permute-start.2 = (bf16[192,512]{1,0:T(8,128)(2,1)S(1)}, bf16[192,512]{1,0:T(8,128)(2,1)S(1)}, u32[]{:S(2)}, u32[]{:S(2)}) collective-permute-start(bf16[192,512]{1,0:T(8,128)(2,1)S(1)} %get-tuple-element.50.g_own), channel_id=1, source_target_pairs={{0,1},{1,0},{2,3},{3,2},{4,5},{5,4},{6,7},{7,6},{8,9},{9,8},{10,11... | collective-permute-start | bytes 589832 | tf_op jit(solution)/shard_map/ppermute | solution.py:393
  16.3 2.1 %collective-permute-start.8 = (f32[400,128]{1,0:T(8,128)S(1)}, f32[400,128]{1,0:T(8,128)S(1)}, u32[]{:S(2)}, u32[]{:S(2)}) collective-permute-start(f32[400,128]{1,0:T(8,128)S(1)} %collective-permute-done.7.far), channel_id=1, source_target_pairs={{0,1},{1,0},{2,3},{3,2},{4,5},{5,4},{6,7},{7,6},{8,9},{9,8},{10,11... | collective-permute-start | bytes 614408 | tf_op jit(solution)/shard_map/ppermute | solution.py:393
  16.9 6.5 %collective-permute-start.13 = (bf16[192,512]{1,0:T(8,128)(2,1)S(1)}, bf16[192,512]{1,0:T(8,128)(2,1)S(1)}, u32[]{:S(2)}, u32[]{:S(2)}) collective-permute-start(bf16[192,512]{1,0:T(8,128)(2,1)S(1)} %bitcast.8), channel_id=1, source_target_pairs={{0,2},{1,3},{2,0},{3,1},{4,6},{5,7},{6,4},{7,5},{8,10},{9,11},{10,... | collective-permute-start | bytes 589832 | tf_op jit(solution)/shard_map/ppermute | solution.py:393
  18.2 8.7 %collective-permute-start.12 = (bf16[192,512]{1,0:T(8,128)(2,1)S(1)}, bf16[192,512]{1,0:T(8,128)(2,1)S(1)}, u32[]{:S(2)}, u32[]{:S(2)}) collective-permute-start(bf16[192,512]{1,0:T(8,128)(2,1)S(1)} %bitcast.9), channel_id=1, source_target_pairs={{0,1},{1,0},{2,3},{3,2},{4,5},{5,4},{6,7},{7,6},{8,9},{9,8},{10,11... | collective-permute-start | bytes 589832 | tf_op jit(solution)/shard_map/ppermute | solution.py:393
  23.5 4.7 %collective-permute-start.14 = (bf16[192,512]{1,0:T(8,128)(2,1)S(1)}, bf16[192,512]{1,0:T(8,128)(2,1)S(1)}, u32[]{:S(2)}, u32[]{:S(2)}) collective-permute-start(bf16[192,512]{1,0:T(8,128)(2,1)S(1)} %collective-permute-done.13.p_far), channel_id=1, source_target_pairs={{0,1},{1,0},{2,3},{3,2},{4,5},{5,4},{6,7},{7,6},{8,9},{9,8},{10,11... | collective-permute-start | bytes 589832 | tf_op jit(solution)/shard_map/ppermute | solution.py:393
  24.2 9.5 %collective-permute-start.16 = (f32[160,128]{1,0:T(8,128)S(1)}, f32[160,128]{1,0:T(8,128)S(1)}, u32[]{:S(2)}, u32[]{:S(2)}) collective-permute-start(f32[160,128]{1,0:T(8,128)S(1)} %get-tuple-element.75), channel_id=1, source_target_pairs={{0,4},{4,0},{8,12},{12,8},{16,20},{20,16},{24,28},{28,24},{1,5},{5... | collective-permute-start | bytes 245768 | tf_op jit(solution)/shard_map/ppermute | solution.py:396
  24.5 9.2 %collective-permute-start.17 = (f32[160,128]{1,0:T(8,128)S(1)}, f32[160,128]{1,0:T(8,128)S(1)}, u32[]{:S(2)}, u32[]{:S(2)}) collective-permute-start(f32[160,128]{1,0:T(8,128)S(1)} %get-tuple-element.69), channel_id=1, source_target_pairs={{0,8},{4,12},{8,0},{12,4},{16,24},{20,28},{24,16},{28,20},{1,9},{5... | collective-permute-start | bytes 245768 | tf_op jit(solution)/shard_map/ppermute | solution.py:396
  24.7 9.0 %collective-permute-start.18 = (f32[160,128]{1,0:T(8,128)S(1)}, f32[160,128]{1,0:T(8,128)S(1)}, u32[]{:S(2)}, u32[]{:S(2)}) collective-permute-start(f32[160,128]{1,0:T(8,128)S(1)} %get-tuple-element.75), channel_id=1, source_target_pairs={{0,12},{4,8},{8,4},{12,0},{16,28},{20,24},{24,20},{28,16},{1,13},{... | collective-permute-start | bytes 245768 | tf_op jit(solution)/shard_map/ppermute | solution.py:396
  26.9 8.6 %collective-permute-start.10 = (f32[640,128]{1,0:T(8,128)S(1)}, f32[640,128]{1,0:T(8,128)S(1)}, u32[]{:S(2)}, u32[]{:S(2)}) collective-permute-start(f32[640,128]{1,0:T(8,128)S(1)} %get-tuple-element.66), channel_id=1, source_target_pairs={{0,2},{1,3},{2,0},{3,1},{4,6},{5,7},{6,4},{7,5},{8,10},{9,11},{10,... | collective-permute-start | bytes 983048 | tf_op jit(solution)/shard_map/ppermute | solution.py:393
  33.7 5.9 %collective-permute-start.19 = (f32[160,128]{1,0:T(8,128)S(1)}, f32[160,128]{1,0:T(8,128)S(1)}, u32[]{:S(2)}, u32[]{:S(2)}) collective-permute-start(f32[160,128]{1,0:T(8,128)S(1)} %add_add_fusion.mine), channel_id=1, source_target_pairs={{0,16},{4,20},{8,24},{12,28},{16,0},{20,4},{24,8},{28,12},{1,17},{... | collective-permute-start | bytes 245768 | tf_op jit(solution)/shard_map/ppermute | solution.py:396
  33.8 7.6 %collective-permute-start.9 = (f32[704,128]{1,0:T(8,128)S(1)}, f32[704,128]{1,0:T(8,128)S(1)}, u32[]{:S(2)}, u32[]{:S(2)}) collective-permute-start(f32[704,128]{1,0:T(8,128)S(1)} %get-tuple-element.65), channel_id=1, source_target_pairs={{0,1},{1,0},{2,3},{3,2},{4,5},{5,4},{6,7},{7,6},{8,9},{9,8},{10,11... | collective-permute-start | bytes 1081352 | tf_op jit(solution)/shard_map/ppermute | solution.py:393
  35.2 9.3 %collective-permute-start.15 = (f32[64,768]{1,0:T(8,128)S(1)}, f32[64,768]{1,0:T(8,128)S(1)}, u32[]{:S(2)}, u32[]{:S(2)}) collective-permute-start(f32[64,768]{1,0:T(8,128)S(1)} %get-tuple-element.73), channel_id=1, source_target_pairs={{0,28},{4,0},{8,4},{12,8},{16,12},{20,16},{24,20},{28,24},{1,29},{... | collective-permute-start | bytes 589832 | tf_op jit(solution)/shard_map/ppermute | solution.py:447
  35.5 12.1 %collective-permute-start.11 = (f32[640,128]{1,0:T(8,128)S(1)}, f32[640,128]{1,0:T(8,128)S(1)}, u32[]{:S(2)}, u32[]{:S(2)}) collective-permute-start(f32[640,128]{1,0:T(8,128)S(1)} %collective-permute-done.10.far), channel_id=1, source_target_pairs={{0,1},{1,0},{2,3},{3,2},{4,5},{5,4},{6,7},{7,6},{8,9},{9,8},{10,11... | collective-permute-start | bytes 983048 | tf_op jit(solution)/shard_map/ppermute | solution.py:393
  39.6 9.5 %collective-permute-start.24 = (f32[160,128]{1,0:T(8,128)S(1)}, f32[160,128]{1,0:T(8,128)S(1)}, u32[]{:S(2)}, u32[]{:S(2)}) collective-permute-start(f32[160,128]{1,0:T(8,128)S(1)} %sum_kernel.1.refs_0_), channel_id=1, source_target_pairs={{0,6},{1,7},{2,4},{3,5},{4,2},{5,3},{6,0},{7,1},{8,14},{9,15},{10,... | collective-permute-start | bytes 245768 | tf_op jit(solution)/shard_map/ppermute | solution.py:402
  39.9 9.3 %collective-permute-start.23 = (f32[160,128]{1,0:T(8,128)S(1)}, f32[160,128]{1,0:T(8,128)S(1)}, u32[]{:S(2)}, u32[]{:S(2)}) collective-permute-start(f32[160,128]{1,0:T(8,128)S(1)} %sum_kernel.1.refs_0_), channel_id=1, source_target_pairs={{0,2},{1,3},{2,0},{3,1},{4,6},{5,7},{6,4},{7,5},{8,10},{9,11},{10,... | collective-permute-start | bytes 245768 | tf_op jit(solution)/shard_map/ppermute | solution.py:393
  41.5 9.0 %collective-permute-start.20 = (f32[160,128]{1,0:T(8,128)S(1)}, f32[160,128]{1,0:T(8,128)S(1)}, u32[]{:S(2)}, u32[]{:S(2)}) collective-permute-start(f32[160,128]{1,0:T(8,128)S(1)} %sum_kernel.1.refs_0_), channel_id=1, source_target_pairs={{0,4},{4,0},{8,12},{12,8},{16,20},{20,16},{24,28},{28,24},{1,5},{5... | collective-permute-start | bytes 245768 | tf_op jit(solution)/shard_map/ppermute | solution.py:396
  44.5 7.5 %collective-permute-start.21 = (f32[160,128]{1,0:T(8,128)S(1)}, f32[160,128]{1,0:T(8,128)S(1)}, u32[]{:S(2)}, u32[]{:S(2)}) collective-permute-start(f32[160,128]{1,0:T(8,128)S(1)} %sum_kernel.1.refs_0_), channel_id=1, source_target_pairs={{0,1},{1,0},{2,3},{3,2},{4,5},{5,4},{6,7},{7,6},{8,9},{9,8},{10,11... | collective-permute-start | bytes 245768 | tf_op jit(solution)/shard_map/ppermute | solution.py:393
  49.2 2.8 %collective-permute-start.26 = (f32[160,128]{1,0:T(8,128)S(1)}, f32[160,128]{1,0:T(8,128)S(1)}, u32[]{:S(2)}, u32[]{:S(2)}) collective-permute-start(f32[160,128]{1,0:T(8,128)S(1)} %collective-permute-done.24.refs_5_), channel_id=1, source_target_pairs={{0,1},{1,0},{2,3},{3,2},{4,5},{5,4},{6,7},{7,6},{8,9},{9,8},{10,11... | collective-permute-start | bytes 245768 | tf_op jit(solution)/shard_map/ppermute | solution.py:393
  49.2 2.8 %collective-permute-start.25 = (f32[160,128]{1,0:T(8,128)S(1)}, f32[160,128]{1,0:T(8,128)S(1)}, u32[]{:S(2)}, u32[]{:S(2)}) collective-permute-start(f32[160,128]{1,0:T(8,128)S(1)} %collective-permute-done.23.refs_4_), channel_id=1, source_target_pairs={{0,1},{1,0},{2,3},{3,2},{4,5},{5,4},{6,7},{7,6},{8,9},{9,8},{10,11... | collective-permute-start | bytes 245768 | tf_op jit(solution)/shard_map/ppermute | solution.py:393
  50.4 2.5 %collective-permute-start.22 = (f32[160,128]{1,0:T(8,128)S(1)}, f32[160,128]{1,0:T(8,128)S(1)}, u32[]{:S(2)}, u32[]{:S(2)}) collective-permute-start(f32[160,128]{1,0:T(8,128)S(1)} %collective-permute-done.20.refs_1_), channel_id=1, source_target_pairs={{0,1},{1,0},{2,3},{3,2},{4,5},{5,4},{6,7},{7,6},{8,9},{9,8},{10,11... | collective-permute-start | bytes 245768 | tf_op jit(solution)/shard_map/ppermute | solution.py:393

commit v8 on v7

--- a/solution.py
+++ b/solution.py
@@ -262,10 +262,7 @@
     own_terms[:, link:] = cross[share:]
 
 
-def start_kernel(
-    s_own, y_own, y_core, far, cross, own_terms, came,
-    start, scaled, link_diag, link_cross, s_rows, y_rows,
-):
+def start_kernel(s_own, y_own, y_core, far, cross, start, scaled, s_rows, y_rows):
     rows, group = y_own.shape
     width = s_rows.shape[1]
     half = width // 2
@@ -295,14 +292,6 @@
     for ref, mask in ((y_own, 0), (y_core, 1), (far, 2), (cross.at[rows:, :], 3)):
         y_rows[:, at((part ^ mask) * group, group, 128)] = ref[:rows, :]
     scaled[...] = times_wide(y_rows[...], start)
-    link = link_diag.shape[1]
-    there = lax.axis_index("tm") + 1 < lax.axis_size("tm")
-    link_diag[...] = own_terms[:, :link] + jnp.where(there, came[:, :link], 0.0)
-    link_cross[...] = own_terms[:, link:] + jnp.where(there, came[:, link:], 0.0)
-
-
-def sum_kernel(mine, came, total):
-    total[...] = mine[...] + came[...]
 
 
 def back_kernel(*refs):
@@ -352,6 +341,13 @@
     back[...] = 2.0 * value - times_wide(times_wide(value, parts), start)
 
 
+def finish_kernel(own_terms, came, link_diag, link_cross):
+    link = link_diag.shape[1]
+    there = lax.axis_index("tm") + 1 < lax.axis_size("tm")
+    link_diag[...] = own_terms[:, :link] + jnp.where(there, came[:, :link], 0.0)
+    link_cross[...] = own_terms[:, link:] + jnp.where(there, came[:, link:], 0.0)
+
+
 def call(kernel, outs, scratch, *args, sizes=None, whole=False, alias={}, flops=0):
     vmem = pl.BlockSpec(memory_space=pltpu.VMEM)
     specs = [pl.BlockSpec(memory_space=pltpu.HBM) if whole else vmem] * len(args)
@@ -437,34 +433,31 @@
     )
 
     y_all = (y_own, tile_swap(y_core, 1), tile_swap(y_far, 2))
+    if blocks > 2:
+        parts = [block_swap(send, 1), block_swap(keep, 2), block_swap(send, 3)]
+        total = (keep + parts[1]) + (parts[0] + parts[2])
+    else:
+        total = keep + block_swap(send, 1)
     p_far = after(p_far, keep)
     own_terms, off_terms, next_terms = call(
         pair_kernel,
         [((share, link + width), F32), ((share, link), F32), ((share, link + width), F32)],
         [vmem((order, 2 * link), BF16)],
-        live_rows, pair, p_core, p_far, tile_swap(p_far, 1), x, k, links,
-    )
-    came = lax.ppermute(next_terms, "tm", [(i, (i - 1) % blocks) for i in range(blocks)])
-    parts = [block_swap(send, 1)]
-    if blocks > 2:
-        parts += [block_swap(keep, 2), block_swap(send, 3)]
-        *parts, off_terms = lax.optimization_barrier((*parts, off_terms))
-        total = (keep + parts[1]) + (parts[0] + parts[2])
-    else:
-        total = keep + parts[0]
+        live_rows, pair, p_core, p_far, tile_swap(p_far, 1), x, k, after(links, total),
+    )
     step = 4
     while step < blocks:
-        total = call(
-            sum_kernel, [(total.shape, F32)], [], total, block_swap(total, step),
-            flops=32 * rows * order * order,
-        )[0]
+        other = block_swap(total, step)
+        if step == 4:
+            other, off_terms, *y_all = lax.optimization_barrier((other, off_terms, *y_all))
+        total = total + other
         step *= 2
-    start, scaled, link_diag, link_cross = call(
+    cross = tile_swap(after(y_all[2], total), 1)
+    start, scaled = call(
         start_kernel,
-        [((width, 2 * width), BF16), ((rows, width), F32), ((share, link), F32),
-         ((share, width), F32)],
+        [((width, 2 * width), BF16), ((rows, width), F32)],
         [vmem((2 * group, width), F32), vmem((rows, width), F32)],
-        s_own, *y_all, tile_swap(y_all[2], 1), own_terms, came,
+        s_own, *y_all, cross,
     )
 
     here = (total, after(block_swap(total, 1), scaled))
@@ -477,6 +470,15 @@
         [((group, width), F32), ((rows, width), F32)],
         [vmem((8 * size, group), F32), vmem((width, 2 * width), BF16)],
         *sums, start, scaled,
+        flops=int(4 * rows * order * order),
+    )
+    next_terms = after(next_terms, cross)
+    came = lax.ppermute(next_terms, "tm", [(i, (i - 1) % blocks) for i in range(blocks)])
+    link_diag, link_cross = call(
+        finish_kernel,
+        [((share, link), F32), ((share, width), F32)],
+        [],
+        own_terms, came,
     )
     return (
         link_diag[None], off_terms[None], link_cross[None], global_schur, back_cols[None],

time: 54.9 us -> 54.2 us (0.987)
  the two profiles are of different devices: /device:TPU:27 before, /device:TPU:0 now
where the time goes in v8:
time: 54.2 us; the launch traced here: 54.1 us
  starting transfers between devices  22.5 us (42%)
  Pallas kernels  16.6 us (31%)
  waiting for transfers between devices  13.5 us (25%)
  between operations  1.38 us (3%)
    pallas_call x7, Pallas kernels, call(): pl.pallas_call(kernel, out_shape=[jax.ShapeDtypeStruct(shape, dtype) for...  16.6 us
    ppermute x20, starting transfers between devices, tile_swap(): return lax.ppermute(value, 'tile', [(i, i ^ mask) for i in range(4)])  11.2 us
    ppermute x20, waiting for transfers between devices, tile_swap(): return lax.ppermute(value, 'tile', [(i, i ^ mask) for i in range(4)])  7.78 us
    ppermute x5, starting transfers between devices, block_swap(): return lax.ppermute(value, 'tm', [(i, i ^ mask) for i in range(blocks)])  7.22 us
    ppermute x5, waiting for transfers between devices, block_swap(): return lax.ppermute(value, 'tm', [(i, i ^ mask) for i in range(blocks)])  5.76 us
    ppermute x1, starting transfers between devices, shards(): lax.ppermute(next_terms, 'tm', [(i, (i - 1) % blocks) for i in range(bloc...  2.12 us
    ppermute x1, starting transfers between devices, diagonal_swap(): return lax.ppermute(value, ('tm', 'tile'), pairs)  1.96 us
  transfers between devices with their start and end apart: 27, of which 9 were waited for; matrix products, arithmetic and copies ran while one was open for 0% of the time, Pallas kernels for 29%

profile of v8, /device:TPU:0, one launch (start us, length us, event | category | flops | bytes accessed | tf_op | source)
XLA Modules:
  0.0 54.1 jit_solution(13188248057689352316)
XLA Ops:
  0.6 3.0 %collective-permute-start.3 = (bf16[192,512]{1,0:T(8,128)(2,1)}, bf16[192,512]{1,0:T(8,128)(2,1)S(1)}, u32[]{:S(2)}, u32[]{:S(2)}) collective-permute-start(bf16[192,512]{1,0:T(8,128)(2,1)} %bitcast.13), channel_id=1, source_target_pairs={{0,2},{1,3},{2,0},{3,1},{4,6},{5,7},{6,4},{7,5},{8,10},{9,11},{10,... | collective-permute-start | bytes 589832 | tf_op jit(solution)/shard_map/ppermute | solution.py:389
  3.7 1.5 %pack_kernel.1 = (f32[392,128]{1,0:T(8,128)S(1)}, f32[400,128]{1,0:T(8,128)S(1)}, f32[192,768]{1,0:T(8,128)S(1)}, f32[192,768]{1,0:T(8,128)S(1)}, bf16[192,512]{...) custom-call(f32[192,768]{1,0:T(8,128)} %bitcast.11, f32[192,768]{1,0:T(8,128)} %bitcast.12, ...), custom_call_target="tpu_custom_call" | custom-call | tf_op jit(solution)/shard_map/pack_kernel/pallas_call | solution.py:358
  5.2 0.1 collective-permute-start
  5.2 0.5 collective-permute-start.1
  5.7 0.0 collective-permute-start.4
  5.8 3.5 %collective-permute-done.3.g_far = bf16[192,512]{1,0:T(8,128)(2,1)S(1)} collective-permute-done((bf16[192,512]{1,0:T(8,128)(2,1)}, bf16[192,512]{1,0:T(8,128)(2,1)S(1)}, u32[]{:S(2)}, u32[]{:S(2)}) %collective-permute-start.3) | collective-permute-done | bytes 196640 | tf_op jit(solution)/shard_map/ppermute | solution.py:389
  9.3 0.0 collective-permute-start.5
  9.3 2.4 %collective-permute-start.9 = (f32[400,128]{1,0:T(8,128)S(1)}, f32[400,128]{1,0:T(8,128)S(1)}, u32[]{:S(2)}, u32[]{:S(2)}) collective-permute-start(f32[400,128]{1,0:T(8,128)S(1)} %get-tuple-element.63), channel_id=1, source_target_pairs={{0,2},{1,3},{2,0},{3,1},{4,6},{5,7},{6,4},{7,5},{8,10},{9,11},{10,... | collective-permute-start | bytes 614408 | tf_op jit(solution)/shard_map/ppermute | solution.py:389
  11.7 1.4 %collective-permute-done.4.far = f32[392,128]{1,0:T(8,128)S(1)} collective-permute-done((f32[392,128]{1,0:T(8,128)S(1)}, f32[392,128]{1,0:T(8,128)S(1)}, u32[]{:S(2)}, u32[]{:S(2)}) %collective-permute-start.4) | collective-permute-done | bytes 200736 | tf_op jit(solution)/shard_map/ppermute | solution.py:389
  13.1 0.0 collective-permute-done.5.g_cross
  13.1 0.0 collective-permute-start.6
  13.1 0.5 collective-permute-start.2
  14.2 0.6 %collective-permute-done.2.g_core = bf16[192,512]{1,0:T(8,128)(2,1)S(1)} collective-permute-done((bf16[192,512]{1,0:T(8,128)(2,1)S(1)}, bf16[192,512]{1,0:T(8,128)(2,1)S(1)}, u32[]{:S(2)}, u32[]{:S(2)}) %collective-permute-start.2) | collective-permute-done | bytes 196640 | tf_op jit(solution)/shard_map/ppermute | solution.py:389
  14.8 0.0 collective-permute-done.x_core
  14.8 0.0 collective-permute-done.6.cross
  14.8 2.0 %prepare_kernel.1 = (bf16[1536,768]{1,0:T(8,128)(2,1)S(1)}, bf16[1536,768]{1,0:T(8,128)(2,1)S(1)}, bf16[768,512]{1,0:T(8,128)(2,1)S(1)}, f32[768,1]{1,0:T(8,128)...) custom-call(s32[1]{0:T(128)S(6)} %copy.15.sizes, ...), custom_call_target="tpu_custom_call" | custom-call | tf_op jit(solution)/shard_map/prepare_kernel/pallas_call | solution.py:358
  16.8 0.7 %collective-permute-done.9.far = f32[400,128]{1,0:T(8,128)S(1)} collective-permute-done((f32[400,128]{1,0:T(8,128)S(1)}, f32[400,128]{1,0:T(8,128)S(1)}, u32[]{:S(2)}, u32[]{:S(2)}) %collective-permute-start.9) | collective-permute-done | bytes 204832 | tf_op jit(solution)/shard_map/ppermute | solution.py:389
  17.5 1.7 %collective-permute-start.8 = (bf16[192,512]{1,0:T(8,128)(2,1)S(1)}, bf16[192,512]{1,0:T(8,128)(2,1)S(1)}, u32[]{:S(2)}, u32[]{:S(2)}) collective-permute-start(bf16[192,512]{1,0:T(8,128)(2,1)S(1)} %bitcast.8), channel_id=1, source_target_pairs={{0,2},{1,3},{2,0},{3,1},{4,6},{5,7},{6,4},{7,5},{8,10},{9,11},{10,... | collective-permute-start | bytes 589832 | tf_op jit(solution)/shard_map/ppermute | solution.py:389
  19.2 0.0 collective-permute-done.10.cross
  19.2 4.1 %global_kernel.1 = (f32[160,128]{1,0:T(8,128)S(1)}, f32[160,128]{1,0:T(8,128)S(1)}, f32[192,128]{1,0:T(8,128)S(1)}, f32[704,128]{1,0:T(8,128)S(1)}, f32[640,128]...) custom-call(f32[1,768]{1,0:T(1,128)S(1)} %get-tuple-element.62.live, ...), custom_call_target="tpu_custom_call", output_to_operand_aliasing={{5}: (4, {})} | custom-call | tf_op jit(solution)/shard_map/global_kernel/pallas_call | solution.py:358
  23.4 1.6 %collective-permute-start.12 = (f32[160,128]{1,0:T(8,128)S(1)}, f32[160,128]{1,0:T(8,128)S(1)}, u32[]{:S(2)}, u32[]{:S(2)}) collective-permute-start(f32[160,128]{1,0:T(8,128)S(1)} %get-tuple-element.70), channel_id=1, source_target_pairs={{0,8},{4,12},{8,0},{12,4},{16,24},{20,28},{24,16},{28,20},{1,9},{5... | collective-permute-start | bytes 245768 | tf_op jit(solution)/shard_map/ppermute | solution.py:392
  25.0 1.5 %collective-permute-start.13 = (f32[160,128]{1,0:T(8,128)S(1)}, f32[160,128]{1,0:T(8,128)S(1)}, u32[]{:S(2)}, u32[]{:S(2)}) collective-permute-start(f32[160,128]{1,0:T(8,128)S(1)} %get-tuple-element.73), channel_id=1, source_target_pairs={{0,4},{4,0},{8,12},{12,8},{16,20},{20,16},{24,28},{28,24},{1,5},{5... | collective-permute-start | bytes 245768 | tf_op jit(solution)/shard_map/ppermute | solution.py:392
  26.5 0.4 collective-permute-start.14
  26.9 0.0 collective-permute-done.8.p_far
  26.9 1.4 %collective-permute-start.17 = (f32[640,128]{1,0:T(8,128)S(1)}, f32[640,128]{1,0:T(8,128)S(1)}, u32[]{:S(2)}, u32[]{:S(2)}) collective-permute-start(f32[640,128]{1,0:T(8,128)S(1)} %get-tuple-element.80), channel_id=1, source_target_pairs={{0,2},{1,3},{2,0},{3,1},{4,6},{5,7},{6,4},{7,5},{8,10},{9,11},{10,... | collective-permute-start | bytes 983048 | tf_op jit(solution)/shard_map/ppermute | solution.py:389
  28.4 0.2 collective-permute-start.7
  28.6 1.6 %collective-permute-done.13 = f32[160,128]{1,0:T(8,128)S(1)} collective-permute-done((f32[160,128]{1,0:T(8,128)S(1)}, f32[160,128]{1,0:T(8,128)S(1)}, u32[]{:S(2)}, u32[]{:S(2)}) %collective-permute-start.13) | collective-permute-done | bytes 81952 | tf_op jit(solution)/shard_map/ppermute | solution.py:392
  30.2 0.0 collective-permute-start.11
  30.2 1.6 %collective-permute-done.14 = f32[160,128]{1,0:T(8,128)S(1)} collective-permute-done((f32[160,128]{1,0:T(8,128)S(1)}, f32[160,128]{1,0:T(8,128)S(1)}, u32[]{:S(2)}, u32[]{:S(2)}) %collective-permute-start.14) | collective-permute-done | bytes 81952 | tf_op jit(solution)/shard_map/ppermute | solution.py:392
  31.9 2.7 %collective-permute-start.15 = (f32[160,128]{1,0:T(8,128)S(1)}, f32[160,128]{1,0:T(8,128)S(1)}, u32[]{:S(2)}, u32[]{:S(2)}) collective-permute-start(f32[160,128]{1,0:T(8,128)S(1)} %add_add_fusion), channel_id=1, source_target_pairs={{0,16},{4,20},{8,24},{12,28},{16,0},{20,4},{24,8},{28,12},{1,17},{... | collective-permute-start | bytes 245768 | tf_op jit(solution)/shard_map/ppermute | solution.py:392
  34.5 5.6 %pair_kernel.1 = (f32[64,768]{1,0:T(8,128)S(1)}, f32[64,256]{1,0:T(8,128)}, f32[64,768]{1,0:T(8,128)S(1)}) custom-call(f32[768,1]{1,0:T(8,128)S(1)} %get-tuple-element.59.live, bf16[192,512]{1,0:T(8,128)(2,1)S(1)} %bitcast.10, bf16[192,512]{1,0:T(8,128)(2,1)S(1)} %collective-permute-done.7.p_core, bf16[192,512]{1,0:T(8,128)(2,1)S(1)} %collective-permute-done.8.p_far, ...), custom_call_target="tpu_custom_call" | custom-call | tf_op jit(solution)/shard_map/pair_kernel/pallas_call | solution.py:358
  40.1 0.1 collective-permute-start.18
  40.2 2.0 %collective-permute-start.24 = (f32[160,128]{1,0:T(8,128)S(1)}, f32[160,128]{1,0:T(8,128)S(1)}, u32[]{:S(2)}, u32[]{:S(2)}) collective-permute-start(f32[160,128]{1,0:T(8,128)S(1)} %add.15.refs_0_), channel_id=1, source_target_pairs={{0,6},{1,7},{2,4},{3,5},{4,2},{5,3},{6,0},{7,1},{8,14},{9,15},{10,... | collective-permute-start | bytes 245768 | tf_op jit(solution)/shard_map/ppermute | solution.py:398
  42.1 0.6 %collective-permute-start.23 = (f32[160,128]{1,0:T(8,128)S(1)}, f32[160,128]{1,0:T(8,128)S(1)}, u32[]{:S(2)}, u32[]{:S(2)}) collective-permute-start(f32[160,128]{1,0:T(8,128)S(1)} %add.15.refs_0_), channel_id=1, source_target_pairs={{0,2},{1,3},{2,0},{3,1},{4,6},{5,7},{6,4},{7,5},{8,10},{9,11},{10,... | collective-permute-start | bytes 245768 | tf_op jit(solution)/shard_map/ppermute | solution.py:389
  42.7 1.0 %collective-permute-start.20 = (f32[160,128]{1,0:T(8,128)S(1)}, f32[160,128]{1,0:T(8,128)S(1)}, u32[]{:S(2)}, u32[]{:S(2)}) collective-permute-start(f32[160,128]{1,0:T(8,128)S(1)} %add.15.refs_0_), channel_id=1, source_target_pairs={{0,4},{4,0},{8,12},{12,8},{16,20},{20,16},{24,28},{28,24},{1,5},{5... | collective-permute-start | bytes 245768 | tf_op jit(solution)/shard_map/ppermute | solution.py:392
  43.8 2.1 %collective-permute-start.19 = (f32[64,768]{1,0:T(8,128)S(1)}, f32[64,768]{1,0:T(8,128)S(1)}, u32[]{:S(2)}, u32[]{:S(2)}) collective-permute-start(f32[64,768]{1,0:T(8,128)S(1)} %get-tuple-element.84), channel_id=1, source_target_pairs={{0,28},{4,0},{8,4},{12,8},{16,12},{20,16},{24,20},{28,24},{1,29},{... | collective-permute-start | bytes 589832 | tf_op jit(solution)/shard_map/ppermute | solution.py:476
  45.9 0.9 %start_kernel.1 = (bf16[512,1024]{1,0:T(8,128)(2,1)S(1)}, f32[192,512]{1,0:T(8,128)S(1)}) custom-call(f32[512,128]{1,0:T(8,128)S(1)} %get-tuple-element.69.s_own, f32[192,128]{1,0:T(8,128)S(1)} %get-tuple-element.88.y_own, f32[704,128]{1,0:T(8,128)S(1)} %collective-permute-done.16.y_core, f32[640,128]{1,0:T(8,128)S(1)} %collective-permute-done.17.far, ...), custom_call_target="tpu_custom_call" | custom-call | tf_op jit(solution)/shard_map/start_kernel/pallas_call | solution.py:358
  46.8 0.0 collective-permute-done.24.refs_5_
  46.8 0.6 %collective-permute-start.26 = (f32[160,128]{1,0:T(8,128)S(1)}, f32[160,128]{1,0:T(8,128)S(1)}, u32[]{:S(2)}, u32[]{:S(2)}) collective-permute-start(f32[160,128]{1,0:T(8,128)S(1)} %collective-permute-done.24.refs_5_), channel_id=1, source_target_pairs={{0,1},{1,0},{2,3},{3,2},{4,5},{5,4},{6,7},{7,6},{8,9},{9,8},{10,11... | collective-permute-start | bytes 245768 | tf_op jit(solution)/shard_map/ppermute | solution.py:389
  47.4 0.3 collective-permute-done.23.refs_4_
  47.7 0.0 collective-permute-start.25
  47.7 2.5 %collective-permute-done.20.refs_1_ = f32[160,128]{1,0:T(8,128)S(1)} collective-permute-done((f32[160,128]{1,0:T(8,128)S(1)}, f32[160,128]{1,0:T(8,128)S(1)}, u32[]{:S(2)}, u32[]{:S(2)}) %collective-permute-start.20) | collective-permute-done | bytes 81952 | tf_op jit(solution)/shard_map/ppermute | solution.py:392
  50.3 0.0 collective-permute-done.26.refs_7_
  50.3 0.0 collective-permute-done.25.refs_6_
  50.3 1.3 %collective-permute-done.22.refs_3_ = f32[160,128]{1,0:T(8,128)S(1)} collective-permute-done((f32[160,128]{1,0:T(8,128)S(1)}, f32[160,128]{1,0:T(8,128)S(1)}, u32[]{:S(2)}, u32[]{:S(2)}) %collective-permute-start.22) | collective-permute-done | bytes 81952 | tf_op jit(solution)/shard_map/ppermute | solution.py:389
  51.5 1.8 %back_kernel.1 = (f32[128,512]{1,0:T(8,128)}, f32[192,512]{1,0:T(8,128)}) custom-call(f32[160,128]{1,0:T(8,128)S(1)} %add.15.refs_0_, f32[160,128]{1,0:T(8,128)S(1)} %collective-permute-done.20.refs_1_, f32[160,128]{1,0:T(8,128)S(1)} %collective-permute-done.21.refs_2_, f32[160,128]{1,0:T(8,128)S(1)} %collective-permute-done.22.refs_3_, ...), custom_call_target="tpu_custom_call" | custom-call | flops 452984832 | tf_op jit(solution)/shard_map/back_kernel/pallas_call | solution.py:358
  53.4 0.0 collective-permute-done.19.came
  53.4 0.7 %finish_kernel.1 = (f32[64,256]{1,0:T(8,128)}, f32[64,512]{1,0:T(8,128)}) custom-call(f32[64,768]{1,0:T(8,128)S(1)} %get-tuple-element.75.own_terms, f32[64,768]{1,0:T(8,128)S(1)} %collective-permute-done.19.came), custom_call_target="tpu_custom_call" | custom-call | tf_op jit(solution)/shard_map/finish_kernel/pallas_call | solution.py:358
  (19 shorter events, 0.1 us)
Async XLA Ops:
  0.6 8.7 %collective-permute-start.3 = (bf16[192,512]{1,0:T(8,128)(2,1)}, bf16[192,512]{1,0:T(8,128)(2,1)S(1)}, u32[]{:S(2)}, u32[]{:S(2)}) collective-permute-start(bf16[192,512]{1,0:T(8,128)(2,1)} %bitcast.13), channel_id=1, source_target_pairs={{0,2},{1,3},{2,0},{3,1},{4,6},{5,7},{6,4},{7,5},{8,10},{9,11},{10,... | collective-permute-start | bytes 589832 | tf_op jit(solution)/shard_map/ppermute | solution.py:389
  3.7 13.8 %copy-start.1 = (bf16[1,192,512]{2,1,0:T(8,128)(2,1)S(1)}, bf16[1,192,512]{2,1,0:T(8,128)(2,1)}, u32[]{:S(2)}) copy-start(bf16[1,192,512]{2,1,0:T(8,128)(2,1)} %param.12) | copy-start | bytes 589828
  3.7 15.6 %copy-start = (f32[128,512]{1,0:T(8,128)S(1)}, f32[128,512]{1,0:T(8,128)}, u32[]{:S(2)}) copy-start(f32[128,512]{1,0:T(8,128)} %base.1) | copy-start | bytes 786436
  5.2 9.7 %collective-permute-start = (f32[192,768]{1,0:T(8,128)S(1)}, f32[192,768]{1,0:T(8,128)S(1)}, u32[]{:S(2)}, u32[]{:S(2)}) collective-permute-start(f32[192,768]{1,0:T(8,128)S(1)} %get-tuple-element.51.x_own), channel_id=1, source_target_pairs={{0,1},{1,0},{2,3},{3,2},{4,5},{5,4},{6,7},{7,6},{8,9},{9,8},{10,11... | collective-permute-start | bytes 1769480 | tf_op jit(solution)/shard_map/ppermute | solution.py:389
  5.2 9.6 %collective-permute-start.1 = (f32[192,768]{1,0:T(8,128)S(1)}, f32[192,768]{1,0:T(8,128)S(1)}, u32[]{:S(2)}, u32[]{:S(2)}) collective-permute-start(f32[192,768]{1,0:T(8,128)S(1)} %get-tuple-element.52.k_own), channel_id=1, source_target_pairs={{0,1},{1,0},{2,3},{3,2},{4,5},{5,4},{6,7},{7,6},{8,9},{9,8},{10,11... | collective-permute-start | bytes 1769480 | tf_op jit(solution)/shard_map/ppermute | solution.py:389
  5.7 7.3 %collective-permute-start.4 = (f32[392,128]{1,0:T(8,128)S(1)}, f32[392,128]{1,0:T(8,128)S(1)}, u32[]{:S(2)}, u32[]{:S(2)}) collective-permute-start(f32[392,128]{1,0:T(8,128)S(1)} %get-tuple-element.54), channel_id=1, source_target_pairs={{0,2},{1,3},{2,0},{3,1},{4,6},{5,7},{6,4},{7,5},{8,10},{9,11},{10,... | collective-permute-start | bytes 602120 | tf_op jit(solution)/shard_map/ppermute | solution.py:389
  9.3 3.8 %collective-permute-start.5 = (bf16[192,512]{1,0:T(8,128)(2,1)S(1)}, bf16[192,512]{1,0:T(8,128)(2,1)S(1)}, u32[]{:S(2)}, u32[]{:S(2)}) collective-permute-start(bf16[192,512]{1,0:T(8,128)(2,1)S(1)} %collective-permute-done.3.g_far), channel_id=1, source_target_pairs={{0,1},{1,0},{2,3},{3,2},{4,5},{5,4},{6,7},{7,6},{8,9},{9,8},{10,11... | collective-permute-start | bytes 589832 | tf_op jit(solution)/shard_map/ppermute | solution.py:389
  9.3 8.2 %collective-permute-start.9 = (f32[400,128]{1,0:T(8,128)S(1)}, f32[400,128]{1,0:T(8,128)S(1)}, u32[]{:S(2)}, u32[]{:S(2)}) collective-permute-start(f32[400,128]{1,0:T(8,128)S(1)} %get-tuple-element.63), channel_id=1, source_target_pairs={{0,2},{1,3},{2,0},{3,1},{4,6},{5,7},{6,4},{7,5},{8,10},{9,11},{10,... | collective-permute-start | bytes 614408 | tf_op jit(solution)/shard_map/ppermute | solution.py:389
  13.1 1.7 %collective-permute-start.6 = (f32[392,128]{1,0:T(8,128)S(1)}, f32[392,128]{1,0:T(8,128)S(1)}, u32[]{:S(2)}, u32[]{:S(2)}) collective-permute-start(f32[392,128]{1,0:T(8,128)S(1)} %collective-permute-done.4.far), channel_id=1, source_target_pairs={{0,1},{1,0},{2,3},{3,2},{4,5},{5,4},{6,7},{7,6},{8,9},{9,8},{10,11... | collective-permute-start | bytes 602120 | tf_op jit(solution)/shard_map/ppermute | solution.py:389
  13.1 1.7 %collective-permute-start.2 = (bf16[192,512]{1,0:T(8,128)(2,1)S(1)}, bf16[192,512]{1,0:T(8,128)(2,1)S(1)}, u32[]{:S(2)}, u32[]{:S(2)}) collective-permute-start(bf16[192,512]{1,0:T(8,128)(2,1)S(1)} %get-tuple-element.53.g_own), channel_id=1, source_target_pairs={{0,1},{1,0},{2,3},{3,2},{4,5},{5,4},{6,7},{7,6},{8,9},{9,8},{10,11... | collective-permute-start | bytes 589832 | tf_op jit(solution)/shard_map/ppermute | solution.py:389
  17.5 1.8 %collective-permute-start.10 = (f32[400,128]{1,0:T(8,128)S(1)}, f32[400,128]{1,0:T(8,128)S(1)}, u32[]{:S(2)}, u32[]{:S(2)}) collective-permute-start(f32[400,128]{1,0:T(8,128)S(1)} %collective-permute-done.9.far), channel_id=1, source_target_pairs={{0,1},{1,0},{2,3},{3,2},{4,5},{5,4},{6,7},{7,6},{8,9},{9,8},{10,11... | collective-permute-start | bytes 614408 | tf_op jit(solution)/shard_map/ppermute | solution.py:389
  17.5 9.4 %collective-permute-start.8 = (bf16[192,512]{1,0:T(8,128)(2,1)S(1)}, bf16[192,512]{1,0:T(8,128)(2,1)S(1)}, u32[]{:S(2)}, u32[]{:S(2)}) collective-permute-start(bf16[192,512]{1,0:T(8,128)(2,1)S(1)} %bitcast.8), channel_id=1, source_target_pairs={{0,2},{1,3},{2,0},{3,1},{4,6},{5,7},{6,4},{7,5},{8,10},{9,11},{10,... | collective-permute-start | bytes 589832 | tf_op jit(solution)/shard_map/ppermute | solution.py:389
  23.4 5.0 %collective-permute-start.12 = (f32[160,128]{1,0:T(8,128)S(1)}, f32[160,128]{1,0:T(8,128)S(1)}, u32[]{:S(2)}, u32[]{:S(2)}) collective-permute-start(f32[160,128]{1,0:T(8,128)S(1)} %get-tuple-element.70), channel_id=1, source_target_pairs={{0,8},{4,12},{8,0},{12,4},{16,24},{20,28},{24,16},{28,20},{1,9},{5... | collective-permute-start | bytes 245768 | tf_op jit(solution)/shard_map/ppermute | solution.py:392
  25.0 5.2 %collective-permute-start.13 = (f32[160,128]{1,0:T(8,128)S(1)}, f32[160,128]{1,0:T(8,128)S(1)}, u32[]{:S(2)}, u32[]{:S(2)}) collective-permute-start(f32[160,128]{1,0:T(8,128)S(1)} %get-tuple-element.73), channel_id=1, source_target_pairs={{0,4},{4,0},{8,12},{12,8},{16,20},{20,16},{24,28},{28,24},{1,5},{5... | collective-permute-start | bytes 245768 | tf_op jit(solution)/shard_map/ppermute | solution.py:392
  26.5 5.3 %collective-permute-start.14 = (f32[160,128]{1,0:T(8,128)S(1)}, f32[160,128]{1,0:T(8,128)S(1)}, u32[]{:S(2)}, u32[]{:S(2)}) collective-permute-start(f32[160,128]{1,0:T(8,128)S(1)} %get-tuple-element.73), channel_id=1, source_target_pairs={{0,12},{4,8},{8,4},{12,0},{16,28},{20,24},{24,20},{28,16},{1,13},{... | collective-permute-start | bytes 245768 | tf_op jit(solution)/shard_map/ppermute | solution.py:392
  26.9 13.2 %collective-permute-start.16 = (f32[704,128]{1,0:T(8,128)S(1)}, f32[704,128]{1,0:T(8,128)S(1)}, u32[]{:S(2)}, u32[]{:S(2)}) collective-permute-start(f32[704,128]{1,0:T(8,128)S(1)} %get-tuple-element.79), channel_id=1, source_target_pairs={{0,1},{1,0},{2,3},{3,2},{4,5},{5,4},{6,7},{7,6},{8,9},{9,8},{10,11... | collective-permute-start | bytes 1081352 | tf_op jit(solution)/shard_map/ppermute | solution.py:389
  26.9 13.2 %collective-permute-start.17 = (f32[640,128]{1,0:T(8,128)S(1)}, f32[640,128]{1,0:T(8,128)S(1)}, u32[]{:S(2)}, u32[]{:S(2)}) collective-permute-start(f32[640,128]{1,0:T(8,128)S(1)} %get-tuple-element.80), channel_id=1, source_target_pairs={{0,2},{1,3},{2,0},{3,1},{4,6},{5,7},{6,4},{7,5},{8,10},{9,11},{10,... | collective-permute-start | bytes 983048 | tf_op jit(solution)/shard_map/ppermute | solution.py:389
  28.4 6.1 %collective-permute-start.7 = (bf16[192,512]{1,0:T(8,128)(2,1)S(1)}, bf16[192,512]{1,0:T(8,128)(2,1)S(1)}, u32[]{:S(2)}, u32[]{:S(2)}) collective-permute-start(bf16[192,512]{1,0:T(8,128)(2,1)S(1)} %bitcast.9), channel_id=1, source_target_pairs={{0,1},{1,0},{2,3},{3,2},{4,5},{5,4},{6,7},{7,6},{8,9},{9,8},{10,11... | collective-permute-start | bytes 589832 | tf_op jit(solution)/shard_map/ppermute | solution.py:389
  30.2 4.3 %collective-permute-start.11 = (bf16[192,512]{1,0:T(8,128)(2,1)S(1)}, bf16[192,512]{1,0:T(8,128)(2,1)S(1)}, u32[]{:S(2)}, u32[]{:S(2)}) collective-permute-start(bf16[192,512]{1,0:T(8,128)(2,1)S(1)} %collective-permute-done.8.p_far), channel_id=1, source_target_pairs={{0,1},{1,0},{2,3},{3,2},{4,5},{5,4},{6,7},{7,6},{8,9},{9,8},{10,11... | collective-permute-start | bytes 589832 | tf_op jit(solution)/shard_map/ppermute | solution.py:389
  31.9 8.2 %collective-permute-start.15 = (f32[160,128]{1,0:T(8,128)S(1)}, f32[160,128]{1,0:T(8,128)S(1)}, u32[]{:S(2)}, u32[]{:S(2)}) collective-permute-start(f32[160,128]{1,0:T(8,128)S(1)} %add_add_fusion), channel_id=1, source_target_pairs={{0,16},{4,20},{8,24},{12,28},{16,0},{20,4},{24,8},{28,12},{1,17},{... | collective-permute-start | bytes 245768 | tf_op jit(solution)/shard_map/ppermute | solution.py:392
  40.1 3.6 %collective-permute-start.18 = (f32[640,128]{1,0:T(8,128)S(1)}, f32[640,128]{1,0:T(8,128)S(1)}, u32[]{:S(2)}, u32[]{:S(2)}) collective-permute-start(f32[640,128]{1,0:T(8,128)S(1)} %collective-permute-done.17.far), channel_id=1, source_target_pairs={{0,1},{1,0},{2,3},{3,2},{4,5},{5,4},{6,7},{7,6},{8,9},{9,8},{10,11... | collective-permute-start | bytes 983048 | tf_op jit(solution)/shard_map/ppermute | solution.py:389
  40.2 6.6 %collective-permute-start.24 = (f32[160,128]{1,0:T(8,128)S(1)}, f32[160,128]{1,0:T(8,128)S(1)}, u32[]{:S(2)}, u32[]{:S(2)}) collective-permute-start(f32[160,128]{1,0:T(8,128)S(1)} %add.15.refs_0_), channel_id=1, source_target_pairs={{0,6},{1,7},{2,4},{3,5},{4,2},{5,3},{6,0},{7,1},{8,14},{9,15},{10,... | collective-permute-start | bytes 245768 | tf_op jit(solution)/shard_map/ppermute | solution.py:398
  42.1 5.6 %collective-permute-start.23 = (f32[160,128]{1,0:T(8,128)S(1)}, f32[160,128]{1,0:T(8,128)S(1)}, u32[]{:S(2)}, u32[]{:S(2)}) collective-permute-start(f32[160,128]{1,0:T(8,128)S(1)} %add.15.refs_0_), channel_id=1, source_target_pairs={{0,2},{1,3},{2,0},{3,1},{4,6},{5,7},{6,4},{7,5},{8,10},{9,11},{10,... | collective-permute-start | bytes 245768 | tf_op jit(solution)/shard_map/ppermute | solution.py:389
  42.7 7.5 %collective-permute-start.20 = (f32[160,128]{1,0:T(8,128)S(1)}, f32[160,128]{1,0:T(8,128)S(1)}, u32[]{:S(2)}, u32[]{:S(2)}) collective-permute-start(f32[160,128]{1,0:T(8,128)S(1)} %add.15.refs_0_), channel_id=1, source_target_pairs={{0,4},{4,0},{8,12},{12,8},{16,20},{20,16},{24,28},{28,24},{1,5},{5... | collective-permute-start | bytes 245768 | tf_op jit(solution)/shard_map/ppermute | solution.py:392
  43.8 9.6 %collective-permute-start.19 = (f32[64,768]{1,0:T(8,128)S(1)}, f32[64,768]{1,0:T(8,128)S(1)}, u32[]{:S(2)}, u32[]{:S(2)}) collective-permute-start(f32[64,768]{1,0:T(8,128)S(1)} %get-tuple-element.84), channel_id=1, source_target_pairs={{0,28},{4,0},{8,4},{12,8},{16,12},{20,16},{24,20},{28,24},{1,29},{... | collective-permute-start | bytes 589832 | tf_op jit(solution)/shard_map/ppermute | solution.py:476
  45.9 4.4 %collective-permute-start.21 = (f32[160,128]{1,0:T(8,128)S(1)}, f32[160,128]{1,0:T(8,128)S(1)}, u32[]{:S(2)}, u32[]{:S(2)}) collective-permute-start(f32[160,128]{1,0:T(8,128)S(1)} %add.15.refs_0_), channel_id=1, source_target_pairs={{0,1},{1,0},{2,3},{3,2},{4,5},{5,4},{6,7},{7,6},{8,9},{9,8},{10,11... | collective-permute-start | bytes 245768 | tf_op jit(solution)/shard_map/ppermute | solution.py:389
  46.8 3.5 %collective-permute-start.26 = (f32[160,128]{1,0:T(8,128)S(1)}, f32[160,128]{1,0:T(8,128)S(1)}, u32[]{:S(2)}, u32[]{:S(2)}) collective-permute-start(f32[160,128]{1,0:T(8,128)S(1)} %collective-permute-done.24.refs_5_), channel_id=1, source_target_pairs={{0,1},{1,0},{2,3},{3,2},{4,5},{5,4},{6,7},{7,6},{8,9},{9,8},{10,11... | collective-permute-start | bytes 245768 | tf_op jit(solution)/shard_map/ppermute | solution.py:389
  47.7 2.6 %collective-permute-start.25 = (f32[160,128]{1,0:T(8,128)S(1)}, f32[160,128]{1,0:T(8,128)S(1)}, u32[]{:S(2)}, u32[]{:S(2)}) collective-permute-start(f32[160,128]{1,0:T(8,128)S(1)} %collective-permute-done.23.refs_4_), channel_id=1, source_target_pairs={{0,1},{1,0},{2,3},{3,2},{4,5},{5,4},{6,7},{7,6},{8,9},{9,8},{10,11... | collective-permute-start | bytes 245768 | tf_op jit(solution)/shard_map/ppermute | solution.py:389
  50.3 1.3 %collective-permute-start.22 = (f32[160,128]{1,0:T(8,128)S(1)}, f32[160,128]{1,0:T(8,128)S(1)}, u32[]{:S(2)}, u32[]{:S(2)}) collective-permute-start(f32[160,128]{1,0:T(8,128)S(1)} %collective-permute-done.20.refs_1_), channel_id=1, source_target_pairs={{0,1},{1,0},{2,3},{3,2},{4,5},{5,4},{6,7},{7,6},{8,9},{9,8},{10,11... | collective-permute-start | bytes 245768 | tf_op jit(solution)/shard_map/ppermute | solution.py:389

commit v9 on v8

--- a/solution.py
+++ b/solution.py
@@ -460,8 +460,9 @@
         s_own, *y_all, cross,
     )
 
-    here = (total, after(block_swap(total, 1), scaled))
-    there = (after(tile_swap(total, 2), scaled), after(diagonal_swap(total), scaled))
+    near = after(block_swap(total, 1), scaled)
+    here = (total, near)
+    there = (after(tile_swap(total, 2), near), after(diagonal_swap(total), near))
     sums = []
     for pieces in (here, there):
         sums += [*pieces, *(tile_swap(piece, 1) for piece in pieces)]

time: 54.2 us -> 53.2 us (0.982)
  waiting for transfers between devices: 13.5 us -> 12.6 us
    ppermute x5, waiting for transfers between devices: 5.76 us -> 3.23 us  [block_swap(): return lax.ppermute(value, 'tm', [(i, i ^ mask) for i in range(blocks)])]
    ppermute x1, waiting for transfers between devices: 0.01 us -> 1.34 us  [diagonal_swap(): return lax.ppermute(value, ('tm', 'tile'), pairs)]
  transfers between devices with their start and end apart: 27 -> 27, of which waited for: 9 -> 10; matrix products, arithmetic and copies ran while one was open for 0% -> 0% of each run, Pallas kernels for 29% -> 30%
where the time goes in v9:
time: 53.2 us; the launch traced here: 53 us
  starting transfers between devices  22.4 us (42%)
  Pallas kernels  16.6 us (31%)
  waiting for transfers between devices  12.6 us (24%)
  between operations  1.37 us (3%)
    pallas_call x7, Pallas kernels, call(): pl.pallas_call(kernel, out_shape=[jax.ShapeDtypeStruct(shape, dtype) for...  16.6 us
    ppermute x20, starting transfers between devices, tile_swap(): return lax.ppermute(value, 'tile', [(i, i ^ mask) for i in range(4)])  11.1 us
    ppermute x20, waiting for transfers between devices, tile_swap(): return lax.ppermute(value, 'tile', [(i, i ^ mask) for i in range(4)])  8.03 us
    ppermute x5, starting transfers between devices, block_swap(): return lax.ppermute(value, 'tm', [(i, i ^ mask) for i in range(blocks)])  7.29 us
    ppermute x5, waiting for transfers between devices, block_swap(): return lax.ppermute(value, 'tm', [(i, i ^ mask) for i in range(blocks)])  3.23 us
    ppermute x1, starting transfers between devices, shards(): lax.ppermute(next_terms, 'tm', [(i, (i - 1) % blocks) for i in range(bloc...  2.12 us
    ppermute x1, starting transfers between devices, diagonal_swap(): return lax.ppermute(value, ('tm', 'tile'), pairs)  1.89 us
    ppermute x1, waiting for transfers between devices, diagonal_swap(): return lax.ppermute(value, ('tm', 'tile'), pairs)  1.34 us
  transfers between devices with their start and end apart: 27, of which 10 were waited for; matrix products, arithmetic and copies ran while one was open for 0% of the time, Pallas kernels for 30%

profile of v9, /device:TPU:0, one launch (start us, length us, event | category | flops | bytes accessed | tf_op | source)
XLA Modules:
  0.0 53.0 jit_solution(4747158592295928787)
XLA Ops:
  0.6 3.0 %collective-permute-start.3 = (bf16[192,512]{1,0:T(8,128)(2,1)}, bf16[192,512]{1,0:T(8,128)(2,1)S(1)}, u32[]{:S(2)}, u32[]{:S(2)}) collective-permute-start(bf16[192,512]{1,0:T(8,128)(2,1)} %bitcast.13), channel_id=1, source_target_pairs={{0,2},{1,3},{2,0},{3,1},{4,6},{5,7},{6,4},{7,5},{8,10},{9,11},{10,... | collective-permute-start | bytes 589832 | tf_op jit(solution)/shard_map/ppermute | solution.py:389
  3.7 1.5 %pack_kernel.1 = (f32[392,128]{1,0:T(8,128)S(1)}, f32[400,128]{1,0:T(8,128)S(1)}, f32[192,768]{1,0:T(8,128)S(1)}, f32[192,768]{1,0:T(8,128)S(1)}, bf16[192,512]{...) custom-call(f32[192,768]{1,0:T(8,128)} %bitcast.11, f32[192,768]{1,0:T(8,128)} %bitcast.12, ...), custom_call_target="tpu_custom_call" | custom-call | tf_op jit(solution)/shard_map/pack_kernel/pallas_call | solution.py:358
  5.2 0.1 collective-permute-start
  5.2 0.5 collective-permute-start.1
  5.7 0.0 collective-permute-start.4
  5.8 3.5 %collective-permute-done.3.g_far = bf16[192,512]{1,0:T(8,128)(2,1)S(1)} collective-permute-done((bf16[192,512]{1,0:T(8,128)(2,1)}, bf16[192,512]{1,0:T(8,128)(2,1)S(1)}, u32[]{:S(2)}, u32[]{:S(2)}) %collective-permute-start.3) | collective-permute-done | bytes 196640 | tf_op jit(solution)/shard_map/ppermute | solution.py:389
  9.3 0.0 collective-permute-start.5
  9.3 2.4 %collective-permute-start.9 = (f32[400,128]{1,0:T(8,128)S(1)}, f32[400,128]{1,0:T(8,128)S(1)}, u32[]{:S(2)}, u32[]{:S(2)}) collective-permute-start(f32[400,128]{1,0:T(8,128)S(1)} %get-tuple-element.63), channel_id=1, source_target_pairs={{0,2},{1,3},{2,0},{3,1},{4,6},{5,7},{6,4},{7,5},{8,10},{9,11},{10,... | collective-permute-start | bytes 614408 | tf_op jit(solution)/shard_map/ppermute | solution.py:389
  11.7 1.4 %collective-permute-done.4.far = f32[392,128]{1,0:T(8,128)S(1)} collective-permute-done((f32[392,128]{1,0:T(8,128)S(1)}, f32[392,128]{1,0:T(8,128)S(1)}, u32[]{:S(2)}, u32[]{:S(2)}) %collective-permute-start.4) | collective-permute-done | bytes 200736 | tf_op jit(solution)/shard_map/ppermute | solution.py:389
  13.1 0.0 collective-permute-done.5.g_cross
  13.1 0.0 collective-permute-start.6
  13.1 0.5 collective-permute-start.2
  14.2 0.6 %collective-permute-done.2.g_core = bf16[192,512]{1,0:T(8,128)(2,1)S(1)} collective-permute-done((bf16[192,512]{1,0:T(8,128)(2,1)S(1)}, bf16[192,512]{1,0:T(8,128)(2,1)S(1)}, u32[]{:S(2)}, u32[]{:S(2)}) %collective-permute-start.2) | collective-permute-done | bytes 196640 | tf_op jit(solution)/shard_map/ppermute | solution.py:389
  14.8 0.0 collective-permute-done.x_core
  14.8 0.0 collective-permute-done.1.k_core
  14.8 0.0 collective-permute-done.6.cross
  14.8 2.0 %prepare_kernel.1 = (bf16[1536,768]{1,0:T(8,128)(2,1)S(1)}, bf16[1536,768]{1,0:T(8,128)(2,1)S(1)}, bf16[768,512]{1,0:T(8,128)(2,1)S(1)}, f32[768,1]{1,0:T(8,128)...) custom-call(s32[1]{0:T(128)S(6)} %copy.15.sizes, ...), custom_call_target="tpu_custom_call" | custom-call | tf_op jit(solution)/shard_map/prepare_kernel/pallas_call | solution.py:358
  16.8 0.7 %collective-permute-done.9.far = f32[400,128]{1,0:T(8,128)S(1)} collective-permute-done((f32[400,128]{1,0:T(8,128)S(1)}, f32[400,128]{1,0:T(8,128)S(1)}, u32[]{:S(2)}, u32[]{:S(2)}) %collective-permute-start.9) | collective-permute-done | bytes 204832 | tf_op jit(solution)/shard_map/ppermute | solution.py:389
  17.5 0.0 collective-permute-start.10
  17.5 1.7 %collective-permute-start.8 = (bf16[192,512]{1,0:T(8,128)(2,1)S(1)}, bf16[192,512]{1,0:T(8,128)(2,1)S(1)}, u32[]{:S(2)}, u32[]{:S(2)}) collective-permute-start(bf16[192,512]{1,0:T(8,128)(2,1)S(1)} %bitcast.8), channel_id=1, source_target_pairs={{0,2},{1,3},{2,0},{3,1},{4,6},{5,7},{6,4},{7,5},{8,10},{9,11},{10,... | collective-permute-start | bytes 589832 | tf_op jit(solution)/shard_map/ppermute | solution.py:389
  19.2 0.0 collective-permute-done.10.cross
  19.2 4.1 %global_kernel.1 = (f32[160,128]{1,0:T(8,128)S(1)}, f32[160,128]{1,0:T(8,128)S(1)}, f32[192,128]{1,0:T(8,128)S(1)}, f32[704,128]{1,0:T(8,128)S(1)}, f32[640,128]...) custom-call(f32[1,768]{1,0:T(1,128)S(1)} %get-tuple-element.62.live, ...), custom_call_target="tpu_custom_call", output_to_operand_aliasing={{5}: (4, {})} | custom-call | tf_op jit(solution)/shard_map/global_kernel/pallas_call | solution.py:358
  23.4 1.6 %collective-permute-start.12 = (f32[160,128]{1,0:T(8,128)S(1)}, f32[160,128]{1,0:T(8,128)S(1)}, u32[]{:S(2)}, u32[]{:S(2)}) collective-permute-start(f32[160,128]{1,0:T(8,128)S(1)} %get-tuple-element.70), channel_id=1, source_target_pairs={{0,8},{4,12},{8,0},{12,4},{16,24},{20,28},{24,16},{28,20},{1,9},{5... | collective-permute-start | bytes 245768 | tf_op jit(solution)/shard_map/ppermute | solution.py:392
  25.0 1.5 %collective-permute-start.13 = (f32[160,128]{1,0:T(8,128)S(1)}, f32[160,128]{1,0:T(8,128)S(1)}, u32[]{:S(2)}, u32[]{:S(2)}) collective-permute-start(f32[160,128]{1,0:T(8,128)S(1)} %get-tuple-element.73), channel_id=1, source_target_pairs={{0,4},{4,0},{8,12},{12,8},{16,20},{20,16},{24,28},{28,24},{1,5},{5... | collective-permute-start | bytes 245768 | tf_op jit(solution)/shard_map/ppermute | solution.py:392
  26.5 0.4 collective-permute-start.14
  26.9 0.0 collective-permute-start.16
  26.9 0.0 collective-permute-done.8.p_far
  26.9 1.4 %collective-permute-start.17 = (f32[640,128]{1,0:T(8,128)S(1)}, f32[640,128]{1,0:T(8,128)S(1)}, u32[]{:S(2)}, u32[]{:S(2)}) collective-permute-start(f32[640,128]{1,0:T(8,128)S(1)} %get-tuple-element.80), channel_id=1, source_target_pairs={{0,2},{1,3},{2,0},{3,1},{4,6},{5,7},{6,4},{7,5},{8,10},{9,11},{10,... | collective-permute-start | bytes 983048 | tf_op jit(solution)/shard_map/ppermute | solution.py:389
  28.4 0.0 collective-permute-done.12
  28.4 0.2 collective-permute-start.7
  28.6 1.6 %collective-permute-done.13 = f32[160,128]{1,0:T(8,128)S(1)} collective-permute-done((f32[160,128]{1,0:T(8,128)S(1)}, f32[160,128]{1,0:T(8,128)S(1)}, u32[]{:S(2)}, u32[]{:S(2)}) %collective-permute-start.13) | collective-permute-done | bytes 81952 | tf_op jit(solution)/shard_map/ppermute | solution.py:392
  30.2 0.0 collective-permute-start.11
  30.2 1.6 %collective-permute-done.14 = f32[160,128]{1,0:T(8,128)S(1)} collective-permute-done((f32[160,128]{1,0:T(8,128)S(1)}, f32[160,128]{1,0:T(8,128)S(1)}, u32[]{:S(2)}, u32[]{:S(2)}) %collective-permute-start.14) | collective-permute-done | bytes 81952 | tf_op jit(solution)/shard_map/ppermute | solution.py:392
  31.9 2.7 %collective-permute-start.15 = (f32[160,128]{1,0:T(8,128)S(1)}, f32[160,128]{1,0:T(8,128)S(1)}, u32[]{:S(2)}, u32[]{:S(2)}) collective-permute-start(f32[160,128]{1,0:T(8,128)S(1)} %add_add_fusion), channel_id=1, source_target_pairs={{0,16},{4,20},{8,24},{12,28},{16,0},{20,4},{24,8},{28,12},{1,17},{... | collective-permute-start | bytes 245768 | tf_op jit(solution)/shard_map/ppermute | solution.py:392
  34.5 5.6 %pair_kernel.1 = (f32[64,768]{1,0:T(8,128)S(1)}, f32[64,256]{1,0:T(8,128)}, f32[64,768]{1,0:T(8,128)S(1)}) custom-call(f32[768,1]{1,0:T(8,128)S(1)} %get-tuple-element.59.live, bf16[192,512]{1,0:T(8,128)(2,1)S(1)} %bitcast.10, bf16[192,512]{1,0:T(8,128)(2,1)S(1)} %collective-permute-done.7.p_core, bf16[192,512]{1,0:T(8,128)(2,1)S(1)} %collective-permute-done.8.p_far, ...), custom_call_target="tpu_custom_call" | custom-call | tf_op jit(solution)/shard_map/pair_kernel/pallas_call | solution.py:358
  40.1 0.1 collective-permute-start.18
  40.2 1.1 %collective-permute-start.20 = (f32[160,128]{1,0:T(8,128)S(1)}, f32[160,128]{1,0:T(8,128)S(1)}, u32[]{:S(2)}, u32[]{:S(2)}) collective-permute-start(f32[160,128]{1,0:T(8,128)S(1)} %add.15.refs_0_), channel_id=1, source_target_pairs={{0,4},{4,0},{8,12},{12,8},{16,20},{20,16},{24,28},{28,24},{1,5},{5... | collective-permute-start | bytes 245768 | tf_op jit(solution)/shard_map/ppermute | solution.py:392
  41.3 1.9 %collective-permute-start.24 = (f32[160,128]{1,0:T(8,128)S(1)}, f32[160,128]{1,0:T(8,128)S(1)}, u32[]{:S(2)}, u32[]{:S(2)}) collective-permute-start(f32[160,128]{1,0:T(8,128)S(1)} %add.15.refs_0_), channel_id=1, source_target_pairs={{0,6},{1,7},{2,4},{3,5},{4,2},{5,3},{6,0},{7,1},{8,14},{9,15},{10,... | collective-permute-start | bytes 245768 | tf_op jit(solution)/shard_map/ppermute | solution.py:398
  43.2 0.6 %collective-permute-start.23 = (f32[160,128]{1,0:T(8,128)S(1)}, f32[160,128]{1,0:T(8,128)S(1)}, u32[]{:S(2)}, u32[]{:S(2)}) collective-permute-start(f32[160,128]{1,0:T(8,128)S(1)} %add.15.refs_0_), channel_id=1, source_target_pairs={{0,2},{1,3},{2,0},{3,1},{4,6},{5,7},{6,4},{7,5},{8,10},{9,11},{10,... | collective-permute-start | bytes 245768 | tf_op jit(solution)/shard_map/ppermute | solution.py:389
  43.7 2.1 %collective-permute-start.19 = (f32[64,768]{1,0:T(8,128)S(1)}, f32[64,768]{1,0:T(8,128)S(1)}, u32[]{:S(2)}, u32[]{:S(2)}) collective-permute-start(f32[64,768]{1,0:T(8,128)S(1)} %get-tuple-element.84), channel_id=1, source_target_pairs={{0,28},{4,0},{8,4},{12,8},{16,12},{20,16},{24,20},{28,24},{1,29},{... | collective-permute-start | bytes 589832 | tf_op jit(solution)/shard_map/ppermute | solution.py:477
  45.9 0.9 %start_kernel.1 = (bf16[512,1024]{1,0:T(8,128)(2,1)S(1)}, f32[192,512]{1,0:T(8,128)S(1)}) custom-call(f32[512,128]{1,0:T(8,128)S(1)} %get-tuple-element.69.s_own, f32[192,128]{1,0:T(8,128)S(1)} %get-tuple-element.88.y_own, f32[704,128]{1,0:T(8,128)S(1)} %collective-permute-done.16.y_core, f32[640,128]{1,0:T(8,128)S(1)} %collective-permute-done.17.far, ...), custom_call_target="tpu_custom_call" | custom-call | tf_op jit(solution)/shard_map/start_kernel/pallas_call | solution.py:358
  46.8 1.3 %collective-permute-done.24.refs_5_ = f32[160,128]{1,0:T(8,128)S(1)} collective-permute-done((f32[160,128]{1,0:T(8,128)S(1)}, f32[160,128]{1,0:T(8,128)S(1)}, u32[]{:S(2)}, u32[]{:S(2)}) %collective-permute-start.24) | collective-permute-done | bytes 81952 | tf_op jit(solution)/shard_map/ppermute | solution.py:398
  48.1 0.9 %collective-permute-done.23.refs_4_ = f32[160,128]{1,0:T(8,128)S(1)} collective-permute-done((f32[160,128]{1,0:T(8,128)S(1)}, f32[160,128]{1,0:T(8,128)S(1)}, u32[]{:S(2)}, u32[]{:S(2)}) %collective-permute-start.23) | collective-permute-done | bytes 81952 | tf_op jit(solution)/shard_map/ppermute | solution.py:389
  49.1 0.5 collective-permute-start.22
  49.6 0.8 %collective-permute-done.25.refs_6_ = f32[160,128]{1,0:T(8,128)S(1)} collective-permute-done((f32[160,128]{1,0:T(8,128)S(1)}, f32[160,128]{1,0:T(8,128)S(1)}, u32[]{:S(2)}, u32[]{:S(2)}) %collective-permute-start.25) | collective-permute-done | bytes 81952 | tf_op jit(solution)/shard_map/ppermute | solution.py:389
  50.3 0.2 collective-permute-done.22.refs_3_
  50.5 1.8 %back_kernel.1 = (f32[128,512]{1,0:T(8,128)}, f32[192,512]{1,0:T(8,128)}) custom-call(f32[160,128]{1,0:T(8,128)S(1)} %add.15.refs_0_, f32[160,128]{1,0:T(8,128)S(1)} %collective-permute-done.20.refs_1_, f32[160,128]{1,0:T(8,128)S(1)} %collective-permute-done.21.refs_2_, f32[160,128]{1,0:T(8,128)S(1)} %collective-permute-done.22.refs_3_, ...), custom_call_target="tpu_custom_call" | custom-call | flops 452984832 | tf_op jit(solution)/shard_map/back_kernel/pallas_call | solution.py:358
  52.3 0.7 %finish_kernel.1 = (f32[64,256]{1,0:T(8,128)}, f32[64,512]{1,0:T(8,128)}) custom-call(f32[64,768]{1,0:T(8,128)S(1)} %get-tuple-element.75.own_terms, f32[64,768]{1,0:T(8,128)S(1)} %collective-permute-done.19.came), custom_call_target="tpu_custom_call" | custom-call | tf_op jit(solution)/shard_map/finish_kernel/pallas_call | solution.py:358
  (19 shorter events, 0.1 us)
Async XLA Ops:
  0.6 8.7 %collective-permute-start.3 = (bf16[192,512]{1,0:T(8,128)(2,1)}, bf16[192,512]{1,0:T(8,128)(2,1)S(1)}, u32[]{:S(2)}, u32[]{:S(2)}) collective-permute-start(bf16[192,512]{1,0:T(8,128)(2,1)} %bitcast.13), channel_id=1, source_target_pairs={{0,2},{1,3},{2,0},{3,1},{4,6},{5,7},{6,4},{7,5},{8,10},{9,11},{10,... | collective-permute-start | bytes 589832 | tf_op jit(solution)/shard_map/ppermute | solution.py:389
  3.7 13.8 %copy-start.1 = (bf16[1,192,512]{2,1,0:T(8,128)(2,1)S(1)}, bf16[1,192,512]{2,1,0:T(8,128)(2,1)}, u32[]{:S(2)}) copy-start(bf16[1,192,512]{2,1,0:T(8,128)(2,1)} %param.12) | copy-start | bytes 589828
  3.7 15.6 %copy-start = (f32[128,512]{1,0:T(8,128)S(1)}, f32[128,512]{1,0:T(8,128)}, u32[]{:S(2)}) copy-start(f32[128,512]{1,0:T(8,128)} %base.1) | copy-start | bytes 786436
  5.2 9.7 %collective-permute-start = (f32[192,768]{1,0:T(8,128)S(1)}, f32[192,768]{1,0:T(8,128)S(1)}, u32[]{:S(2)}, u32[]{:S(2)}) collective-permute-start(f32[192,768]{1,0:T(8,128)S(1)} %get-tuple-element.51.x_own), channel_id=1, source_target_pairs={{0,1},{1,0},{2,3},{3,2},{4,5},{5,4},{6,7},{7,6},{8,9},{9,8},{10,11... | collective-permute-start | bytes 1769480 | tf_op jit(solution)/shard_map/ppermute | solution.py:389
  5.2 9.6 %collective-permute-start.1 = (f32[192,768]{1,0:T(8,128)S(1)}, f32[192,768]{1,0:T(8,128)S(1)}, u32[]{:S(2)}, u32[]{:S(2)}) collective-permute-start(f32[192,768]{1,0:T(8,128)S(1)} %get-tuple-element.52.k_own), channel_id=1, source_target_pairs={{0,1},{1,0},{2,3},{3,2},{4,5},{5,4},{6,7},{7,6},{8,9},{9,8},{10,11... | collective-permute-start | bytes 1769480 | tf_op jit(solution)/shard_map/ppermute | solution.py:389
  5.7 7.3 %collective-permute-start.4 = (f32[392,128]{1,0:T(8,128)S(1)}, f32[392,128]{1,0:T(8,128)S(1)}, u32[]{:S(2)}, u32[]{:S(2)}) collective-permute-start(f32[392,128]{1,0:T(8,128)S(1)} %get-tuple-element.54), channel_id=1, source_target_pairs={{0,2},{1,3},{2,0},{3,1},{4,6},{5,7},{6,4},{7,5},{8,10},{9,11},{10,... | collective-permute-start | bytes 602120 | tf_op jit(solution)/shard_map/ppermute | solution.py:389
  9.3 3.8 %collective-permute-start.5 = (bf16[192,512]{1,0:T(8,128)(2,1)S(1)}, bf16[192,512]{1,0:T(8,128)(2,1)S(1)}, u32[]{:S(2)}, u32[]{:S(2)}) collective-permute-start(bf16[192,512]{1,0:T(8,128)(2,1)S(1)} %collective-permute-done.3.g_far), channel_id=1, source_target_pairs={{0,1},{1,0},{2,3},{3,2},{4,5},{5,4},{6,7},{7,6},{8,9},{9,8},{10,11... | collective-permute-start | bytes 589832 | tf_op jit(solution)/shard_map/ppermute | solution.py:389
  9.3 8.2 %collective-permute-start.9 = (f32[400,128]{1,0:T(8,128)S(1)}, f32[400,128]{1,0:T(8,128)S(1)}, u32[]{:S(2)}, u32[]{:S(2)}) collective-permute-start(f32[400,128]{1,0:T(8,128)S(1)} %get-tuple-element.63), channel_id=1, source_target_pairs={{0,2},{1,3},{2,0},{3,1},{4,6},{5,7},{6,4},{7,5},{8,10},{9,11},{10,... | collective-permute-start | bytes 614408 | tf_op jit(solution)/shard_map/ppermute | solution.py:389
  13.1 1.7 %collective-permute-start.6 = (f32[392,128]{1,0:T(8,128)S(1)}, f32[392,128]{1,0:T(8,128)S(1)}, u32[]{:S(2)}, u32[]{:S(2)}) collective-permute-start(f32[392,128]{1,0:T(8,128)S(1)} %collective-permute-done.4.far), channel_id=1, source_target_pairs={{0,1},{1,0},{2,3},{3,2},{4,5},{5,4},{6,7},{7,6},{8,9},{9,8},{10,11... | collective-permute-start | bytes 602120 | tf_op jit(solution)/shard_map/ppermute | solution.py:389
  13.1 1.7 %collective-permute-start.2 = (bf16[192,512]{1,0:T(8,128)(2,1)S(1)}, bf16[192,512]{1,0:T(8,128)(2,1)S(1)}, u32[]{:S(2)}, u32[]{:S(2)}) collective-permute-start(bf16[192,512]{1,0:T(8,128)(2,1)S(1)} %get-tuple-element.53.g_own), channel_id=1, source_target_pairs={{0,1},{1,0},{2,3},{3,2},{4,5},{5,4},{6,7},{7,6},{8,9},{9,8},{10,11... | collective-permute-start | bytes 589832 | tf_op jit(solution)/shard_map/ppermute | solution.py:389
  17.5 1.8 %collective-permute-start.10 = (f32[400,128]{1,0:T(8,128)S(1)}, f32[400,128]{1,0:T(8,128)S(1)}, u32[]{:S(2)}, u32[]{:S(2)}) collective-permute-start(f32[400,128]{1,0:T(8,128)S(1)} %collective-permute-done.9.far), channel_id=1, source_target_pairs={{0,1},{1,0},{2,3},{3,2},{4,5},{5,4},{6,7},{7,6},{8,9},{9,8},{10,11... | collective-permute-start | bytes 614408 | tf_op jit(solution)/shard_map/ppermute | solution.py:389
  17.5 9.4 %collective-permute-start.8 = (bf16[192,512]{1,0:T(8,128)(2,1)S(1)}, bf16[192,512]{1,0:T(8,128)(2,1)S(1)}, u32[]{:S(2)}, u32[]{:S(2)}) collective-permute-start(bf16[192,512]{1,0:T(8,128)(2,1)S(1)} %bitcast.8), channel_id=1, source_target_pairs={{0,2},{1,3},{2,0},{3,1},{4,6},{5,7},{6,4},{7,5},{8,10},{9,11},{10,... | collective-permute-start | bytes 589832 | tf_op jit(solution)/shard_map/ppermute | solution.py:389
  23.4 5.0 %collective-permute-start.12 = (f32[160,128]{1,0:T(8,128)S(1)}, f32[160,128]{1,0:T(8,128)S(1)}, u32[]{:S(2)}, u32[]{:S(2)}) collective-permute-start(f32[160,128]{1,0:T(8,128)S(1)} %get-tuple-element.70), channel_id=1, source_target_pairs={{0,8},{4,12},{8,0},{12,4},{16,24},{20,28},{24,16},{28,20},{1,9},{5... | collective-permute-start | bytes 245768 | tf_op jit(solution)/shard_map/ppermute | solution.py:392
  25.0 5.2 %collective-permute-start.13 = (f32[160,128]{1,0:T(8,128)S(1)}, f32[160,128]{1,0:T(8,128)S(1)}, u32[]{:S(2)}, u32[]{:S(2)}) collective-permute-start(f32[160,128]{1,0:T(8,128)S(1)} %get-tuple-element.73), channel_id=1, source_target_pairs={{0,4},{4,0},{8,12},{12,8},{16,20},{20,16},{24,28},{28,24},{1,5},{5... | collective-permute-start | bytes 245768 | tf_op jit(solution)/shard_map/ppermute | solution.py:392
  26.5 5.3 %collective-permute-start.14 = (f32[160,128]{1,0:T(8,128)S(1)}, f32[160,128]{1,0:T(8,128)S(1)}, u32[]{:S(2)}, u32[]{:S(2)}) collective-permute-start(f32[160,128]{1,0:T(8,128)S(1)} %get-tuple-element.73), channel_id=1, source_target_pairs={{0,12},{4,8},{8,4},{12,0},{16,28},{20,24},{24,20},{28,16},{1,13},{... | collective-permute-start | bytes 245768 | tf_op jit(solution)/shard_map/ppermute | solution.py:392
  26.9 13.2 %collective-permute-start.16 = (f32[704,128]{1,0:T(8,128)S(1)}, f32[704,128]{1,0:T(8,128)S(1)}, u32[]{:S(2)}, u32[]{:S(2)}) collective-permute-start(f32[704,128]{1,0:T(8,128)S(1)} %get-tuple-element.79), channel_id=1, source_target_pairs={{0,1},{1,0},{2,3},{3,2},{4,5},{5,4},{6,7},{7,6},{8,9},{9,8},{10,11... | collective-permute-start | bytes 1081352 | tf_op jit(solution)/shard_map/ppermute | solution.py:389
  26.9 13.2 %collective-permute-start.17 = (f32[640,128]{1,0:T(8,128)S(1)}, f32[640,128]{1,0:T(8,128)S(1)}, u32[]{:S(2)}, u32[]{:S(2)}) collective-permute-start(f32[640,128]{1,0:T(8,128)S(1)} %get-tuple-element.80), channel_id=1, source_target_pairs={{0,2},{1,3},{2,0},{3,1},{4,6},{5,7},{6,4},{7,5},{8,10},{9,11},{10,... | collective-permute-start | bytes 983048 | tf_op jit(solution)/shard_map/ppermute | solution.py:389
  28.4 6.1 %collective-permute-start.7 = (bf16[192,512]{1,0:T(8,128)(2,1)S(1)}, bf16[192,512]{1,0:T(8,128)(2,1)S(1)}, u32[]{:S(2)}, u32[]{:S(2)}) collective-permute-start(bf16[192,512]{1,0:T(8,128)(2,1)S(1)} %bitcast.9), channel_id=1, source_target_pairs={{0,1},{1,0},{2,3},{3,2},{4,5},{5,4},{6,7},{7,6},{8,9},{9,8},{10,11... | collective-permute-start | bytes 589832 | tf_op jit(solution)/shard_map/ppermute | solution.py:389
  30.2 4.3 %collective-permute-start.11 = (bf16[192,512]{1,0:T(8,128)(2,1)S(1)}, bf16[192,512]{1,0:T(8,128)(2,1)S(1)}, u32[]{:S(2)}, u32[]{:S(2)}) collective-permute-start(bf16[192,512]{1,0:T(8,128)(2,1)S(1)} %collective-permute-done.8.p_far), channel_id=1, source_target_pairs={{0,1},{1,0},{2,3},{3,2},{4,5},{5,4},{6,7},{7,6},{8,9},{9,8},{10,11... | collective-permute-start | bytes 589832 | tf_op jit(solution)/shard_map/ppermute | solution.py:389
  31.9 8.2 %collective-permute-start.15 = (f32[160,128]{1,0:T(8,128)S(1)}, f32[160,128]{1,0:T(8,128)S(1)}, u32[]{:S(2)}, u32[]{:S(2)}) collective-permute-start(f32[160,128]{1,0:T(8,128)S(1)} %add_add_fusion), channel_id=1, source_target_pairs={{0,16},{4,20},{8,24},{12,28},{16,0},{20,4},{24,8},{28,12},{1,17},{... | collective-permute-start | bytes 245768 | tf_op jit(solution)/shard_map/ppermute | solution.py:392
  40.1 3.6 %collective-permute-start.18 = (f32[640,128]{1,0:T(8,128)S(1)}, f32[640,128]{1,0:T(8,128)S(1)}, u32[]{:S(2)}, u32[]{:S(2)}) collective-permute-start(f32[640,128]{1,0:T(8,128)S(1)} %collective-permute-done.17.far), channel_id=1, source_target_pairs={{0,1},{1,0},{2,3},{3,2},{4,5},{5,4},{6,7},{7,6},{8,9},{9,8},{10,11... | collective-permute-start | bytes 983048 | tf_op jit(solution)/shard_map/ppermute | solution.py:389
  40.2 6.6 %collective-permute-start.20 = (f32[160,128]{1,0:T(8,128)S(1)}, f32[160,128]{1,0:T(8,128)S(1)}, u32[]{:S(2)}, u32[]{:S(2)}) collective-permute-start(f32[160,128]{1,0:T(8,128)S(1)} %add.15.refs_0_), channel_id=1, source_target_pairs={{0,4},{4,0},{8,12},{12,8},{16,20},{20,16},{24,28},{28,24},{1,5},{5... | collective-permute-start | bytes 245768 | tf_op jit(solution)/shard_map/ppermute | solution.py:392
  41.3 6.9 %collective-permute-start.24 = (f32[160,128]{1,0:T(8,128)S(1)}, f32[160,128]{1,0:T(8,128)S(1)}, u32[]{:S(2)}, u32[]{:S(2)}) collective-permute-start(f32[160,128]{1,0:T(8,128)S(1)} %add.15.refs_0_), channel_id=1, source_target_pairs={{0,6},{1,7},{2,4},{3,5},{4,2},{5,3},{6,0},{7,1},{8,14},{9,15},{10,... | collective-permute-start | bytes 245768 | tf_op jit(solution)/shard_map/ppermute | solution.py:398
  43.2 5.9 %collective-permute-start.23 = (f32[160,128]{1,0:T(8,128)S(1)}, f32[160,128]{1,0:T(8,128)S(1)}, u32[]{:S(2)}, u32[]{:S(2)}) collective-permute-start(f32[160,128]{1,0:T(8,128)S(1)} %add.15.refs_0_), channel_id=1, source_target_pairs={{0,2},{1,3},{2,0},{3,1},{4,6},{5,7},{6,4},{7,5},{8,10},{9,11},{10,... | collective-permute-start | bytes 245768 | tf_op jit(solution)/shard_map/ppermute | solution.py:389
  43.7 8.6 %collective-permute-start.19 = (f32[64,768]{1,0:T(8,128)S(1)}, f32[64,768]{1,0:T(8,128)S(1)}, u32[]{:S(2)}, u32[]{:S(2)}) collective-permute-start(f32[64,768]{1,0:T(8,128)S(1)} %get-tuple-element.84), channel_id=1, source_target_pairs={{0,28},{4,0},{8,4},{12,8},{16,12},{20,16},{24,20},{28,24},{1,29},{... | collective-permute-start | bytes 589832 | tf_op jit(solution)/shard_map/ppermute | solution.py:477
  45.9 3.7 %collective-permute-start.21 = (f32[160,128]{1,0:T(8,128)S(1)}, f32[160,128]{1,0:T(8,128)S(1)}, u32[]{:S(2)}, u32[]{:S(2)}) collective-permute-start(f32[160,128]{1,0:T(8,128)S(1)} %add.15.refs_0_), channel_id=1, source_target_pairs={{0,1},{1,0},{2,3},{3,2},{4,5},{5,4},{6,7},{7,6},{8,9},{9,8},{10,11... | collective-permute-start | bytes 245768 | tf_op jit(solution)/shard_map/ppermute | solution.py:389
  48.1 1.4 %collective-permute-start.26 = (f32[160,128]{1,0:T(8,128)S(1)}, f32[160,128]{1,0:T(8,128)S(1)}, u32[]{:S(2)}, u32[]{:S(2)}) collective-permute-start(f32[160,128]{1,0:T(8,128)S(1)} %collective-permute-done.24.refs_5_), channel_id=1, source_target_pairs={{0,1},{1,0},{2,3},{3,2},{4,5},{5,4},{6,7},{7,6},{8,9},{9,8},{10,11... | collective-permute-start | bytes 245768 | tf_op jit(solution)/shard_map/ppermute | solution.py:389
  49.1 1.3 %collective-permute-start.25 = (f32[160,128]{1,0:T(8,128)S(1)}, f32[160,128]{1,0:T(8,128)S(1)}, u32[]{:S(2)}, u32[]{:S(2)}) collective-permute-start(f32[160,128]{1,0:T(8,128)S(1)} %collective-permute-done.23.refs_4_), channel_id=1, source_target_pairs={{0,1},{1,0},{2,3},{3,2},{4,5},{5,4},{6,7},{7,6},{8,9},{9,8},{10,11... | collective-permute-start | bytes 245768 | tf_op jit(solution)/shard_map/ppermute | solution.py:389
  49.1 1.4 %collective-permute-start.22 = (f32[160,128]{1,0:T(8,128)S(1)}, f32[160,128]{1,0:T(8,128)S(1)}, u32[]{:S(2)}, u32[]{:S(2)}) collective-permute-start(f32[160,128]{1,0:T(8,128)S(1)} %collective-permute-done.20.refs_1_), channel_id=1, source_target_pairs={{0,1},{1,0},{2,3},{3,2},{4,5},{5,4},{6,7},{7,6},{8,9},{9,8},{10,11... | collective-permute-start | bytes 245768 | tf_op jit(solution)/shard_map/ppermute | solution.py:389

commit v10 on v9

--- a/solution.py
+++ b/solution.py
@@ -39,6 +39,22 @@
 def place():
     part = lax.axis_index("tile")
     return part, part // 2, part % 2
+
+
+def folded(square):
+    half = square.shape[0] // 2
+    last = square[half:, half:]
+    last = jnp.concatenate([last[: half // 2, :], last[half // 2 :, :]], axis=1)
+    return jnp.concatenate([square[:half, :], last], axis=0)
+
+
+def unfolded(rows):
+    half = rows.shape[1] // 2
+    upper, last = rows[:half, :], rows[half:, :]
+    last = jnp.concatenate([last[:, :half], last[:, half:]], axis=0)
+    return jnp.concatenate(
+        [upper, jnp.concatenate([upper[:, half:].T, last], axis=1)], axis=0
+    )
 
 
 def put_rows(own, other, target, offset=0):
@@ -190,7 +206,7 @@
 
 
 def global_kernel(
-    live, far, cross, x, k_in, links, columns, first, base, s_own,
+    live, far, cross, x, k_in, links, columns, product, base, s_own,
     keep, send, y_own, y_core, y_far, k, pack, solved,
 ):
     del k_in
@@ -201,7 +217,7 @@
     part, near, core = place()
     block = lax.axis_index("tm")
     corner(far, cross, k, live)
-    value = 2.0 * columns[...] - times(first[...], k)
+    value = 2.0 * columns[...] - times(product[...], k)
     for step in range(TERMS - 1):
         value = columns[...] + value - times(times(value, x), k)
     result = times(value, x)
@@ -220,10 +236,11 @@
         added = jnp.where(block == 0, base[:, cols], 0.0)
         return parts[:group] + parts[group:] + added
 
-    pack[0:group, :] = square(0)
-    pack[group : 2 * group, :] = square(1)
+    first = group * 3 // 4
+    pack[0:first, :] = folded(square(0))
+    pack[first : first + group, :] = square(1)
     across = square(2)
-    pack[2 * group :, :] = jnp.where(
+    pack[first + group :, :] = jnp.where(
         part < 2, across[: group // 2, :], across.T[group // 2 :, :]
     )
     size = keep.shape[0]
@@ -300,7 +317,7 @@
     side = lax.axis_index("tm") % 2
     size = sums[0].shape[0]
     group, width = schur.shape
-    span = 2 * size
+    span, diagonal = 2 * size, group * 3 // 4
     for mask in range(4):
         for half in range(2):
             rows = at((part ^ mask) * span + (side ^ half) * size, size, 8)
@@ -313,15 +330,16 @@
         parts[rows, width + col * group : width + (col + 1) * group] = low
 
     def across(row):
-        first, other = row * span + 2 * group, (row + 2) * span + 2 * group
+        first = row * span + diagonal + group
+        other = first + 2 * span
         return jnp.concatenate(
             [whole[at(first, group // 2, 8), :], whole[at(other, group // 2, 8), :]], axis=0
         )
 
     for row in range(4):
         first = row * span
-        put(row, row, whole[first : first + group, :])
-        value = whole[first + group : first + 2 * group, :]
+        put(row, row, unfolded(whole[first : first + diagonal, :]))
+        value = whole[first + diagonal : first + diagonal + group, :]
         put(row, (row + 1) % 4, value)
         put((row + 1) % 4, row, value.T)
         if row < 2:
@@ -331,10 +349,10 @@
     before = (part + 3) % 4
     value = across(part % 2)
     for col, value in (
-        (part, whole[at(part * span, group, 8), :]),
-        ((part + 1) % 4, whole[at(part * span + group, group, 8), :]),
+        (part, unfolded(whole[at(part * span, diagonal, 8), :])),
+        ((part + 1) % 4, whole[at(part * span + diagonal, group, 8), :]),
         ((part + 2) % 4, jnp.where(part < 2, value, value.T)),
-        (before, whole[at(before * span + group, group, 8), :].T),
+        (before, whole[at(before * span + diagonal, group, 8), :].T),
     ):
         schur[:, at(col * group, group, 128)] = value
     value = scaled[...]
@@ -383,7 +401,7 @@
     unit = half // 3
     link, width = pair.shape[1] // 2, glob.shape[1]
     group, share = width // 4, link // 4
-    size = group + group // 4
+    size = group * 9 // 8
 
     def tile_swap(value, mask):
         return lax.ppermute(value, "tile", [(i, i ^ mask) for i in range(4)])
@@ -423,12 +441,13 @@
     )
     k_far = after(k_far, first)
     p_core, p_far = (tile_swap(after(pair, first), m) for m in (1, 2))
+    k_cross, p_core = lax.optimization_barrier((tile_swap(k_far, 1), p_core))
     keep, send, y_own, y_core, y_far, k = call(
         global_kernel,
         [((size, group), F32)] * 2 + [((rows, group), F32), ((rows + width, group), F32)]
         + [((2 * rows + 2 * group, group), F32), matrix],
         [vmem((2 * size, group), F32), vmem((order, group), F32)],
-        live_cols, k_far, tile_swap(k_far, 1), x, k, links, columns, first, schur_base, s_own,
+        live_cols, k_far, k_cross, x, k, links, columns, first, schur_base, s_own,
         alias={4: 5},
     )
 
@@ -471,7 +490,7 @@
         [((group, width), F32), ((rows, width), F32)],
         [vmem((8 * size, group), F32), vmem((width, 2 * width), BF16)],
         *sums, start, scaled,
-        flops=int(4 * rows * order * order),
+        flops=int(6 * rows * order * order),
     )
     next_terms = after(next_terms, cross)
     came = lax.ppermute(next_terms, "tm", [(i, (i - 1) % blocks) for i in range(blocks)])

time: 53.2 us -> 53.2 us (level)
    ppermute x1, starting transfers between devices: 2.12 us -> 1.58 us  [shards(): lax.ppermute(next_terms, 'tm', [(i, (i - 1) % blocks) for i in range(bloc...]
where the time goes in v10:
time: 53.2 us; the launch traced here: 53 us
  starting transfers between devices  22.1 us (42%)
  Pallas kernels  16.9 us (32%)
  waiting for transfers between devices  12.6 us (24%)
  between operations  1.37 us (3%)
    pallas_call x7, Pallas kernels, call(): pl.pallas_call(kernel, out_shape=[jax.ShapeDtypeStruct(shape, dtype) for...  16.9 us
    ppermute x20, starting transfers between devices, tile_swap(): return lax.ppermute(value, 'tile', [(i, i ^ mask) for i in range(4)])  11.6 us
    ppermute x20, waiting for transfers between devices, tile_swap(): return lax.ppermute(value, 'tile', [(i, i ^ mask) for i in range(4)])  7.92 us
    ppermute x5, starting transfers between devices, block_swap(): return lax.ppermute(value, 'tm', [(i, i ^ mask) for i in range(blocks)])  6.8 us
    ppermute x5, waiting for transfers between devices, block_swap(): return lax.ppermute(value, 'tm', [(i, i ^ mask) for i in range(blocks)])  3.38 us
    ppermute x1, starting transfers between devices, diagonal_swap(): return lax.ppermute(value, ('tm', 'tile'), pairs)  2.15 us
    ppermute x1, starting transfers between devices, shards(): lax.ppermute(next_terms, 'tm', [(i, (i - 1) % blocks) for i in range(bloc...  1.58 us
    ppermute x1, waiting for transfers between devices, diagonal_swap(): return lax.ppermute(value, ('tm', 'tile'), pairs)  1.3 us
  transfers between devices with their start and end apart: 27, of which 10 were waited for; matrix products, arithmetic and copies ran while one was open for 0% of the time, Pallas kernels for 30%

profile of v10, /device:TPU:0, one launch (start us, length us, event | category | flops | bytes accessed | tf_op | source)
XLA Modules:
  0.0 53.0 jit_solution(14333833267781632155)
XLA Ops:
  0.6 3.0 %collective-permute-start.3 = (bf16[192,512]{1,0:T(8,128)(2,1)}, bf16[192,512]{1,0:T(8,128)(2,1)S(1)}, u32[]{:S(2)}, u32[]{:S(2)}) collective-permute-start(bf16[192,512]{1,0:T(8,128)(2,1)} %bitcast.13), channel_id=1, source_target_pairs={{0,2},{1,3},{2,0},{3,1},{4,6},{5,7},{6,4},{7,5},{8,10},{9,11},{10,... | collective-permute-start | bytes 589832 | tf_op jit(solution)/shard_map/ppermute | solution.py:407
  3.7 1.5 %pack_kernel.1 = (f32[392,128]{1,0:T(8,128)S(1)}, f32[400,128]{1,0:T(8,128)S(1)}, f32[192,768]{1,0:T(8,128)S(1)}, f32[192,768]{1,0:T(8,128)S(1)}, bf16[192,512]{...) custom-call(f32[192,768]{1,0:T(8,128)} %bitcast.11, f32[192,768]{1,0:T(8,128)} %bitcast.12, ...), custom_call_target="tpu_custom_call" | custom-call | tf_op jit(solution)/shard_map/pack_kernel/pallas_call | solution.py:376
  5.2 0.1 collective-permute-start
  5.2 0.5 collective-permute-start.1
  5.7 0.0 collective-permute-start.4
  5.8 3.5 %collective-permute-done.3.g_far = bf16[192,512]{1,0:T(8,128)(2,1)S(1)} collective-permute-done((bf16[192,512]{1,0:T(8,128)(2,1)}, bf16[192,512]{1,0:T(8,128)(2,1)S(1)}, u32[]{:S(2)}, u32[]{:S(2)}) %collective-permute-start.3) | collective-permute-done | bytes 196640 | tf_op jit(solution)/shard_map/ppermute | solution.py:407
  9.3 0.0 collective-permute-start.5
  9.3 2.4 %collective-permute-start.7 = (f32[400,128]{1,0:T(8,128)S(1)}, f32[400,128]{1,0:T(8,128)S(1)}, u32[]{:S(2)}, u32[]{:S(2)}) collective-permute-start(f32[400,128]{1,0:T(8,128)S(1)} %get-tuple-element.62), channel_id=1, source_target_pairs={{0,2},{1,3},{2,0},{3,1},{4,6},{5,7},{6,4},{7,5},{8,10},{9,11},{10,... | collective-permute-start | bytes 614408 | tf_op jit(solution)/shard_map/ppermute | solution.py:407
  11.7 1.4 %collective-permute-done.4.far = f32[392,128]{1,0:T(8,128)S(1)} collective-permute-done((f32[392,128]{1,0:T(8,128)S(1)}, f32[392,128]{1,0:T(8,128)S(1)}, u32[]{:S(2)}, u32[]{:S(2)}) %collective-permute-start.4) | collective-permute-done | bytes 200736 | tf_op jit(solution)/shard_map/ppermute | solution.py:407
  13.1 0.0 collective-permute-done.5.g_cross
  13.1 0.5 collective-permute-start.2
  14.2 0.6 %collective-permute-done.2.g_core = bf16[192,512]{1,0:T(8,128)(2,1)S(1)} collective-permute-done((bf16[192,512]{1,0:T(8,128)(2,1)S(1)}, bf16[192,512]{1,0:T(8,128)(2,1)S(1)}, u32[]{:S(2)}, u32[]{:S(2)}) %collective-permute-start.2) | collective-permute-done | bytes 196640 | tf_op jit(solution)/shard_map/ppermute | solution.py:407
  14.8 0.0 collective-permute-done.x_core
  14.8 0.0 collective-permute-done.1.k_core
  14.8 0.0 collective-permute-done.6.cross
  14.8 2.0 %prepare_kernel.1 = (bf16[1536,768]{1,0:T(8,128)(2,1)S(1)}, bf16[1536,768]{1,0:T(8,128)(2,1)S(1)}, bf16[768,512]{1,0:T(8,128)(2,1)S(1)}, f32[768,1]{1,0:T(8,128)...) custom-call(s32[1]{0:T(128)S(6)} %copy.15.sizes, ...), custom_call_target="tpu_custom_call" | custom-call | tf_op jit(solution)/shard_map/prepare_kernel/pallas_call | solution.py:376
  16.8 0.6 %collective-permute-done.7.far = f32[400,128]{1,0:T(8,128)S(1)} collective-permute-done((f32[400,128]{1,0:T(8,128)S(1)}, f32[400,128]{1,0:T(8,128)S(1)}, u32[]{:S(2)}, u32[]{:S(2)}) %collective-permute-start.7) | collective-permute-done | bytes 204832 | tf_op jit(solution)/shard_map/ppermute | solution.py:407
  17.5 0.0 collective-permute-start.8
  17.5 0.5 collective-permute-start.9
  18.0 1.7 %collective-permute-start.10 = (bf16[192,512]{1,0:T(8,128)(2,1)S(1)}, bf16[192,512]{1,0:T(8,128)(2,1)S(1)}, u32[]{:S(2)}, u32[]{:S(2)}) collective-permute-start(bf16[192,512]{1,0:T(8,128)(2,1)S(1)} %bitcast.9), channel_id=1, source_target_pairs={{0,2},{1,3},{2,0},{3,1},{4,6},{5,7},{6,4},{7,5},{8,10},{9,11},{10,... | collective-permute-start | bytes 589832 | tf_op jit(solution)/shard_map/ppermute | solution.py:407
  19.7 4.1 %global_kernel.1 = (f32[144,128]{1,0:T(8,128)S(1)}, f32[144,128]{1,0:T(8,128)S(1)}, f32[192,128]{1,0:T(8,128)S(1)}, f32[704,128]{1,0:T(8,128)S(1)}, f32[640,128]...) custom-call(f32[1,768]{1,0:T(1,128)S(1)} %get-tuple-element.67.live, ...), custom_call_target="tpu_custom_call", output_to_operand_aliasing={{5}: (4, {})} | custom-call | tf_op jit(solution)/shard_map/global_kernel/pallas_call | solution.py:376
  23.9 1.6 %collective-permute-start.12 = (f32[144,128]{1,0:T(8,128)S(1)}, f32[144,128]{1,0:T(8,128)S(1)}, u32[]{:S(2)}, u32[]{:S(2)}) collective-permute-start(f32[144,128]{1,0:T(8,128)S(1)} %get-tuple-element.74), channel_id=1, source_target_pairs={{0,8},{4,12},{8,0},{12,4},{16,24},{20,28},{24,16},{28,20},{1,9},{5... | collective-permute-start | bytes 221192 | tf_op jit(solution)/shard_map/ppermute | solution.py:410
  25.5 1.5 %collective-permute-start.13 = (f32[144,128]{1,0:T(8,128)S(1)}, f32[144,128]{1,0:T(8,128)S(1)}, u32[]{:S(2)}, u32[]{:S(2)}) collective-permute-start(f32[144,128]{1,0:T(8,128)S(1)} %get-tuple-element.77), channel_id=1, source_target_pairs={{0,4},{4,0},{8,12},{12,8},{16,20},{20,16},{24,28},{28,24},{1,5},{5... | collective-permute-start | bytes 221192 | tf_op jit(solution)/shard_map/ppermute | solution.py:410
  27.0 0.4 collective-permute-start.14
  27.4 1.2 %collective-permute-start.17 = (f32[640,128]{1,0:T(8,128)S(1)}, f32[640,128]{1,0:T(8,128)S(1)}, u32[]{:S(2)}, u32[]{:S(2)}) collective-permute-start(f32[640,128]{1,0:T(8,128)S(1)} %get-tuple-element.84), channel_id=1, source_target_pairs={{0,2},{1,3},{2,0},{3,1},{4,6},{5,7},{6,4},{7,5},{8,10},{9,11},{10,... | collective-permute-start | bytes 983048 | tf_op jit(solution)/shard_map/ppermute | solution.py:407
  28.7 0.0 collective-permute-done.12
  28.7 0.2 collective-permute-start.11
  28.9 1.0 %collective-permute-done.13 = f32[144,128]{1,0:T(8,128)S(1)} collective-permute-done((f32[144,128]{1,0:T(8,128)S(1)}, f32[144,128]{1,0:T(8,128)S(1)}, u32[]{:S(2)}, u32[]{:S(2)}) %collective-permute-start.13) | collective-permute-done | bytes 73760 | tf_op jit(solution)/shard_map/ppermute | solution.py:410
  29.9 2.4 %collective-permute-done.14 = f32[144,128]{1,0:T(8,128)S(1)} collective-permute-done((f32[144,128]{1,0:T(8,128)S(1)}, f32[144,128]{1,0:T(8,128)S(1)}, u32[]{:S(2)}, u32[]{:S(2)}) %collective-permute-start.14) | collective-permute-done | bytes 73760 | tf_op jit(solution)/shard_map/ppermute | solution.py:410
  32.3 2.7 %collective-permute-start.15 = (f32[144,128]{1,0:T(8,128)S(1)}, f32[144,128]{1,0:T(8,128)S(1)}, u32[]{:S(2)}, u32[]{:S(2)}) collective-permute-start(f32[144,128]{1,0:T(8,128)S(1)} %add_add_fusion), channel_id=1, source_target_pairs={{0,16},{4,20},{8,24},{12,28},{16,0},{20,4},{24,8},{28,12},{1,17},{... | collective-permute-start | bytes 221192 | tf_op jit(solution)/shard_map/ppermute | solution.py:410
  34.9 0.0 collective-permute-done.11.p_cross
  34.9 5.6 %pair_kernel.1 = (f32[64,768]{1,0:T(8,128)S(1)}, f32[64,256]{1,0:T(8,128)}, f32[64,768]{1,0:T(8,128)S(1)}) custom-call(f32[768,1]{1,0:T(8,128)S(1)} %get-tuple-element.61.live, bf16[192,512]{1,0:T(8,128)(2,1)S(1)} %bitcast.10, bf16[192,512]{1,0:T(8,128)(2,1)S(1)} %collective-permute-done.9.p_core, bf16[192,512]{1,0:T(8,128)(2,1)S(1)} %collective-permute-done.10.p_far, ...), custom_call_target="tpu_custom_call" | custom-call | tf_op jit(solution)/shard_map/pair_kernel/pallas_call | solution.py:376
  40.5 0.1 collective-permute-start.18
  40.6 0.6 %collective-permute-start.20 = (f32[144,128]{1,0:T(8,128)S(1)}, f32[144,128]{1,0:T(8,128)S(1)}, u32[]{:S(2)}, u32[]{:S(2)}) collective-permute-start(f32[144,128]{1,0:T(8,128)S(1)} %add.15.refs_0_), channel_id=1, source_target_pairs={{0,4},{4,0},{8,12},{12,8},{16,20},{20,16},{24,28},{28,24},{1,5},{5... | collective-permute-start | bytes 221192 | tf_op jit(solution)/shard_map/ppermute | solution.py:410
  41.2 2.2 %collective-permute-start.24 = (f32[144,128]{1,0:T(8,128)S(1)}, f32[144,128]{1,0:T(8,128)S(1)}, u32[]{:S(2)}, u32[]{:S(2)}) collective-permute-start(f32[144,128]{1,0:T(8,128)S(1)} %add.15.refs_0_), channel_id=1, source_target_pairs={{0,6},{1,7},{2,4},{3,5},{4,2},{5,3},{6,0},{7,1},{8,14},{9,15},{10,... | collective-permute-start | bytes 221192 | tf_op jit(solution)/shard_map/ppermute | solution.py:416
  43.4 0.8 %collective-permute-start.23 = (f32[144,128]{1,0:T(8,128)S(1)}, f32[144,128]{1,0:T(8,128)S(1)}, u32[]{:S(2)}, u32[]{:S(2)}) collective-permute-start(f32[144,128]{1,0:T(8,128)S(1)} %add.15.refs_0_), channel_id=1, source_target_pairs={{0,2},{1,3},{2,0},{3,1},{4,6},{5,7},{6,4},{7,5},{8,10},{9,11},{10,... | collective-permute-start | bytes 221192 | tf_op jit(solution)/shard_map/ppermute | solution.py:407
  44.2 1.6 %collective-permute-start.19 = (f32[64,768]{1,0:T(8,128)S(1)}, f32[64,768]{1,0:T(8,128)S(1)}, u32[]{:S(2)}, u32[]{:S(2)}) collective-permute-start(f32[64,768]{1,0:T(8,128)S(1)} %get-tuple-element.88), channel_id=1, source_target_pairs={{0,28},{4,0},{8,4},{12,8},{16,12},{20,16},{24,20},{28,24},{1,29},{... | collective-permute-start | bytes 589832 | tf_op jit(solution)/shard_map/ppermute | solution.py:496
  45.7 0.9 %start_kernel.1 = (bf16[512,1024]{1,0:T(8,128)(2,1)S(1)}, f32[192,512]{1,0:T(8,128)S(1)}) custom-call(f32[512,128]{1,0:T(8,128)S(1)} %get-tuple-element.73.s_own, f32[192,128]{1,0:T(8,128)S(1)} %get-tuple-element.92.y_own, f32[704,128]{1,0:T(8,128)S(1)} %collective-permute-done.16.y_core, f32[640,128]{1,0:T(8,128)S(1)} %collective-permute-done.17.far, ...), custom_call_target="tpu_custom_call" | custom-call | tf_op jit(solution)/shard_map/start_kernel/pallas_call | solution.py:376
  46.7 1.3 %collective-permute-done.24.refs_5_ = f32[144,128]{1,0:T(8,128)S(1)} collective-permute-done((f32[144,128]{1,0:T(8,128)S(1)}, f32[144,128]{1,0:T(8,128)S(1)}, u32[]{:S(2)}, u32[]{:S(2)}) %collective-permute-start.24) | collective-permute-done | bytes 73760 | tf_op jit(solution)/shard_map/ppermute | solution.py:416
  48.0 0.0 collective-permute-start.26
  48.0 0.8 %collective-permute-done.23.refs_4_ = f32[144,128]{1,0:T(8,128)S(1)} collective-permute-done((f32[144,128]{1,0:T(8,128)S(1)}, f32[144,128]{1,0:T(8,128)S(1)}, u32[]{:S(2)}, u32[]{:S(2)}) %collective-permute-start.23) | collective-permute-done | bytes 73760 | tf_op jit(solution)/shard_map/ppermute | solution.py:407
  48.8 0.0 collective-permute-start.25
  48.8 0.5 collective-permute-start.22
  49.3 0.7 %collective-permute-done.25.refs_6_ = f32[144,128]{1,0:T(8,128)S(1)} collective-permute-done((f32[144,128]{1,0:T(8,128)S(1)}, f32[144,128]{1,0:T(8,128)S(1)}, u32[]{:S(2)}, u32[]{:S(2)}) %collective-permute-start.25) | collective-permute-done | bytes 73760 | tf_op jit(solution)/shard_map/ppermute | solution.py:407
  50.1 0.2 collective-permute-done.22.refs_3_
  50.3 2.1 %back_kernel.1 = (f32[128,512]{1,0:T(8,128)}, f32[192,512]{1,0:T(8,128)}) custom-call(f32[144,128]{1,0:T(8,128)S(1)} %add.15.refs_0_, f32[144,128]{1,0:T(8,128)S(1)} %collective-permute-done.20.refs_1_, f32[144,128]{1,0:T(8,128)S(1)} %collective-permute-done.21.refs_2_, f32[144,128]{1,0:T(8,128)S(1)} %collective-permute-done.22.refs_3_, ...), custom_call_target="tpu_custom_call" | custom-call | flops 679477248 | tf_op jit(solution)/shard_map/back_kernel/pallas_call | solution.py:376
  52.3 0.0 collective-permute-done.19.came
  52.3 0.7 %finish_kernel.1 = (f32[64,256]{1,0:T(8,128)}, f32[64,512]{1,0:T(8,128)}) custom-call(f32[64,768]{1,0:T(8,128)S(1)} %get-tuple-element.79.own_terms, f32[64,768]{1,0:T(8,128)S(1)} %collective-permute-done.19.came), custom_call_target="tpu_custom_call" | custom-call | tf_op jit(solution)/shard_map/finish_kernel/pallas_call | solution.py:376
  (19 shorter events, 0.1 us)
Async XLA Ops:
  0.6 8.7 %collective-permute-start.3 = (bf16[192,512]{1,0:T(8,128)(2,1)}, bf16[192,512]{1,0:T(8,128)(2,1)S(1)}, u32[]{:S(2)}, u32[]{:S(2)}) collective-permute-start(bf16[192,512]{1,0:T(8,128)(2,1)} %bitcast.13), channel_id=1, source_target_pairs={{0,2},{1,3},{2,0},{3,1},{4,6},{5,7},{6,4},{7,5},{8,10},{9,11},{10,... | collective-permute-start | bytes 589832 | tf_op jit(solution)/shard_map/ppermute | solution.py:407
  3.7 13.8 %copy-start.1 = (bf16[1,192,512]{2,1,0:T(8,128)(2,1)S(1)}, bf16[1,192,512]{2,1,0:T(8,128)(2,1)}, u32[]{:S(2)}) copy-start(bf16[1,192,512]{2,1,0:T(8,128)(2,1)} %param.12) | copy-start | bytes 589828
  3.7 16.1 %copy-start = (f32[128,512]{1,0:T(8,128)S(1)}, f32[128,512]{1,0:T(8,128)}, u32[]{:S(2)}) copy-start(f32[128,512]{1,0:T(8,128)} %base.1) | copy-start | bytes 786436
  5.2 9.7 %collective-permute-start = (f32[192,768]{1,0:T(8,128)S(1)}, f32[192,768]{1,0:T(8,128)S(1)}, u32[]{:S(2)}, u32[]{:S(2)}) collective-permute-start(f32[192,768]{1,0:T(8,128)S(1)} %get-tuple-element.53.x_own), channel_id=1, source_target_pairs={{0,1},{1,0},{2,3},{3,2},{4,5},{5,4},{6,7},{7,6},{8,9},{9,8},{10,11... | collective-permute-start | bytes 1769480 | tf_op jit(solution)/shard_map/ppermute | solution.py:407
  5.2 9.6 %collective-permute-start.1 = (f32[192,768]{1,0:T(8,128)S(1)}, f32[192,768]{1,0:T(8,128)S(1)}, u32[]{:S(2)}, u32[]{:S(2)}) collective-permute-start(f32[192,768]{1,0:T(8,128)S(1)} %get-tuple-element.54.k_own), channel_id=1, source_target_pairs={{0,1},{1,0},{2,3},{3,2},{4,5},{5,4},{6,7},{7,6},{8,9},{9,8},{10,11... | collective-permute-start | bytes 1769480 | tf_op jit(solution)/shard_map/ppermute | solution.py:407
  5.7 7.3 %collective-permute-start.4 = (f32[392,128]{1,0:T(8,128)S(1)}, f32[392,128]{1,0:T(8,128)S(1)}, u32[]{:S(2)}, u32[]{:S(2)}) collective-permute-start(f32[392,128]{1,0:T(8,128)S(1)} %get-tuple-element.56), channel_id=1, source_target_pairs={{0,2},{1,3},{2,0},{3,1},{4,6},{5,7},{6,4},{7,5},{8,10},{9,11},{10,... | collective-permute-start | bytes 602120 | tf_op jit(solution)/shard_map/ppermute | solution.py:407
  9.3 3.8 %collective-permute-start.5 = (bf16[192,512]{1,0:T(8,128)(2,1)S(1)}, bf16[192,512]{1,0:T(8,128)(2,1)S(1)}, u32[]{:S(2)}, u32[]{:S(2)}) collective-permute-start(bf16[192,512]{1,0:T(8,128)(2,1)S(1)} %collective-permute-done.3.g_far), channel_id=1, source_target_pairs={{0,1},{1,0},{2,3},{3,2},{4,5},{5,4},{6,7},{7,6},{8,9},{9,8},{10,11... | collective-permute-start | bytes 589832 | tf_op jit(solution)/shard_map/ppermute | solution.py:407
  9.3 8.2 %collective-permute-start.7 = (f32[400,128]{1,0:T(8,128)S(1)}, f32[400,128]{1,0:T(8,128)S(1)}, u32[]{:S(2)}, u32[]{:S(2)}) collective-permute-start(f32[400,128]{1,0:T(8,128)S(1)} %get-tuple-element.62), channel_id=1, source_target_pairs={{0,2},{1,3},{2,0},{3,1},{4,6},{5,7},{6,4},{7,5},{8,10},{9,11},{10,... | collective-permute-start | bytes 614408 | tf_op jit(solution)/shard_map/ppermute | solution.py:407
  13.1 1.7 %collective-permute-start.6 = (f32[392,128]{1,0:T(8,128)S(1)}, f32[392,128]{1,0:T(8,128)S(1)}, u32[]{:S(2)}, u32[]{:S(2)}) collective-permute-start(f32[392,128]{1,0:T(8,128)S(1)} %collective-permute-done.4.far), channel_id=1, source_target_pairs={{0,1},{1,0},{2,3},{3,2},{4,5},{5,4},{6,7},{7,6},{8,9},{9,8},{10,11... | collective-permute-start | bytes 602120 | tf_op jit(solution)/shard_map/ppermute | solution.py:407
  13.1 1.7 %collective-permute-start.2 = (bf16[192,512]{1,0:T(8,128)(2,1)S(1)}, bf16[192,512]{1,0:T(8,128)(2,1)S(1)}, u32[]{:S(2)}, u32[]{:S(2)}) collective-permute-start(bf16[192,512]{1,0:T(8,128)(2,1)S(1)} %get-tuple-element.55.g_own), channel_id=1, source_target_pairs={{0,1},{1,0},{2,3},{3,2},{4,5},{5,4},{6,7},{7,6},{8,9},{9,8},{10,11... | collective-permute-start | bytes 589832 | tf_op jit(solution)/shard_map/ppermute | solution.py:407
  17.5 2.3 %collective-permute-start.8 = (f32[400,128]{1,0:T(8,128)S(1)}, f32[400,128]{1,0:T(8,128)S(1)}, u32[]{:S(2)}, u32[]{:S(2)}) collective-permute-start(f32[400,128]{1,0:T(8,128)S(1)} %collective-permute-done.7.far), channel_id=1, source_target_pairs={{0,1},{1,0},{2,3},{3,2},{4,5},{5,4},{6,7},{7,6},{8,9},{9,8},{10,11... | collective-permute-start | bytes 614408 | tf_op jit(solution)/shard_map/ppermute | solution.py:407
  17.5 2.3 %collective-permute-start.9 = (bf16[192,512]{1,0:T(8,128)(2,1)S(1)}, bf16[192,512]{1,0:T(8,128)(2,1)S(1)}, u32[]{:S(2)}, u32[]{:S(2)}) collective-permute-start(bf16[192,512]{1,0:T(8,128)(2,1)S(1)} %bitcast.8), channel_id=1, source_target_pairs={{0,1},{1,0},{2,3},{3,2},{4,5},{5,4},{6,7},{7,6},{8,9},{9,8},{10,11... | collective-permute-start | bytes 589832 | tf_op jit(solution)/shard_map/ppermute | solution.py:407
  18.0 9.5 %collective-permute-start.10 = (bf16[192,512]{1,0:T(8,128)(2,1)S(1)}, bf16[192,512]{1,0:T(8,128)(2,1)S(1)}, u32[]{:S(2)}, u32[]{:S(2)}) collective-permute-start(bf16[192,512]{1,0:T(8,128)(2,1)S(1)} %bitcast.9), channel_id=1, source_target_pairs={{0,2},{1,3},{2,0},{3,1},{4,6},{5,7},{6,4},{7,5},{8,10},{9,11},{10,... | collective-permute-start | bytes 589832 | tf_op jit(solution)/shard_map/ppermute | solution.py:407
  23.9 4.8 %collective-permute-start.12 = (f32[144,128]{1,0:T(8,128)S(1)}, f32[144,128]{1,0:T(8,128)S(1)}, u32[]{:S(2)}, u32[]{:S(2)}) collective-permute-start(f32[144,128]{1,0:T(8,128)S(1)} %get-tuple-element.74), channel_id=1, source_target_pairs={{0,8},{4,12},{8,0},{12,4},{16,24},{20,28},{24,16},{28,20},{1,9},{5... | collective-permute-start | bytes 221192 | tf_op jit(solution)/shard_map/ppermute | solution.py:410
  25.5 4.4 %collective-permute-start.13 = (f32[144,128]{1,0:T(8,128)S(1)}, f32[144,128]{1,0:T(8,128)S(1)}, u32[]{:S(2)}, u32[]{:S(2)}) collective-permute-start(f32[144,128]{1,0:T(8,128)S(1)} %get-tuple-element.77), channel_id=1, source_target_pairs={{0,4},{4,0},{8,12},{12,8},{16,20},{20,16},{24,28},{28,24},{1,5},{5... | collective-permute-start | bytes 221192 | tf_op jit(solution)/shard_map/ppermute | solution.py:410
  27.0 5.3 %collective-permute-start.14 = (f32[144,128]{1,0:T(8,128)S(1)}, f32[144,128]{1,0:T(8,128)S(1)}, u32[]{:S(2)}, u32[]{:S(2)}) collective-permute-start(f32[144,128]{1,0:T(8,128)S(1)} %get-tuple-element.77), channel_id=1, source_target_pairs={{0,12},{4,8},{8,4},{12,0},{16,28},{20,24},{24,20},{28,16},{1,13},{... | collective-permute-start | bytes 221192 | tf_op jit(solution)/shard_map/ppermute | solution.py:410
  27.4 13.1 %collective-permute-start.16 = (f32[704,128]{1,0:T(8,128)S(1)}, f32[704,128]{1,0:T(8,128)S(1)}, u32[]{:S(2)}, u32[]{:S(2)}) collective-permute-start(f32[704,128]{1,0:T(8,128)S(1)} %get-tuple-element.83), channel_id=1, source_target_pairs={{0,1},{1,0},{2,3},{3,2},{4,5},{5,4},{6,7},{7,6},{8,9},{9,8},{10,11... | collective-permute-start | bytes 1081352 | tf_op jit(solution)/shard_map/ppermute | solution.py:407
  27.4 13.1 %collective-permute-start.17 = (f32[640,128]{1,0:T(8,128)S(1)}, f32[640,128]{1,0:T(8,128)S(1)}, u32[]{:S(2)}, u32[]{:S(2)}) collective-permute-start(f32[640,128]{1,0:T(8,128)S(1)} %get-tuple-element.84), channel_id=1, source_target_pairs={{0,2},{1,3},{2,0},{3,1},{4,6},{5,7},{6,4},{7,5},{8,10},{9,11},{10,... | collective-permute-start | bytes 983048 | tf_op jit(solution)/shard_map/ppermute | solution.py:407
  28.7 6.3 %collective-permute-start.11 = (bf16[192,512]{1,0:T(8,128)(2,1)S(1)}, bf16[192,512]{1,0:T(8,128)(2,1)S(1)}, u32[]{:S(2)}, u32[]{:S(2)}) collective-permute-start(bf16[192,512]{1,0:T(8,128)(2,1)S(1)} %collective-permute-done.10.p_far), channel_id=1, source_target_pairs={{0,1},{1,0},{2,3},{3,2},{4,5},{5,4},{6,7},{7,6},{8,9},{9,8},{10,11... | collective-permute-start | bytes 589832 | tf_op jit(solution)/shard_map/ppermute | solution.py:407
  32.3 8.2 %collective-permute-start.15 = (f32[144,128]{1,0:T(8,128)S(1)}, f32[144,128]{1,0:T(8,128)S(1)}, u32[]{:S(2)}, u32[]{:S(2)}) collective-permute-start(f32[144,128]{1,0:T(8,128)S(1)} %add_add_fusion), channel_id=1, source_target_pairs={{0,16},{4,20},{8,24},{12,28},{16,0},{20,4},{24,8},{28,12},{1,17},{... | collective-permute-start | bytes 221192 | tf_op jit(solution)/shard_map/ppermute | solution.py:410
  40.5 3.6 %collective-permute-start.18 = (f32[640,128]{1,0:T(8,128)S(1)}, f32[640,128]{1,0:T(8,128)S(1)}, u32[]{:S(2)}, u32[]{:S(2)}) collective-permute-start(f32[640,128]{1,0:T(8,128)S(1)} %collective-permute-done.17.far), channel_id=1, source_target_pairs={{0,1},{1,0},{2,3},{3,2},{4,5},{5,4},{6,7},{7,6},{8,9},{9,8},{10,11... | collective-permute-start | bytes 983048 | tf_op jit(solution)/shard_map/ppermute | solution.py:407
  40.6 6.1 %collective-permute-start.20 = (f32[144,128]{1,0:T(8,128)S(1)}, f32[144,128]{1,0:T(8,128)S(1)}, u32[]{:S(2)}, u32[]{:S(2)}) collective-permute-start(f32[144,128]{1,0:T(8,128)S(1)} %add.15.refs_0_), channel_id=1, source_target_pairs={{0,4},{4,0},{8,12},{12,8},{16,20},{20,16},{24,28},{28,24},{1,5},{5... | collective-permute-start | bytes 221192 | tf_op jit(solution)/shard_map/ppermute | solution.py:410
  41.2 6.8 %collective-permute-start.24 = (f32[144,128]{1,0:T(8,128)S(1)}, f32[144,128]{1,0:T(8,128)S(1)}, u32[]{:S(2)}, u32[]{:S(2)}) collective-permute-start(f32[144,128]{1,0:T(8,128)S(1)} %add.15.refs_0_), channel_id=1, source_target_pairs={{0,6},{1,7},{2,4},{3,5},{4,2},{5,3},{6,0},{7,1},{8,14},{9,15},{10,... | collective-permute-start | bytes 221192 | tf_op jit(solution)/shard_map/ppermute | solution.py:416
  43.4 5.5 %collective-permute-start.23 = (f32[144,128]{1,0:T(8,128)S(1)}, f32[144,128]{1,0:T(8,128)S(1)}, u32[]{:S(2)}, u32[]{:S(2)}) collective-permute-start(f32[144,128]{1,0:T(8,128)S(1)} %add.15.refs_0_), channel_id=1, source_target_pairs={{0,2},{1,3},{2,0},{3,1},{4,6},{5,7},{6,4},{7,5},{8,10},{9,11},{10,... | collective-permute-start | bytes 221192 | tf_op jit(solution)/shard_map/ppermute | solution.py:407
  44.2 8.1 %collective-permute-start.19 = (f32[64,768]{1,0:T(8,128)S(1)}, f32[64,768]{1,0:T(8,128)S(1)}, u32[]{:S(2)}, u32[]{:S(2)}) collective-permute-start(f32[64,768]{1,0:T(8,128)S(1)} %get-tuple-element.88), channel_id=1, source_target_pairs={{0,28},{4,0},{8,4},{12,8},{16,12},{20,16},{24,20},{28,24},{1,29},{... | collective-permute-start | bytes 589832 | tf_op jit(solution)/shard_map/ppermute | solution.py:496
  45.7 3.6 %collective-permute-start.21 = (f32[144,128]{1,0:T(8,128)S(1)}, f32[144,128]{1,0:T(8,128)S(1)}, u32[]{:S(2)}, u32[]{:S(2)}) collective-permute-start(f32[144,128]{1,0:T(8,128)S(1)} %add.15.refs_0_), channel_id=1, source_target_pairs={{0,1},{1,0},{2,3},{3,2},{4,5},{5,4},{6,7},{7,6},{8,9},{9,8},{10,11... | collective-permute-start | bytes 221192 | tf_op jit(solution)/shard_map/ppermute | solution.py:407
  48.0 1.4 %collective-permute-start.26 = (f32[144,128]{1,0:T(8,128)S(1)}, f32[144,128]{1,0:T(8,128)S(1)}, u32[]{:S(2)}, u32[]{:S(2)}) collective-permute-start(f32[144,128]{1,0:T(8,128)S(1)} %collective-permute-done.24.refs_5_), channel_id=1, source_target_pairs={{0,1},{1,0},{2,3},{3,2},{4,5},{5,4},{6,7},{7,6},{8,9},{9,8},{10,11... | collective-permute-start | bytes 221192 | tf_op jit(solution)/shard_map/ppermute | solution.py:407
  48.8 1.3 %collective-permute-start.25 = (f32[144,128]{1,0:T(8,128)S(1)}, f32[144,128]{1,0:T(8,128)S(1)}, u32[]{:S(2)}, u32[]{:S(2)}) collective-permute-start(f32[144,128]{1,0:T(8,128)S(1)} %collective-permute-done.23.refs_4_), channel_id=1, source_target_pairs={{0,1},{1,0},{2,3},{3,2},{4,5},{5,4},{6,7},{7,6},{8,9},{9,8},{10,11... | collective-permute-start | bytes 221192 | tf_op jit(solution)/shard_map/ppermute | solution.py:407
  48.8 1.4 %collective-permute-start.22 = (f32[144,128]{1,0:T(8,128)S(1)}, f32[144,128]{1,0:T(8,128)S(1)}, u32[]{:S(2)}, u32[]{:S(2)}) collective-permute-start(f32[144,128]{1,0:T(8,128)S(1)} %collective-permute-done.20.refs_1_), channel_id=1, source_target_pairs={{0,1},{1,0},{2,3},{3,2},{4,5},{5,4},{6,7},{7,6},{8,9},{9,8},{10,11... | collective-permute-start | bytes 221192 | tf_op jit(solution)/shard_map/ppermute | solution.py:407

commit v11 on v10

--- a/solution.py
+++ b/solution.py
@@ -215,7 +215,7 @@
     rows = half // 2
     group = width // 4
     part, near, core = place()
-    block = lax.axis_index("tm")
+    time = lax.axis_index("tm")
     corner(far, cross, k, live)
     value = 2.0 * columns[...] - times(product[...], k)
     for step in range(TERMS - 1):
@@ -225,7 +225,9 @@
     solved[...] = result.T
     y_own[...] = solved[at(core * rows, rows), :]
     y_core[:rows, :] = solved[at((1 - core) * rows, rows), :]
-    y_core[rows:, :] = s_own[...]
+    for i, block in enumerate((part, 2 * (1 - near), 2 * (1 - near) + 1)):
+        first = rows + i * group
+        y_core[first : first + group, :] = s_own[at(block * group, group, 8), :]
     y_far[:rows, :] = solved[at(half + core * rows, rows), :]
     y_far[rows : 2 * rows, :] = solved[at(half + (1 - core) * rows, rows), :]
     y_far[2 * rows :, :] = s_own[at(2 * near * group, 2 * group, 8), :]
@@ -233,7 +235,7 @@
     def square(shift):
         cols = at(((part + shift) % 4) * group, group, 128)
         parts = dot(left_side, links[:, cols])
-        added = jnp.where(block == 0, base[:, cols], 0.0)
+        added = jnp.where(time == 0, base[:, cols], 0.0)
         return parts[:group] + parts[group:] + added
 
     first = group * 3 // 4
@@ -244,7 +246,7 @@
         part < 2, across[: group // 2, :], across.T[group // 2 :, :]
     )
     size = keep.shape[0]
-    side = block % 2
+    side = time % 2
     keep[...] = pack[at(side * size, size, 8), :]
     send[...] = pack[at((1 - side) * size, size, 8), :]
 
@@ -291,13 +293,14 @@
     def put(rows, cols, low_cols, value):
         start[rows, cols], start[rows, low_cols] = halves(value)
 
+    mine, theirs = at(core * group, group), at((1 - core) * group, group)
     for i in range(width // group):
-        first, cols = i * group, slice(i * group, (i + 1) * group)
-        put_rows(
-            s_own.at[first : first + group, :],
-            y_core.at[rows + first : rows + first + group, :],
-            s_rows.at[:, cols],
-        )
+        first = i * group
+        s_rows[mine, first : first + group] = s_own[first : first + group, :]
+    for i, block in enumerate((part ^ 1, 2 * (1 - near), 2 * (1 - near) + 1)):
+        first = rows + i * group
+        s_rows[theirs, at(block * group, group, 128)] = y_core[first : first + group, :]
+    s_rows[theirs, at(part * group, group, 128)] = s_own[at((part ^ 1) * group, group, 8), :].T
     put(top, left, low_left, s_rows[:, left])
     side = s_rows[:, right]
     put(top, right, low_right, side)
@@ -444,7 +447,7 @@
     k_cross, p_core = lax.optimization_barrier((tile_swap(k_far, 1), p_core))
     keep, send, y_own, y_core, y_far, k = call(
         global_kernel,
-        [((size, group), F32)] * 2 + [((rows, group), F32), ((rows + width, group), F32)]
+        [((size, group), F32)] * 2 + [((rows, group), F32), ((rows + 3 * group, group), F32)]
         + [((2 * rows + 2 * group, group), F32), matrix],
         [vmem((2 * size, group), F32), vmem((order, group), F32)],
         live_cols, k_far, k_cross, x, k, links, columns, first, schur_base, s_own,

time: 53.2 us -> 53.1 us (level)
  starting transfers between devices: 22.1 us -> 21.1 us
  waiting for transfers between devices: 12.6 us -> 13.6 us
    ppermute x1, starting transfers between devices: 1.58 us -> 0.21 us  [shards(): lax.ppermute(next_terms, 'tm', [(i, (i - 1) % blocks) for i in range(bloc...]
    ppermute x1, waiting for transfers between devices: 1.3 us -> 2.22 us  [diagonal_swap(): return lax.ppermute(value, ('tm', 'tile'), pairs)]
  transfers between devices with their start and end apart: 27 -> 27, of which waited for: 10 -> 11; matrix products, arithmetic and copies ran while one was open for 0% -> 0% of each run, Pallas kernels for 30% -> 31%
where the time goes in v11:
time: 53.1 us; the launch traced here: 53 us
  starting transfers between devices  21.1 us (40%)
  Pallas kernels  16.9 us (32%)
  waiting for transfers between devices  13.6 us (26%)
  between operations  1.37 us (3%)
    pallas_call x7, Pallas kernels, call(): pl.pallas_call(kernel, out_shape=[jax.ShapeDtypeStruct(shape, dtype) for...  16.9 us
    ppermute x20, starting transfers between devices, tile_swap(): return lax.ppermute(value, 'tile', [(i, i ^ mask) for i in range(4)])  11.9 us
    ppermute x20, waiting for transfers between devices, tile_swap(): return lax.ppermute(value, 'tile', [(i, i ^ mask) for i in range(4)])  7.92 us
    ppermute x5, starting transfers between devices, block_swap(): return lax.ppermute(value, 'tm', [(i, i ^ mask) for i in range(blocks)])  6.81 us
    ppermute x5, waiting for transfers between devices, block_swap(): return lax.ppermute(value, 'tm', [(i, i ^ mask) for i in range(blocks)])  3.46 us
    ppermute x1, waiting for transfers between devices, diagonal_swap(): return lax.ppermute(value, ('tm', 'tile'), pairs)  2.22 us
    ppermute x1, starting transfers between devices, diagonal_swap(): return lax.ppermute(value, ('tm', 'tile'), pairs)  2.13 us
  transfers between devices with their start and end apart: 27, of which 11 were waited for; matrix products, arithmetic and copies ran while one was open for 0% of the time, Pallas kernels for 31%

profile of v11, /device:TPU:0, one launch (start us, length us, event | category | flops | bytes accessed | tf_op | source)
XLA Modules:
  0.0 53.0 jit_solution(5271849768172124788)
XLA Ops:
  0.6 3.0 %collective-permute-start.3 = (bf16[192,512]{1,0:T(8,128)(2,1)}, bf16[192,512]{1,0:T(8,128)(2,1)S(1)}, u32[]{:S(2)}, u32[]{:S(2)}) collective-permute-start(bf16[192,512]{1,0:T(8,128)(2,1)} %bitcast.13), channel_id=1, source_target_pairs={{0,2},{1,3},{2,0},{3,1},{4,6},{5,7},{6,4},{7,5},{8,10},{9,11},{10,... | collective-permute-start | bytes 589832 | tf_op jit(solution)/shard_map/ppermute | solution.py:410
  3.7 1.5 %pack_kernel.1 = (f32[392,128]{1,0:T(8,128)S(1)}, f32[400,128]{1,0:T(8,128)S(1)}, f32[192,768]{1,0:T(8,128)S(1)}, f32[192,768]{1,0:T(8,128)S(1)}, bf16[192,512]{...) custom-call(f32[192,768]{1,0:T(8,128)} %bitcast.11, f32[192,768]{1,0:T(8,128)} %bitcast.12, ...), custom_call_target="tpu_custom_call" | custom-call | tf_op jit(solution)/shard_map/pack_kernel/pallas_call | solution.py:379
  5.2 0.1 collective-permute-start
  5.2 0.5 collective-permute-start.1
  5.7 0.0 collective-permute-start.4
  5.8 3.5 %collective-permute-done.3.g_far = bf16[192,512]{1,0:T(8,128)(2,1)S(1)} collective-permute-done((bf16[192,512]{1,0:T(8,128)(2,1)}, bf16[192,512]{1,0:T(8,128)(2,1)S(1)}, u32[]{:S(2)}, u32[]{:S(2)}) %collective-permute-start.3) | collective-permute-done | bytes 196640 | tf_op jit(solution)/shard_map/ppermute | solution.py:410
  9.3 0.0 collective-permute-start.5
  9.3 2.4 %collective-permute-start.7 = (f32[400,128]{1,0:T(8,128)S(1)}, f32[400,128]{1,0:T(8,128)S(1)}, u32[]{:S(2)}, u32[]{:S(2)}) collective-permute-start(f32[400,128]{1,0:T(8,128)S(1)} %get-tuple-element.62), channel_id=1, source_target_pairs={{0,2},{1,3},{2,0},{3,1},{4,6},{5,7},{6,4},{7,5},{8,10},{9,11},{10,... | collective-permute-start | bytes 614408 | tf_op jit(solution)/shard_map/ppermute | solution.py:410
  11.7 1.4 %collective-permute-done.4.far = f32[392,128]{1,0:T(8,128)S(1)} collective-permute-done((f32[392,128]{1,0:T(8,128)S(1)}, f32[392,128]{1,0:T(8,128)S(1)}, u32[]{:S(2)}, u32[]{:S(2)}) %collective-permute-start.4) | collective-permute-done | bytes 200736 | tf_op jit(solution)/shard_map/ppermute | solution.py:410
  13.1 0.0 collective-permute-done.5.g_cross
  13.1 0.0 collective-permute-start.6
  13.1 0.5 collective-permute-start.2
  14.2 0.6 %collective-permute-done.2.g_core = bf16[192,512]{1,0:T(8,128)(2,1)S(1)} collective-permute-done((bf16[192,512]{1,0:T(8,128)(2,1)S(1)}, bf16[192,512]{1,0:T(8,128)(2,1)S(1)}, u32[]{:S(2)}, u32[]{:S(2)}) %collective-permute-start.2) | collective-permute-done | bytes 196640 | tf_op jit(solution)/shard_map/ppermute | solution.py:410
  14.8 0.0 collective-permute-done.x_core
  14.8 0.0 collective-permute-done.1.k_core
  14.8 0.0 collective-permute-done.6.cross
  14.8 2.0 %prepare_kernel.1 = (bf16[1536,768]{1,0:T(8,128)(2,1)S(1)}, bf16[1536,768]{1,0:T(8,128)(2,1)S(1)}, bf16[768,512]{1,0:T(8,128)(2,1)S(1)}, f32[768,1]{1,0:T(8,128)...) custom-call(s32[1]{0:T(128)S(6)} %copy.15.sizes, ...), custom_call_target="tpu_custom_call" | custom-call | tf_op jit(solution)/shard_map/prepare_kernel/pallas_call | solution.py:379
  16.8 0.6 %collective-permute-done.7.far = f32[400,128]{1,0:T(8,128)S(1)} collective-permute-done((f32[400,128]{1,0:T(8,128)S(1)}, f32[400,128]{1,0:T(8,128)S(1)}, u32[]{:S(2)}, u32[]{:S(2)}) %collective-permute-start.7) | collective-permute-done | bytes 204832 | tf_op jit(solution)/shard_map/ppermute | solution.py:410
  17.5 0.0 collective-permute-start.8
  17.5 0.5 collective-permute-start.9
  18.0 1.7 %collective-permute-start.10 = (bf16[192,512]{1,0:T(8,128)(2,1)S(1)}, bf16[192,512]{1,0:T(8,128)(2,1)S(1)}, u32[]{:S(2)}, u32[]{:S(2)}) collective-permute-start(bf16[192,512]{1,0:T(8,128)(2,1)S(1)} %bitcast.9), channel_id=1, source_target_pairs={{0,2},{1,3},{2,0},{3,1},{4,6},{5,7},{6,4},{7,5},{8,10},{9,11},{10,... | collective-permute-start | bytes 589832 | tf_op jit(solution)/shard_map/ppermute | solution.py:410
  19.7 0.0 collective-permute-done.9.p_core
  19.7 4.1 %global_kernel.1 = (f32[144,128]{1,0:T(8,128)S(1)}, f32[144,128]{1,0:T(8,128)S(1)}, f32[192,128]{1,0:T(8,128)S(1)}, f32[576,128]{1,0:T(8,128)S(1)}, f32[640,128]...) custom-call(f32[1,768]{1,0:T(1,128)S(1)} %get-tuple-element.67.live, ...), custom_call_target="tpu_custom_call", output_to_operand_aliasing={{5}: (4, {})} | custom-call | tf_op jit(solution)/shard_map/global_kernel/pallas_call | solution.py:379
  23.9 1.6 %collective-permute-start.12 = (f32[144,128]{1,0:T(8,128)S(1)}, f32[144,128]{1,0:T(8,128)S(1)}, u32[]{:S(2)}, u32[]{:S(2)}) collective-permute-start(f32[144,128]{1,0:T(8,128)S(1)} %get-tuple-element.74), channel_id=1, source_target_pairs={{0,8},{4,12},{8,0},{12,4},{16,24},{20,28},{24,16},{28,20},{1,9},{5... | collective-permute-start | bytes 221192 | tf_op jit(solution)/shard_map/ppermute | solution.py:413
  25.5 1.5 %collective-permute-start.13 = (f32[144,128]{1,0:T(8,128)S(1)}, f32[144,128]{1,0:T(8,128)S(1)}, u32[]{:S(2)}, u32[]{:S(2)}) collective-permute-start(f32[144,128]{1,0:T(8,128)S(1)} %get-tuple-element.77), channel_id=1, source_target_pairs={{0,4},{4,0},{8,12},{12,8},{16,20},{20,16},{24,28},{28,24},{1,5},{5... | collective-permute-start | bytes 221192 | tf_op jit(solution)/shard_map/ppermute | solution.py:413
  27.0 0.4 collective-permute-start.14
  27.4 1.2 %collective-permute-start.17 = (f32[640,128]{1,0:T(8,128)S(1)}, f32[640,128]{1,0:T(8,128)S(1)}, u32[]{:S(2)}, u32[]{:S(2)}) collective-permute-start(f32[640,128]{1,0:T(8,128)S(1)} %get-tuple-element.84), channel_id=1, source_target_pairs={{0,2},{1,3},{2,0},{3,1},{4,6},{5,7},{6,4},{7,5},{8,10},{9,11},{10,... | collective-permute-start | bytes 983048 | tf_op jit(solution)/shard_map/ppermute | solution.py:410
  28.7 0.0 collective-permute-done.10.p_far
  28.7 0.0 collective-permute-start.11
  28.7 0.5 collective-permute-start.16
  29.2 0.7 %collective-permute-done.13 = f32[144,128]{1,0:T(8,128)S(1)} collective-permute-done((f32[144,128]{1,0:T(8,128)S(1)}, f32[144,128]{1,0:T(8,128)S(1)}, u32[]{:S(2)}, u32[]{:S(2)}) %collective-permute-start.13) | collective-permute-done | bytes 73760 | tf_op jit(solution)/shard_map/ppermute | solution.py:413
  29.9 2.4 %collective-permute-done.14 = f32[144,128]{1,0:T(8,128)S(1)} collective-permute-done((f32[144,128]{1,0:T(8,128)S(1)}, f32[144,128]{1,0:T(8,128)S(1)}, u32[]{:S(2)}, u32[]{:S(2)}) %collective-permute-start.14) | collective-permute-done | bytes 73760 | tf_op jit(solution)/shard_map/ppermute | solution.py:413
  32.3 2.7 %collective-permute-start.15 = (f32[144,128]{1,0:T(8,128)S(1)}, f32[144,128]{1,0:T(8,128)S(1)}, u32[]{:S(2)}, u32[]{:S(2)}) collective-permute-start(f32[144,128]{1,0:T(8,128)S(1)} %add_add_fusion), channel_id=1, source_target_pairs={{0,16},{4,20},{8,24},{12,28},{16,0},{20,4},{24,8},{28,12},{1,17},{... | collective-permute-start | bytes 221192 | tf_op jit(solution)/shard_map/ppermute | solution.py:413
  34.9 5.6 %pair_kernel.1 = (f32[64,768]{1,0:T(8,128)S(1)}, f32[64,256]{1,0:T(8,128)}, f32[64,768]{1,0:T(8,128)S(1)}) custom-call(f32[768,1]{1,0:T(8,128)S(1)} %get-tuple-element.61.live, bf16[192,512]{1,0:T(8,128)(2,1)S(1)} %bitcast.10, bf16[192,512]{1,0:T(8,128)(2,1)S(1)} %collective-permute-done.9.p_core, bf16[192,512]{1,0:T(8,128)(2,1)S(1)} %collective-permute-done.10.p_far, ...), custom_call_target="tpu_custom_call" | custom-call | tf_op jit(solution)/shard_map/pair_kernel/pallas_call | solution.py:379
  40.5 0.1 collective-permute-start.18
  40.6 0.6 %collective-permute-start.20 = (f32[144,128]{1,0:T(8,128)S(1)}, f32[144,128]{1,0:T(8,128)S(1)}, u32[]{:S(2)}, u32[]{:S(2)}) collective-permute-start(f32[144,128]{1,0:T(8,128)S(1)} %add.15.refs_0_), channel_id=1, source_target_pairs={{0,4},{4,0},{8,12},{12,8},{16,20},{20,16},{24,28},{28,24},{1,5},{5... | collective-permute-start | bytes 221192 | tf_op jit(solution)/shard_map/ppermute | solution.py:413
  41.2 2.1 %collective-permute-start.24 = (f32[144,128]{1,0:T(8,128)S(1)}, f32[144,128]{1,0:T(8,128)S(1)}, u32[]{:S(2)}, u32[]{:S(2)}) collective-permute-start(f32[144,128]{1,0:T(8,128)S(1)} %add.15.refs_0_), channel_id=1, source_target_pairs={{0,6},{1,7},{2,4},{3,5},{4,2},{5,3},{6,0},{7,1},{8,14},{9,15},{10,... | collective-permute-start | bytes 221192 | tf_op jit(solution)/shard_map/ppermute | solution.py:419
  43.3 0.8 %collective-permute-start.23 = (f32[144,128]{1,0:T(8,128)S(1)}, f32[144,128]{1,0:T(8,128)S(1)}, u32[]{:S(2)}, u32[]{:S(2)}) collective-permute-start(f32[144,128]{1,0:T(8,128)S(1)} %add.15.refs_0_), channel_id=1, source_target_pairs={{0,2},{1,3},{2,0},{3,1},{4,6},{5,7},{6,4},{7,5},{8,10},{9,11},{10,... | collective-permute-start | bytes 221192 | tf_op jit(solution)/shard_map/ppermute | solution.py:410
  44.2 0.2 collective-permute-start.19
  44.4 1.0 %start_kernel.1 = (bf16[512,1024]{1,0:T(8,128)(2,1)S(1)}, f32[192,512]{1,0:T(8,128)S(1)}) custom-call(f32[512,128]{1,0:T(8,128)S(1)} %get-tuple-element.73.s_own, f32[192,128]{1,0:T(8,128)S(1)} %get-tuple-element.92.y_own, f32[576,128]{1,0:T(8,128)S(1)} %collective-permute-done.16.y_core, f32[640,128]{1,0:T(8,128)S(1)} %collective-permute-done.17.far, ...), custom_call_target="tpu_custom_call" | custom-call | tf_op jit(solution)/shard_map/start_kernel/pallas_call | solution.py:379
  45.4 0.4 collective-permute-done.20.refs_1_
  45.7 2.2 %collective-permute-done.24.refs_5_ = f32[144,128]{1,0:T(8,128)S(1)} collective-permute-done((f32[144,128]{1,0:T(8,128)S(1)}, f32[144,128]{1,0:T(8,128)S(1)}, u32[]{:S(2)}, u32[]{:S(2)}) %collective-permute-start.24) | collective-permute-done | bytes 73760 | tf_op jit(solution)/shard_map/ppermute | solution.py:419
  48.0 0.8 %collective-permute-done.23.refs_4_ = f32[144,128]{1,0:T(8,128)S(1)} collective-permute-done((f32[144,128]{1,0:T(8,128)S(1)}, f32[144,128]{1,0:T(8,128)S(1)}, u32[]{:S(2)}, u32[]{:S(2)}) %collective-permute-start.23) | collective-permute-done | bytes 73760 | tf_op jit(solution)/shard_map/ppermute | solution.py:410
  48.8 0.5 collective-permute-start.22
  49.3 0.7 %collective-permute-done.25.refs_6_ = f32[144,128]{1,0:T(8,128)S(1)} collective-permute-done((f32[144,128]{1,0:T(8,128)S(1)}, f32[144,128]{1,0:T(8,128)S(1)}, u32[]{:S(2)}, u32[]{:S(2)}) %collective-permute-start.25) | collective-permute-done | bytes 73760 | tf_op jit(solution)/shard_map/ppermute | solution.py:410
  50.1 0.2 collective-permute-done.22.refs_3_
  50.2 2.0 %back_kernel.1 = (f32[128,512]{1,0:T(8,128)}, f32[192,512]{1,0:T(8,128)}) custom-call(f32[144,128]{1,0:T(8,128)S(1)} %add.15.refs_0_, f32[144,128]{1,0:T(8,128)S(1)} %collective-permute-done.20.refs_1_, f32[144,128]{1,0:T(8,128)S(1)} %collective-permute-done.21.refs_2_, f32[144,128]{1,0:T(8,128)S(1)} %collective-permute-done.22.refs_3_, ...), custom_call_target="tpu_custom_call" | custom-call | flops 679477248 | tf_op jit(solution)/shard_map/back_kernel/pallas_call | solution.py:379
  52.3 0.7 %finish_kernel.1 = (f32[64,256]{1,0:T(8,128)}, f32[64,512]{1,0:T(8,128)}) custom-call(f32[64,768]{1,0:T(8,128)S(1)} %get-tuple-element.79.own_terms, f32[64,768]{1,0:T(8,128)S(1)} %collective-permute-done.19.came), custom_call_target="tpu_custom_call" | custom-call | tf_op jit(solution)/shard_map/finish_kernel/pallas_call | solution.py:379
  (19 shorter events, 0.1 us)
Async XLA Ops:
  0.6 8.7 %collective-permute-start.3 = (bf16[192,512]{1,0:T(8,128)(2,1)}, bf16[192,512]{1,0:T(8,128)(2,1)S(1)}, u32[]{:S(2)}, u32[]{:S(2)}) collective-permute-start(bf16[192,512]{1,0:T(8,128)(2,1)} %bitcast.13), channel_id=1, source_target_pairs={{0,2},{1,3},{2,0},{3,1},{4,6},{5,7},{6,4},{7,5},{8,10},{9,11},{10,... | collective-permute-start | bytes 589832 | tf_op jit(solution)/shard_map/ppermute | solution.py:410
  3.7 13.8 %copy-start.1 = (bf16[1,192,512]{2,1,0:T(8,128)(2,1)S(1)}, bf16[1,192,512]{2,1,0:T(8,128)(2,1)}, u32[]{:S(2)}) copy-start(bf16[1,192,512]{2,1,0:T(8,128)(2,1)} %param.12) | copy-start | bytes 589828
  3.7 16.1 %copy-start = (f32[128,512]{1,0:T(8,128)S(1)}, f32[128,512]{1,0:T(8,128)}, u32[]{:S(2)}) copy-start(f32[128,512]{1,0:T(8,128)} %base.1) | copy-start | bytes 786436
  5.2 9.7 %collective-permute-start = (f32[192,768]{1,0:T(8,128)S(1)}, f32[192,768]{1,0:T(8,128)S(1)}, u32[]{:S(2)}, u32[]{:S(2)}) collective-permute-start(f32[192,768]{1,0:T(8,128)S(1)} %get-tuple-element.53.x_own), channel_id=1, source_target_pairs={{0,1},{1,0},{2,3},{3,2},{4,5},{5,4},{6,7},{7,6},{8,9},{9,8},{10,11... | collective-permute-start | bytes 1769480 | tf_op jit(solution)/shard_map/ppermute | solution.py:410
  5.2 9.6 %collective-permute-start.1 = (f32[192,768]{1,0:T(8,128)S(1)}, f32[192,768]{1,0:T(8,128)S(1)}, u32[]{:S(2)}, u32[]{:S(2)}) collective-permute-start(f32[192,768]{1,0:T(8,128)S(1)} %get-tuple-element.54.k_own), channel_id=1, source_target_pairs={{0,1},{1,0},{2,3},{3,2},{4,5},{5,4},{6,7},{7,6},{8,9},{9,8},{10,11... | collective-permute-start | bytes 1769480 | tf_op jit(solution)/shard_map/ppermute | solution.py:410
  5.7 7.3 %collective-permute-start.4 = (f32[392,128]{1,0:T(8,128)S(1)}, f32[392,128]{1,0:T(8,128)S(1)}, u32[]{:S(2)}, u32[]{:S(2)}) collective-permute-start(f32[392,128]{1,0:T(8,128)S(1)} %get-tuple-element.56), channel_id=1, source_target_pairs={{0,2},{1,3},{2,0},{3,1},{4,6},{5,7},{6,4},{7,5},{8,10},{9,11},{10,... | collective-permute-start | bytes 602120 | tf_op jit(solution)/shard_map/ppermute | solution.py:410
  9.3 3.8 %collective-permute-start.5 = (bf16[192,512]{1,0:T(8,128)(2,1)S(1)}, bf16[192,512]{1,0:T(8,128)(2,1)S(1)}, u32[]{:S(2)}, u32[]{:S(2)}) collective-permute-start(bf16[192,512]{1,0:T(8,128)(2,1)S(1)} %collective-permute-done.3.g_far), channel_id=1, source_target_pairs={{0,1},{1,0},{2,3},{3,2},{4,5},{5,4},{6,7},{7,6},{8,9},{9,8},{10,11... | collective-permute-start | bytes 589832 | tf_op jit(solution)/shard_map/ppermute | solution.py:410
  9.3 8.2 %collective-permute-start.7 = (f32[400,128]{1,0:T(8,128)S(1)}, f32[400,128]{1,0:T(8,128)S(1)}, u32[]{:S(2)}, u32[]{:S(2)}) collective-permute-start(f32[400,128]{1,0:T(8,128)S(1)} %get-tuple-element.62), channel_id=1, source_target_pairs={{0,2},{1,3},{2,0},{3,1},{4,6},{5,7},{6,4},{7,5},{8,10},{9,11},{10,... | collective-permute-start | bytes 614408 | tf_op jit(solution)/shard_map/ppermute | solution.py:410
  13.1 1.7 %collective-permute-start.6 = (f32[392,128]{1,0:T(8,128)S(1)}, f32[392,128]{1,0:T(8,128)S(1)}, u32[]{:S(2)}, u32[]{:S(2)}) collective-permute-start(f32[392,128]{1,0:T(8,128)S(1)} %collective-permute-done.4.far), channel_id=1, source_target_pairs={{0,1},{1,0},{2,3},{3,2},{4,5},{5,4},{6,7},{7,6},{8,9},{9,8},{10,11... | collective-permute-start | bytes 602120 | tf_op jit(solution)/shard_map/ppermute | solution.py:410
  13.1 1.7 %collective-permute-start.2 = (bf16[192,512]{1,0:T(8,128)(2,1)S(1)}, bf16[192,512]{1,0:T(8,128)(2,1)S(1)}, u32[]{:S(2)}, u32[]{:S(2)}) collective-permute-start(bf16[192,512]{1,0:T(8,128)(2,1)S(1)} %get-tuple-element.55.g_own), channel_id=1, source_target_pairs={{0,1},{1,0},{2,3},{3,2},{4,5},{5,4},{6,7},{7,6},{8,9},{9,8},{10,11... | collective-permute-start | bytes 589832 | tf_op jit(solution)/shard_map/ppermute | solution.py:410
  17.5 2.3 %collective-permute-start.8 = (f32[400,128]{1,0:T(8,128)S(1)}, f32[400,128]{1,0:T(8,128)S(1)}, u32[]{:S(2)}, u32[]{:S(2)}) collective-permute-start(f32[400,128]{1,0:T(8,128)S(1)} %collective-permute-done.7.far), channel_id=1, source_target_pairs={{0,1},{1,0},{2,3},{3,2},{4,5},{5,4},{6,7},{7,6},{8,9},{9,8},{10,11... | collective-permute-start | bytes 614408 | tf_op jit(solution)/shard_map/ppermute | solution.py:410
  17.5 2.3 %collective-permute-start.9 = (bf16[192,512]{1,0:T(8,128)(2,1)S(1)}, bf16[192,512]{1,0:T(8,128)(2,1)S(1)}, u32[]{:S(2)}, u32[]{:S(2)}) collective-permute-start(bf16[192,512]{1,0:T(8,128)(2,1)S(1)} %bitcast.8), channel_id=1, source_target_pairs={{0,1},{1,0},{2,3},{3,2},{4,5},{5,4},{6,7},{7,6},{8,9},{9,8},{10,11... | collective-permute-start | bytes 589832 | tf_op jit(solution)/shard_map/ppermute | solution.py:410
  18.0 10.7 %collective-permute-start.10 = (bf16[192,512]{1,0:T(8,128)(2,1)S(1)}, bf16[192,512]{1,0:T(8,128)(2,1)S(1)}, u32[]{:S(2)}, u32[]{:S(2)}) collective-permute-start(bf16[192,512]{1,0:T(8,128)(2,1)S(1)} %bitcast.9), channel_id=1, source_target_pairs={{0,2},{1,3},{2,0},{3,1},{4,6},{5,7},{6,4},{7,5},{8,10},{9,11},{10,... | collective-permute-start | bytes 589832 | tf_op jit(solution)/shard_map/ppermute | solution.py:410
  23.9 4.8 %collective-permute-start.12 = (f32[144,128]{1,0:T(8,128)S(1)}, f32[144,128]{1,0:T(8,128)S(1)}, u32[]{:S(2)}, u32[]{:S(2)}) collective-permute-start(f32[144,128]{1,0:T(8,128)S(1)} %get-tuple-element.74), channel_id=1, source_target_pairs={{0,8},{4,12},{8,0},{12,4},{16,24},{20,28},{24,16},{28,20},{1,9},{5... | collective-permute-start | bytes 221192 | tf_op jit(solution)/shard_map/ppermute | solution.py:413
  25.5 4.4 %collective-permute-start.13 = (f32[144,128]{1,0:T(8,128)S(1)}, f32[144,128]{1,0:T(8,128)S(1)}, u32[]{:S(2)}, u32[]{:S(2)}) collective-permute-start(f32[144,128]{1,0:T(8,128)S(1)} %get-tuple-element.77), channel_id=1, source_target_pairs={{0,4},{4,0},{8,12},{12,8},{16,20},{20,16},{24,28},{28,24},{1,5},{5... | collective-permute-start | bytes 221192 | tf_op jit(solution)/shard_map/ppermute | solution.py:413
  27.0 5.3 %collective-permute-start.14 = (f32[144,128]{1,0:T(8,128)S(1)}, f32[144,128]{1,0:T(8,128)S(1)}, u32[]{:S(2)}, u32[]{:S(2)}) collective-permute-start(f32[144,128]{1,0:T(8,128)S(1)} %get-tuple-element.77), channel_id=1, source_target_pairs={{0,12},{4,8},{8,4},{12,0},{16,28},{20,24},{24,20},{28,16},{1,13},{... | collective-permute-start | bytes 221192 | tf_op jit(solution)/shard_map/ppermute | solution.py:413
  27.4 13.1 %collective-permute-start.17 = (f32[640,128]{1,0:T(8,128)S(1)}, f32[640,128]{1,0:T(8,128)S(1)}, u32[]{:S(2)}, u32[]{:S(2)}) collective-permute-start(f32[640,128]{1,0:T(8,128)S(1)} %get-tuple-element.84), channel_id=1, source_target_pairs={{0,2},{1,3},{2,0},{3,1},{4,6},{5,7},{6,4},{7,5},{8,10},{9,11},{10,... | collective-permute-start | bytes 983048 | tf_op jit(solution)/shard_map/ppermute | solution.py:410
  28.7 6.3 %collective-permute-start.11 = (bf16[192,512]{1,0:T(8,128)(2,1)S(1)}, bf16[192,512]{1,0:T(8,128)(2,1)S(1)}, u32[]{:S(2)}, u32[]{:S(2)}) collective-permute-start(bf16[192,512]{1,0:T(8,128)(2,1)S(1)} %collective-permute-done.10.p_far), channel_id=1, source_target_pairs={{0,1},{1,0},{2,3},{3,2},{4,5},{5,4},{6,7},{7,6},{8,9},{9,8},{10,11... | collective-permute-start | bytes 589832 | tf_op jit(solution)/shard_map/ppermute | solution.py:410
  28.7 11.8 %collective-permute-start.16 = (f32[576,128]{1,0:T(8,128)S(1)}, f32[576,128]{1,0:T(8,128)S(1)}, u32[]{:S(2)}, u32[]{:S(2)}) collective-permute-start(f32[576,128]{1,0:T(8,128)S(1)} %get-tuple-element.83), channel_id=1, source_target_pairs={{0,1},{1,0},{2,3},{3,2},{4,5},{5,4},{6,7},{7,6},{8,9},{9,8},{10,11... | collective-permute-start | bytes 884744 | tf_op jit(solution)/shard_map/ppermute | solution.py:410
  32.3 8.2 %collective-permute-start.15 = (f32[144,128]{1,0:T(8,128)S(1)}, f32[144,128]{1,0:T(8,128)S(1)}, u32[]{:S(2)}, u32[]{:S(2)}) collective-permute-start(f32[144,128]{1,0:T(8,128)S(1)} %add_add_fusion), channel_id=1, source_target_pairs={{0,16},{4,20},{8,24},{12,28},{16,0},{20,4},{24,8},{28,12},{1,17},{... | collective-permute-start | bytes 221192 | tf_op jit(solution)/shard_map/ppermute | solution.py:413
  40.5 3.6 %collective-permute-start.18 = (f32[640,128]{1,0:T(8,128)S(1)}, f32[640,128]{1,0:T(8,128)S(1)}, u32[]{:S(2)}, u32[]{:S(2)}) collective-permute-start(f32[640,128]{1,0:T(8,128)S(1)} %collective-permute-done.17.far), channel_id=1, source_target_pairs={{0,1},{1,0},{2,3},{3,2},{4,5},{5,4},{6,7},{7,6},{8,9},{9,8},{10,11... | collective-permute-start | bytes 983048 | tf_op jit(solution)/shard_map/ppermute | solution.py:410
  40.6 5.1 %collective-permute-start.20 = (f32[144,128]{1,0:T(8,128)S(1)}, f32[144,128]{1,0:T(8,128)S(1)}, u32[]{:S(2)}, u32[]{:S(2)}) collective-permute-start(f32[144,128]{1,0:T(8,128)S(1)} %add.15.refs_0_), channel_id=1, source_target_pairs={{0,4},{4,0},{8,12},{12,8},{16,20},{20,16},{24,28},{28,24},{1,5},{5... | collective-permute-start | bytes 221192 | tf_op jit(solution)/shard_map/ppermute | solution.py:413
  41.2 6.8 %collective-permute-start.24 = (f32[144,128]{1,0:T(8,128)S(1)}, f32[144,128]{1,0:T(8,128)S(1)}, u32[]{:S(2)}, u32[]{:S(2)}) collective-permute-start(f32[144,128]{1,0:T(8,128)S(1)} %add.15.refs_0_), channel_id=1, source_target_pairs={{0,6},{1,7},{2,4},{3,5},{4,2},{5,3},{6,0},{7,1},{8,14},{9,15},{10,... | collective-permute-start | bytes 221192 | tf_op jit(solution)/shard_map/ppermute | solution.py:419
  43.3 5.5 %collective-permute-start.23 = (f32[144,128]{1,0:T(8,128)S(1)}, f32[144,128]{1,0:T(8,128)S(1)}, u32[]{:S(2)}, u32[]{:S(2)}) collective-permute-start(f32[144,128]{1,0:T(8,128)S(1)} %add.15.refs_0_), channel_id=1, source_target_pairs={{0,2},{1,3},{2,0},{3,1},{4,6},{5,7},{6,4},{7,5},{8,10},{9,11},{10,... | collective-permute-start | bytes 221192 | tf_op jit(solution)/shard_map/ppermute | solution.py:410
  44.2 8.1 %collective-permute-start.19 = (f32[64,768]{1,0:T(8,128)S(1)}, f32[64,768]{1,0:T(8,128)S(1)}, u32[]{:S(2)}, u32[]{:S(2)}) collective-permute-start(f32[64,768]{1,0:T(8,128)S(1)} %get-tuple-element.88), channel_id=1, source_target_pairs={{0,28},{4,0},{8,4},{12,8},{16,12},{20,16},{24,20},{28,24},{1,29},{... | collective-permute-start | bytes 589832 | tf_op jit(solution)/shard_map/ppermute | solution.py:499
  44.4 5.0 %collective-permute-start.21 = (f32[144,128]{1,0:T(8,128)S(1)}, f32[144,128]{1,0:T(8,128)S(1)}, u32[]{:S(2)}, u32[]{:S(2)}) collective-permute-start(f32[144,128]{1,0:T(8,128)S(1)} %add.15.refs_0_), channel_id=1, source_target_pairs={{0,1},{1,0},{2,3},{3,2},{4,5},{5,4},{6,7},{7,6},{8,9},{9,8},{10,11... | collective-permute-start | bytes 221192 | tf_op jit(solution)/shard_map/ppermute | solution.py:410
  48.0 1.4 %collective-permute-start.26 = (f32[144,128]{1,0:T(8,128)S(1)}, f32[144,128]{1,0:T(8,128)S(1)}, u32[]{:S(2)}, u32[]{:S(2)}) collective-permute-start(f32[144,128]{1,0:T(8,128)S(1)} %collective-permute-done.24.refs_5_), channel_id=1, source_target_pairs={{0,1},{1,0},{2,3},{3,2},{4,5},{5,4},{6,7},{7,6},{8,9},{9,8},{10,11... | collective-permute-start | bytes 221192 | tf_op jit(solution)/shard_map/ppermute | solution.py:410
  48.8 1.3 %collective-permute-start.25 = (f32[144,128]{1,0:T(8,128)S(1)}, f32[144,128]{1,0:T(8,128)S(1)}, u32[]{:S(2)}, u32[]{:S(2)}) collective-permute-start(f32[144,128]{1,0:T(8,128)S(1)} %collective-permute-done.23.refs_4_), channel_id=1, source_target_pairs={{0,1},{1,0},{2,3},{3,2},{4,5},{5,4},{6,7},{7,6},{8,9},{9,8},{10,11... | collective-permute-start | bytes 221192 | tf_op jit(solution)/shard_map/ppermute | solution.py:410
  48.8 1.4 %collective-permute-start.22 = (f32[144,128]{1,0:T(8,128)S(1)}, f32[144,128]{1,0:T(8,128)S(1)}, u32[]{:S(2)}, u32[]{:S(2)}) collective-permute-start(f32[144,128]{1,0:T(8,128)S(1)} %collective-permute-done.20.refs_1_), channel_id=1, source_target_pairs={{0,1},{1,0},{2,3},{3,2},{4,5},{5,4},{6,7},{7,6},{8,9},{9,8},{10,11... | collective-permute-start | bytes 221192 | tf_op jit(solution)/shard_map/ppermute | solution.py:410

commit v12 on v11

--- a/solution.py
+++ b/solution.py
@@ -457,7 +457,7 @@
     y_all = (y_own, tile_swap(y_core, 1), tile_swap(y_far, 2))
     if blocks > 2:
         parts = [block_swap(send, 1), block_swap(keep, 2), block_swap(send, 3)]
-        total = (keep + parts[1]) + (parts[0] + parts[2])
+        total = (parts[2] + parts[0]) + (parts[1] + keep)
     else:
         total = keep + block_swap(send, 1)
     p_far = after(p_far, keep)

time: 53.1 us -> 52.4 us (0.987)
  waiting for transfers between devices: 13.6 us -> 11.8 us
  starting transfers between devices: 21.1 us -> 22.1 us
    ppermute x1, starting transfers between devices: 0.21 us -> 1.77 us  [shards(): lax.ppermute(next_terms, 'tm', [(i, (i - 1) % blocks) for i in range(bloc...]
    ppermute x1, waiting for transfers between devices: 2.22 us -> 1.08 us  [diagonal_swap(): return lax.ppermute(value, ('tm', 'tile'), pairs)]
    ppermute x1, starting transfers between devices: 2.13 us -> 1.19 us  [diagonal_swap(): return lax.ppermute(value, ('tm', 'tile'), pairs)]
    ppermute x5, starting transfers between devices: 6.81 us -> 7.75 us  [block_swap(): return lax.ppermute(value, 'tm', [(i, i ^ mask) for i in range(blocks)])]
    ppermute x5, waiting for transfers between devices: 3.46 us -> 2.68 us  [block_swap(): return lax.ppermute(value, 'tm', [(i, i ^ mask) for i in range(blocks)])]
where the time goes in v12:
time: 52.4 us; the launch traced here: 52.2 us
  starting transfers between devices  22.1 us (42%)
  Pallas kernels  16.9 us (32%)
  waiting for transfers between devices  11.8 us (23%)
  between operations  1.37 us (3%)
    pallas_call x7, Pallas kernels, call(): pl.pallas_call(kernel, out_shape=[jax.ShapeDtypeStruct(shape, dtype) for...  16.9 us
    ppermute x20, starting transfers between devices, tile_swap(): return lax.ppermute(value, 'tile', [(i, i ^ mask) for i in range(4)])  11.4 us
    ppermute x20, waiting for transfers between devices, tile_swap(): return lax.ppermute(value, 'tile', [(i, i ^ mask) for i in range(4)])  8.01 us
    ppermute x5, starting transfers between devices, block_swap(): return lax.ppermute(value, 'tm', [(i, i ^ mask) for i in range(blocks)])  7.75 us
    ppermute x5, waiting for transfers between devices, block_swap(): return lax.ppermute(value, 'tm', [(i, i ^ mask) for i in range(blocks)])  2.68 us
    ppermute x1, starting transfers between devices, shards(): lax.ppermute(next_terms, 'tm', [(i, (i - 1) % blocks) for i in range(bloc...  1.77 us
    ppermute x1, starting transfers between devices, diagonal_swap(): return lax.ppermute(value, ('tm', 'tile'), pairs)  1.19 us
    ppermute x1, waiting for transfers between devices, diagonal_swap(): return lax.ppermute(value, ('tm', 'tile'), pairs)  1.08 us
  transfers between devices with their start and end apart: 27, of which 11 were waited for; matrix products, arithmetic and copies ran while one was open for 0% of the time, Pallas kernels for 31%

profile of v12, /device:TPU:0, one launch (start us, length us, event | category | flops | bytes accessed | tf_op | source)
XLA Modules:
  0.0 52.2 jit_solution(15835270423546402974)
XLA Ops:
  0.6 3.0 %collective-permute-start.3 = (bf16[192,512]{1,0:T(8,128)(2,1)}, bf16[192,512]{1,0:T(8,128)(2,1)S(1)}, u32[]{:S(2)}, u32[]{:S(2)}) collective-permute-start(bf16[192,512]{1,0:T(8,128)(2,1)} %bitcast.13), channel_id=1, source_target_pairs={{0,2},{1,3},{2,0},{3,1},{4,6},{5,7},{6,4},{7,5},{8,10},{9,11},{10,... | collective-permute-start | bytes 589832 | tf_op jit(solution)/shard_map/ppermute | solution.py:410
  3.7 1.5 %pack_kernel.1 = (f32[392,128]{1,0:T(8,128)S(1)}, f32[400,128]{1,0:T(8,128)S(1)}, f32[192,768]{1,0:T(8,128)S(1)}, f32[192,768]{1,0:T(8,128)S(1)}, bf16[192,512]{...) custom-call(f32[192,768]{1,0:T(8,128)} %bitcast.11, f32[192,768]{1,0:T(8,128)} %bitcast.12, ...), custom_call_target="tpu_custom_call" | custom-call | tf_op jit(solution)/shard_map/pack_kernel/pallas_call | solution.py:379
  5.2 0.1 collective-permute-start
  5.2 0.5 collective-permute-start.1
  5.7 0.0 collective-permute-start.4
  5.8 3.5 %collective-permute-done.3.g_far = bf16[192,512]{1,0:T(8,128)(2,1)S(1)} collective-permute-done((bf16[192,512]{1,0:T(8,128)(2,1)}, bf16[192,512]{1,0:T(8,128)(2,1)S(1)}, u32[]{:S(2)}, u32[]{:S(2)}) %collective-permute-start.3) | collective-permute-done | bytes 196640 | tf_op jit(solution)/shard_map/ppermute | solution.py:410
  9.3 2.4 %collective-permute-start.7 = (f32[400,128]{1,0:T(8,128)S(1)}, f32[400,128]{1,0:T(8,128)S(1)}, u32[]{:S(2)}, u32[]{:S(2)}) collective-permute-start(f32[400,128]{1,0:T(8,128)S(1)} %get-tuple-element.62), channel_id=1, source_target_pairs={{0,2},{1,3},{2,0},{3,1},{4,6},{5,7},{6,4},{7,5},{8,10},{9,11},{10,... | collective-permute-start | bytes 614408 | tf_op jit(solution)/shard_map/ppermute | solution.py:410
  11.7 1.4 %collective-permute-done.4.far = f32[392,128]{1,0:T(8,128)S(1)} collective-permute-done((f32[392,128]{1,0:T(8,128)S(1)}, f32[392,128]{1,0:T(8,128)S(1)}, u32[]{:S(2)}, u32[]{:S(2)}) %collective-permute-start.4) | collective-permute-done | bytes 200736 | tf_op jit(solution)/shard_map/ppermute | solution.py:410
  13.1 0.5 collective-permute-start.2
  14.2 0.6 %collective-permute-done.2.g_core = bf16[192,512]{1,0:T(8,128)(2,1)S(1)} collective-permute-done((bf16[192,512]{1,0:T(8,128)(2,1)S(1)}, bf16[192,512]{1,0:T(8,128)(2,1)S(1)}, u32[]{:S(2)}, u32[]{:S(2)}) %collective-permute-start.2) | collective-permute-done | bytes 196640 | tf_op jit(solution)/shard_map/ppermute | solution.py:410
  14.8 2.0 %prepare_kernel.1 = (bf16[1536,768]{1,0:T(8,128)(2,1)S(1)}, bf16[1536,768]{1,0:T(8,128)(2,1)S(1)}, bf16[768,512]{1,0:T(8,128)(2,1)S(1)}, f32[768,1]{1,0:T(8,128)...) custom-call(s32[1]{0:T(128)S(6)} %copy.15.sizes, ...), custom_call_target="tpu_custom_call" | custom-call | tf_op jit(solution)/shard_map/prepare_kernel/pallas_call | solution.py:379
  16.8 0.6 %collective-permute-done.7.far = f32[400,128]{1,0:T(8,128)S(1)} collective-permute-done((f32[400,128]{1,0:T(8,128)S(1)}, f32[400,128]{1,0:T(8,128)S(1)}, u32[]{:S(2)}, u32[]{:S(2)}) %collective-permute-start.7) | collective-permute-done | bytes 204832 | tf_op jit(solution)/shard_map/ppermute | solution.py:410
  17.5 0.5 collective-permute-start.9
  18.0 1.7 %collective-permute-start.10 = (bf16[192,512]{1,0:T(8,128)(2,1)S(1)}, bf16[192,512]{1,0:T(8,128)(2,1)S(1)}, u32[]{:S(2)}, u32[]{:S(2)}) collective-permute-start(bf16[192,512]{1,0:T(8,128)(2,1)S(1)} %bitcast.9), channel_id=1, source_target_pairs={{0,2},{1,3},{2,0},{3,1},{4,6},{5,7},{6,4},{7,5},{8,10},{9,11},{10,... | collective-permute-start | bytes 589832 | tf_op jit(solution)/shard_map/ppermute | solution.py:410
  19.7 0.0 collective-permute-done.8.cross
  19.7 4.1 %global_kernel.1 = (f32[144,128]{1,0:T(8,128)S(1)}, f32[144,128]{1,0:T(8,128)S(1)}, f32[192,128]{1,0:T(8,128)S(1)}, f32[576,128]{1,0:T(8,128)S(1)}, f32[640,128]...) custom-call(f32[1,768]{1,0:T(1,128)S(1)} %get-tuple-element.67.live, ...), custom_call_target="tpu_custom_call", output_to_operand_aliasing={{5}: (4, {})} | custom-call | tf_op jit(solution)/shard_map/global_kernel/pallas_call | solution.py:379
  23.9 2.6 %collective-permute-start.12 = (f32[144,128]{1,0:T(8,128)S(1)}, f32[144,128]{1,0:T(8,128)S(1)}, u32[]{:S(2)}, u32[]{:S(2)}) collective-permute-start(f32[144,128]{1,0:T(8,128)S(1)} %get-tuple-element.77), channel_id=1, source_target_pairs={{0,12},{4,8},{8,4},{12,0},{16,28},{20,24},{24,20},{28,16},{1,13},{... | collective-permute-start | bytes 221192 | tf_op jit(solution)/shard_map/ppermute | solution.py:413
  26.4 0.5 %collective-permute-start.13 = (f32[144,128]{1,0:T(8,128)S(1)}, f32[144,128]{1,0:T(8,128)S(1)}, u32[]{:S(2)}, u32[]{:S(2)}) collective-permute-start(f32[144,128]{1,0:T(8,128)S(1)} %get-tuple-element.77), channel_id=1, source_target_pairs={{0,4},{4,0},{8,12},{12,8},{16,20},{20,16},{24,28},{28,24},{1,5},{5... | collective-permute-start | bytes 221192 | tf_op jit(solution)/shard_map/ppermute | solution.py:413
  27.0 0.4 collective-permute-start.14
  27.4 1.2 %collective-permute-start.17 = (f32[640,128]{1,0:T(8,128)S(1)}, f32[640,128]{1,0:T(8,128)S(1)}, u32[]{:S(2)}, u32[]{:S(2)}) collective-permute-start(f32[640,128]{1,0:T(8,128)S(1)} %get-tuple-element.84), channel_id=1, source_target_pairs={{0,2},{1,3},{2,0},{3,1},{4,6},{5,7},{6,4},{7,5},{8,10},{9,11},{10,... | collective-permute-start | bytes 983048 | tf_op jit(solution)/shard_map/ppermute | solution.py:410
  28.7 0.0 collective-permute-done.10.p_far
  28.7 0.0 collective-permute-start.11
  28.7 0.6 %collective-permute-done.12 = f32[144,128]{1,0:T(8,128)S(1)} collective-permute-done((f32[144,128]{1,0:T(8,128)S(1)}, f32[144,128]{1,0:T(8,128)S(1)}, u32[]{:S(2)}, u32[]{:S(2)}) %collective-permute-start.12) | collective-permute-done | bytes 73760 | tf_op jit(solution)/shard_map/ppermute | solution.py:413
  29.3 1.5 %collective-permute-done.13 = f32[144,128]{1,0:T(8,128)S(1)} collective-permute-done((f32[144,128]{1,0:T(8,128)S(1)}, f32[144,128]{1,0:T(8,128)S(1)}, u32[]{:S(2)}, u32[]{:S(2)}) %collective-permute-start.13) | collective-permute-done | bytes 73760 | tf_op jit(solution)/shard_map/ppermute | solution.py:413
  30.8 0.5 %collective-permute-done.14 = f32[144,128]{1,0:T(8,128)S(1)} collective-permute-done((f32[144,128]{1,0:T(8,128)S(1)}, f32[144,128]{1,0:T(8,128)S(1)}, u32[]{:S(2)}, u32[]{:S(2)}) %collective-permute-start.14) | collective-permute-done | bytes 73760 | tf_op jit(solution)/shard_map/ppermute | solution.py:413
  31.4 2.7 %collective-permute-start.15 = (f32[144,128]{1,0:T(8,128)S(1)}, f32[144,128]{1,0:T(8,128)S(1)}, u32[]{:S(2)}, u32[]{:S(2)}) collective-permute-start(f32[144,128]{1,0:T(8,128)S(1)} %add_add_fusion), channel_id=1, source_target_pairs={{0,16},{4,20},{8,24},{12,28},{16,0},{20,4},{24,8},{28,12},{1,17},{... | collective-permute-start | bytes 221192 | tf_op jit(solution)/shard_map/ppermute | solution.py:413
  34.0 0.0 collective-permute-done.11.p_cross
  34.0 5.6 %pair_kernel.1 = (f32[64,768]{1,0:T(8,128)S(1)}, f32[64,256]{1,0:T(8,128)}, f32[64,768]{1,0:T(8,128)S(1)}) custom-call(f32[768,1]{1,0:T(8,128)S(1)} %get-tuple-element.61.live, bf16[192,512]{1,0:T(8,128)(2,1)S(1)} %bitcast.10, bf16[192,512]{1,0:T(8,128)(2,1)S(1)} %collective-permute-done.9.p_core, bf16[192,512]{1,0:T(8,128)(2,1)S(1)} %collective-permute-done.10.p_far, ...), custom_call_target="tpu_custom_call" | custom-call | tf_op jit(solution)/shard_map/pair_kernel/pallas_call | solution.py:379
  39.6 0.0 collective-permute-done.15
  39.6 0.0 collective-permute-done.16.y_core
  39.6 0.1 collective-permute-start.18
  39.7 1.5 %collective-permute-start.20 = (f32[144,128]{1,0:T(8,128)S(1)}, f32[144,128]{1,0:T(8,128)S(1)}, u32[]{:S(2)}, u32[]{:S(2)}) collective-permute-start(f32[144,128]{1,0:T(8,128)S(1)} %add.15.refs_0_), channel_id=1, source_target_pairs={{0,4},{4,0},{8,12},{12,8},{16,20},{20,16},{24,28},{28,24},{1,5},{5... | collective-permute-start | bytes 221192 | tf_op jit(solution)/shard_map/ppermute | solution.py:413
  41.2 1.2 %collective-permute-start.24 = (f32[144,128]{1,0:T(8,128)S(1)}, f32[144,128]{1,0:T(8,128)S(1)}, u32[]{:S(2)}, u32[]{:S(2)}) collective-permute-start(f32[144,128]{1,0:T(8,128)S(1)} %add.15.refs_0_), channel_id=1, source_target_pairs={{0,6},{1,7},{2,4},{3,5},{4,2},{5,3},{6,0},{7,1},{8,14},{9,15},{10,... | collective-permute-start | bytes 221192 | tf_op jit(solution)/shard_map/ppermute | solution.py:419
  42.4 0.8 %collective-permute-start.23 = (f32[144,128]{1,0:T(8,128)S(1)}, f32[144,128]{1,0:T(8,128)S(1)}, u32[]{:S(2)}, u32[]{:S(2)}) collective-permute-start(f32[144,128]{1,0:T(8,128)S(1)} %add.15.refs_0_), channel_id=1, source_target_pairs={{0,2},{1,3},{2,0},{3,1},{4,6},{5,7},{6,4},{7,5},{8,10},{9,11},{10,... | collective-permute-start | bytes 221192 | tf_op jit(solution)/shard_map/ppermute | solution.py:410
  43.2 1.8 %collective-permute-start.19 = (f32[64,768]{1,0:T(8,128)S(1)}, f32[64,768]{1,0:T(8,128)S(1)}, u32[]{:S(2)}, u32[]{:S(2)}) collective-permute-start(f32[64,768]{1,0:T(8,128)S(1)} %get-tuple-element.88), channel_id=1, source_target_pairs={{0,28},{4,0},{8,4},{12,8},{16,12},{20,16},{24,20},{28,24},{1,29},{... | collective-permute-start | bytes 589832 | tf_op jit(solution)/shard_map/ppermute | solution.py:499
  45.0 0.0 collective-permute-start.21
  45.0 1.0 %start_kernel.1 = (bf16[512,1024]{1,0:T(8,128)(2,1)S(1)}, f32[192,512]{1,0:T(8,128)S(1)}) custom-call(f32[512,128]{1,0:T(8,128)S(1)} %get-tuple-element.73.s_own, f32[192,128]{1,0:T(8,128)S(1)} %get-tuple-element.92.y_own, f32[576,128]{1,0:T(8,128)S(1)} %collective-permute-done.16.y_core, f32[640,128]{1,0:T(8,128)S(1)} %collective-permute-done.17.far, ...), custom_call_target="tpu_custom_call" | custom-call | tf_op jit(solution)/shard_map/start_kernel/pallas_call | solution.py:379
  46.0 0.0 collective-permute-done.20.refs_1_
  46.0 1.1 %collective-permute-done.24.refs_5_ = f32[144,128]{1,0:T(8,128)S(1)} collective-permute-done((f32[144,128]{1,0:T(8,128)S(1)}, f32[144,128]{1,0:T(8,128)S(1)}, u32[]{:S(2)}, u32[]{:S(2)}) %collective-permute-start.24) | collective-permute-done | bytes 73760 | tf_op jit(solution)/shard_map/ppermute | solution.py:419
  47.1 0.0 collective-permute-start.26
  47.1 0.9 %collective-permute-done.23.refs_4_ = f32[144,128]{1,0:T(8,128)S(1)} collective-permute-done((f32[144,128]{1,0:T(8,128)S(1)}, f32[144,128]{1,0:T(8,128)S(1)}, u32[]{:S(2)}, u32[]{:S(2)}) %collective-permute-start.23) | collective-permute-done | bytes 73760 | tf_op jit(solution)/shard_map/ppermute | solution.py:410
  48.1 0.0 collective-permute-start.25
  48.1 0.5 collective-permute-start.22
  48.6 0.7 %collective-permute-done.25.refs_6_ = f32[144,128]{1,0:T(8,128)S(1)} collective-permute-done((f32[144,128]{1,0:T(8,128)S(1)}, f32[144,128]{1,0:T(8,128)S(1)}, u32[]{:S(2)}, u32[]{:S(2)}) %collective-permute-start.25) | collective-permute-done | bytes 73760 | tf_op jit(solution)/shard_map/ppermute | solution.py:410
  49.3 0.2 collective-permute-done.22.refs_3_
  49.5 2.1 %back_kernel.1 = (f32[128,512]{1,0:T(8,128)}, f32[192,512]{1,0:T(8,128)}) custom-call(f32[144,128]{1,0:T(8,128)S(1)} %add.15.refs_0_, f32[144,128]{1,0:T(8,128)S(1)} %collective-permute-done.20.refs_1_, f32[144,128]{1,0:T(8,128)S(1)} %collective-permute-done.21.refs_2_, f32[144,128]{1,0:T(8,128)S(1)} %collective-permute-done.22.refs_3_, ...), custom_call_target="tpu_custom_call" | custom-call | flops 679477248 | tf_op jit(solution)/shard_map/back_kernel/pallas_call | solution.py:379
  51.5 0.0 collective-permute-done.19.came
  51.5 0.7 %finish_kernel.1 = (f32[64,256]{1,0:T(8,128)}, f32[64,512]{1,0:T(8,128)}) custom-call(f32[64,768]{1,0:T(8,128)S(1)} %get-tuple-element.79.own_terms, f32[64,768]{1,0:T(8,128)S(1)} %collective-permute-done.19.came), custom_call_target="tpu_custom_call" | custom-call | tf_op jit(solution)/shard_map/finish_kernel/pallas_call | solution.py:379
  (19 shorter events, 0.1 us)
Async XLA Ops:
  0.6 8.7 %collective-permute-start.3 = (bf16[192,512]{1,0:T(8,128)(2,1)}, bf16[192,512]{1,0:T(8,128)(2,1)S(1)}, u32[]{:S(2)}, u32[]{:S(2)}) collective-permute-start(bf16[192,512]{1,0:T(8,128)(2,1)} %bitcast.13), channel_id=1, source_target_pairs={{0,2},{1,3},{2,0},{3,1},{4,6},{5,7},{6,4},{7,5},{8,10},{9,11},{10,... | collective-permute-start | bytes 589832 | tf_op jit(solution)/shard_map/ppermute | solution.py:410
  3.7 13.8 %copy-start.1 = (bf16[1,192,512]{2,1,0:T(8,128)(2,1)S(1)}, bf16[1,192,512]{2,1,0:T(8,128)(2,1)}, u32[]{:S(2)}) copy-start(bf16[1,192,512]{2,1,0:T(8,128)(2,1)} %param.12) | copy-start | bytes 589828
  3.7 16.1 %copy-start = (f32[128,512]{1,0:T(8,128)S(1)}, f32[128,512]{1,0:T(8,128)}, u32[]{:S(2)}) copy-start(f32[128,512]{1,0:T(8,128)} %base.1) | copy-start | bytes 786436
  5.2 9.7 %collective-permute-start = (f32[192,768]{1,0:T(8,128)S(1)}, f32[192,768]{1,0:T(8,128)S(1)}, u32[]{:S(2)}, u32[]{:S(2)}) collective-permute-start(f32[192,768]{1,0:T(8,128)S(1)} %get-tuple-element.53.x_own), channel_id=1, source_target_pairs={{0,1},{1,0},{2,3},{3,2},{4,5},{5,4},{6,7},{7,6},{8,9},{9,8},{10,11... | collective-permute-start | bytes 1769480 | tf_op jit(solution)/shard_map/ppermute | solution.py:410
  5.2 9.6 %collective-permute-start.1 = (f32[192,768]{1,0:T(8,128)S(1)}, f32[192,768]{1,0:T(8,128)S(1)}, u32[]{:S(2)}, u32[]{:S(2)}) collective-permute-start(f32[192,768]{1,0:T(8,128)S(1)} %get-tuple-element.54.k_own), channel_id=1, source_target_pairs={{0,1},{1,0},{2,3},{3,2},{4,5},{5,4},{6,7},{7,6},{8,9},{9,8},{10,11... | collective-permute-start | bytes 1769480 | tf_op jit(solution)/shard_map/ppermute | solution.py:410
  5.7 7.3 %collective-permute-start.4 = (f32[392,128]{1,0:T(8,128)S(1)}, f32[392,128]{1,0:T(8,128)S(1)}, u32[]{:S(2)}, u32[]{:S(2)}) collective-permute-start(f32[392,128]{1,0:T(8,128)S(1)} %get-tuple-element.56), channel_id=1, source_target_pairs={{0,2},{1,3},{2,0},{3,1},{4,6},{5,7},{6,4},{7,5},{8,10},{9,11},{10,... | collective-permute-start | bytes 602120 | tf_op jit(solution)/shard_map/ppermute | solution.py:410
  9.3 3.8 %collective-permute-start.5 = (bf16[192,512]{1,0:T(8,128)(2,1)S(1)}, bf16[192,512]{1,0:T(8,128)(2,1)S(1)}, u32[]{:S(2)}, u32[]{:S(2)}) collective-permute-start(bf16[192,512]{1,0:T(8,128)(2,1)S(1)} %collective-permute-done.3.g_far), channel_id=1, source_target_pairs={{0,1},{1,0},{2,3},{3,2},{4,5},{5,4},{6,7},{7,6},{8,9},{9,8},{10,11... | collective-permute-start | bytes 589832 | tf_op jit(solution)/shard_map/ppermute | solution.py:410
  9.3 8.2 %collective-permute-start.7 = (f32[400,128]{1,0:T(8,128)S(1)}, f32[400,128]{1,0:T(8,128)S(1)}, u32[]{:S(2)}, u32[]{:S(2)}) collective-permute-start(f32[400,128]{1,0:T(8,128)S(1)} %get-tuple-element.62), channel_id=1, source_target_pairs={{0,2},{1,3},{2,0},{3,1},{4,6},{5,7},{6,4},{7,5},{8,10},{9,11},{10,... | collective-permute-start | bytes 614408 | tf_op jit(solution)/shard_map/ppermute | solution.py:410
  13.1 1.7 %collective-permute-start.6 = (f32[392,128]{1,0:T(8,128)S(1)}, f32[392,128]{1,0:T(8,128)S(1)}, u32[]{:S(2)}, u32[]{:S(2)}) collective-permute-start(f32[392,128]{1,0:T(8,128)S(1)} %collective-permute-done.4.far), channel_id=1, source_target_pairs={{0,1},{1,0},{2,3},{3,2},{4,5},{5,4},{6,7},{7,6},{8,9},{9,8},{10,11... | collective-permute-start | bytes 602120 | tf_op jit(solution)/shard_map/ppermute | solution.py:410
  13.1 1.7 %collective-permute-start.2 = (bf16[192,512]{1,0:T(8,128)(2,1)S(1)}, bf16[192,512]{1,0:T(8,128)(2,1)S(1)}, u32[]{:S(2)}, u32[]{:S(2)}) collective-permute-start(bf16[192,512]{1,0:T(8,128)(2,1)S(1)} %get-tuple-element.55.g_own), channel_id=1, source_target_pairs={{0,1},{1,0},{2,3},{3,2},{4,5},{5,4},{6,7},{7,6},{8,9},{9,8},{10,11... | collective-permute-start | bytes 589832 | tf_op jit(solution)/shard_map/ppermute | solution.py:410
  17.5 2.3 %collective-permute-start.8 = (f32[400,128]{1,0:T(8,128)S(1)}, f32[400,128]{1,0:T(8,128)S(1)}, u32[]{:S(2)}, u32[]{:S(2)}) collective-permute-start(f32[400,128]{1,0:T(8,128)S(1)} %collective-permute-done.7.far), channel_id=1, source_target_pairs={{0,1},{1,0},{2,3},{3,2},{4,5},{5,4},{6,7},{7,6},{8,9},{9,8},{10,11... | collective-permute-start | bytes 614408 | tf_op jit(solution)/shard_map/ppermute | solution.py:410
  17.5 2.3 %collective-permute-start.9 = (bf16[192,512]{1,0:T(8,128)(2,1)S(1)}, bf16[192,512]{1,0:T(8,128)(2,1)S(1)}, u32[]{:S(2)}, u32[]{:S(2)}) collective-permute-start(bf16[192,512]{1,0:T(8,128)(2,1)S(1)} %bitcast.8), channel_id=1, source_target_pairs={{0,1},{1,0},{2,3},{3,2},{4,5},{5,4},{6,7},{7,6},{8,9},{9,8},{10,11... | collective-permute-start | bytes 589832 | tf_op jit(solution)/shard_map/ppermute | solution.py:410
  18.0 10.7 %collective-permute-start.10 = (bf16[192,512]{1,0:T(8,128)(2,1)S(1)}, bf16[192,512]{1,0:T(8,128)(2,1)S(1)}, u32[]{:S(2)}, u32[]{:S(2)}) collective-permute-start(bf16[192,512]{1,0:T(8,128)(2,1)S(1)} %bitcast.9), channel_id=1, source_target_pairs={{0,2},{1,3},{2,0},{3,1},{4,6},{5,7},{6,4},{7,5},{8,10},{9,11},{10,... | collective-permute-start | bytes 589832 | tf_op jit(solution)/shard_map/ppermute | solution.py:410
  23.9 5.4 %collective-permute-start.12 = (f32[144,128]{1,0:T(8,128)S(1)}, f32[144,128]{1,0:T(8,128)S(1)}, u32[]{:S(2)}, u32[]{:S(2)}) collective-permute-start(f32[144,128]{1,0:T(8,128)S(1)} %get-tuple-element.77), channel_id=1, source_target_pairs={{0,12},{4,8},{8,4},{12,0},{16,28},{20,24},{24,20},{28,16},{1,13},{... | collective-permute-start | bytes 221192 | tf_op jit(solution)/shard_map/ppermute | solution.py:413
  26.4 4.4 %collective-permute-start.13 = (f32[144,128]{1,0:T(8,128)S(1)}, f32[144,128]{1,0:T(8,128)S(1)}, u32[]{:S(2)}, u32[]{:S(2)}) collective-permute-start(f32[144,128]{1,0:T(8,128)S(1)} %get-tuple-element.77), channel_id=1, source_target_pairs={{0,4},{4,0},{8,12},{12,8},{16,20},{20,16},{24,28},{28,24},{1,5},{5... | collective-permute-start | bytes 221192 | tf_op jit(solution)/shard_map/ppermute | solution.py:413
  27.0 4.4 %collective-permute-start.14 = (f32[144,128]{1,0:T(8,128)S(1)}, f32[144,128]{1,0:T(8,128)S(1)}, u32[]{:S(2)}, u32[]{:S(2)}) collective-permute-start(f32[144,128]{1,0:T(8,128)S(1)} %get-tuple-element.74), channel_id=1, source_target_pairs={{0,8},{4,12},{8,0},{12,4},{16,24},{20,28},{24,16},{28,20},{1,9},{5... | collective-permute-start | bytes 221192 | tf_op jit(solution)/shard_map/ppermute | solution.py:413
  27.4 12.1 %collective-permute-start.17 = (f32[640,128]{1,0:T(8,128)S(1)}, f32[640,128]{1,0:T(8,128)S(1)}, u32[]{:S(2)}, u32[]{:S(2)}) collective-permute-start(f32[640,128]{1,0:T(8,128)S(1)} %get-tuple-element.84), channel_id=1, source_target_pairs={{0,2},{1,3},{2,0},{3,1},{4,6},{5,7},{6,4},{7,5},{8,10},{9,11},{10,... | collective-permute-start | bytes 983048 | tf_op jit(solution)/shard_map/ppermute | solution.py:410
  28.7 5.4 %collective-permute-start.11 = (bf16[192,512]{1,0:T(8,128)(2,1)S(1)}, bf16[192,512]{1,0:T(8,128)(2,1)S(1)}, u32[]{:S(2)}, u32[]{:S(2)}) collective-permute-start(bf16[192,512]{1,0:T(8,128)(2,1)S(1)} %collective-permute-done.10.p_far), channel_id=1, source_target_pairs={{0,1},{1,0},{2,3},{3,2},{4,5},{5,4},{6,7},{7,6},{8,9},{9,8},{10,11... | collective-permute-start | bytes 589832 | tf_op jit(solution)/shard_map/ppermute | solution.py:410
  29.3 10.3 %collective-permute-start.16 = (f32[576,128]{1,0:T(8,128)S(1)}, f32[576,128]{1,0:T(8,128)S(1)}, u32[]{:S(2)}, u32[]{:S(2)}) collective-permute-start(f32[576,128]{1,0:T(8,128)S(1)} %get-tuple-element.83), channel_id=1, source_target_pairs={{0,1},{1,0},{2,3},{3,2},{4,5},{5,4},{6,7},{7,6},{8,9},{9,8},{10,11... | collective-permute-start | bytes 884744 | tf_op jit(solution)/shard_map/ppermute | solution.py:410
  31.4 8.2 %collective-permute-start.15 = (f32[144,128]{1,0:T(8,128)S(1)}, f32[144,128]{1,0:T(8,128)S(1)}, u32[]{:S(2)}, u32[]{:S(2)}) collective-permute-start(f32[144,128]{1,0:T(8,128)S(1)} %add_add_fusion), channel_id=1, source_target_pairs={{0,16},{4,20},{8,24},{12,28},{16,0},{20,4},{24,8},{28,12},{1,17},{... | collective-permute-start | bytes 221192 | tf_op jit(solution)/shard_map/ppermute | solution.py:413
  39.6 3.6 %collective-permute-start.18 = (f32[640,128]{1,0:T(8,128)S(1)}, f32[640,128]{1,0:T(8,128)S(1)}, u32[]{:S(2)}, u32[]{:S(2)}) collective-permute-start(f32[640,128]{1,0:T(8,128)S(1)} %collective-permute-done.17.far), channel_id=1, source_target_pairs={{0,1},{1,0},{2,3},{3,2},{4,5},{5,4},{6,7},{7,6},{8,9},{9,8},{10,11... | collective-permute-start | bytes 983048 | tf_op jit(solution)/shard_map/ppermute | solution.py:410
  39.7 6.3 %collective-permute-start.20 = (f32[144,128]{1,0:T(8,128)S(1)}, f32[144,128]{1,0:T(8,128)S(1)}, u32[]{:S(2)}, u32[]{:S(2)}) collective-permute-start(f32[144,128]{1,0:T(8,128)S(1)} %add.15.refs_0_), channel_id=1, source_target_pairs={{0,4},{4,0},{8,12},{12,8},{16,20},{20,16},{24,28},{28,24},{1,5},{5... | collective-permute-start | bytes 221192 | tf_op jit(solution)/shard_map/ppermute | solution.py:413
  41.2 5.9 %collective-permute-start.24 = (f32[144,128]{1,0:T(8,128)S(1)}, f32[144,128]{1,0:T(8,128)S(1)}, u32[]{:S(2)}, u32[]{:S(2)}) collective-permute-start(f32[144,128]{1,0:T(8,128)S(1)} %add.15.refs_0_), channel_id=1, source_target_pairs={{0,6},{1,7},{2,4},{3,5},{4,2},{5,3},{6,0},{7,1},{8,14},{9,15},{10,... | collective-permute-start | bytes 221192 | tf_op jit(solution)/shard_map/ppermute | solution.py:419
  42.4 5.6 %collective-permute-start.23 = (f32[144,128]{1,0:T(8,128)S(1)}, f32[144,128]{1,0:T(8,128)S(1)}, u32[]{:S(2)}, u32[]{:S(2)}) collective-permute-start(f32[144,128]{1,0:T(8,128)S(1)} %add.15.refs_0_), channel_id=1, source_target_pairs={{0,2},{1,3},{2,0},{3,1},{4,6},{5,7},{6,4},{7,5},{8,10},{9,11},{10,... | collective-permute-start | bytes 221192 | tf_op jit(solution)/shard_map/ppermute | solution.py:410
  43.2 8.3 %collective-permute-start.19 = (f32[64,768]{1,0:T(8,128)S(1)}, f32[64,768]{1,0:T(8,128)S(1)}, u32[]{:S(2)}, u32[]{:S(2)}) collective-permute-start(f32[64,768]{1,0:T(8,128)S(1)} %get-tuple-element.88), channel_id=1, source_target_pairs={{0,28},{4,0},{8,4},{12,8},{16,12},{20,16},{24,20},{28,24},{1,29},{... | collective-permute-start | bytes 589832 | tf_op jit(solution)/shard_map/ppermute | solution.py:499
  45.0 3.5 %collective-permute-start.21 = (f32[144,128]{1,0:T(8,128)S(1)}, f32[144,128]{1,0:T(8,128)S(1)}, u32[]{:S(2)}, u32[]{:S(2)}) collective-permute-start(f32[144,128]{1,0:T(8,128)S(1)} %add.15.refs_0_), channel_id=1, source_target_pairs={{0,1},{1,0},{2,3},{3,2},{4,5},{5,4},{6,7},{7,6},{8,9},{9,8},{10,11... | collective-permute-start | bytes 221192 | tf_op jit(solution)/shard_map/ppermute | solution.py:410
  47.1 1.5 %collective-permute-start.26 = (f32[144,128]{1,0:T(8,128)S(1)}, f32[144,128]{1,0:T(8,128)S(1)}, u32[]{:S(2)}, u32[]{:S(2)}) collective-permute-start(f32[144,128]{1,0:T(8,128)S(1)} %collective-permute-done.24.refs_5_), channel_id=1, source_target_pairs={{0,1},{1,0},{2,3},{3,2},{4,5},{5,4},{6,7},{7,6},{8,9},{9,8},{10,11... | collective-permute-start | bytes 221192 | tf_op jit(solution)/shard_map/ppermute | solution.py:410
  48.1 1.3 %collective-permute-start.25 = (f32[144,128]{1,0:T(8,128)S(1)}, f32[144,128]{1,0:T(8,128)S(1)}, u32[]{:S(2)}, u32[]{:S(2)}) collective-permute-start(f32[144,128]{1,0:T(8,128)S(1)} %collective-permute-done.23.refs_4_), channel_id=1, source_target_pairs={{0,1},{1,0},{2,3},{3,2},{4,5},{5,4},{6,7},{7,6},{8,9},{9,8},{10,11... | collective-permute-start | bytes 221192 | tf_op jit(solution)/shard_map/ppermute | solution.py:410
  48.1 1.4 %collective-permute-start.22 = (f32[144,128]{1,0:T(8,128)S(1)}, f32[144,128]{1,0:T(8,128)S(1)}, u32[]{:S(2)}, u32[]{:S(2)}) collective-permute-start(f32[144,128]{1,0:T(8,128)S(1)} %collective-permute-done.20.refs_1_), channel_id=1, source_target_pairs={{0,1},{1,0},{2,3},{3,2},{4,5},{5,4},{6,7},{7,6},{8,9},{9,8},{10,11... | collective-permute-start | bytes 221192 | tf_op jit(solution)/shard_map/ppermute | solution.py:410

commit v13 on v12

--- a/solution.py
+++ b/solution.py
@@ -315,7 +315,8 @@
 
 
 def back_kernel(*refs):
-    sums, (start, scaled, schur, back, whole, parts) = refs[:8], refs[8:]
+    sums, (start, scaled, schur_out, back_out) = refs[:8], refs[8:12]
+    whole, parts, schur, back, sems = refs[12:]
     part = place()[0]
     side = lax.axis_index("tm") % 2
     size = sums[0].shape[0]
@@ -358,8 +359,22 @@
         (before, whole[at(before * span + diagonal, group, 8), :].T),
     ):
         schur[:, at(col * group, group, 128)] = value
+    copies = [pltpu.make_async_copy(schur, schur_out, sems.at[0])]
+    copies[0].start()
     value = scaled[...]
-    back[...] = 2.0 * value - times_wide(times_wide(value, parts), start)
+    high, low = halves(times_wide(value, parts))
+    half = width // 2
+    for i, first in enumerate((0, half)):
+        cols = slice(first, first + half)
+        right_side = start[:, cols]
+        product = dot(high, right_side) + dot(high, start[:, width + first : width + first + half])
+        back[:, cols] = 2.0 * value[:, cols] - (product + dot(low, right_side))
+        copies.append(
+            pltpu.make_async_copy(back.at[:, cols], back_out.at[:, cols], sems.at[1 + i])
+        )
+        copies[-1].start()
+    for copy in copies:
+        copy.wait()
 
 
 def finish_kernel(own_terms, came, link_diag, link_cross):
@@ -369,7 +384,7 @@
     link_cross[...] = own_terms[:, link:] + jnp.where(there, came[:, link:], 0.0)
 
 
-def call(kernel, outs, scratch, *args, sizes=None, whole=False, alias={}, flops=0):
+def call(kernel, outs, scratch, *args, sizes=None, whole=False, out_whole=False, alias={}, flops=0):
     vmem = pl.BlockSpec(memory_space=pltpu.VMEM)
     specs = [pl.BlockSpec(memory_space=pltpu.HBM) if whole else vmem] * len(args)
     if whole:
@@ -380,7 +395,7 @@
         kernel,
         out_shape=[jax.ShapeDtypeStruct(shape, dtype) for shape, dtype in outs],
         in_specs=specs,
-        out_specs=[vmem] * len(outs),
+        out_specs=[pl.BlockSpec(memory_space=pltpu.HBM) if out_whole else vmem] * len(outs),
         scratch_shapes=scratch,
         input_output_aliases=alias,
         compiler_params=pltpu.CompilerParams(vmem_limit_bytes=VMEM_BYTES),
@@ -491,8 +506,9 @@
     global_schur, back_cols = call(
         back_kernel,
         [((group, width), F32), ((rows, width), F32)],
-        [vmem((8 * size, group), F32), vmem((width, 2 * width), BF16)],
-        *sums, start, scaled,
+        [vmem((8 * size, group), F32), vmem((width, 2 * width), BF16), vmem((group, width), F32),
+         vmem((rows, width), F32), pltpu.SemaphoreType.DMA((3,))],
+        *sums, start, scaled, out_whole=True,
         flops=int(6 * rows * order * order),
     )
     next_terms = after(next_terms, cross)

time: 52.4 us -> 52.4 us (level)
  no operation moved by 1% of the time
where the time goes in v13:
time: 52.4 us; the launch traced here: 52.3 us
  starting transfers between devices  22.1 us (42%)
  Pallas kernels  17 us (32%)
  waiting for transfers between devices  11.8 us (23%)
  between operations  1.39 us (3%)
    pallas_call x7, Pallas kernels, call(): pl.pallas_call(kernel, out_shape=[jax.ShapeDtypeStruct(shape, dtype) for...  17 us
    ppermute x20, starting transfers between devices, tile_swap(): return lax.ppermute(value, 'tile', [(i, i ^ mask) for i in range(4)])  11.4 us
    ppermute x20, waiting for transfers between devices, tile_swap(): return lax.ppermute(value, 'tile', [(i, i ^ mask) for i in range(4)])  8.01 us
    ppermute x5, starting transfers between devices, block_swap(): return lax.ppermute(value, 'tm', [(i, i ^ mask) for i in range(blocks)])  7.75 us
    ppermute x5, waiting for transfers between devices, block_swap(): return lax.ppermute(value, 'tm', [(i, i ^ mask) for i in range(blocks)])  2.68 us
    ppermute x1, starting transfers between devices, shards(): lax.ppermute(next_terms, 'tm', [(i, (i - 1) % blocks) for i in range(bloc...  1.77 us
    ppermute x1, starting transfers between devices, diagonal_swap(): return lax.ppermute(value, ('tm', 'tile'), pairs)  1.19 us
    ppermute x1, waiting for transfers between devices, diagonal_swap(): return lax.ppermute(value, ('tm', 'tile'), pairs)  1.08 us
  transfers between devices with their start and end apart: 27, of which 11 were waited for; matrix products, arithmetic and copies ran while one was open for 0% of the time, Pallas kernels for 31%

profile of v13, /device:TPU:0, one launch (start us, length us, event | category | flops | bytes accessed | tf_op | source)
XLA Modules:
  0.0 52.3 jit_solution(4372730445062266534)
XLA Ops:
  0.6 3.0 %collective-permute-start.3 = (bf16[192,512]{1,0:T(8,128)(2,1)}, bf16[192,512]{1,0:T(8,128)(2,1)S(1)}, u32[]{:S(2)}, u32[]{:S(2)}) collective-permute-start(bf16[192,512]{1,0:T(8,128)(2,1)} %bitcast.13), channel_id=1, source_target_pairs={{0,2},{1,3},{2,0},{3,1},{4,6},{5,7},{6,4},{7,5},{8,10},{9,11},{10,... | collective-permute-start | bytes 589832 | tf_op jit(solution)/shard_map/ppermute | solution.py:425
  3.7 1.5 %pack_kernel.1 = (f32[392,128]{1,0:T(8,128)S(1)}, f32[400,128]{1,0:T(8,128)S(1)}, f32[192,768]{1,0:T(8,128)S(1)}, f32[192,768]{1,0:T(8,128)S(1)}, bf16[192,512]{...) custom-call(f32[192,768]{1,0:T(8,128)} %bitcast.11, f32[192,768]{1,0:T(8,128)} %bitcast.12, ...), custom_call_target="tpu_custom_call" | custom-call | tf_op jit(solution)/shard_map/pack_kernel/pallas_call | solution.py:394
  5.2 0.1 collective-permute-start
  5.2 0.5 collective-permute-start.1
  5.7 0.0 collective-permute-start.4
  5.8 3.5 %collective-permute-done.3.g_far = bf16[192,512]{1,0:T(8,128)(2,1)S(1)} collective-permute-done((bf16[192,512]{1,0:T(8,128)(2,1)}, bf16[192,512]{1,0:T(8,128)(2,1)S(1)}, u32[]{:S(2)}, u32[]{:S(2)}) %collective-permute-start.3) | collective-permute-done | bytes 196640 | tf_op jit(solution)/shard_map/ppermute | solution.py:425
  9.3 2.4 %collective-permute-start.7 = (f32[400,128]{1,0:T(8,128)S(1)}, f32[400,128]{1,0:T(8,128)S(1)}, u32[]{:S(2)}, u32[]{:S(2)}) collective-permute-start(f32[400,128]{1,0:T(8,128)S(1)} %get-tuple-element.62), channel_id=1, source_target_pairs={{0,2},{1,3},{2,0},{3,1},{4,6},{5,7},{6,4},{7,5},{8,10},{9,11},{10,... | collective-permute-start | bytes 614408 | tf_op jit(solution)/shard_map/ppermute | solution.py:425
  11.7 1.4 %collective-permute-done.4.far = f32[392,128]{1,0:T(8,128)S(1)} collective-permute-done((f32[392,128]{1,0:T(8,128)S(1)}, f32[392,128]{1,0:T(8,128)S(1)}, u32[]{:S(2)}, u32[]{:S(2)}) %collective-permute-start.4) | collective-permute-done | bytes 200736 | tf_op jit(solution)/shard_map/ppermute | solution.py:425
  13.1 0.0 collective-permute-start.6
  13.1 0.5 collective-permute-start.2
  14.2 0.6 %collective-permute-done.2.g_core = bf16[192,512]{1,0:T(8,128)(2,1)S(1)} collective-permute-done((bf16[192,512]{1,0:T(8,128)(2,1)S(1)}, bf16[192,512]{1,0:T(8,128)(2,1)S(1)}, u32[]{:S(2)}, u32[]{:S(2)}) %collective-permute-start.2) | collective-permute-done | bytes 196640 | tf_op jit(solution)/shard_map/ppermute | solution.py:425
  14.8 2.0 %prepare_kernel.1 = (bf16[1536,768]{1,0:T(8,128)(2,1)S(1)}, bf16[1536,768]{1,0:T(8,128)(2,1)S(1)}, bf16[768,512]{1,0:T(8,128)(2,1)S(1)}, f32[768,1]{1,0:T(8,128)...) custom-call(s32[1]{0:T(128)S(6)} %copy.15.sizes, ...), custom_call_target="tpu_custom_call" | custom-call | tf_op jit(solution)/shard_map/prepare_kernel/pallas_call | solution.py:394
  16.8 0.6 %collective-permute-done.7.far = f32[400,128]{1,0:T(8,128)S(1)} collective-permute-done((f32[400,128]{1,0:T(8,128)S(1)}, f32[400,128]{1,0:T(8,128)S(1)}, u32[]{:S(2)}, u32[]{:S(2)}) %collective-permute-start.7) | collective-permute-done | bytes 204832 | tf_op jit(solution)/shard_map/ppermute | solution.py:425
  17.5 0.5 collective-permute-start.9
  18.0 1.7 %collective-permute-start.10 = (bf16[192,512]{1,0:T(8,128)(2,1)S(1)}, bf16[192,512]{1,0:T(8,128)(2,1)S(1)}, u32[]{:S(2)}, u32[]{:S(2)}) collective-permute-start(bf16[192,512]{1,0:T(8,128)(2,1)S(1)} %bitcast.9), channel_id=1, source_target_pairs={{0,2},{1,3},{2,0},{3,1},{4,6},{5,7},{6,4},{7,5},{8,10},{9,11},{10,... | collective-permute-start | bytes 589832 | tf_op jit(solution)/shard_map/ppermute | solution.py:425
  19.7 0.0 collective-permute-done.9.p_core
  19.7 0.0 collective-permute-done.8.cross
  19.7 4.1 %global_kernel.1 = (f32[144,128]{1,0:T(8,128)S(1)}, f32[144,128]{1,0:T(8,128)S(1)}, f32[192,128]{1,0:T(8,128)S(1)}, f32[576,128]{1,0:T(8,128)S(1)}, f32[640,128]...) custom-call(f32[1,768]{1,0:T(1,128)S(1)} %get-tuple-element.67.live, ...), custom_call_target="tpu_custom_call", output_to_operand_aliasing={{5}: (4, {})} | custom-call | tf_op jit(solution)/shard_map/global_kernel/pallas_call | solution.py:394
  23.9 2.6 %collective-permute-start.12 = (f32[144,128]{1,0:T(8,128)S(1)}, f32[144,128]{1,0:T(8,128)S(1)}, u32[]{:S(2)}, u32[]{:S(2)}) collective-permute-start(f32[144,128]{1,0:T(8,128)S(1)} %get-tuple-element.77), channel_id=1, source_target_pairs={{0,12},{4,8},{8,4},{12,0},{16,28},{20,24},{24,20},{28,16},{1,13},{... | collective-permute-start | bytes 221192 | tf_op jit(solution)/shard_map/ppermute | solution.py:428
  26.4 0.5 %collective-permute-start.13 = (f32[144,128]{1,0:T(8,128)S(1)}, f32[144,128]{1,0:T(8,128)S(1)}, u32[]{:S(2)}, u32[]{:S(2)}) collective-permute-start(f32[144,128]{1,0:T(8,128)S(1)} %get-tuple-element.77), channel_id=1, source_target_pairs={{0,4},{4,0},{8,12},{12,8},{16,20},{20,16},{24,28},{28,24},{1,5},{5... | collective-permute-start | bytes 221192 | tf_op jit(solution)/shard_map/ppermute | solution.py:428
  27.0 0.4 collective-permute-start.14
  27.4 1.2 %collective-permute-start.17 = (f32[640,128]{1,0:T(8,128)S(1)}, f32[640,128]{1,0:T(8,128)S(1)}, u32[]{:S(2)}, u32[]{:S(2)}) collective-permute-start(f32[640,128]{1,0:T(8,128)S(1)} %get-tuple-element.84), channel_id=1, source_target_pairs={{0,2},{1,3},{2,0},{3,1},{4,6},{5,7},{6,4},{7,5},{8,10},{9,11},{10,... | collective-permute-start | bytes 983048 | tf_op jit(solution)/shard_map/ppermute | solution.py:425
  28.7 0.0 collective-permute-done.10.p_far
  28.7 0.0 collective-permute-start.11
  28.7 0.6 %collective-permute-done.12 = f32[144,128]{1,0:T(8,128)S(1)} collective-permute-done((f32[144,128]{1,0:T(8,128)S(1)}, f32[144,128]{1,0:T(8,128)S(1)}, u32[]{:S(2)}, u32[]{:S(2)}) %collective-permute-start.12) | collective-permute-done | bytes 73760 | tf_op jit(solution)/shard_map/ppermute | solution.py:428
  29.3 1.5 %collective-permute-done.13 = f32[144,128]{1,0:T(8,128)S(1)} collective-permute-done((f32[144,128]{1,0:T(8,128)S(1)}, f32[144,128]{1,0:T(8,128)S(1)}, u32[]{:S(2)}, u32[]{:S(2)}) %collective-permute-start.13) | collective-permute-done | bytes 73760 | tf_op jit(solution)/shard_map/ppermute | solution.py:428
  30.8 0.5 %collective-permute-done.14 = f32[144,128]{1,0:T(8,128)S(1)} collective-permute-done((f32[144,128]{1,0:T(8,128)S(1)}, f32[144,128]{1,0:T(8,128)S(1)}, u32[]{:S(2)}, u32[]{:S(2)}) %collective-permute-start.14) | collective-permute-done | bytes 73760 | tf_op jit(solution)/shard_map/ppermute | solution.py:428
  31.4 2.7 %collective-permute-start.15 = (f32[144,128]{1,0:T(8,128)S(1)}, f32[144,128]{1,0:T(8,128)S(1)}, u32[]{:S(2)}, u32[]{:S(2)}) collective-permute-start(f32[144,128]{1,0:T(8,128)S(1)} %add_add_fusion), channel_id=1, source_target_pairs={{0,16},{4,20},{8,24},{12,28},{16,0},{20,4},{24,8},{28,12},{1,17},{... | collective-permute-start | bytes 221192 | tf_op jit(solution)/shard_map/ppermute | solution.py:428
  34.0 0.0 collective-permute-done.11.p_cross
  34.0 5.6 %pair_kernel.1 = (f32[64,768]{1,0:T(8,128)S(1)}, f32[64,256]{1,0:T(8,128)}, f32[64,768]{1,0:T(8,128)S(1)}) custom-call(f32[768,1]{1,0:T(8,128)S(1)} %get-tuple-element.61.live, bf16[192,512]{1,0:T(8,128)(2,1)S(1)} %bitcast.10, bf16[192,512]{1,0:T(8,128)(2,1)S(1)} %collective-permute-done.9.p_core, bf16[192,512]{1,0:T(8,128)(2,1)S(1)} %collective-permute-done.10.p_far, ...), custom_call_target="tpu_custom_call" | custom-call | tf_op jit(solution)/shard_map/pair_kernel/pallas_call | solution.py:394
  39.6 0.0 collective-permute-done.15
  39.6 0.1 collective-permute-start.18
  39.7 1.5 %collective-permute-start.20 = (f32[144,128]{1,0:T(8,128)S(1)}, f32[144,128]{1,0:T(8,128)S(1)}, u32[]{:S(2)}, u32[]{:S(2)}) collective-permute-start(f32[144,128]{1,0:T(8,128)S(1)} %add.15.refs_0_), channel_id=1, source_target_pairs={{0,4},{4,0},{8,12},{12,8},{16,20},{20,16},{24,28},{28,24},{1,5},{5... | collective-permute-start | bytes 221192 | tf_op jit(solution)/shard_map/ppermute | solution.py:428
  41.2 1.2 %collective-permute-start.24 = (f32[144,128]{1,0:T(8,128)S(1)}, f32[144,128]{1,0:T(8,128)S(1)}, u32[]{:S(2)}, u32[]{:S(2)}) collective-permute-start(f32[144,128]{1,0:T(8,128)S(1)} %add.15.refs_0_), channel_id=1, source_target_pairs={{0,6},{1,7},{2,4},{3,5},{4,2},{5,3},{6,0},{7,1},{8,14},{9,15},{10,... | collective-permute-start | bytes 221192 | tf_op jit(solution)/shard_map/ppermute | solution.py:434
  42.4 0.8 %collective-permute-start.23 = (f32[144,128]{1,0:T(8,128)S(1)}, f32[144,128]{1,0:T(8,128)S(1)}, u32[]{:S(2)}, u32[]{:S(2)}) collective-permute-start(f32[144,128]{1,0:T(8,128)S(1)} %add.15.refs_0_), channel_id=1, source_target_pairs={{0,2},{1,3},{2,0},{3,1},{4,6},{5,7},{6,4},{7,5},{8,10},{9,11},{10,... | collective-permute-start | bytes 221192 | tf_op jit(solution)/shard_map/ppermute | solution.py:425
  43.2 1.8 %collective-permute-start.19 = (f32[64,768]{1,0:T(8,128)S(1)}, f32[64,768]{1,0:T(8,128)S(1)}, u32[]{:S(2)}, u32[]{:S(2)}) collective-permute-start(f32[64,768]{1,0:T(8,128)S(1)} %get-tuple-element.88), channel_id=1, source_target_pairs={{0,28},{4,0},{8,4},{12,8},{16,12},{20,16},{24,20},{28,24},{1,29},{... | collective-permute-start | bytes 589832 | tf_op jit(solution)/shard_map/ppermute | solution.py:515
  45.0 0.0 collective-permute-start.21
  45.0 1.0 %start_kernel.1 = (bf16[512,1024]{1,0:T(8,128)(2,1)S(1)}, f32[192,512]{1,0:T(8,128)S(1)}) custom-call(f32[512,128]{1,0:T(8,128)S(1)} %get-tuple-element.73.s_own, f32[192,128]{1,0:T(8,128)S(1)} %get-tuple-element.92.y_own, f32[576,128]{1,0:T(8,128)S(1)} %collective-permute-done.16.y_core, f32[640,128]{1,0:T(8,128)S(1)} %collective-permute-done.17.far, ...), custom_call_target="tpu_custom_call" | custom-call | tf_op jit(solution)/shard_map/start_kernel/pallas_call | solution.py:394
  46.0 0.0 collective-permute-done.20.refs_1_
  46.0 1.1 %collective-permute-done.24.refs_5_ = f32[144,128]{1,0:T(8,128)S(1)} collective-permute-done((f32[144,128]{1,0:T(8,128)S(1)}, f32[144,128]{1,0:T(8,128)S(1)}, u32[]{:S(2)}, u32[]{:S(2)}) %collective-permute-start.24) | collective-permute-done | bytes 73760 | tf_op jit(solution)/shard_map/ppermute | solution.py:434
  47.1 0.0 collective-permute-start.26
  47.1 0.9 %collective-permute-done.23.refs_4_ = f32[144,128]{1,0:T(8,128)S(1)} collective-permute-done((f32[144,128]{1,0:T(8,128)S(1)}, f32[144,128]{1,0:T(8,128)S(1)}, u32[]{:S(2)}, u32[]{:S(2)}) %collective-permute-start.23) | collective-permute-done | bytes 73760 | tf_op jit(solution)/shard_map/ppermute | solution.py:425
  48.1 0.0 collective-permute-start.25
  48.1 0.5 collective-permute-start.22
  48.6 0.7 %collective-permute-done.25.refs_6_ = f32[144,128]{1,0:T(8,128)S(1)} collective-permute-done((f32[144,128]{1,0:T(8,128)S(1)}, f32[144,128]{1,0:T(8,128)S(1)}, u32[]{:S(2)}, u32[]{:S(2)}) %collective-permute-start.25) | collective-permute-done | bytes 73760 | tf_op jit(solution)/shard_map/ppermute | solution.py:425
  49.3 0.2 collective-permute-done.22.refs_3_
  49.5 2.1 %back_kernel.1 = (f32[128,512]{1,0:T(8,128)}, f32[192,512]{1,0:T(8,128)}) custom-call(f32[144,128]{1,0:T(8,128)S(1)} %add.15.refs_0_, f32[144,128]{1,0:T(8,128)S(1)} %collective-permute-done.20.refs_1_, f32[144,128]{1,0:T(8,128)S(1)} %collective-permute-done.21.refs_2_, f32[144,128]{1,0:T(8,128)S(1)} %collective-permute-done.22.refs_3_, ...), custom_call_target="tpu_custom_call" | custom-call | flops 679477248 | tf_op jit(solution)/shard_map/back_kernel/pallas_call | solution.py:394
  51.6 0.7 %finish_kernel.1 = (f32[64,256]{1,0:T(8,128)}, f32[64,512]{1,0:T(8,128)}) custom-call(f32[64,768]{1,0:T(8,128)S(1)} %get-tuple-element.79.own_terms, f32[64,768]{1,0:T(8,128)S(1)} %collective-permute-done.19.came), custom_call_target="tpu_custom_call" | custom-call | tf_op jit(solution)/shard_map/finish_kernel/pallas_call | solution.py:394
  (19 shorter events, 0.1 us)
Async XLA Ops:
  0.6 8.7 %collective-permute-start.3 = (bf16[192,512]{1,0:T(8,128)(2,1)}, bf16[192,512]{1,0:T(8,128)(2,1)S(1)}, u32[]{:S(2)}, u32[]{:S(2)}) collective-permute-start(bf16[192,512]{1,0:T(8,128)(2,1)} %bitcast.13), channel_id=1, source_target_pairs={{0,2},{1,3},{2,0},{3,1},{4,6},{5,7},{6,4},{7,5},{8,10},{9,11},{10,... | collective-permute-start | bytes 589832 | tf_op jit(solution)/shard_map/ppermute | solution.py:425
  3.7 13.8 %copy-start.1 = (bf16[1,192,512]{2,1,0:T(8,128)(2,1)S(1)}, bf16[1,192,512]{2,1,0:T(8,128)(2,1)}, u32[]{:S(2)}) copy-start(bf16[1,192,512]{2,1,0:T(8,128)(2,1)} %param.12) | copy-start | bytes 589828
  3.7 16.1 %copy-start = (f32[128,512]{1,0:T(8,128)S(1)}, f32[128,512]{1,0:T(8,128)}, u32[]{:S(2)}) copy-start(f32[128,512]{1,0:T(8,128)} %base.1) | copy-start | bytes 786436
  5.2 9.7 %collective-permute-start = (f32[192,768]{1,0:T(8,128)S(1)}, f32[192,768]{1,0:T(8,128)S(1)}, u32[]{:S(2)}, u32[]{:S(2)}) collective-permute-start(f32[192,768]{1,0:T(8,128)S(1)} %get-tuple-element.53.x_own), channel_id=1, source_target_pairs={{0,1},{1,0},{2,3},{3,2},{4,5},{5,4},{6,7},{7,6},{8,9},{9,8},{10,11... | collective-permute-start | bytes 1769480 | tf_op jit(solution)/shard_map/ppermute | solution.py:425
  5.2 9.6 %collective-permute-start.1 = (f32[192,768]{1,0:T(8,128)S(1)}, f32[192,768]{1,0:T(8,128)S(1)}, u32[]{:S(2)}, u32[]{:S(2)}) collective-permute-start(f32[192,768]{1,0:T(8,128)S(1)} %get-tuple-element.54.k_own), channel_id=1, source_target_pairs={{0,1},{1,0},{2,3},{3,2},{4,5},{5,4},{6,7},{7,6},{8,9},{9,8},{10,11... | collective-permute-start | bytes 1769480 | tf_op jit(solution)/shard_map/ppermute | solution.py:425
  5.7 7.3 %collective-permute-start.4 = (f32[392,128]{1,0:T(8,128)S(1)}, f32[392,128]{1,0:T(8,128)S(1)}, u32[]{:S(2)}, u32[]{:S(2)}) collective-permute-start(f32[392,128]{1,0:T(8,128)S(1)} %get-tuple-element.56), channel_id=1, source_target_pairs={{0,2},{1,3},{2,0},{3,1},{4,6},{5,7},{6,4},{7,5},{8,10},{9,11},{10,... | collective-permute-start | bytes 602120 | tf_op jit(solution)/shard_map/ppermute | solution.py:425
  9.3 3.8 %collective-permute-start.5 = (bf16[192,512]{1,0:T(8,128)(2,1)S(1)}, bf16[192,512]{1,0:T(8,128)(2,1)S(1)}, u32[]{:S(2)}, u32[]{:S(2)}) collective-permute-start(bf16[192,512]{1,0:T(8,128)(2,1)S(1)} %collective-permute-done.3.g_far), channel_id=1, source_target_pairs={{0,1},{1,0},{2,3},{3,2},{4,5},{5,4},{6,7},{7,6},{8,9},{9,8},{10,11... | collective-permute-start | bytes 589832 | tf_op jit(solution)/shard_map/ppermute | solution.py:425
  9.3 8.2 %collective-permute-start.7 = (f32[400,128]{1,0:T(8,128)S(1)}, f32[400,128]{1,0:T(8,128)S(1)}, u32[]{:S(2)}, u32[]{:S(2)}) collective-permute-start(f32[400,128]{1,0:T(8,128)S(1)} %get-tuple-element.62), channel_id=1, source_target_pairs={{0,2},{1,3},{2,0},{3,1},{4,6},{5,7},{6,4},{7,5},{8,10},{9,11},{10,... | collective-permute-start | bytes 614408 | tf_op jit(solution)/shard_map/ppermute | solution.py:425
  13.1 1.7 %collective-permute-start.6 = (f32[392,128]{1,0:T(8,128)S(1)}, f32[392,128]{1,0:T(8,128)S(1)}, u32[]{:S(2)}, u32[]{:S(2)}) collective-permute-start(f32[392,128]{1,0:T(8,128)S(1)} %collective-permute-done.4.far), channel_id=1, source_target_pairs={{0,1},{1,0},{2,3},{3,2},{4,5},{5,4},{6,7},{7,6},{8,9},{9,8},{10,11... | collective-permute-start | bytes 602120 | tf_op jit(solution)/shard_map/ppermute | solution.py:425
  13.1 1.7 %collective-permute-start.2 = (bf16[192,512]{1,0:T(8,128)(2,1)S(1)}, bf16[192,512]{1,0:T(8,128)(2,1)S(1)}, u32[]{:S(2)}, u32[]{:S(2)}) collective-permute-start(bf16[192,512]{1,0:T(8,128)(2,1)S(1)} %get-tuple-element.55.g_own), channel_id=1, source_target_pairs={{0,1},{1,0},{2,3},{3,2},{4,5},{5,4},{6,7},{7,6},{8,9},{9,8},{10,11... | collective-permute-start | bytes 589832 | tf_op jit(solution)/shard_map/ppermute | solution.py:425
  17.5 2.3 %collective-permute-start.8 = (f32[400,128]{1,0:T(8,128)S(1)}, f32[400,128]{1,0:T(8,128)S(1)}, u32[]{:S(2)}, u32[]{:S(2)}) collective-permute-start(f32[400,128]{1,0:T(8,128)S(1)} %collective-permute-done.7.far), channel_id=1, source_target_pairs={{0,1},{1,0},{2,3},{3,2},{4,5},{5,4},{6,7},{7,6},{8,9},{9,8},{10,11... | collective-permute-start | bytes 614408 | tf_op jit(solution)/shard_map/ppermute | solution.py:425
  17.5 2.3 %collective-permute-start.9 = (bf16[192,512]{1,0:T(8,128)(2,1)S(1)}, bf16[192,512]{1,0:T(8,128)(2,1)S(1)}, u32[]{:S(2)}, u32[]{:S(2)}) collective-permute-start(bf16[192,512]{1,0:T(8,128)(2,1)S(1)} %bitcast.8), channel_id=1, source_target_pairs={{0,1},{1,0},{2,3},{3,2},{4,5},{5,4},{6,7},{7,6},{8,9},{9,8},{10,11... | collective-permute-start | bytes 589832 | tf_op jit(solution)/shard_map/ppermute | solution.py:425
  18.0 10.7 %collective-permute-start.10 = (bf16[192,512]{1,0:T(8,128)(2,1)S(1)}, bf16[192,512]{1,0:T(8,128)(2,1)S(1)}, u32[]{:S(2)}, u32[]{:S(2)}) collective-permute-start(bf16[192,512]{1,0:T(8,128)(2,1)S(1)} %bitcast.9), channel_id=1, source_target_pairs={{0,2},{1,3},{2,0},{3,1},{4,6},{5,7},{6,4},{7,5},{8,10},{9,11},{10,... | collective-permute-start | bytes 589832 | tf_op jit(solution)/shard_map/ppermute | solution.py:425
  23.9 5.4 %collective-permute-start.12 = (f32[144,128]{1,0:T(8,128)S(1)}, f32[144,128]{1,0:T(8,128)S(1)}, u32[]{:S(2)}, u32[]{:S(2)}) collective-permute-start(f32[144,128]{1,0:T(8,128)S(1)} %get-tuple-element.77), channel_id=1, source_target_pairs={{0,12},{4,8},{8,4},{12,0},{16,28},{20,24},{24,20},{28,16},{1,13},{... | collective-permute-start | bytes 221192 | tf_op jit(solution)/shard_map/ppermute | solution.py:428
  26.4 4.4 %collective-permute-start.13 = (f32[144,128]{1,0:T(8,128)S(1)}, f32[144,128]{1,0:T(8,128)S(1)}, u32[]{:S(2)}, u32[]{:S(2)}) collective-permute-start(f32[144,128]{1,0:T(8,128)S(1)} %get-tuple-element.77), channel_id=1, source_target_pairs={{0,4},{4,0},{8,12},{12,8},{16,20},{20,16},{24,28},{28,24},{1,5},{5... | collective-permute-start | bytes 221192 | tf_op jit(solution)/shard_map/ppermute | solution.py:428
  27.0 4.4 %collective-permute-start.14 = (f32[144,128]{1,0:T(8,128)S(1)}, f32[144,128]{1,0:T(8,128)S(1)}, u32[]{:S(2)}, u32[]{:S(2)}) collective-permute-start(f32[144,128]{1,0:T(8,128)S(1)} %get-tuple-element.74), channel_id=1, source_target_pairs={{0,8},{4,12},{8,0},{12,4},{16,24},{20,28},{24,16},{28,20},{1,9},{5... | collective-permute-start | bytes 221192 | tf_op jit(solution)/shard_map/ppermute | solution.py:428
  27.4 12.1 %collective-permute-start.17 = (f32[640,128]{1,0:T(8,128)S(1)}, f32[640,128]{1,0:T(8,128)S(1)}, u32[]{:S(2)}, u32[]{:S(2)}) collective-permute-start(f32[640,128]{1,0:T(8,128)S(1)} %get-tuple-element.84), channel_id=1, source_target_pairs={{0,2},{1,3},{2,0},{3,1},{4,6},{5,7},{6,4},{7,5},{8,10},{9,11},{10,... | collective-permute-start | bytes 983048 | tf_op jit(solution)/shard_map/ppermute | solution.py:425
  28.7 5.4 %collective-permute-start.11 = (bf16[192,512]{1,0:T(8,128)(2,1)S(1)}, bf16[192,512]{1,0:T(8,128)(2,1)S(1)}, u32[]{:S(2)}, u32[]{:S(2)}) collective-permute-start(bf16[192,512]{1,0:T(8,128)(2,1)S(1)} %collective-permute-done.10.p_far), channel_id=1, source_target_pairs={{0,1},{1,0},{2,3},{3,2},{4,5},{5,4},{6,7},{7,6},{8,9},{9,8},{10,11... | collective-permute-start | bytes 589832 | tf_op jit(solution)/shard_map/ppermute | solution.py:425
  29.3 10.3 %collective-permute-start.16 = (f32[576,128]{1,0:T(8,128)S(1)}, f32[576,128]{1,0:T(8,128)S(1)}, u32[]{:S(2)}, u32[]{:S(2)}) collective-permute-start(f32[576,128]{1,0:T(8,128)S(1)} %get-tuple-element.83), channel_id=1, source_target_pairs={{0,1},{1,0},{2,3},{3,2},{4,5},{5,4},{6,7},{7,6},{8,9},{9,8},{10,11... | collective-permute-start | bytes 884744 | tf_op jit(solution)/shard_map/ppermute | solution.py:425
  31.4 8.2 %collective-permute-start.15 = (f32[144,128]{1,0:T(8,128)S(1)}, f32[144,128]{1,0:T(8,128)S(1)}, u32[]{:S(2)}, u32[]{:S(2)}) collective-permute-start(f32[144,128]{1,0:T(8,128)S(1)} %add_add_fusion), channel_id=1, source_target_pairs={{0,16},{4,20},{8,24},{12,28},{16,0},{20,4},{24,8},{28,12},{1,17},{... | collective-permute-start | bytes 221192 | tf_op jit(solution)/shard_map/ppermute | solution.py:428
  39.6 3.6 %collective-permute-start.18 = (f32[640,128]{1,0:T(8,128)S(1)}, f32[640,128]{1,0:T(8,128)S(1)}, u32[]{:S(2)}, u32[]{:S(2)}) collective-permute-start(f32[640,128]{1,0:T(8,128)S(1)} %collective-permute-done.17.far), channel_id=1, source_target_pairs={{0,1},{1,0},{2,3},{3,2},{4,5},{5,4},{6,7},{7,6},{8,9},{9,8},{10,11... | collective-permute-start | bytes 983048 | tf_op jit(solution)/shard_map/ppermute | solution.py:425
  39.7 6.3 %collective-permute-start.20 = (f32[144,128]{1,0:T(8,128)S(1)}, f32[144,128]{1,0:T(8,128)S(1)}, u32[]{:S(2)}, u32[]{:S(2)}) collective-permute-start(f32[144,128]{1,0:T(8,128)S(1)} %add.15.refs_0_), channel_id=1, source_target_pairs={{0,4},{4,0},{8,12},{12,8},{16,20},{20,16},{24,28},{28,24},{1,5},{5... | collective-permute-start | bytes 221192 | tf_op jit(solution)/shard_map/ppermute | solution.py:428
  41.2 5.9 %collective-permute-start.24 = (f32[144,128]{1,0:T(8,128)S(1)}, f32[144,128]{1,0:T(8,128)S(1)}, u32[]{:S(2)}, u32[]{:S(2)}) collective-permute-start(f32[144,128]{1,0:T(8,128)S(1)} %add.15.refs_0_), channel_id=1, source_target_pairs={{0,6},{1,7},{2,4},{3,5},{4,2},{5,3},{6,0},{7,1},{8,14},{9,15},{10,... | collective-permute-start | bytes 221192 | tf_op jit(solution)/shard_map/ppermute | solution.py:434
  42.4 5.6 %collective-permute-start.23 = (f32[144,128]{1,0:T(8,128)S(1)}, f32[144,128]{1,0:T(8,128)S(1)}, u32[]{:S(2)}, u32[]{:S(2)}) collective-permute-start(f32[144,128]{1,0:T(8,128)S(1)} %add.15.refs_0_), channel_id=1, source_target_pairs={{0,2},{1,3},{2,0},{3,1},{4,6},{5,7},{6,4},{7,5},{8,10},{9,11},{10,... | collective-permute-start | bytes 221192 | tf_op jit(solution)/shard_map/ppermute | solution.py:425
  43.2 8.3 %collective-permute-start.19 = (f32[64,768]{1,0:T(8,128)S(1)}, f32[64,768]{1,0:T(8,128)S(1)}, u32[]{:S(2)}, u32[]{:S(2)}) collective-permute-start(f32[64,768]{1,0:T(8,128)S(1)} %get-tuple-element.88), channel_id=1, source_target_pairs={{0,28},{4,0},{8,4},{12,8},{16,12},{20,16},{24,20},{28,24},{1,29},{... | collective-permute-start | bytes 589832 | tf_op jit(solution)/shard_map/ppermute | solution.py:515
  45.0 3.5 %collective-permute-start.21 = (f32[144,128]{1,0:T(8,128)S(1)}, f32[144,128]{1,0:T(8,128)S(1)}, u32[]{:S(2)}, u32[]{:S(2)}) collective-permute-start(f32[144,128]{1,0:T(8,128)S(1)} %add.15.refs_0_), channel_id=1, source_target_pairs={{0,1},{1,0},{2,3},{3,2},{4,5},{5,4},{6,7},{7,6},{8,9},{9,8},{10,11... | collective-permute-start | bytes 221192 | tf_op jit(solution)/shard_map/ppermute | solution.py:425
  47.1 1.5 %collective-permute-start.26 = (f32[144,128]{1,0:T(8,128)S(1)}, f32[144,128]{1,0:T(8,128)S(1)}, u32[]{:S(2)}, u32[]{:S(2)}) collective-permute-start(f32[144,128]{1,0:T(8,128)S(1)} %collective-permute-done.24.refs_5_), channel_id=1, source_target_pairs={{0,1},{1,0},{2,3},{3,2},{4,5},{5,4},{6,7},{7,6},{8,9},{9,8},{10,11... | collective-permute-start | bytes 221192 | tf_op jit(solution)/shard_map/ppermute | solution.py:425
  48.1 1.3 %collective-permute-start.25 = (f32[144,128]{1,0:T(8,128)S(1)}, f32[144,128]{1,0:T(8,128)S(1)}, u32[]{:S(2)}, u32[]{:S(2)}) collective-permute-start(f32[144,128]{1,0:T(8,128)S(1)} %collective-permute-done.23.refs_4_), channel_id=1, source_target_pairs={{0,1},{1,0},{2,3},{3,2},{4,5},{5,4},{6,7},{7,6},{8,9},{9,8},{10,11... | collective-permute-start | bytes 221192 | tf_op jit(solution)/shard_map/ppermute | solution.py:425
  48.1 1.4 %collective-permute-start.22 = (f32[144,128]{1,0:T(8,128)S(1)}, f32[144,128]{1,0:T(8,128)S(1)}, u32[]{:S(2)}, u32[]{:S(2)}) collective-permute-start(f32[144,128]{1,0:T(8,128)S(1)} %collective-permute-done.20.refs_1_), channel_id=1, source_target_pairs={{0,1},{1,0},{2,3},{3,2},{4,5},{5,4},{6,7},{7,6},{8,9},{9,8},{10,11... | collective-permute-start | bytes 221192 | tf_op jit(solution)/shard_map/ppermute | solution.py:425

commit v14 on v13

--- a/solution.py
+++ b/solution.py
@@ -167,11 +167,13 @@
     return jnp.concatenate(result, axis=1)
 
 
-def times_wide(left_side, right_side):
-    width = right_side.shape[1] // 2
-    high, low = halves(left_side)
-    product = dot(high, right_side[...])
-    return (product[:, :width] + product[:, width:]) + dot(low, right_side[:, :width])
+def times_wide(left_side, right_side, first, last):
+    count, width = left_side.shape[0], right_side.shape[1] // 2
+    parts = stacked(left_side)
+    product = dot(parts, right_side[:, first:last])
+    return (product[:count] + product[count:]) + dot(
+        parts[:count], right_side[:, width + first : width + last]
+    )
 
 
 def prepare_kernel(
@@ -311,7 +313,8 @@
     put(bottom, right, low_right, s_rows[:, :half])
     for ref, mask in ((y_own, 0), (y_core, 1), (far, 2), (cross.at[rows:, :], 3)):
         y_rows[:, at((part ^ mask) * group, group, 128)] = ref[:rows, :]
-    scaled[...] = times_wide(y_rows[...], start)
+    for first in range(0, width, half):
+        scaled[:, first : first + half] = times_wide(y_rows[...], start, first, first + half)
 
 
 def back_kernel(*refs):
@@ -362,13 +365,13 @@
     copies = [pltpu.make_async_copy(schur, schur_out, sems.at[0])]
     copies[0].start()
     value = scaled[...]
-    high, low = halves(times_wide(value, parts))
     half = width // 2
+    result = jnp.concatenate(
+        [times_wide(value, parts, first, first + half) for first in (0, half)], axis=1
+    )
     for i, first in enumerate((0, half)):
         cols = slice(first, first + half)
-        right_side = start[:, cols]
-        product = dot(high, right_side) + dot(high, start[:, width + first : width + first + half])
-        back[:, cols] = 2.0 * value[:, cols] - (product + dot(low, right_side))
+        back[:, cols] = 2.0 * value[:, cols] - times_wide(result, start, first, first + half)
         copies.append(
             pltpu.make_async_copy(back.at[:, cols], back_out.at[:, cols], sems.at[1 + i])
         )

time: 52.4 us -> 52.3 us (level)
  no operation moved by 1% of the time
where the time goes in v14:
time: 52.3 us; the launch traced here: 52.2 us
  starting transfers between devices  22.1 us (42%)
  Pallas kernels  16.8 us (32%)
  waiting for transfers between devices  11.8 us (23%)
  between operations  1.39 us (3%)
    pallas_call x7, Pallas kernels, call(): pl.pallas_call(kernel, out_shape=[jax.ShapeDtypeStruct(shape, dtype) for...  16.8 us
    ppermute x20, starting transfers between devices, tile_swap(): return lax.ppermute(value, 'tile', [(i, i ^ mask) for i in range(4)])  11.4 us
    ppermute x20, waiting for transfers between devices, tile_swap(): return lax.ppermute(value, 'tile', [(i, i ^ mask) for i in range(4)])  8.01 us
    ppermute x5, starting transfers between devices, block_swap(): return lax.ppermute(value, 'tm', [(i, i ^ mask) for i in range(blocks)])  7.75 us
    ppermute x5, waiting for transfers between devices, block_swap(): return lax.ppermute(value, 'tm', [(i, i ^ mask) for i in range(blocks)])  2.68 us
    ppermute x1, starting transfers between devices, shards(): lax.ppermute(next_terms, 'tm', [(i, (i - 1) % blocks) for i in range(bloc...  1.77 us
    ppermute x1, starting transfers between devices, diagonal_swap(): return lax.ppermute(value, ('tm', 'tile'), pairs)  1.19 us
    ppermute x1, waiting for transfers between devices, diagonal_swap(): return lax.ppermute(value, ('tm', 'tile'), pairs)  1.1 us
  transfers between devices with their start and end apart: 27, of which 11 were waited for; matrix products, arithmetic and copies ran while one was open for 0% of the time, Pallas kernels for 31%

profile of v14, /device:TPU:0, one launch (start us, length us, event | category | flops | bytes accessed | tf_op | source)
XLA Modules:
  0.0 52.2 jit_solution(6952751912329345359)
XLA Ops:
  0.6 3.0 %collective-permute-start.3 = (bf16[192,512]{1,0:T(8,128)(2,1)}, bf16[192,512]{1,0:T(8,128)(2,1)S(1)}, u32[]{:S(2)}, u32[]{:S(2)}) collective-permute-start(bf16[192,512]{1,0:T(8,128)(2,1)} %bitcast.13), channel_id=1, source_target_pairs={{0,2},{1,3},{2,0},{3,1},{4,6},{5,7},{6,4},{7,5},{8,10},{9,11},{10,... | collective-permute-start | bytes 589832 | tf_op jit(solution)/shard_map/ppermute | solution.py:428
  3.7 1.5 %pack_kernel.1 = (f32[392,128]{1,0:T(8,128)S(1)}, f32[400,128]{1,0:T(8,128)S(1)}, f32[192,768]{1,0:T(8,128)S(1)}, f32[192,768]{1,0:T(8,128)S(1)}, bf16[192,512]{...) custom-call(f32[192,768]{1,0:T(8,128)} %bitcast.11, f32[192,768]{1,0:T(8,128)} %bitcast.12, ...), custom_call_target="tpu_custom_call" | custom-call | tf_op jit(solution)/shard_map/pack_kernel/pallas_call | solution.py:397
  5.2 0.1 collective-permute-start
  5.2 0.5 collective-permute-start.1
  5.7 0.0 collective-permute-start.4
  5.8 3.5 %collective-permute-done.3.g_far = bf16[192,512]{1,0:T(8,128)(2,1)S(1)} collective-permute-done((bf16[192,512]{1,0:T(8,128)(2,1)}, bf16[192,512]{1,0:T(8,128)(2,1)S(1)}, u32[]{:S(2)}, u32[]{:S(2)}) %collective-permute-start.3) | collective-permute-done | bytes 196640 | tf_op jit(solution)/shard_map/ppermute | solution.py:428
  9.3 2.4 %collective-permute-start.7 = (f32[400,128]{1,0:T(8,128)S(1)}, f32[400,128]{1,0:T(8,128)S(1)}, u32[]{:S(2)}, u32[]{:S(2)}) collective-permute-start(f32[400,128]{1,0:T(8,128)S(1)} %get-tuple-element.62), channel_id=1, source_target_pairs={{0,2},{1,3},{2,0},{3,1},{4,6},{5,7},{6,4},{7,5},{8,10},{9,11},{10,... | collective-permute-start | bytes 614408 | tf_op jit(solution)/shard_map/ppermute | solution.py:428
  11.7 1.4 %collective-permute-done.4.far = f32[392,128]{1,0:T(8,128)S(1)} collective-permute-done((f32[392,128]{1,0:T(8,128)S(1)}, f32[392,128]{1,0:T(8,128)S(1)}, u32[]{:S(2)}, u32[]{:S(2)}) %collective-permute-start.4) | collective-permute-done | bytes 200736 | tf_op jit(solution)/shard_map/ppermute | solution.py:428
  13.1 0.5 collective-permute-start.2
  14.2 0.6 %collective-permute-done.2.g_core = bf16[192,512]{1,0:T(8,128)(2,1)S(1)} collective-permute-done((bf16[192,512]{1,0:T(8,128)(2,1)S(1)}, bf16[192,512]{1,0:T(8,128)(2,1)S(1)}, u32[]{:S(2)}, u32[]{:S(2)}) %collective-permute-start.2) | collective-permute-done | bytes 196640 | tf_op jit(solution)/shard_map/ppermute | solution.py:428
  14.8 0.0 collective-permute-done.x_core
  14.8 2.0 %prepare_kernel.1 = (bf16[1536,768]{1,0:T(8,128)(2,1)S(1)}, bf16[1536,768]{1,0:T(8,128)(2,1)S(1)}, bf16[768,512]{1,0:T(8,128)(2,1)S(1)}, f32[768,1]{1,0:T(8,128)...) custom-call(s32[1]{0:T(128)S(6)} %copy.15.sizes, ...), custom_call_target="tpu_custom_call" | custom-call | tf_op jit(solution)/shard_map/prepare_kernel/pallas_call | solution.py:397
  16.8 0.6 %collective-permute-done.7.far = f32[400,128]{1,0:T(8,128)S(1)} collective-permute-done((f32[400,128]{1,0:T(8,128)S(1)}, f32[400,128]{1,0:T(8,128)S(1)}, u32[]{:S(2)}, u32[]{:S(2)}) %collective-permute-start.7) | collective-permute-done | bytes 204832 | tf_op jit(solution)/shard_map/ppermute | solution.py:428
  17.5 0.5 collective-permute-start.9
  18.0 1.7 %collective-permute-start.10 = (bf16[192,512]{1,0:T(8,128)(2,1)S(1)}, bf16[192,512]{1,0:T(8,128)(2,1)S(1)}, u32[]{:S(2)}, u32[]{:S(2)}) collective-permute-start(bf16[192,512]{1,0:T(8,128)(2,1)S(1)} %bitcast.9), channel_id=1, source_target_pairs={{0,2},{1,3},{2,0},{3,1},{4,6},{5,7},{6,4},{7,5},{8,10},{9,11},{10,... | collective-permute-start | bytes 589832 | tf_op jit(solution)/shard_map/ppermute | solution.py:428
  19.7 4.1 %global_kernel.1 = (f32[144,128]{1,0:T(8,128)S(1)}, f32[144,128]{1,0:T(8,128)S(1)}, f32[192,128]{1,0:T(8,128)S(1)}, f32[576,128]{1,0:T(8,128)S(1)}, f32[640,128]...) custom-call(f32[1,768]{1,0:T(1,128)S(1)} %get-tuple-element.67.live, ...), custom_call_target="tpu_custom_call", output_to_operand_aliasing={{5}: (4, {})} | custom-call | tf_op jit(solution)/shard_map/global_kernel/pallas_call | solution.py:397
  23.9 2.6 %collective-permute-start.12 = (f32[144,128]{1,0:T(8,128)S(1)}, f32[144,128]{1,0:T(8,128)S(1)}, u32[]{:S(2)}, u32[]{:S(2)}) collective-permute-start(f32[144,128]{1,0:T(8,128)S(1)} %get-tuple-element.77), channel_id=1, source_target_pairs={{0,12},{4,8},{8,4},{12,0},{16,28},{20,24},{24,20},{28,16},{1,13},{... | collective-permute-start | bytes 221192 | tf_op jit(solution)/shard_map/ppermute | solution.py:431
  26.4 0.5 %collective-permute-start.13 = (f32[144,128]{1,0:T(8,128)S(1)}, f32[144,128]{1,0:T(8,128)S(1)}, u32[]{:S(2)}, u32[]{:S(2)}) collective-permute-start(f32[144,128]{1,0:T(8,128)S(1)} %get-tuple-element.77), channel_id=1, source_target_pairs={{0,4},{4,0},{8,12},{12,8},{16,20},{20,16},{24,28},{28,24},{1,5},{5... | collective-permute-start | bytes 221192 | tf_op jit(solution)/shard_map/ppermute | solution.py:431
  27.0 0.4 collective-permute-start.14
  27.4 1.2 %collective-permute-start.17 = (f32[640,128]{1,0:T(8,128)S(1)}, f32[640,128]{1,0:T(8,128)S(1)}, u32[]{:S(2)}, u32[]{:S(2)}) collective-permute-start(f32[640,128]{1,0:T(8,128)S(1)} %get-tuple-element.84), channel_id=1, source_target_pairs={{0,2},{1,3},{2,0},{3,1},{4,6},{5,7},{6,4},{7,5},{8,10},{9,11},{10,... | collective-permute-start | bytes 983048 | tf_op jit(solution)/shard_map/ppermute | solution.py:428
  28.7 0.0 collective-permute-done.10.p_far
  28.7 0.0 collective-permute-start.11
  28.7 0.6 %collective-permute-done.12 = f32[144,128]{1,0:T(8,128)S(1)} collective-permute-done((f32[144,128]{1,0:T(8,128)S(1)}, f32[144,128]{1,0:T(8,128)S(1)}, u32[]{:S(2)}, u32[]{:S(2)}) %collective-permute-start.12) | collective-permute-done | bytes 73760 | tf_op jit(solution)/shard_map/ppermute | solution.py:431
  29.3 0.0 collective-permute-start.16
  29.3 1.5 %collective-permute-done.13 = f32[144,128]{1,0:T(8,128)S(1)} collective-permute-done((f32[144,128]{1,0:T(8,128)S(1)}, f32[144,128]{1,0:T(8,128)S(1)}, u32[]{:S(2)}, u32[]{:S(2)}) %collective-permute-start.13) | collective-permute-done | bytes 73760 | tf_op jit(solution)/shard_map/ppermute | solution.py:431
  30.8 0.5 %collective-permute-done.14 = f32[144,128]{1,0:T(8,128)S(1)} collective-permute-done((f32[144,128]{1,0:T(8,128)S(1)}, f32[144,128]{1,0:T(8,128)S(1)}, u32[]{:S(2)}, u32[]{:S(2)}) %collective-permute-start.14) | collective-permute-done | bytes 73760 | tf_op jit(solution)/shard_map/ppermute | solution.py:431
  31.4 2.7 %collective-permute-start.15 = (f32[144,128]{1,0:T(8,128)S(1)}, f32[144,128]{1,0:T(8,128)S(1)}, u32[]{:S(2)}, u32[]{:S(2)}) collective-permute-start(f32[144,128]{1,0:T(8,128)S(1)} %add_add_fusion), channel_id=1, source_target_pairs={{0,16},{4,20},{8,24},{12,28},{16,0},{20,4},{24,8},{28,12},{1,17},{... | collective-permute-start | bytes 221192 | tf_op jit(solution)/shard_map/ppermute | solution.py:431
  34.0 0.0 collective-permute-done.11.p_cross
  34.0 5.6 %pair_kernel.1 = (f32[64,768]{1,0:T(8,128)S(1)}, f32[64,256]{1,0:T(8,128)}, f32[64,768]{1,0:T(8,128)S(1)}) custom-call(f32[768,1]{1,0:T(8,128)S(1)} %get-tuple-element.61.live, bf16[192,512]{1,0:T(8,128)(2,1)S(1)} %bitcast.10, bf16[192,512]{1,0:T(8,128)(2,1)S(1)} %collective-permute-done.9.p_core, bf16[192,512]{1,0:T(8,128)(2,1)S(1)} %collective-permute-done.10.p_far, ...), custom_call_target="tpu_custom_call" | custom-call | tf_op jit(solution)/shard_map/pair_kernel/pallas_call | solution.py:397
  39.6 0.0 collective-permute-done.15
  39.6 0.0 collective-permute-done.16.y_core
  39.6 0.0 collective-permute-done.17.far
  39.6 0.1 collective-permute-start.18
  39.7 1.5 %collective-permute-start.20 = (f32[144,128]{1,0:T(8,128)S(1)}, f32[144,128]{1,0:T(8,128)S(1)}, u32[]{:S(2)}, u32[]{:S(2)}) collective-permute-start(f32[144,128]{1,0:T(8,128)S(1)} %add.15.refs_0_), channel_id=1, source_target_pairs={{0,4},{4,0},{8,12},{12,8},{16,20},{20,16},{24,28},{28,24},{1,5},{5... | collective-permute-start | bytes 221192 | tf_op jit(solution)/shard_map/ppermute | solution.py:431
  41.2 1.2 %collective-permute-start.24 = (f32[144,128]{1,0:T(8,128)S(1)}, f32[144,128]{1,0:T(8,128)S(1)}, u32[]{:S(2)}, u32[]{:S(2)}) collective-permute-start(f32[144,128]{1,0:T(8,128)S(1)} %add.15.refs_0_), channel_id=1, source_target_pairs={{0,6},{1,7},{2,4},{3,5},{4,2},{5,3},{6,0},{7,1},{8,14},{9,15},{10,... | collective-permute-start | bytes 221192 | tf_op jit(solution)/shard_map/ppermute | solution.py:437
  42.4 0.8 %collective-permute-start.23 = (f32[144,128]{1,0:T(8,128)S(1)}, f32[144,128]{1,0:T(8,128)S(1)}, u32[]{:S(2)}, u32[]{:S(2)}) collective-permute-start(f32[144,128]{1,0:T(8,128)S(1)} %add.15.refs_0_), channel_id=1, source_target_pairs={{0,2},{1,3},{2,0},{3,1},{4,6},{5,7},{6,4},{7,5},{8,10},{9,11},{10,... | collective-permute-start | bytes 221192 | tf_op jit(solution)/shard_map/ppermute | solution.py:428
  43.2 0.0 collective-permute-done.18.cross
  43.2 1.8 %collective-permute-start.19 = (f32[64,768]{1,0:T(8,128)S(1)}, f32[64,768]{1,0:T(8,128)S(1)}, u32[]{:S(2)}, u32[]{:S(2)}) collective-permute-start(f32[64,768]{1,0:T(8,128)S(1)} %get-tuple-element.88), channel_id=1, source_target_pairs={{0,28},{4,0},{8,4},{12,8},{16,12},{20,16},{24,20},{28,24},{1,29},{... | collective-permute-start | bytes 589832 | tf_op jit(solution)/shard_map/ppermute | solution.py:518
  45.0 0.0 collective-permute-start.21
  45.0 1.0 %start_kernel.1 = (bf16[512,1024]{1,0:T(8,128)(2,1)S(1)}, f32[192,512]{1,0:T(8,128)S(1)}) custom-call(f32[512,128]{1,0:T(8,128)S(1)} %get-tuple-element.73.s_own, f32[192,128]{1,0:T(8,128)S(1)} %get-tuple-element.92.y_own, f32[576,128]{1,0:T(8,128)S(1)} %collective-permute-done.16.y_core, f32[640,128]{1,0:T(8,128)S(1)} %collective-permute-done.17.far, ...), custom_call_target="tpu_custom_call" | custom-call | tf_op jit(solution)/shard_map/start_kernel/pallas_call | solution.py:397
  46.0 0.0 collective-permute-done.20.refs_1_
  46.0 1.1 %collective-permute-done.24.refs_5_ = f32[144,128]{1,0:T(8,128)S(1)} collective-permute-done((f32[144,128]{1,0:T(8,128)S(1)}, f32[144,128]{1,0:T(8,128)S(1)}, u32[]{:S(2)}, u32[]{:S(2)}) %collective-permute-start.24) | collective-permute-done | bytes 73760 | tf_op jit(solution)/shard_map/ppermute | solution.py:437
  47.1 0.9 %collective-permute-done.23.refs_4_ = f32[144,128]{1,0:T(8,128)S(1)} collective-permute-done((f32[144,128]{1,0:T(8,128)S(1)}, f32[144,128]{1,0:T(8,128)S(1)}, u32[]{:S(2)}, u32[]{:S(2)}) %collective-permute-start.23) | collective-permute-done | bytes 73760 | tf_op jit(solution)/shard_map/ppermute | solution.py:428
  48.1 0.5 collective-permute-start.22
  48.6 0.7 %collective-permute-done.25.refs_6_ = f32[144,128]{1,0:T(8,128)S(1)} collective-permute-done((f32[144,128]{1,0:T(8,128)S(1)}, f32[144,128]{1,0:T(8,128)S(1)}, u32[]{:S(2)}, u32[]{:S(2)}) %collective-permute-start.25) | collective-permute-done | bytes 73760 | tf_op jit(solution)/shard_map/ppermute | solution.py:428
  49.3 0.2 collective-permute-done.22.refs_3_
  49.5 2.0 %back_kernel.1 = (f32[128,512]{1,0:T(8,128)}, f32[192,512]{1,0:T(8,128)}) custom-call(f32[144,128]{1,0:T(8,128)S(1)} %add.15.refs_0_, f32[144,128]{1,0:T(8,128)S(1)} %collective-permute-done.20.refs_1_, f32[144,128]{1,0:T(8,128)S(1)} %collective-permute-done.21.refs_2_, f32[144,128]{1,0:T(8,128)S(1)} %collective-permute-done.22.refs_3_, ...), custom_call_target="tpu_custom_call" | custom-call | flops 679477248 | tf_op jit(solution)/shard_map/back_kernel/pallas_call | solution.py:397
  51.5 0.7 %finish_kernel.1 = (f32[64,256]{1,0:T(8,128)}, f32[64,512]{1,0:T(8,128)}) custom-call(f32[64,768]{1,0:T(8,128)S(1)} %get-tuple-element.79.own_terms, f32[64,768]{1,0:T(8,128)S(1)} %collective-permute-done.19.came), custom_call_target="tpu_custom_call" | custom-call | tf_op jit(solution)/shard_map/finish_kernel/pallas_call | solution.py:397
  (19 shorter events, 0.1 us)
Async XLA Ops:
  0.6 8.7 %collective-permute-start.3 = (bf16[192,512]{1,0:T(8,128)(2,1)}, bf16[192,512]{1,0:T(8,128)(2,1)S(1)}, u32[]{:S(2)}, u32[]{:S(2)}) collective-permute-start(bf16[192,512]{1,0:T(8,128)(2,1)} %bitcast.13), channel_id=1, source_target_pairs={{0,2},{1,3},{2,0},{3,1},{4,6},{5,7},{6,4},{7,5},{8,10},{9,11},{10,... | collective-permute-start | bytes 589832 | tf_op jit(solution)/shard_map/ppermute | solution.py:428
  3.7 13.8 %copy-start.1 = (bf16[1,192,512]{2,1,0:T(8,128)(2,1)S(1)}, bf16[1,192,512]{2,1,0:T(8,128)(2,1)}, u32[]{:S(2)}) copy-start(bf16[1,192,512]{2,1,0:T(8,128)(2,1)} %param.12) | copy-start | bytes 589828
  3.7 16.1 %copy-start = (f32[128,512]{1,0:T(8,128)S(1)}, f32[128,512]{1,0:T(8,128)}, u32[]{:S(2)}) copy-start(f32[128,512]{1,0:T(8,128)} %base.1) | copy-start | bytes 786436
  5.2 9.7 %collective-permute-start = (f32[192,768]{1,0:T(8,128)S(1)}, f32[192,768]{1,0:T(8,128)S(1)}, u32[]{:S(2)}, u32[]{:S(2)}) collective-permute-start(f32[192,768]{1,0:T(8,128)S(1)} %get-tuple-element.53.x_own), channel_id=1, source_target_pairs={{0,1},{1,0},{2,3},{3,2},{4,5},{5,4},{6,7},{7,6},{8,9},{9,8},{10,11... | collective-permute-start | bytes 1769480 | tf_op jit(solution)/shard_map/ppermute | solution.py:428
  5.2 9.6 %collective-permute-start.1 = (f32[192,768]{1,0:T(8,128)S(1)}, f32[192,768]{1,0:T(8,128)S(1)}, u32[]{:S(2)}, u32[]{:S(2)}) collective-permute-start(f32[192,768]{1,0:T(8,128)S(1)} %get-tuple-element.54.k_own), channel_id=1, source_target_pairs={{0,1},{1,0},{2,3},{3,2},{4,5},{5,4},{6,7},{7,6},{8,9},{9,8},{10,11... | collective-permute-start | bytes 1769480 | tf_op jit(solution)/shard_map/ppermute | solution.py:428
  5.7 7.3 %collective-permute-start.4 = (f32[392,128]{1,0:T(8,128)S(1)}, f32[392,128]{1,0:T(8,128)S(1)}, u32[]{:S(2)}, u32[]{:S(2)}) collective-permute-start(f32[392,128]{1,0:T(8,128)S(1)} %get-tuple-element.56), channel_id=1, source_target_pairs={{0,2},{1,3},{2,0},{3,1},{4,6},{5,7},{6,4},{7,5},{8,10},{9,11},{10,... | collective-permute-start | bytes 602120 | tf_op jit(solution)/shard_map/ppermute | solution.py:428
  9.3 3.8 %collective-permute-start.5 = (bf16[192,512]{1,0:T(8,128)(2,1)S(1)}, bf16[192,512]{1,0:T(8,128)(2,1)S(1)}, u32[]{:S(2)}, u32[]{:S(2)}) collective-permute-start(bf16[192,512]{1,0:T(8,128)(2,1)S(1)} %collective-permute-done.3.g_far), channel_id=1, source_target_pairs={{0,1},{1,0},{2,3},{3,2},{4,5},{5,4},{6,7},{7,6},{8,9},{9,8},{10,11... | collective-permute-start | bytes 589832 | tf_op jit(solution)/shard_map/ppermute | solution.py:428
  9.3 8.2 %collective-permute-start.7 = (f32[400,128]{1,0:T(8,128)S(1)}, f32[400,128]{1,0:T(8,128)S(1)}, u32[]{:S(2)}, u32[]{:S(2)}) collective-permute-start(f32[400,128]{1,0:T(8,128)S(1)} %get-tuple-element.62), channel_id=1, source_target_pairs={{0,2},{1,3},{2,0},{3,1},{4,6},{5,7},{6,4},{7,5},{8,10},{9,11},{10,... | collective-permute-start | bytes 614408 | tf_op jit(solution)/shard_map/ppermute | solution.py:428
  13.1 1.7 %collective-permute-start.6 = (f32[392,128]{1,0:T(8,128)S(1)}, f32[392,128]{1,0:T(8,128)S(1)}, u32[]{:S(2)}, u32[]{:S(2)}) collective-permute-start(f32[392,128]{1,0:T(8,128)S(1)} %collective-permute-done.4.far), channel_id=1, source_target_pairs={{0,1},{1,0},{2,3},{3,2},{4,5},{5,4},{6,7},{7,6},{8,9},{9,8},{10,11... | collective-permute-start | bytes 602120 | tf_op jit(solution)/shard_map/ppermute | solution.py:428
  13.1 1.7 %collective-permute-start.2 = (bf16[192,512]{1,0:T(8,128)(2,1)S(1)}, bf16[192,512]{1,0:T(8,128)(2,1)S(1)}, u32[]{:S(2)}, u32[]{:S(2)}) collective-permute-start(bf16[192,512]{1,0:T(8,128)(2,1)S(1)} %get-tuple-element.55.g_own), channel_id=1, source_target_pairs={{0,1},{1,0},{2,3},{3,2},{4,5},{5,4},{6,7},{7,6},{8,9},{9,8},{10,11... | collective-permute-start | bytes 589832 | tf_op jit(solution)/shard_map/ppermute | solution.py:428
  17.5 2.3 %collective-permute-start.8 = (f32[400,128]{1,0:T(8,128)S(1)}, f32[400,128]{1,0:T(8,128)S(1)}, u32[]{:S(2)}, u32[]{:S(2)}) collective-permute-start(f32[400,128]{1,0:T(8,128)S(1)} %collective-permute-done.7.far), channel_id=1, source_target_pairs={{0,1},{1,0},{2,3},{3,2},{4,5},{5,4},{6,7},{7,6},{8,9},{9,8},{10,11... | collective-permute-start | bytes 614408 | tf_op jit(solution)/shard_map/ppermute | solution.py:428
  17.5 2.3 %collective-permute-start.9 = (bf16[192,512]{1,0:T(8,128)(2,1)S(1)}, bf16[192,512]{1,0:T(8,128)(2,1)S(1)}, u32[]{:S(2)}, u32[]{:S(2)}) collective-permute-start(bf16[192,512]{1,0:T(8,128)(2,1)S(1)} %bitcast.8), channel_id=1, source_target_pairs={{0,1},{1,0},{2,3},{3,2},{4,5},{5,4},{6,7},{7,6},{8,9},{9,8},{10,11... | collective-permute-start | bytes 589832 | tf_op jit(solution)/shard_map/ppermute | solution.py:428
  18.0 10.7 %collective-permute-start.10 = (bf16[192,512]{1,0:T(8,128)(2,1)S(1)}, bf16[192,512]{1,0:T(8,128)(2,1)S(1)}, u32[]{:S(2)}, u32[]{:S(2)}) collective-permute-start(bf16[192,512]{1,0:T(8,128)(2,1)S(1)} %bitcast.9), channel_id=1, source_target_pairs={{0,2},{1,3},{2,0},{3,1},{4,6},{5,7},{6,4},{7,5},{8,10},{9,11},{10,... | collective-permute-start | bytes 589832 | tf_op jit(solution)/shard_map/ppermute | solution.py:428
  23.9 5.4 %collective-permute-start.12 = (f32[144,128]{1,0:T(8,128)S(1)}, f32[144,128]{1,0:T(8,128)S(1)}, u32[]{:S(2)}, u32[]{:S(2)}) collective-permute-start(f32[144,128]{1,0:T(8,128)S(1)} %get-tuple-element.77), channel_id=1, source_target_pairs={{0,12},{4,8},{8,4},{12,0},{16,28},{20,24},{24,20},{28,16},{1,13},{... | collective-permute-start | bytes 221192 | tf_op jit(solution)/shard_map/ppermute | solution.py:431
  26.4 4.4 %collective-permute-start.13 = (f32[144,128]{1,0:T(8,128)S(1)}, f32[144,128]{1,0:T(8,128)S(1)}, u32[]{:S(2)}, u32[]{:S(2)}) collective-permute-start(f32[144,128]{1,0:T(8,128)S(1)} %get-tuple-element.77), channel_id=1, source_target_pairs={{0,4},{4,0},{8,12},{12,8},{16,20},{20,16},{24,28},{28,24},{1,5},{5... | collective-permute-start | bytes 221192 | tf_op jit(solution)/shard_map/ppermute | solution.py:431
  27.0 4.4 %collective-permute-start.14 = (f32[144,128]{1,0:T(8,128)S(1)}, f32[144,128]{1,0:T(8,128)S(1)}, u32[]{:S(2)}, u32[]{:S(2)}) collective-permute-start(f32[144,128]{1,0:T(8,128)S(1)} %get-tuple-element.74), channel_id=1, source_target_pairs={{0,8},{4,12},{8,0},{12,4},{16,24},{20,28},{24,16},{28,20},{1,9},{5... | collective-permute-start | bytes 221192 | tf_op jit(solution)/shard_map/ppermute | solution.py:431
  27.4 12.1 %collective-permute-start.17 = (f32[640,128]{1,0:T(8,128)S(1)}, f32[640,128]{1,0:T(8,128)S(1)}, u32[]{:S(2)}, u32[]{:S(2)}) collective-permute-start(f32[640,128]{1,0:T(8,128)S(1)} %get-tuple-element.84), channel_id=1, source_target_pairs={{0,2},{1,3},{2,0},{3,1},{4,6},{5,7},{6,4},{7,5},{8,10},{9,11},{10,... | collective-permute-start | bytes 983048 | tf_op jit(solution)/shard_map/ppermute | solution.py:428
  28.7 5.4 %collective-permute-start.11 = (bf16[192,512]{1,0:T(8,128)(2,1)S(1)}, bf16[192,512]{1,0:T(8,128)(2,1)S(1)}, u32[]{:S(2)}, u32[]{:S(2)}) collective-permute-start(bf16[192,512]{1,0:T(8,128)(2,1)S(1)} %collective-permute-done.10.p_far), channel_id=1, source_target_pairs={{0,1},{1,0},{2,3},{3,2},{4,5},{5,4},{6,7},{7,6},{8,9},{9,8},{10,11... | collective-permute-start | bytes 589832 | tf_op jit(solution)/shard_map/ppermute | solution.py:428
  29.3 10.3 %collective-permute-start.16 = (f32[576,128]{1,0:T(8,128)S(1)}, f32[576,128]{1,0:T(8,128)S(1)}, u32[]{:S(2)}, u32[]{:S(2)}) collective-permute-start(f32[576,128]{1,0:T(8,128)S(1)} %get-tuple-element.83), channel_id=1, source_target_pairs={{0,1},{1,0},{2,3},{3,2},{4,5},{5,4},{6,7},{7,6},{8,9},{9,8},{10,11... | collective-permute-start | bytes 884744 | tf_op jit(solution)/shard_map/ppermute | solution.py:428
  31.4 8.2 %collective-permute-start.15 = (f32[144,128]{1,0:T(8,128)S(1)}, f32[144,128]{1,0:T(8,128)S(1)}, u32[]{:S(2)}, u32[]{:S(2)}) collective-permute-start(f32[144,128]{1,0:T(8,128)S(1)} %add_add_fusion), channel_id=1, source_target_pairs={{0,16},{4,20},{8,24},{12,28},{16,0},{20,4},{24,8},{28,12},{1,17},{... | collective-permute-start | bytes 221192 | tf_op jit(solution)/shard_map/ppermute | solution.py:431
  39.6 3.6 %collective-permute-start.18 = (f32[640,128]{1,0:T(8,128)S(1)}, f32[640,128]{1,0:T(8,128)S(1)}, u32[]{:S(2)}, u32[]{:S(2)}) collective-permute-start(f32[640,128]{1,0:T(8,128)S(1)} %collective-permute-done.17.far), channel_id=1, source_target_pairs={{0,1},{1,0},{2,3},{3,2},{4,5},{5,4},{6,7},{7,6},{8,9},{9,8},{10,11... | collective-permute-start | bytes 983048 | tf_op jit(solution)/shard_map/ppermute | solution.py:428
  39.7 6.3 %collective-permute-start.20 = (f32[144,128]{1,0:T(8,128)S(1)}, f32[144,128]{1,0:T(8,128)S(1)}, u32[]{:S(2)}, u32[]{:S(2)}) collective-permute-start(f32[144,128]{1,0:T(8,128)S(1)} %add.15.refs_0_), channel_id=1, source_target_pairs={{0,4},{4,0},{8,12},{12,8},{16,20},{20,16},{24,28},{28,24},{1,5},{5... | collective-permute-start | bytes 221192 | tf_op jit(solution)/shard_map/ppermute | solution.py:431
  41.2 5.9 %collective-permute-start.24 = (f32[144,128]{1,0:T(8,128)S(1)}, f32[144,128]{1,0:T(8,128)S(1)}, u32[]{:S(2)}, u32[]{:S(2)}) collective-permute-start(f32[144,128]{1,0:T(8,128)S(1)} %add.15.refs_0_), channel_id=1, source_target_pairs={{0,6},{1,7},{2,4},{3,5},{4,2},{5,3},{6,0},{7,1},{8,14},{9,15},{10,... | collective-permute-start | bytes 221192 | tf_op jit(solution)/shard_map/ppermute | solution.py:437
  42.4 5.6 %collective-permute-start.23 = (f32[144,128]{1,0:T(8,128)S(1)}, f32[144,128]{1,0:T(8,128)S(1)}, u32[]{:S(2)}, u32[]{:S(2)}) collective-permute-start(f32[144,128]{1,0:T(8,128)S(1)} %add.15.refs_0_), channel_id=1, source_target_pairs={{0,2},{1,3},{2,0},{3,1},{4,6},{5,7},{6,4},{7,5},{8,10},{9,11},{10,... | collective-permute-start | bytes 221192 | tf_op jit(solution)/shard_map/ppermute | solution.py:428
  43.2 8.2 %collective-permute-start.19 = (f32[64,768]{1,0:T(8,128)S(1)}, f32[64,768]{1,0:T(8,128)S(1)}, u32[]{:S(2)}, u32[]{:S(2)}) collective-permute-start(f32[64,768]{1,0:T(8,128)S(1)} %get-tuple-element.88), channel_id=1, source_target_pairs={{0,28},{4,0},{8,4},{12,8},{16,12},{20,16},{24,20},{28,24},{1,29},{... | collective-permute-start | bytes 589832 | tf_op jit(solution)/shard_map/ppermute | solution.py:518
  45.0 3.5 %collective-permute-start.21 = (f32[144,128]{1,0:T(8,128)S(1)}, f32[144,128]{1,0:T(8,128)S(1)}, u32[]{:S(2)}, u32[]{:S(2)}) collective-permute-start(f32[144,128]{1,0:T(8,128)S(1)} %add.15.refs_0_), channel_id=1, source_target_pairs={{0,1},{1,0},{2,3},{3,2},{4,5},{5,4},{6,7},{7,6},{8,9},{9,8},{10,11... | collective-permute-start | bytes 221192 | tf_op jit(solution)/shard_map/ppermute | solution.py:428
  47.1 1.5 %collective-permute-start.26 = (f32[144,128]{1,0:T(8,128)S(1)}, f32[144,128]{1,0:T(8,128)S(1)}, u32[]{:S(2)}, u32[]{:S(2)}) collective-permute-start(f32[144,128]{1,0:T(8,128)S(1)} %collective-permute-done.24.refs_5_), channel_id=1, source_target_pairs={{0,1},{1,0},{2,3},{3,2},{4,5},{5,4},{6,7},{7,6},{8,9},{9,8},{10,11... | collective-permute-start | bytes 221192 | tf_op jit(solution)/shard_map/ppermute | solution.py:428
  48.1 1.3 %collective-permute-start.25 = (f32[144,128]{1,0:T(8,128)S(1)}, f32[144,128]{1,0:T(8,128)S(1)}, u32[]{:S(2)}, u32[]{:S(2)}) collective-permute-start(f32[144,128]{1,0:T(8,128)S(1)} %collective-permute-done.23.refs_4_), channel_id=1, source_target_pairs={{0,1},{1,0},{2,3},{3,2},{4,5},{5,4},{6,7},{7,6},{8,9},{9,8},{10,11... | collective-permute-start | bytes 221192 | tf_op jit(solution)/shard_map/ppermute | solution.py:428
  48.1 1.4 %collective-permute-start.22 = (f32[144,128]{1,0:T(8,128)S(1)}, f32[144,128]{1,0:T(8,128)S(1)}, u32[]{:S(2)}, u32[]{:S(2)}) collective-permute-start(f32[144,128]{1,0:T(8,128)S(1)} %collective-permute-done.20.refs_1_), channel_id=1, source_target_pairs={{0,1},{1,0},{2,3},{3,2},{4,5},{5,4},{6,7},{7,6},{8,9},{9,8},{10,11... | collective-permute-start | bytes 221192 | tf_op jit(solution)/shard_map/ppermute | solution.py:428

commit v15 on v14

--- a/solution.py
+++ b/solution.py
@@ -255,7 +255,7 @@
 
 def pair_kernel(
     live, p_own, p_core, p_far, p_cross, x, k, links,
-    own_terms, off_terms, next_terms, gathered,
+    own_terms, off_terms, next_terms, gathered, turned, columns,
 ):
     half = x.shape[1] // 2
     rows, width = p_far.shape
@@ -264,13 +264,20 @@
     put_rows(p_own, p_core, gathered)
     put_rows(p_far, p_cross, gathered, half)
     masked = gathered[...] * live[...].astype(BF16)
-    source = lax.broadcasted_iota(jnp.int32, (width, 2 * share), 0)
-    target = lax.broadcasted_iota(jnp.int32, (width, 2 * share), 1)
-    wanted = place()[0] * share + target + jnp.where(target < share, 0, link - share)
-    columns = dot(masked, (source == wanted).astype(F32).astype(BF16)).T
-    value = columns
-    for step in range(TERMS):
-        value = columns + value - times(times(value, x), k)
+    gathered[...] = masked
+    part = place()[0]
+    for first in (0, link):
+        block = gathered[:, at(first + (part // 2) * 2 * share, 2 * share, 128)]
+        turned[...] = block.astype(F32).T
+        half = first * share // link
+        columns[half : half + share, :] = turned[at((part % 2) * share, share, 8), :]
+    value = columns[...]
+    order = x.shape[1]
+    high = value.astype(BF16)
+    product = dot(high, x[:order, :]) + dot(high, x[order:, :])
+    value = 2.0 * value - times(product, k)
+    for step in range(TERMS - 1):
+        value = columns[...] + value - times(times(value, x), k)
     left_side = stacked(times(value, x))
     terms = dot(left_side, masked)
     terms = terms[: 2 * share] + terms[2 * share :]
@@ -482,7 +489,8 @@
     own_terms, off_terms, next_terms = call(
         pair_kernel,
         [((share, link + width), F32), ((share, link), F32), ((share, link + width), F32)],
-        [vmem((order, 2 * link), BF16)],
+        [vmem((order, 2 * link), BF16), vmem((2 * share, order), F32),
+         vmem((2 * share, order), F32)],
         live_rows, pair, p_core, p_far, tile_swap(p_far, 1), x, k, after(links, total),
     )
     step = 4

time: 52.3 us -> 52 us (level)
  transfers between devices with their start and end apart: 27 -> 27, of which waited for: 11 -> 11; matrix products, arithmetic and copies ran while one was open for 0% -> 0% of each run, Pallas kernels for 31% -> 30%
where the time goes in v15:
time: 52 us; the launch traced here: 51.8 us
  starting transfers between devices  22.5 us (43%)
  Pallas kernels  16.4 us (32%)
  waiting for transfers between devices  11.4 us (22%)
  between operations  1.39 us (3%)
    pallas_call x7, Pallas kernels, call(): pl.pallas_call(kernel, out_shape=[jax.ShapeDtypeStruct(shape, dtype) for...  16.4 us
    ppermute x20, starting transfers between devices, tile_swap(): return lax.ppermute(value, 'tile', [(i, i ^ mask) for i in range(4)])  11.4 us
    ppermute x20, waiting for transfers between devices, tile_swap(): return lax.ppermute(value, 'tile', [(i, i ^ mask) for i in range(4)])  8.01 us
    ppermute x5, starting transfers between devices, block_swap(): return lax.ppermute(value, 'tm', [(i, i ^ mask) for i in range(blocks)])  7.77 us
    ppermute x5, waiting for transfers between devices, block_swap(): return lax.ppermute(value, 'tm', [(i, i ^ mask) for i in range(blocks)])  2.68 us
    ppermute x1, starting transfers between devices, shards(): lax.ppermute(next_terms, 'tm', [(i, (i - 1) % blocks) for i in range(bloc...  2.18 us
    ppermute x1, starting transfers between devices, diagonal_swap(): return lax.ppermute(value, ('tm', 'tile'), pairs)  1.19 us
  transfers between devices with their start and end apart: 27, of which 11 were waited for; matrix products, arithmetic and copies ran while one was open for 0% of the time, Pallas kernels for 30%

profile of v15, /device:TPU:0, one launch (start us, length us, event | category | flops | bytes accessed | tf_op | source)
XLA Modules:
  0.0 51.8 jit_solution(1552315810513736466)
XLA Ops:
  0.6 3.0 %collective-permute-start.3 = (bf16[192,512]{1,0:T(8,128)(2,1)}, bf16[192,512]{1,0:T(8,128)(2,1)S(1)}, u32[]{:S(2)}, u32[]{:S(2)}) collective-permute-start(bf16[192,512]{1,0:T(8,128)(2,1)} %bitcast.13), channel_id=1, source_target_pairs={{0,2},{1,3},{2,0},{3,1},{4,6},{5,7},{6,4},{7,5},{8,10},{9,11},{10,... | collective-permute-start | bytes 589832 | tf_op jit(solution)/shard_map/ppermute | solution.py:435
  3.7 1.5 %pack_kernel.1 = (f32[392,128]{1,0:T(8,128)S(1)}, f32[400,128]{1,0:T(8,128)S(1)}, f32[192,768]{1,0:T(8,128)S(1)}, f32[192,768]{1,0:T(8,128)S(1)}, bf16[192,512]{...) custom-call(f32[192,768]{1,0:T(8,128)} %bitcast.11, f32[192,768]{1,0:T(8,128)} %bitcast.12, ...), custom_call_target="tpu_custom_call" | custom-call | tf_op jit(solution)/shard_map/pack_kernel/pallas_call | solution.py:404
  5.2 0.1 collective-permute-start
  5.2 0.5 collective-permute-start.1
  5.7 0.0 collective-permute-start.4
  5.8 3.5 %collective-permute-done.3.g_far = bf16[192,512]{1,0:T(8,128)(2,1)S(1)} collective-permute-done((bf16[192,512]{1,0:T(8,128)(2,1)}, bf16[192,512]{1,0:T(8,128)(2,1)S(1)}, u32[]{:S(2)}, u32[]{:S(2)}) %collective-permute-start.3) | collective-permute-done | bytes 196640 | tf_op jit(solution)/shard_map/ppermute | solution.py:435
  9.3 2.4 %collective-permute-start.7 = (f32[400,128]{1,0:T(8,128)S(1)}, f32[400,128]{1,0:T(8,128)S(1)}, u32[]{:S(2)}, u32[]{:S(2)}) collective-permute-start(f32[400,128]{1,0:T(8,128)S(1)} %get-tuple-element.62), channel_id=1, source_target_pairs={{0,2},{1,3},{2,0},{3,1},{4,6},{5,7},{6,4},{7,5},{8,10},{9,11},{10,... | collective-permute-start | bytes 614408 | tf_op jit(solution)/shard_map/ppermute | solution.py:435
  11.7 1.4 %collective-permute-done.4.far = f32[392,128]{1,0:T(8,128)S(1)} collective-permute-done((f32[392,128]{1,0:T(8,128)S(1)}, f32[392,128]{1,0:T(8,128)S(1)}, u32[]{:S(2)}, u32[]{:S(2)}) %collective-permute-start.4) | collective-permute-done | bytes 200736 | tf_op jit(solution)/shard_map/ppermute | solution.py:435
  13.1 0.0 collective-permute-start.6
  13.1 0.5 collective-permute-start.2
  14.2 0.6 %collective-permute-done.2.g_core = bf16[192,512]{1,0:T(8,128)(2,1)S(1)} collective-permute-done((bf16[192,512]{1,0:T(8,128)(2,1)S(1)}, bf16[192,512]{1,0:T(8,128)(2,1)S(1)}, u32[]{:S(2)}, u32[]{:S(2)}) %collective-permute-start.2) | collective-permute-done | bytes 196640 | tf_op jit(solution)/shard_map/ppermute | solution.py:435
  14.8 2.0 %prepare_kernel.1 = (bf16[1536,768]{1,0:T(8,128)(2,1)S(1)}, bf16[1536,768]{1,0:T(8,128)(2,1)S(1)}, bf16[768,512]{1,0:T(8,128)(2,1)S(1)}, f32[768,1]{1,0:T(8,128)...) custom-call(s32[1]{0:T(128)S(6)} %copy.15.sizes, ...), custom_call_target="tpu_custom_call" | custom-call | tf_op jit(solution)/shard_map/prepare_kernel/pallas_call | solution.py:404
  16.8 0.6 %collective-permute-done.7.far = f32[400,128]{1,0:T(8,128)S(1)} collective-permute-done((f32[400,128]{1,0:T(8,128)S(1)}, f32[400,128]{1,0:T(8,128)S(1)}, u32[]{:S(2)}, u32[]{:S(2)}) %collective-permute-start.7) | collective-permute-done | bytes 204832 | tf_op jit(solution)/shard_map/ppermute | solution.py:435
  17.5 0.5 collective-permute-start.9
  18.0 1.7 %collective-permute-start.10 = (bf16[192,512]{1,0:T(8,128)(2,1)S(1)}, bf16[192,512]{1,0:T(8,128)(2,1)S(1)}, u32[]{:S(2)}, u32[]{:S(2)}) collective-permute-start(bf16[192,512]{1,0:T(8,128)(2,1)S(1)} %bitcast.9), channel_id=1, source_target_pairs={{0,2},{1,3},{2,0},{3,1},{4,6},{5,7},{6,4},{7,5},{8,10},{9,11},{10,... | collective-permute-start | bytes 589832 | tf_op jit(solution)/shard_map/ppermute | solution.py:435
  19.7 0.0 collective-permute-done.9.p_core
  19.7 0.0 collective-permute-done.8.cross
  19.7 4.1 %global_kernel.1 = (f32[144,128]{1,0:T(8,128)S(1)}, f32[144,128]{1,0:T(8,128)S(1)}, f32[192,128]{1,0:T(8,128)S(1)}, f32[576,128]{1,0:T(8,128)S(1)}, f32[640,128]...) custom-call(f32[1,768]{1,0:T(1,128)S(1)} %get-tuple-element.67.live, ...), custom_call_target="tpu_custom_call", output_to_operand_aliasing={{5}: (4, {})} | custom-call | tf_op jit(solution)/shard_map/global_kernel/pallas_call | solution.py:404
  23.9 2.6 %collective-permute-start.12 = (f32[144,128]{1,0:T(8,128)S(1)}, f32[144,128]{1,0:T(8,128)S(1)}, u32[]{:S(2)}, u32[]{:S(2)}) collective-permute-start(f32[144,128]{1,0:T(8,128)S(1)} %get-tuple-element.77), channel_id=1, source_target_pairs={{0,12},{4,8},{8,4},{12,0},{16,28},{20,24},{24,20},{28,16},{1,13},{... | collective-permute-start | bytes 221192 | tf_op jit(solution)/shard_map/ppermute | solution.py:438
  26.4 0.5 %collective-permute-start.13 = (f32[144,128]{1,0:T(8,128)S(1)}, f32[144,128]{1,0:T(8,128)S(1)}, u32[]{:S(2)}, u32[]{:S(2)}) collective-permute-start(f32[144,128]{1,0:T(8,128)S(1)} %get-tuple-element.77), channel_id=1, source_target_pairs={{0,4},{4,0},{8,12},{12,8},{16,20},{20,16},{24,28},{28,24},{1,5},{5... | collective-permute-start | bytes 221192 | tf_op jit(solution)/shard_map/ppermute | solution.py:438
  27.0 0.4 collective-permute-start.14
  27.4 1.2 %collective-permute-start.17 = (f32[640,128]{1,0:T(8,128)S(1)}, f32[640,128]{1,0:T(8,128)S(1)}, u32[]{:S(2)}, u32[]{:S(2)}) collective-permute-start(f32[640,128]{1,0:T(8,128)S(1)} %get-tuple-element.84), channel_id=1, source_target_pairs={{0,2},{1,3},{2,0},{3,1},{4,6},{5,7},{6,4},{7,5},{8,10},{9,11},{10,... | collective-permute-start | bytes 983048 | tf_op jit(solution)/shard_map/ppermute | solution.py:435
  28.7 0.0 collective-permute-done.10.p_far
  28.7 0.0 collective-permute-start.11
  28.7 0.6 %collective-permute-done.12 = f32[144,128]{1,0:T(8,128)S(1)} collective-permute-done((f32[144,128]{1,0:T(8,128)S(1)}, f32[144,128]{1,0:T(8,128)S(1)}, u32[]{:S(2)}, u32[]{:S(2)}) %collective-permute-start.12) | collective-permute-done | bytes 73760 | tf_op jit(solution)/shard_map/ppermute | solution.py:438
  29.3 1.5 %collective-permute-done.13 = f32[144,128]{1,0:T(8,128)S(1)} collective-permute-done((f32[144,128]{1,0:T(8,128)S(1)}, f32[144,128]{1,0:T(8,128)S(1)}, u32[]{:S(2)}, u32[]{:S(2)}) %collective-permute-start.13) | collective-permute-done | bytes 73760 | tf_op jit(solution)/shard_map/ppermute | solution.py:438
  30.8 0.5 %collective-permute-done.14 = f32[144,128]{1,0:T(8,128)S(1)} collective-permute-done((f32[144,128]{1,0:T(8,128)S(1)}, f32[144,128]{1,0:T(8,128)S(1)}, u32[]{:S(2)}, u32[]{:S(2)}) %collective-permute-start.14) | collective-permute-done | bytes 73760 | tf_op jit(solution)/shard_map/ppermute | solution.py:438
  31.4 2.7 %collective-permute-start.15 = (f32[144,128]{1,0:T(8,128)S(1)}, f32[144,128]{1,0:T(8,128)S(1)}, u32[]{:S(2)}, u32[]{:S(2)}) collective-permute-start(f32[144,128]{1,0:T(8,128)S(1)} %add_add_fusion), channel_id=1, source_target_pairs={{0,16},{4,20},{8,24},{12,28},{16,0},{20,4},{24,8},{28,12},{1,17},{... | collective-permute-start | bytes 221192 | tf_op jit(solution)/shard_map/ppermute | solution.py:438
  34.0 5.2 %pair_kernel.1 = (f32[64,768]{1,0:T(8,128)S(1)}, f32[64,256]{1,0:T(8,128)}, f32[64,768]{1,0:T(8,128)S(1)}) custom-call(f32[768,1]{1,0:T(8,128)S(1)} %get-tuple-element.61.live, bf16[192,512]{1,0:T(8,128)(2,1)S(1)} %bitcast.10, bf16[192,512]{1,0:T(8,128)(2,1)S(1)} %collective-permute-done.9.p_core, bf16[192,512]{1,0:T(8,128)(2,1)S(1)} %collective-permute-done.10.p_far, ...), custom_call_target="tpu_custom_call" | custom-call | tf_op jit(solution)/shard_map/pair_kernel/pallas_call | solution.py:404
  39.2 0.0 collective-permute-done.15
  39.2 0.0 collective-permute-done.16.y_core
  39.2 0.0 collective-permute-done.17.far
  39.2 0.1 collective-permute-start.18
  39.3 1.6 %collective-permute-start.20 = (f32[144,128]{1,0:T(8,128)S(1)}, f32[144,128]{1,0:T(8,128)S(1)}, u32[]{:S(2)}, u32[]{:S(2)}) collective-permute-start(f32[144,128]{1,0:T(8,128)S(1)} %add.15.refs_0_), channel_id=1, source_target_pairs={{0,4},{4,0},{8,12},{12,8},{16,20},{20,16},{24,28},{28,24},{1,5},{5... | collective-permute-start | bytes 221192 | tf_op jit(solution)/shard_map/ppermute | solution.py:438
  40.8 1.2 %collective-permute-start.24 = (f32[144,128]{1,0:T(8,128)S(1)}, f32[144,128]{1,0:T(8,128)S(1)}, u32[]{:S(2)}, u32[]{:S(2)}) collective-permute-start(f32[144,128]{1,0:T(8,128)S(1)} %add.15.refs_0_), channel_id=1, source_target_pairs={{0,6},{1,7},{2,4},{3,5},{4,2},{5,3},{6,0},{7,1},{8,14},{9,15},{10,... | collective-permute-start | bytes 221192 | tf_op jit(solution)/shard_map/ppermute | solution.py:444
  42.0 0.8 %collective-permute-start.23 = (f32[144,128]{1,0:T(8,128)S(1)}, f32[144,128]{1,0:T(8,128)S(1)}, u32[]{:S(2)}, u32[]{:S(2)}) collective-permute-start(f32[144,128]{1,0:T(8,128)S(1)} %add.15.refs_0_), channel_id=1, source_target_pairs={{0,2},{1,3},{2,0},{3,1},{4,6},{5,7},{6,4},{7,5},{8,10},{9,11},{10,... | collective-permute-start | bytes 221192 | tf_op jit(solution)/shard_map/ppermute | solution.py:435
  42.8 0.0 collective-permute-done.18.cross
  42.8 2.2 %collective-permute-start.19 = (f32[64,768]{1,0:T(8,128)S(1)}, f32[64,768]{1,0:T(8,128)S(1)}, u32[]{:S(2)}, u32[]{:S(2)}) collective-permute-start(f32[64,768]{1,0:T(8,128)S(1)} %get-tuple-element.88), channel_id=1, source_target_pairs={{0,28},{4,0},{8,4},{12,8},{16,12},{20,16},{24,20},{28,24},{1,29},{... | collective-permute-start | bytes 589832 | tf_op jit(solution)/shard_map/ppermute | solution.py:526
  45.0 1.0 %start_kernel.1 = (bf16[512,1024]{1,0:T(8,128)(2,1)S(1)}, f32[192,512]{1,0:T(8,128)S(1)}) custom-call(f32[512,128]{1,0:T(8,128)S(1)} %get-tuple-element.73.s_own, f32[192,128]{1,0:T(8,128)S(1)} %get-tuple-element.92.y_own, f32[576,128]{1,0:T(8,128)S(1)} %collective-permute-done.16.y_core, f32[640,128]{1,0:T(8,128)S(1)} %collective-permute-done.17.far, ...), custom_call_target="tpu_custom_call" | custom-call | tf_op jit(solution)/shard_map/start_kernel/pallas_call | solution.py:404
  46.0 0.7 %collective-permute-done.24.refs_5_ = f32[144,128]{1,0:T(8,128)S(1)} collective-permute-done((f32[144,128]{1,0:T(8,128)S(1)}, f32[144,128]{1,0:T(8,128)S(1)}, u32[]{:S(2)}, u32[]{:S(2)}) %collective-permute-start.24) | collective-permute-done | bytes 73760 | tf_op jit(solution)/shard_map/ppermute | solution.py:444
  46.7 0.0 collective-permute-start.26
  46.7 0.9 %collective-permute-done.23.refs_4_ = f32[144,128]{1,0:T(8,128)S(1)} collective-permute-done((f32[144,128]{1,0:T(8,128)S(1)}, f32[144,128]{1,0:T(8,128)S(1)}, u32[]{:S(2)}, u32[]{:S(2)}) %collective-permute-start.23) | collective-permute-done | bytes 73760 | tf_op jit(solution)/shard_map/ppermute | solution.py:435
  47.7 0.0 collective-permute-start.25
  47.7 0.5 collective-permute-start.22
  48.2 0.7 %collective-permute-done.25.refs_6_ = f32[144,128]{1,0:T(8,128)S(1)} collective-permute-done((f32[144,128]{1,0:T(8,128)S(1)}, f32[144,128]{1,0:T(8,128)S(1)}, u32[]{:S(2)}, u32[]{:S(2)}) %collective-permute-start.25) | collective-permute-done | bytes 73760 | tf_op jit(solution)/shard_map/ppermute | solution.py:435
  48.9 0.2 collective-permute-done.22.refs_3_
  49.1 2.0 %back_kernel.1 = (f32[128,512]{1,0:T(8,128)}, f32[192,512]{1,0:T(8,128)}) custom-call(f32[144,128]{1,0:T(8,128)S(1)} %add.15.refs_0_, f32[144,128]{1,0:T(8,128)S(1)} %collective-permute-done.20.refs_1_, f32[144,128]{1,0:T(8,128)S(1)} %collective-permute-done.21.refs_2_, f32[144,128]{1,0:T(8,128)S(1)} %collective-permute-done.22.refs_3_, ...), custom_call_target="tpu_custom_call" | custom-call | flops 679477248 | tf_op jit(solution)/shard_map/back_kernel/pallas_call | solution.py:404
  51.1 0.7 %finish_kernel.1 = (f32[64,256]{1,0:T(8,128)}, f32[64,512]{1,0:T(8,128)}) custom-call(f32[64,768]{1,0:T(8,128)S(1)} %get-tuple-element.79.own_terms, f32[64,768]{1,0:T(8,128)S(1)} %collective-permute-done.19.came), custom_call_target="tpu_custom_call" | custom-call | tf_op jit(solution)/shard_map/finish_kernel/pallas_call | solution.py:404
  (19 shorter events, 0.1 us)
Async XLA Ops:
  0.6 8.7 %collective-permute-start.3 = (bf16[192,512]{1,0:T(8,128)(2,1)}, bf16[192,512]{1,0:T(8,128)(2,1)S(1)}, u32[]{:S(2)}, u32[]{:S(2)}) collective-permute-start(bf16[192,512]{1,0:T(8,128)(2,1)} %bitcast.13), channel_id=1, source_target_pairs={{0,2},{1,3},{2,0},{3,1},{4,6},{5,7},{6,4},{7,5},{8,10},{9,11},{10,... | collective-permute-start | bytes 589832 | tf_op jit(solution)/shard_map/ppermute | solution.py:435
  3.7 13.8 %copy-start.1 = (bf16[1,192,512]{2,1,0:T(8,128)(2,1)S(1)}, bf16[1,192,512]{2,1,0:T(8,128)(2,1)}, u32[]{:S(2)}) copy-start(bf16[1,192,512]{2,1,0:T(8,128)(2,1)} %param.12) | copy-start | bytes 589828
  3.7 16.1 %copy-start = (f32[128,512]{1,0:T(8,128)S(1)}, f32[128,512]{1,0:T(8,128)}, u32[]{:S(2)}) copy-start(f32[128,512]{1,0:T(8,128)} %base.1) | copy-start | bytes 786436
  5.2 9.7 %collective-permute-start = (f32[192,768]{1,0:T(8,128)S(1)}, f32[192,768]{1,0:T(8,128)S(1)}, u32[]{:S(2)}, u32[]{:S(2)}) collective-permute-start(f32[192,768]{1,0:T(8,128)S(1)} %get-tuple-element.53.x_own), channel_id=1, source_target_pairs={{0,1},{1,0},{2,3},{3,2},{4,5},{5,4},{6,7},{7,6},{8,9},{9,8},{10,11... | collective-permute-start | bytes 1769480 | tf_op jit(solution)/shard_map/ppermute | solution.py:435
  5.2 9.6 %collective-permute-start.1 = (f32[192,768]{1,0:T(8,128)S(1)}, f32[192,768]{1,0:T(8,128)S(1)}, u32[]{:S(2)}, u32[]{:S(2)}) collective-permute-start(f32[192,768]{1,0:T(8,128)S(1)} %get-tuple-element.54.k_own), channel_id=1, source_target_pairs={{0,1},{1,0},{2,3},{3,2},{4,5},{5,4},{6,7},{7,6},{8,9},{9,8},{10,11... | collective-permute-start | bytes 1769480 | tf_op jit(solution)/shard_map/ppermute | solution.py:435
  5.7 7.3 %collective-permute-start.4 = (f32[392,128]{1,0:T(8,128)S(1)}, f32[392,128]{1,0:T(8,128)S(1)}, u32[]{:S(2)}, u32[]{:S(2)}) collective-permute-start(f32[392,128]{1,0:T(8,128)S(1)} %get-tuple-element.56), channel_id=1, source_target_pairs={{0,2},{1,3},{2,0},{3,1},{4,6},{5,7},{6,4},{7,5},{8,10},{9,11},{10,... | collective-permute-start | bytes 602120 | tf_op jit(solution)/shard_map/ppermute | solution.py:435
  9.3 3.8 %collective-permute-start.5 = (bf16[192,512]{1,0:T(8,128)(2,1)S(1)}, bf16[192,512]{1,0:T(8,128)(2,1)S(1)}, u32[]{:S(2)}, u32[]{:S(2)}) collective-permute-start(bf16[192,512]{1,0:T(8,128)(2,1)S(1)} %collective-permute-done.3.g_far), channel_id=1, source_target_pairs={{0,1},{1,0},{2,3},{3,2},{4,5},{5,4},{6,7},{7,6},{8,9},{9,8},{10,11... | collective-permute-start | bytes 589832 | tf_op jit(solution)/shard_map/ppermute | solution.py:435
  9.3 8.2 %collective-permute-start.7 = (f32[400,128]{1,0:T(8,128)S(1)}, f32[400,128]{1,0:T(8,128)S(1)}, u32[]{:S(2)}, u32[]{:S(2)}) collective-permute-start(f32[400,128]{1,0:T(8,128)S(1)} %get-tuple-element.62), channel_id=1, source_target_pairs={{0,2},{1,3},{2,0},{3,1},{4,6},{5,7},{6,4},{7,5},{8,10},{9,11},{10,... | collective-permute-start | bytes 614408 | tf_op jit(solution)/shard_map/ppermute | solution.py:435
  13.1 1.7 %collective-permute-start.6 = (f32[392,128]{1,0:T(8,128)S(1)}, f32[392,128]{1,0:T(8,128)S(1)}, u32[]{:S(2)}, u32[]{:S(2)}) collective-permute-start(f32[392,128]{1,0:T(8,128)S(1)} %collective-permute-done.4.far), channel_id=1, source_target_pairs={{0,1},{1,0},{2,3},{3,2},{4,5},{5,4},{6,7},{7,6},{8,9},{9,8},{10,11... | collective-permute-start | bytes 602120 | tf_op jit(solution)/shard_map/ppermute | solution.py:435
  13.1 1.7 %collective-permute-start.2 = (bf16[192,512]{1,0:T(8,128)(2,1)S(1)}, bf16[192,512]{1,0:T(8,128)(2,1)S(1)}, u32[]{:S(2)}, u32[]{:S(2)}) collective-permute-start(bf16[192,512]{1,0:T(8,128)(2,1)S(1)} %get-tuple-element.55.g_own), channel_id=1, source_target_pairs={{0,1},{1,0},{2,3},{3,2},{4,5},{5,4},{6,7},{7,6},{8,9},{9,8},{10,11... | collective-permute-start | bytes 589832 | tf_op jit(solution)/shard_map/ppermute | solution.py:435
  17.5 2.3 %collective-permute-start.8 = (f32[400,128]{1,0:T(8,128)S(1)}, f32[400,128]{1,0:T(8,128)S(1)}, u32[]{:S(2)}, u32[]{:S(2)}) collective-permute-start(f32[400,128]{1,0:T(8,128)S(1)} %collective-permute-done.7.far), channel_id=1, source_target_pairs={{0,1},{1,0},{2,3},{3,2},{4,5},{5,4},{6,7},{7,6},{8,9},{9,8},{10,11... | collective-permute-start | bytes 614408 | tf_op jit(solution)/shard_map/ppermute | solution.py:435
  17.5 2.3 %collective-permute-start.9 = (bf16[192,512]{1,0:T(8,128)(2,1)S(1)}, bf16[192,512]{1,0:T(8,128)(2,1)S(1)}, u32[]{:S(2)}, u32[]{:S(2)}) collective-permute-start(bf16[192,512]{1,0:T(8,128)(2,1)S(1)} %bitcast.8), channel_id=1, source_target_pairs={{0,1},{1,0},{2,3},{3,2},{4,5},{5,4},{6,7},{7,6},{8,9},{9,8},{10,11... | collective-permute-start | bytes 589832 | tf_op jit(solution)/shard_map/ppermute | solution.py:435
  18.0 10.7 %collective-permute-start.10 = (bf16[192,512]{1,0:T(8,128)(2,1)S(1)}, bf16[192,512]{1,0:T(8,128)(2,1)S(1)}, u32[]{:S(2)}, u32[]{:S(2)}) collective-permute-start(bf16[192,512]{1,0:T(8,128)(2,1)S(1)} %bitcast.9), channel_id=1, source_target_pairs={{0,2},{1,3},{2,0},{3,1},{4,6},{5,7},{6,4},{7,5},{8,10},{9,11},{10,... | collective-permute-start | bytes 589832 | tf_op jit(solution)/shard_map/ppermute | solution.py:435
  23.9 5.4 %collective-permute-start.12 = (f32[144,128]{1,0:T(8,128)S(1)}, f32[144,128]{1,0:T(8,128)S(1)}, u32[]{:S(2)}, u32[]{:S(2)}) collective-permute-start(f32[144,128]{1,0:T(8,128)S(1)} %get-tuple-element.77), channel_id=1, source_target_pairs={{0,12},{4,8},{8,4},{12,0},{16,28},{20,24},{24,20},{28,16},{1,13},{... | collective-permute-start | bytes 221192 | tf_op jit(solution)/shard_map/ppermute | solution.py:438
  26.4 4.4 %collective-permute-start.13 = (f32[144,128]{1,0:T(8,128)S(1)}, f32[144,128]{1,0:T(8,128)S(1)}, u32[]{:S(2)}, u32[]{:S(2)}) collective-permute-start(f32[144,128]{1,0:T(8,128)S(1)} %get-tuple-element.77), channel_id=1, source_target_pairs={{0,4},{4,0},{8,12},{12,8},{16,20},{20,16},{24,28},{28,24},{1,5},{5... | collective-permute-start | bytes 221192 | tf_op jit(solution)/shard_map/ppermute | solution.py:438
  27.0 4.4 %collective-permute-start.14 = (f32[144,128]{1,0:T(8,128)S(1)}, f32[144,128]{1,0:T(8,128)S(1)}, u32[]{:S(2)}, u32[]{:S(2)}) collective-permute-start(f32[144,128]{1,0:T(8,128)S(1)} %get-tuple-element.74), channel_id=1, source_target_pairs={{0,8},{4,12},{8,0},{12,4},{16,24},{20,28},{24,16},{28,20},{1,9},{5... | collective-permute-start | bytes 221192 | tf_op jit(solution)/shard_map/ppermute | solution.py:438
  27.4 11.7 %collective-permute-start.17 = (f32[640,128]{1,0:T(8,128)S(1)}, f32[640,128]{1,0:T(8,128)S(1)}, u32[]{:S(2)}, u32[]{:S(2)}) collective-permute-start(f32[640,128]{1,0:T(8,128)S(1)} %get-tuple-element.84), channel_id=1, source_target_pairs={{0,2},{1,3},{2,0},{3,1},{4,6},{5,7},{6,4},{7,5},{8,10},{9,11},{10,... | collective-permute-start | bytes 983048 | tf_op jit(solution)/shard_map/ppermute | solution.py:435
  28.7 5.4 %collective-permute-start.11 = (bf16[192,512]{1,0:T(8,128)(2,1)S(1)}, bf16[192,512]{1,0:T(8,128)(2,1)S(1)}, u32[]{:S(2)}, u32[]{:S(2)}) collective-permute-start(bf16[192,512]{1,0:T(8,128)(2,1)S(1)} %collective-permute-done.10.p_far), channel_id=1, source_target_pairs={{0,1},{1,0},{2,3},{3,2},{4,5},{5,4},{6,7},{7,6},{8,9},{9,8},{10,11... | collective-permute-start | bytes 589832 | tf_op jit(solution)/shard_map/ppermute | solution.py:435
  29.3 9.9 %collective-permute-start.16 = (f32[576,128]{1,0:T(8,128)S(1)}, f32[576,128]{1,0:T(8,128)S(1)}, u32[]{:S(2)}, u32[]{:S(2)}) collective-permute-start(f32[576,128]{1,0:T(8,128)S(1)} %get-tuple-element.83), channel_id=1, source_target_pairs={{0,1},{1,0},{2,3},{3,2},{4,5},{5,4},{6,7},{7,6},{8,9},{9,8},{10,11... | collective-permute-start | bytes 884744 | tf_op jit(solution)/shard_map/ppermute | solution.py:435
  31.4 7.8 %collective-permute-start.15 = (f32[144,128]{1,0:T(8,128)S(1)}, f32[144,128]{1,0:T(8,128)S(1)}, u32[]{:S(2)}, u32[]{:S(2)}) collective-permute-start(f32[144,128]{1,0:T(8,128)S(1)} %add_add_fusion), channel_id=1, source_target_pairs={{0,16},{4,20},{8,24},{12,28},{16,0},{20,4},{24,8},{28,12},{1,17},{... | collective-permute-start | bytes 221192 | tf_op jit(solution)/shard_map/ppermute | solution.py:438
  39.2 3.6 %collective-permute-start.18 = (f32[640,128]{1,0:T(8,128)S(1)}, f32[640,128]{1,0:T(8,128)S(1)}, u32[]{:S(2)}, u32[]{:S(2)}) collective-permute-start(f32[640,128]{1,0:T(8,128)S(1)} %collective-permute-done.17.far), channel_id=1, source_target_pairs={{0,1},{1,0},{2,3},{3,2},{4,5},{5,4},{6,7},{7,6},{8,9},{9,8},{10,11... | collective-permute-start | bytes 983048 | tf_op jit(solution)/shard_map/ppermute | solution.py:435
  39.3 6.7 %collective-permute-start.20 = (f32[144,128]{1,0:T(8,128)S(1)}, f32[144,128]{1,0:T(8,128)S(1)}, u32[]{:S(2)}, u32[]{:S(2)}) collective-permute-start(f32[144,128]{1,0:T(8,128)S(1)} %add.15.refs_0_), channel_id=1, source_target_pairs={{0,4},{4,0},{8,12},{12,8},{16,20},{20,16},{24,28},{28,24},{1,5},{5... | collective-permute-start | bytes 221192 | tf_op jit(solution)/shard_map/ppermute | solution.py:438
  40.8 5.9 %collective-permute-start.24 = (f32[144,128]{1,0:T(8,128)S(1)}, f32[144,128]{1,0:T(8,128)S(1)}, u32[]{:S(2)}, u32[]{:S(2)}) collective-permute-start(f32[144,128]{1,0:T(8,128)S(1)} %add.15.refs_0_), channel_id=1, source_target_pairs={{0,6},{1,7},{2,4},{3,5},{4,2},{5,3},{6,0},{7,1},{8,14},{9,15},{10,... | collective-permute-start | bytes 221192 | tf_op jit(solution)/shard_map/ppermute | solution.py:444
  42.0 5.6 %collective-permute-start.23 = (f32[144,128]{1,0:T(8,128)S(1)}, f32[144,128]{1,0:T(8,128)S(1)}, u32[]{:S(2)}, u32[]{:S(2)}) collective-permute-start(f32[144,128]{1,0:T(8,128)S(1)} %add.15.refs_0_), channel_id=1, source_target_pairs={{0,2},{1,3},{2,0},{3,1},{4,6},{5,7},{6,4},{7,5},{8,10},{9,11},{10,... | collective-permute-start | bytes 221192 | tf_op jit(solution)/shard_map/ppermute | solution.py:435
  42.8 8.2 %collective-permute-start.19 = (f32[64,768]{1,0:T(8,128)S(1)}, f32[64,768]{1,0:T(8,128)S(1)}, u32[]{:S(2)}, u32[]{:S(2)}) collective-permute-start(f32[64,768]{1,0:T(8,128)S(1)} %get-tuple-element.88), channel_id=1, source_target_pairs={{0,28},{4,0},{8,4},{12,8},{16,12},{20,16},{24,20},{28,24},{1,29},{... | collective-permute-start | bytes 589832 | tf_op jit(solution)/shard_map/ppermute | solution.py:526
  45.0 3.2 %collective-permute-start.21 = (f32[144,128]{1,0:T(8,128)S(1)}, f32[144,128]{1,0:T(8,128)S(1)}, u32[]{:S(2)}, u32[]{:S(2)}) collective-permute-start(f32[144,128]{1,0:T(8,128)S(1)} %add.15.refs_0_), channel_id=1, source_target_pairs={{0,1},{1,0},{2,3},{3,2},{4,5},{5,4},{6,7},{7,6},{8,9},{9,8},{10,11... | collective-permute-start | bytes 221192 | tf_op jit(solution)/shard_map/ppermute | solution.py:435
  46.7 1.5 %collective-permute-start.26 = (f32[144,128]{1,0:T(8,128)S(1)}, f32[144,128]{1,0:T(8,128)S(1)}, u32[]{:S(2)}, u32[]{:S(2)}) collective-permute-start(f32[144,128]{1,0:T(8,128)S(1)} %collective-permute-done.24.refs_5_), channel_id=1, source_target_pairs={{0,1},{1,0},{2,3},{3,2},{4,5},{5,4},{6,7},{7,6},{8,9},{9,8},{10,11... | collective-permute-start | bytes 221192 | tf_op jit(solution)/shard_map/ppermute | solution.py:435
  47.7 1.3 %collective-permute-start.25 = (f32[144,128]{1,0:T(8,128)S(1)}, f32[144,128]{1,0:T(8,128)S(1)}, u32[]{:S(2)}, u32[]{:S(2)}) collective-permute-start(f32[144,128]{1,0:T(8,128)S(1)} %collective-permute-done.23.refs_4_), channel_id=1, source_target_pairs={{0,1},{1,0},{2,3},{3,2},{4,5},{5,4},{6,7},{7,6},{8,9},{9,8},{10,11... | collective-permute-start | bytes 221192 | tf_op jit(solution)/shard_map/ppermute | solution.py:435
  47.7 1.4 %collective-permute-start.22 = (f32[144,128]{1,0:T(8,128)S(1)}, f32[144,128]{1,0:T(8,128)S(1)}, u32[]{:S(2)}, u32[]{:S(2)}) collective-permute-start(f32[144,128]{1,0:T(8,128)S(1)} %collective-permute-done.20.refs_1_), channel_id=1, source_target_pairs={{0,1},{1,0},{2,3},{3,2},{4,5},{5,4},{6,7},{7,6},{8,9},{9,8},{10,11... | collective-permute-start | bytes 221192 | tf_op jit(solution)/shard_map/ppermute | solution.py:435

commit v16 on v15

--- a/solution.py
+++ b/solution.py
@@ -523,7 +523,7 @@
         flops=int(6 * rows * order * order),
     )
     next_terms = after(next_terms, cross)
-    came = lax.ppermute(next_terms, "tm", [(i, (i - 1) % blocks) for i in range(blocks)])
+    came = lax.ppermute(next_terms, "tm", [(i, i - 1) for i in range(1, blocks)])
     link_diag, link_cross = call(
         finish_kernel,
         [((share, link), F32), ((share, width), F32)],

time: 52 us -> 52 us (level)
  waiting for transfers between devices: 11.4 us -> 12.3 us
  starting transfers between devices: 22.5 us -> 21.7 us
    ppermute x1, starting transfers between devices: 2.18 us -> 1.28 us  [shards(): lax.ppermute(next_terms, 'tm', [(i, i - 1) for i in range(1, blocks)])]
  transfers between devices with their start and end apart: 27 -> 27, of which waited for: 11 -> 12; matrix products, arithmetic and copies ran while one was open for 0% -> 0% of each run, Pallas kernels for 30% -> 30%
where the time goes in v16:
time: 52 us; the launch traced here: 51.8 us
  starting transfers between devices  21.7 us (42%)
  Pallas kernels  16.4 us (32%)
  waiting for transfers between devices  12.3 us (24%)
  between operations  1.4 us (3%)
    pallas_call x7, Pallas kernels, call(): pl.pallas_call(kernel, out_shape=[jax.ShapeDtypeStruct(shape, dtype) for...  16.4 us
    ppermute x20, starting transfers between devices, tile_swap(): return lax.ppermute(value, 'tile', [(i, i ^ mask) for i in range(4)])  11.5 us
    ppermute x20, waiting for transfers between devices, tile_swap(): return lax.ppermute(value, 'tile', [(i, i ^ mask) for i in range(4)])  8.43 us
    ppermute x5, starting transfers between devices, block_swap(): return lax.ppermute(value, 'tm', [(i, i ^ mask) for i in range(blocks)])  7.77 us
    ppermute x5, waiting for transfers between devices, block_swap(): return lax.ppermute(value, 'tm', [(i, i ^ mask) for i in range(blocks)])  2.68 us
    ppermute x1, starting transfers between devices, shards(): lax.ppermute(next_terms, 'tm', [(i, i - 1) for i in range(1, blocks)])  1.28 us
    ppermute x1, starting transfers between devices, diagonal_swap(): return lax.ppermute(value, ('tm', 'tile'), pairs)  1.19 us
    ppermute x1, waiting for transfers between devices, diagonal_swap(): return lax.ppermute(value, ('tm', 'tile'), pairs)  1.11 us
  transfers between devices with their start and end apart: 27, of which 12 were waited for; matrix products, arithmetic and copies ran while one was open for 0% of the time, Pallas kernels for 30%

profile of v16, /device:TPU:0, one launch (start us, length us, event | category | flops | bytes accessed | tf_op | source)
XLA Modules:
  0.0 51.8 jit_solution(15305903997314545012)
XLA Ops:
  0.6 3.0 %collective-permute-start.3 = (bf16[192,512]{1,0:T(8,128)(2,1)}, bf16[192,512]{1,0:T(8,128)(2,1)S(1)}, u32[]{:S(2)}, u32[]{:S(2)}) collective-permute-start(bf16[192,512]{1,0:T(8,128)(2,1)} %bitcast.13), channel_id=1, source_target_pairs={{0,2},{1,3},{2,0},{3,1},{4,6},{5,7},{6,4},{7,5},{8,10},{9,11},{10,... | collective-permute-start | bytes 589832 | tf_op jit(solution)/shard_map/ppermute | solution.py:435
  3.7 1.5 %pack_kernel.1 = (f32[392,128]{1,0:T(8,128)S(1)}, f32[400,128]{1,0:T(8,128)S(1)}, f32[192,768]{1,0:T(8,128)S(1)}, f32[192,768]{1,0:T(8,128)S(1)}, bf16[192,512]{...) custom-call(f32[192,768]{1,0:T(8,128)} %bitcast.11, f32[192,768]{1,0:T(8,128)} %bitcast.12, ...), custom_call_target="tpu_custom_call" | custom-call | tf_op jit(solution)/shard_map/pack_kernel/pallas_call | solution.py:404
  5.2 0.1 collective-permute-start
  5.2 0.5 collective-permute-start.1
  5.7 0.0 collective-permute-start.4
  5.8 3.5 %collective-permute-done.3.g_far = bf16[192,512]{1,0:T(8,128)(2,1)S(1)} collective-permute-done((bf16[192,512]{1,0:T(8,128)(2,1)}, bf16[192,512]{1,0:T(8,128)(2,1)S(1)}, u32[]{:S(2)}, u32[]{:S(2)}) %collective-permute-start.3) | collective-permute-done | bytes 196640 | tf_op jit(solution)/shard_map/ppermute | solution.py:435
  9.3 2.4 %collective-permute-start.7 = (f32[400,128]{1,0:T(8,128)S(1)}, f32[400,128]{1,0:T(8,128)S(1)}, u32[]{:S(2)}, u32[]{:S(2)}) collective-permute-start(f32[400,128]{1,0:T(8,128)S(1)} %get-tuple-element.62), channel_id=1, source_target_pairs={{0,2},{1,3},{2,0},{3,1},{4,6},{5,7},{6,4},{7,5},{8,10},{9,11},{10,... | collective-permute-start | bytes 614408 | tf_op jit(solution)/shard_map/ppermute | solution.py:435
  11.7 1.4 %collective-permute-done.4.far = f32[392,128]{1,0:T(8,128)S(1)} collective-permute-done((f32[392,128]{1,0:T(8,128)S(1)}, f32[392,128]{1,0:T(8,128)S(1)}, u32[]{:S(2)}, u32[]{:S(2)}) %collective-permute-start.4) | collective-permute-done | bytes 200736 | tf_op jit(solution)/shard_map/ppermute | solution.py:435
  13.1 0.5 collective-permute-start.2
  14.2 0.6 %collective-permute-done.2.g_core = bf16[192,512]{1,0:T(8,128)(2,1)S(1)} collective-permute-done((bf16[192,512]{1,0:T(8,128)(2,1)S(1)}, bf16[192,512]{1,0:T(8,128)(2,1)S(1)}, u32[]{:S(2)}, u32[]{:S(2)}) %collective-permute-start.2) | collective-permute-done | bytes 196640 | tf_op jit(solution)/shard_map/ppermute | solution.py:435
  14.8 0.0 collective-permute-done.x_core
  14.8 0.0 collective-permute-done.1.k_core
  14.8 2.0 %prepare_kernel.1 = (bf16[1536,768]{1,0:T(8,128)(2,1)S(1)}, bf16[1536,768]{1,0:T(8,128)(2,1)S(1)}, bf16[768,512]{1,0:T(8,128)(2,1)S(1)}, f32[768,1]{1,0:T(8,128)...) custom-call(s32[1]{0:T(128)S(6)} %copy.15.sizes, ...), custom_call_target="tpu_custom_call" | custom-call | tf_op jit(solution)/shard_map/prepare_kernel/pallas_call | solution.py:404
  16.8 0.6 %collective-permute-done.7.far = f32[400,128]{1,0:T(8,128)S(1)} collective-permute-done((f32[400,128]{1,0:T(8,128)S(1)}, f32[400,128]{1,0:T(8,128)S(1)}, u32[]{:S(2)}, u32[]{:S(2)}) %collective-permute-start.7) | collective-permute-done | bytes 204832 | tf_op jit(solution)/shard_map/ppermute | solution.py:435
  17.5 0.5 collective-permute-start.9
  18.0 1.7 %collective-permute-start.10 = (bf16[192,512]{1,0:T(8,128)(2,1)S(1)}, bf16[192,512]{1,0:T(8,128)(2,1)S(1)}, u32[]{:S(2)}, u32[]{:S(2)}) collective-permute-start(bf16[192,512]{1,0:T(8,128)(2,1)S(1)} %bitcast.9), channel_id=1, source_target_pairs={{0,2},{1,3},{2,0},{3,1},{4,6},{5,7},{6,4},{7,5},{8,10},{9,11},{10,... | collective-permute-start | bytes 589832 | tf_op jit(solution)/shard_map/ppermute | solution.py:435
  19.7 4.1 %global_kernel.1 = (f32[144,128]{1,0:T(8,128)S(1)}, f32[144,128]{1,0:T(8,128)S(1)}, f32[192,128]{1,0:T(8,128)S(1)}, f32[576,128]{1,0:T(8,128)S(1)}, f32[640,128]...) custom-call(f32[1,768]{1,0:T(1,128)S(1)} %get-tuple-element.67.live, ...), custom_call_target="tpu_custom_call", output_to_operand_aliasing={{5}: (4, {})} | custom-call | tf_op jit(solution)/shard_map/global_kernel/pallas_call | solution.py:404
  23.9 2.6 %collective-permute-start.12 = (f32[144,128]{1,0:T(8,128)S(1)}, f32[144,128]{1,0:T(8,128)S(1)}, u32[]{:S(2)}, u32[]{:S(2)}) collective-permute-start(f32[144,128]{1,0:T(8,128)S(1)} %get-tuple-element.77), channel_id=1, source_target_pairs={{0,12},{4,8},{8,4},{12,0},{16,28},{20,24},{24,20},{28,16},{1,13},{... | collective-permute-start | bytes 221192 | tf_op jit(solution)/shard_map/ppermute | solution.py:438
  26.4 0.5 %collective-permute-start.13 = (f32[144,128]{1,0:T(8,128)S(1)}, f32[144,128]{1,0:T(8,128)S(1)}, u32[]{:S(2)}, u32[]{:S(2)}) collective-permute-start(f32[144,128]{1,0:T(8,128)S(1)} %get-tuple-element.77), channel_id=1, source_target_pairs={{0,4},{4,0},{8,12},{12,8},{16,20},{20,16},{24,28},{28,24},{1,5},{5... | collective-permute-start | bytes 221192 | tf_op jit(solution)/shard_map/ppermute | solution.py:438
  27.0 0.4 collective-permute-start.14
  27.4 1.2 %collective-permute-start.17 = (f32[640,128]{1,0:T(8,128)S(1)}, f32[640,128]{1,0:T(8,128)S(1)}, u32[]{:S(2)}, u32[]{:S(2)}) collective-permute-start(f32[640,128]{1,0:T(8,128)S(1)} %get-tuple-element.84), channel_id=1, source_target_pairs={{0,2},{1,3},{2,0},{3,1},{4,6},{5,7},{6,4},{7,5},{8,10},{9,11},{10,... | collective-permute-start | bytes 983048 | tf_op jit(solution)/shard_map/ppermute | solution.py:435
  28.7 0.0 collective-permute-done.10.p_far
  28.7 0.0 collective-permute-start.11
  28.7 0.6 %collective-permute-done.12 = f32[144,128]{1,0:T(8,128)S(1)} collective-permute-done((f32[144,128]{1,0:T(8,128)S(1)}, f32[144,128]{1,0:T(8,128)S(1)}, u32[]{:S(2)}, u32[]{:S(2)}) %collective-permute-start.12) | collective-permute-done | bytes 73760 | tf_op jit(solution)/shard_map/ppermute | solution.py:438
  29.3 0.0 collective-permute-start.16
  29.3 1.5 %collective-permute-done.13 = f32[144,128]{1,0:T(8,128)S(1)} collective-permute-done((f32[144,128]{1,0:T(8,128)S(1)}, f32[144,128]{1,0:T(8,128)S(1)}, u32[]{:S(2)}, u32[]{:S(2)}) %collective-permute-start.13) | collective-permute-done | bytes 73760 | tf_op jit(solution)/shard_map/ppermute | solution.py:438
  30.8 0.5 %collective-permute-done.14 = f32[144,128]{1,0:T(8,128)S(1)} collective-permute-done((f32[144,128]{1,0:T(8,128)S(1)}, f32[144,128]{1,0:T(8,128)S(1)}, u32[]{:S(2)}, u32[]{:S(2)}) %collective-permute-start.14) | collective-permute-done | bytes 73760 | tf_op jit(solution)/shard_map/ppermute | solution.py:438
  31.4 2.7 %collective-permute-start.15 = (f32[144,128]{1,0:T(8,128)S(1)}, f32[144,128]{1,0:T(8,128)S(1)}, u32[]{:S(2)}, u32[]{:S(2)}) collective-permute-start(f32[144,128]{1,0:T(8,128)S(1)} %add_add_fusion), channel_id=1, source_target_pairs={{0,16},{4,20},{8,24},{12,28},{16,0},{20,4},{24,8},{28,12},{1,17},{... | collective-permute-start | bytes 221192 | tf_op jit(solution)/shard_map/ppermute | solution.py:438
  34.0 0.0 collective-permute-done.11.p_cross
  34.0 5.2 %pair_kernel.1 = (f32[64,768]{1,0:T(8,128)S(1)}, f32[64,256]{1,0:T(8,128)}, f32[64,768]{1,0:T(8,128)S(1)}) custom-call(f32[768,1]{1,0:T(8,128)S(1)} %get-tuple-element.61.live, bf16[192,512]{1,0:T(8,128)(2,1)S(1)} %bitcast.10, bf16[192,512]{1,0:T(8,128)(2,1)S(1)} %collective-permute-done.9.p_core, bf16[192,512]{1,0:T(8,128)(2,1)S(1)} %collective-permute-done.10.p_far, ...), custom_call_target="tpu_custom_call" | custom-call | tf_op jit(solution)/shard_map/pair_kernel/pallas_call | solution.py:404
  39.2 0.0 collective-permute-done.17.far
  39.2 0.1 collective-permute-start.18
  39.3 1.6 %collective-permute-start.20 = (f32[144,128]{1,0:T(8,128)S(1)}, f32[144,128]{1,0:T(8,128)S(1)}, u32[]{:S(2)}, u32[]{:S(2)}) collective-permute-start(f32[144,128]{1,0:T(8,128)S(1)} %add.15.refs_0_), channel_id=1, source_target_pairs={{0,4},{4,0},{8,12},{12,8},{16,20},{20,16},{24,28},{28,24},{1,5},{5... | collective-permute-start | bytes 221192 | tf_op jit(solution)/shard_map/ppermute | solution.py:438
  40.8 1.2 %collective-permute-start.24 = (f32[144,128]{1,0:T(8,128)S(1)}, f32[144,128]{1,0:T(8,128)S(1)}, u32[]{:S(2)}, u32[]{:S(2)}) collective-permute-start(f32[144,128]{1,0:T(8,128)S(1)} %add.15.refs_0_), channel_id=1, source_target_pairs={{0,6},{1,7},{2,4},{3,5},{4,2},{5,3},{6,0},{7,1},{8,14},{9,15},{10,... | collective-permute-start | bytes 221192 | tf_op jit(solution)/shard_map/ppermute | solution.py:444
  42.0 0.8 %collective-permute-start.23 = (f32[144,128]{1,0:T(8,128)S(1)}, f32[144,128]{1,0:T(8,128)S(1)}, u32[]{:S(2)}, u32[]{:S(2)}) collective-permute-start(f32[144,128]{1,0:T(8,128)S(1)} %add.15.refs_0_), channel_id=1, source_target_pairs={{0,2},{1,3},{2,0},{3,1},{4,6},{5,7},{6,4},{7,5},{8,10},{9,11},{10,... | collective-permute-start | bytes 221192 | tf_op jit(solution)/shard_map/ppermute | solution.py:435
  42.8 1.3 %collective-permute-start.19 = (f32[64,768]{1,0:T(8,128)S(1)}, f32[64,768]{1,0:T(8,128)S(1)}, u32[]{:S(2)}, u32[]{:S(2)}) collective-permute-start(f32[64,768]{1,0:T(8,128)S(1)} %get-tuple-element.88), channel_id=1, source_target_pairs={{4,0},{8,4},{12,8},{16,12},{20,16},{24,20},{28,24},{5,1},{9,5},{13... | collective-permute-start | bytes 589832 | tf_op jit(solution)/shard_map/ppermute | solution.py:526
  44.1 0.1 collective-permute-start.21
  44.2 1.0 %start_kernel.1 = (bf16[512,1024]{1,0:T(8,128)(2,1)S(1)}, f32[192,512]{1,0:T(8,128)S(1)}) custom-call(f32[512,128]{1,0:T(8,128)S(1)} %get-tuple-element.73.s_own, f32[192,128]{1,0:T(8,128)S(1)} %get-tuple-element.92.y_own, f32[576,128]{1,0:T(8,128)S(1)} %collective-permute-done.16.y_core, f32[640,128]{1,0:T(8,128)S(1)} %collective-permute-done.17.far, ...), custom_call_target="tpu_custom_call" | custom-call | tf_op jit(solution)/shard_map/start_kernel/pallas_call | solution.py:404
  45.2 1.1 %collective-permute-done.24.refs_5_ = f32[144,128]{1,0:T(8,128)S(1)} collective-permute-done((f32[144,128]{1,0:T(8,128)S(1)}, f32[144,128]{1,0:T(8,128)S(1)}, u32[]{:S(2)}, u32[]{:S(2)}) %collective-permute-start.24) | collective-permute-done | bytes 73760 | tf_op jit(solution)/shard_map/ppermute | solution.py:444
  46.3 0.0 collective-permute-start.26
  46.3 1.4 %collective-permute-done.23.refs_4_ = f32[144,128]{1,0:T(8,128)S(1)} collective-permute-done((f32[144,128]{1,0:T(8,128)S(1)}, f32[144,128]{1,0:T(8,128)S(1)}, u32[]{:S(2)}, u32[]{:S(2)}) %collective-permute-start.23) | collective-permute-done | bytes 73760 | tf_op jit(solution)/shard_map/ppermute | solution.py:435
  47.7 0.0 collective-permute-start.25
  47.7 0.5 collective-permute-start.22
  48.2 0.7 %collective-permute-done.25.refs_6_ = f32[144,128]{1,0:T(8,128)S(1)} collective-permute-done((f32[144,128]{1,0:T(8,128)S(1)}, f32[144,128]{1,0:T(8,128)S(1)}, u32[]{:S(2)}, u32[]{:S(2)}) %collective-permute-start.25) | collective-permute-done | bytes 73760 | tf_op jit(solution)/shard_map/ppermute | solution.py:435
  48.9 0.2 collective-permute-done.22.refs_3_
  49.1 2.0 %back_kernel.1 = (f32[128,512]{1,0:T(8,128)}, f32[192,512]{1,0:T(8,128)}) custom-call(f32[144,128]{1,0:T(8,128)S(1)} %add.15.refs_0_, f32[144,128]{1,0:T(8,128)S(1)} %collective-permute-done.20.refs_1_, f32[144,128]{1,0:T(8,128)S(1)} %collective-permute-done.21.refs_2_, f32[144,128]{1,0:T(8,128)S(1)} %collective-permute-done.22.refs_3_, ...), custom_call_target="tpu_custom_call" | custom-call | flops 679477248 | tf_op jit(solution)/shard_map/back_kernel/pallas_call | solution.py:404
  51.1 0.1 collective-permute-done.19.came
  51.1 0.7 %finish_kernel.1 = (f32[64,256]{1,0:T(8,128)}, f32[64,512]{1,0:T(8,128)}) custom-call(f32[64,768]{1,0:T(8,128)S(1)} %get-tuple-element.79.own_terms, f32[64,768]{1,0:T(8,128)S(1)} %collective-permute-done.19.came), custom_call_target="tpu_custom_call" | custom-call | tf_op jit(solution)/shard_map/finish_kernel/pallas_call | solution.py:404
  (19 shorter events, 0.1 us)
Async XLA Ops:
  0.6 8.7 %collective-permute-start.3 = (bf16[192,512]{1,0:T(8,128)(2,1)}, bf16[192,512]{1,0:T(8,128)(2,1)S(1)}, u32[]{:S(2)}, u32[]{:S(2)}) collective-permute-start(bf16[192,512]{1,0:T(8,128)(2,1)} %bitcast.13), channel_id=1, source_target_pairs={{0,2},{1,3},{2,0},{3,1},{4,6},{5,7},{6,4},{7,5},{8,10},{9,11},{10,... | collective-permute-start | bytes 589832 | tf_op jit(solution)/shard_map/ppermute | solution.py:435
  3.7 13.8 %copy-start.1 = (bf16[1,192,512]{2,1,0:T(8,128)(2,1)S(1)}, bf16[1,192,512]{2,1,0:T(8,128)(2,1)}, u32[]{:S(2)}) copy-start(bf16[1,192,512]{2,1,0:T(8,128)(2,1)} %param.12) | copy-start | bytes 589828
  3.7 16.1 %copy-start = (f32[128,512]{1,0:T(8,128)S(1)}, f32[128,512]{1,0:T(8,128)}, u32[]{:S(2)}) copy-start(f32[128,512]{1,0:T(8,128)} %base.1) | copy-start | bytes 786436
  5.2 9.7 %collective-permute-start = (f32[192,768]{1,0:T(8,128)S(1)}, f32[192,768]{1,0:T(8,128)S(1)}, u32[]{:S(2)}, u32[]{:S(2)}) collective-permute-start(f32[192,768]{1,0:T(8,128)S(1)} %get-tuple-element.53.x_own), channel_id=1, source_target_pairs={{0,1},{1,0},{2,3},{3,2},{4,5},{5,4},{6,7},{7,6},{8,9},{9,8},{10,11... | collective-permute-start | bytes 1769480 | tf_op jit(solution)/shard_map/ppermute | solution.py:435
  5.2 9.6 %collective-permute-start.1 = (f32[192,768]{1,0:T(8,128)S(1)}, f32[192,768]{1,0:T(8,128)S(1)}, u32[]{:S(2)}, u32[]{:S(2)}) collective-permute-start(f32[192,768]{1,0:T(8,128)S(1)} %get-tuple-element.54.k_own), channel_id=1, source_target_pairs={{0,1},{1,0},{2,3},{3,2},{4,5},{5,4},{6,7},{7,6},{8,9},{9,8},{10,11... | collective-permute-start | bytes 1769480 | tf_op jit(solution)/shard_map/ppermute | solution.py:435
  5.7 7.3 %collective-permute-start.4 = (f32[392,128]{1,0:T(8,128)S(1)}, f32[392,128]{1,0:T(8,128)S(1)}, u32[]{:S(2)}, u32[]{:S(2)}) collective-permute-start(f32[392,128]{1,0:T(8,128)S(1)} %get-tuple-element.56), channel_id=1, source_target_pairs={{0,2},{1,3},{2,0},{3,1},{4,6},{5,7},{6,4},{7,5},{8,10},{9,11},{10,... | collective-permute-start | bytes 602120 | tf_op jit(solution)/shard_map/ppermute | solution.py:435
  9.3 3.8 %collective-permute-start.5 = (bf16[192,512]{1,0:T(8,128)(2,1)S(1)}, bf16[192,512]{1,0:T(8,128)(2,1)S(1)}, u32[]{:S(2)}, u32[]{:S(2)}) collective-permute-start(bf16[192,512]{1,0:T(8,128)(2,1)S(1)} %collective-permute-done.3.g_far), channel_id=1, source_target_pairs={{0,1},{1,0},{2,3},{3,2},{4,5},{5,4},{6,7},{7,6},{8,9},{9,8},{10,11... | collective-permute-start | bytes 589832 | tf_op jit(solution)/shard_map/ppermute | solution.py:435
  9.3 8.2 %collective-permute-start.7 = (f32[400,128]{1,0:T(8,128)S(1)}, f32[400,128]{1,0:T(8,128)S(1)}, u32[]{:S(2)}, u32[]{:S(2)}) collective-permute-start(f32[400,128]{1,0:T(8,128)S(1)} %get-tuple-element.62), channel_id=1, source_target_pairs={{0,2},{1,3},{2,0},{3,1},{4,6},{5,7},{6,4},{7,5},{8,10},{9,11},{10,... | collective-permute-start | bytes 614408 | tf_op jit(solution)/shard_map/ppermute | solution.py:435
  13.1 1.7 %collective-permute-start.6 = (f32[392,128]{1,0:T(8,128)S(1)}, f32[392,128]{1,0:T(8,128)S(1)}, u32[]{:S(2)}, u32[]{:S(2)}) collective-permute-start(f32[392,128]{1,0:T(8,128)S(1)} %collective-permute-done.4.far), channel_id=1, source_target_pairs={{0,1},{1,0},{2,3},{3,2},{4,5},{5,4},{6,7},{7,6},{8,9},{9,8},{10,11... | collective-permute-start | bytes 602120 | tf_op jit(solution)/shard_map/ppermute | solution.py:435
  13.1 1.7 %collective-permute-start.2 = (bf16[192,512]{1,0:T(8,128)(2,1)S(1)}, bf16[192,512]{1,0:T(8,128)(2,1)S(1)}, u32[]{:S(2)}, u32[]{:S(2)}) collective-permute-start(bf16[192,512]{1,0:T(8,128)(2,1)S(1)} %get-tuple-element.55.g_own), channel_id=1, source_target_pairs={{0,1},{1,0},{2,3},{3,2},{4,5},{5,4},{6,7},{7,6},{8,9},{9,8},{10,11... | collective-permute-start | bytes 589832 | tf_op jit(solution)/shard_map/ppermute | solution.py:435
  17.5 2.3 %collective-permute-start.8 = (f32[400,128]{1,0:T(8,128)S(1)}, f32[400,128]{1,0:T(8,128)S(1)}, u32[]{:S(2)}, u32[]{:S(2)}) collective-permute-start(f32[400,128]{1,0:T(8,128)S(1)} %collective-permute-done.7.far), channel_id=1, source_target_pairs={{0,1},{1,0},{2,3},{3,2},{4,5},{5,4},{6,7},{7,6},{8,9},{9,8},{10,11... | collective-permute-start | bytes 614408 | tf_op jit(solution)/shard_map/ppermute | solution.py:435
  17.5 2.3 %collective-permute-start.9 = (bf16[192,512]{1,0:T(8,128)(2,1)S(1)}, bf16[192,512]{1,0:T(8,128)(2,1)S(1)}, u32[]{:S(2)}, u32[]{:S(2)}) collective-permute-start(bf16[192,512]{1,0:T(8,128)(2,1)S(1)} %bitcast.8), channel_id=1, source_target_pairs={{0,1},{1,0},{2,3},{3,2},{4,5},{5,4},{6,7},{7,6},{8,9},{9,8},{10,11... | collective-permute-start | bytes 589832 | tf_op jit(solution)/shard_map/ppermute | solution.py:435
  18.0 10.7 %collective-permute-start.10 = (bf16[192,512]{1,0:T(8,128)(2,1)S(1)}, bf16[192,512]{1,0:T(8,128)(2,1)S(1)}, u32[]{:S(2)}, u32[]{:S(2)}) collective-permute-start(bf16[192,512]{1,0:T(8,128)(2,1)S(1)} %bitcast.9), channel_id=1, source_target_pairs={{0,2},{1,3},{2,0},{3,1},{4,6},{5,7},{6,4},{7,5},{8,10},{9,11},{10,... | collective-permute-start | bytes 589832 | tf_op jit(solution)/shard_map/ppermute | solution.py:435
  23.9 5.4 %collective-permute-start.12 = (f32[144,128]{1,0:T(8,128)S(1)}, f32[144,128]{1,0:T(8,128)S(1)}, u32[]{:S(2)}, u32[]{:S(2)}) collective-permute-start(f32[144,128]{1,0:T(8,128)S(1)} %get-tuple-element.77), channel_id=1, source_target_pairs={{0,12},{4,8},{8,4},{12,0},{16,28},{20,24},{24,20},{28,16},{1,13},{... | collective-permute-start | bytes 221192 | tf_op jit(solution)/shard_map/ppermute | solution.py:438
  26.4 4.4 %collective-permute-start.13 = (f32[144,128]{1,0:T(8,128)S(1)}, f32[144,128]{1,0:T(8,128)S(1)}, u32[]{:S(2)}, u32[]{:S(2)}) collective-permute-start(f32[144,128]{1,0:T(8,128)S(1)} %get-tuple-element.77), channel_id=1, source_target_pairs={{0,4},{4,0},{8,12},{12,8},{16,20},{20,16},{24,28},{28,24},{1,5},{5... | collective-permute-start | bytes 221192 | tf_op jit(solution)/shard_map/ppermute | solution.py:438
  27.0 4.4 %collective-permute-start.14 = (f32[144,128]{1,0:T(8,128)S(1)}, f32[144,128]{1,0:T(8,128)S(1)}, u32[]{:S(2)}, u32[]{:S(2)}) collective-permute-start(f32[144,128]{1,0:T(8,128)S(1)} %get-tuple-element.74), channel_id=1, source_target_pairs={{0,8},{4,12},{8,0},{12,4},{16,24},{20,28},{24,16},{28,20},{1,9},{5... | collective-permute-start | bytes 221192 | tf_op jit(solution)/shard_map/ppermute | solution.py:438
  27.4 11.7 %collective-permute-start.17 = (f32[640,128]{1,0:T(8,128)S(1)}, f32[640,128]{1,0:T(8,128)S(1)}, u32[]{:S(2)}, u32[]{:S(2)}) collective-permute-start(f32[640,128]{1,0:T(8,128)S(1)} %get-tuple-element.84), channel_id=1, source_target_pairs={{0,2},{1,3},{2,0},{3,1},{4,6},{5,7},{6,4},{7,5},{8,10},{9,11},{10,... | collective-permute-start | bytes 983048 | tf_op jit(solution)/shard_map/ppermute | solution.py:435
  28.7 5.4 %collective-permute-start.11 = (bf16[192,512]{1,0:T(8,128)(2,1)S(1)}, bf16[192,512]{1,0:T(8,128)(2,1)S(1)}, u32[]{:S(2)}, u32[]{:S(2)}) collective-permute-start(bf16[192,512]{1,0:T(8,128)(2,1)S(1)} %collective-permute-done.10.p_far), channel_id=1, source_target_pairs={{0,1},{1,0},{2,3},{3,2},{4,5},{5,4},{6,7},{7,6},{8,9},{9,8},{10,11... | collective-permute-start | bytes 589832 | tf_op jit(solution)/shard_map/ppermute | solution.py:435
  29.3 9.9 %collective-permute-start.16 = (f32[576,128]{1,0:T(8,128)S(1)}, f32[576,128]{1,0:T(8,128)S(1)}, u32[]{:S(2)}, u32[]{:S(2)}) collective-permute-start(f32[576,128]{1,0:T(8,128)S(1)} %get-tuple-element.83), channel_id=1, source_target_pairs={{0,1},{1,0},{2,3},{3,2},{4,5},{5,4},{6,7},{7,6},{8,9},{9,8},{10,11... | collective-permute-start | bytes 884744 | tf_op jit(solution)/shard_map/ppermute | solution.py:435
  31.4 7.8 %collective-permute-start.15 = (f32[144,128]{1,0:T(8,128)S(1)}, f32[144,128]{1,0:T(8,128)S(1)}, u32[]{:S(2)}, u32[]{:S(2)}) collective-permute-start(f32[144,128]{1,0:T(8,128)S(1)} %add_add_fusion), channel_id=1, source_target_pairs={{0,16},{4,20},{8,24},{12,28},{16,0},{20,4},{24,8},{28,12},{1,17},{... | collective-permute-start | bytes 221192 | tf_op jit(solution)/shard_map/ppermute | solution.py:438
  39.2 3.6 %collective-permute-start.18 = (f32[640,128]{1,0:T(8,128)S(1)}, f32[640,128]{1,0:T(8,128)S(1)}, u32[]{:S(2)}, u32[]{:S(2)}) collective-permute-start(f32[640,128]{1,0:T(8,128)S(1)} %collective-permute-done.17.far), channel_id=1, source_target_pairs={{0,1},{1,0},{2,3},{3,2},{4,5},{5,4},{6,7},{7,6},{8,9},{9,8},{10,11... | collective-permute-start | bytes 983048 | tf_op jit(solution)/shard_map/ppermute | solution.py:435
  39.3 5.9 %collective-permute-start.20 = (f32[144,128]{1,0:T(8,128)S(1)}, f32[144,128]{1,0:T(8,128)S(1)}, u32[]{:S(2)}, u32[]{:S(2)}) collective-permute-start(f32[144,128]{1,0:T(8,128)S(1)} %add.15.refs_0_), channel_id=1, source_target_pairs={{0,4},{4,0},{8,12},{12,8},{16,20},{20,16},{24,28},{28,24},{1,5},{5... | collective-permute-start | bytes 221192 | tf_op jit(solution)/shard_map/ppermute | solution.py:438
  40.8 5.5 %collective-permute-start.24 = (f32[144,128]{1,0:T(8,128)S(1)}, f32[144,128]{1,0:T(8,128)S(1)}, u32[]{:S(2)}, u32[]{:S(2)}) collective-permute-start(f32[144,128]{1,0:T(8,128)S(1)} %add.15.refs_0_), channel_id=1, source_target_pairs={{0,6},{1,7},{2,4},{3,5},{4,2},{5,3},{6,0},{7,1},{8,14},{9,15},{10,... | collective-permute-start | bytes 221192 | tf_op jit(solution)/shard_map/ppermute | solution.py:444
  42.0 5.6 %collective-permute-start.23 = (f32[144,128]{1,0:T(8,128)S(1)}, f32[144,128]{1,0:T(8,128)S(1)}, u32[]{:S(2)}, u32[]{:S(2)}) collective-permute-start(f32[144,128]{1,0:T(8,128)S(1)} %add.15.refs_0_), channel_id=1, source_target_pairs={{0,2},{1,3},{2,0},{3,1},{4,6},{5,7},{6,4},{7,5},{8,10},{9,11},{10,... | collective-permute-start | bytes 221192 | tf_op jit(solution)/shard_map/ppermute | solution.py:435
  42.8 8.3 %collective-permute-start.19 = (f32[64,768]{1,0:T(8,128)S(1)}, f32[64,768]{1,0:T(8,128)S(1)}, u32[]{:S(2)}, u32[]{:S(2)}) collective-permute-start(f32[64,768]{1,0:T(8,128)S(1)} %get-tuple-element.88), channel_id=1, source_target_pairs={{4,0},{8,4},{12,8},{16,12},{20,16},{24,20},{28,24},{5,1},{9,5},{13... | collective-permute-start | bytes 589832 | tf_op jit(solution)/shard_map/ppermute | solution.py:526
  44.1 4.0 %collective-permute-start.21 = (f32[144,128]{1,0:T(8,128)S(1)}, f32[144,128]{1,0:T(8,128)S(1)}, u32[]{:S(2)}, u32[]{:S(2)}) collective-permute-start(f32[144,128]{1,0:T(8,128)S(1)} %add.15.refs_0_), channel_id=1, source_target_pairs={{0,1},{1,0},{2,3},{3,2},{4,5},{5,4},{6,7},{7,6},{8,9},{9,8},{10,11... | collective-permute-start | bytes 221192 | tf_op jit(solution)/shard_map/ppermute | solution.py:435
  46.3 1.9 %collective-permute-start.26 = (f32[144,128]{1,0:T(8,128)S(1)}, f32[144,128]{1,0:T(8,128)S(1)}, u32[]{:S(2)}, u32[]{:S(2)}) collective-permute-start(f32[144,128]{1,0:T(8,128)S(1)} %collective-permute-done.24.refs_5_), channel_id=1, source_target_pairs={{0,1},{1,0},{2,3},{3,2},{4,5},{5,4},{6,7},{7,6},{8,9},{9,8},{10,11... | collective-permute-start | bytes 221192 | tf_op jit(solution)/shard_map/ppermute | solution.py:435
  47.7 1.3 %collective-permute-start.25 = (f32[144,128]{1,0:T(8,128)S(1)}, f32[144,128]{1,0:T(8,128)S(1)}, u32[]{:S(2)}, u32[]{:S(2)}) collective-permute-start(f32[144,128]{1,0:T(8,128)S(1)} %collective-permute-done.23.refs_4_), channel_id=1, source_target_pairs={{0,1},{1,0},{2,3},{3,2},{4,5},{5,4},{6,7},{7,6},{8,9},{9,8},{10,11... | collective-permute-start | bytes 221192 | tf_op jit(solution)/shard_map/ppermute | solution.py:435
  47.7 1.4 %collective-permute-start.22 = (f32[144,128]{1,0:T(8,128)S(1)}, f32[144,128]{1,0:T(8,128)S(1)}, u32[]{:S(2)}, u32[]{:S(2)}) collective-permute-start(f32[144,128]{1,0:T(8,128)S(1)} %collective-permute-done.20.refs_1_), channel_id=1, source_target_pairs={{0,1},{1,0},{2,3},{3,2},{4,5},{5,4},{6,7},{7,6},{8,9},{9,8},{10,11... | collective-permute-start | bytes 221192 | tf_op jit(solution)/shard_map/ppermute | solution.py:435
